TPU v7x, 32 devices: a whole 2x2x4 slice. The times are simulated.
32 devices in a mesh: row: 2 (over y), col: 16 (over z, x, core).
Axes of the slice: x: 2, y: 2, z: 4, core: 2. Of those that a mesh axis runs over, the one named last changes fastest.
Arguments:
- latent: bfloat16 [2, 128, 128, 320], P(None, 'row', 'col'), may hold values from -28 to 28
- timestep: int32 [2], replicated, may hold values from 0 to 999
- group_norm_gain: float32 [320], replicated, may hold values from 0.5 to 1.5
- group_norm_bias: float32 [320], replicated, may hold values from -0.5 to 0.5
- conv_w: bfloat16 [3, 3, 320, 320], replicated, may hold values from -0.109375 to 0.109375
- conv_b: float32 [320], replicated, may hold values from -0.5 to 0.5
- embed_in: bfloat16 [320, 1280], replicated, may hold values from -0.3125 to 0.3125
- embed_out: bfloat16 [1280, 1280], replicated, may hold values from -0.15625 to 0.15625
- time_w: bfloat16 [1280, 320], replicated, may hold values from -0.15625 to 0.15625
- cotangent: bfloat16 [2, 128, 128, 320], P(None, 'row', 'col'), may hold values from -6 to 6
Outputs:
- block_out: bfloat16 [2, 128, 128, 320], P(None, 'row', 'col')
- input_grad: float32 [2, 128, 128, 320], P(None, 'row', 'col')
- conv_w_grad: float32 [320, 3, 3, 320], P('row')
- gain_grad: float32 [320], replicated
- bias_grad: float32 [320], replicated
- conv_b_grad: float32 [320], replicated
- time_w_grad: float32 [1280, 320], replicated
All inputs are finite; a program needn't handle non-finite values.
Results may differ from a plain program's by a relative error of at most 0.0055.
Values may be sent and summed in bfloat16 or wider, within the bound.
No kernel may reach another device: no remote copies, remote signals or barrier semaphores. Data moves between devices by JAX's collectives and lax.ppermute only.
A program may use at most 128 MiB of HBM per device.

v0:
```python
import math

import jax
import jax.numpy as jnp
from jax import lax
from jax.sharding import PartitionSpec as P

NORM_GROUPS = 32


EPS = 1e-05


def with_halo(shard, sides, width):
    for axis, dim in sides:
        devices, length = (lax.axis_size(axis), shard.shape[dim])
        up = [(i, (i + 1) % devices) for i in range(devices - 1)]
        down = [(j, i) for i, j in up]
        last = lax.slice_in_dim(shard, length - width, length, axis=dim)
        first = lax.slice_in_dim(shard, 0, width, axis=dim)
        before = lax.ppermute(last, axis, up)
        after = lax.ppermute(first, axis, down)
        shard = jnp.concatenate([before, shard, after], axis=dim)
    return shard


def embed(timestep, embed_in, embed_out):
    half = embed_in.shape[0] // 2
    freqs = jnp.exp(-math.log(10000.0) * jnp.arange(half, dtype=jnp.float32) / half)
    angles = timestep.astype(jnp.float32)[:, None] * freqs[None, :]
    sinus = jnp.concatenate([jnp.cos(angles), jnp.sin(angles)], axis=1).astype(jnp.bfloat16)
    first_hidden = jax.nn.silu(jnp.dot(sinus, embed_in, preferred_element_type=jnp.float32)).astype(
        jnp.bfloat16
    )
    return jax.nn.silu(jnp.dot(first_hidden, embed_out, preferred_element_type=jnp.float32)).astype(
        jnp.bfloat16
    )


def local(
    latent,
    timestep,
    group_norm_gain,
    group_norm_bias,
    conv_w,
    conv_b,
    embed_in,
    embed_out,
    time_w,
    cotangent,
):
    batch_images, row_count, column_count, channel_count = latent.shape
    channels_per_group = channel_count // NORM_GROUPS
    total_rows = row_count * lax.axis_size("row")
    total_cols = column_count * lax.axis_size("col")
    count = total_rows * total_cols * channels_per_group
    scale = 1.0 / math.sqrt(batch_images * total_rows * total_cols)
    x = latent.astype(jnp.float32)
    grouped = x.reshape(batch_images, row_count, column_count, NORM_GROUPS, channels_per_group)
    first_sum, second_sum = lax.psum(
        (jnp.sum(grouped, axis=(1, 2, 4)), jnp.sum(grouped * grouped, axis=(1, 2, 4))),
        ("row", "col"),
    )
    mean = first_sum / count
    var = second_sum / count - mean * mean
    group_centered = grouped - mean[:, None, None, :, None]
    inverse_deviation = lax.rsqrt(var + EPS)
    input_standardized = (group_centered * inverse_deviation[:, None, None, :, None]).reshape(
        batch_images, row_count, column_count, channel_count
    )
    normed_output = input_standardized * group_norm_gain + group_norm_bias
    acts = jax.nn.silu(normed_output).astype(jnp.bfloat16)
    padded = with_halo(acts, (("row", 1), ("col", 2)), 1)
    conv = jnp.zeros((batch_images, row_count, column_count, channel_count), jnp.float32)
    for kh in range(3):
        for kw in range(3):
            conv = conv + jnp.einsum(
                "bhwc,cd->bhwd",
                padded[:, kh : kh + row_count, kw : kw + column_count],
                conv_w[kh, kw],
                preferred_element_type=jnp.float32,
            )
    emb = embed(timestep, embed_in, embed_out)
    temb = jnp.dot(emb, time_w, preferred_element_type=jnp.float32)
    block_out = (x + conv + conv_b + temb[:, None, None, :]).astype(jnp.bfloat16)
    gpad = with_halo(cotangent, (("row", 1), ("col", 2)), 1)
    dacts = jnp.zeros((batch_images, row_count, column_count, channel_count), jnp.float32)
    for kh in range(3):
        for kw in range(3):
            dacts = dacts + jnp.einsum(
                "bhwd,cd->bhwc",
                gpad[:, 2 - kh : 2 - kh + row_count, 2 - kw : 2 - kw + column_count],
                conv_w[kh, kw],
                preferred_element_type=jnp.float32,
            )
    share = channel_count // lax.axis_size("row")
    pieces = []
    for kh in range(3):
        for kw in range(3):
            pieces.append(
                jnp.einsum(
                    "bhwc,bhwd->dc",
                    padded[:, kh : kh + row_count, kw : kw + column_count],
                    cotangent,
                    preferred_element_type=jnp.float32,
                )
            )
    summed = lax.psum(
        jnp.stack(pieces, axis=1).reshape(channel_count, 3, 3, channel_count) * scale,
        ("row", "col"),
    )
    conv_w_grad = lax.dynamic_slice_in_dim(summed, lax.axis_index("row") * share, share, 0)
    sig = jax.nn.sigmoid(normed_output)
    normed_gradient = dacts * sig * (1.0 + normed_output * (1.0 - sig))
    grad = cotangent.astype(jnp.float32)
    first, second_moment, gsum = lax.psum(
        (
            jnp.sum(normed_gradient, axis=(1, 2)),
            jnp.sum(normed_gradient * input_standardized, axis=(1, 2)),
            jnp.sum(grad, axis=(1, 2)),
        ),
        ("row", "col"),
    )
    m_one = (
        jnp.sum(
            (group_norm_gain * first).reshape(batch_images, NORM_GROUPS, channels_per_group), axis=2
        )
        / count
    )
    m_two = (
        jnp.sum(
            (group_norm_gain * second_moment).reshape(
                batch_images, NORM_GROUPS, channels_per_group
            ),
            axis=2,
        )
        / count
    )
    dxhat = (normed_gradient * group_norm_gain).reshape(
        batch_images, row_count, column_count, NORM_GROUPS, channels_per_group
    )
    input_grouped = input_standardized.reshape(
        batch_images, row_count, column_count, NORM_GROUPS, channels_per_group
    )
    dx = inverse_deviation[:, None, None, :, None] * (
        dxhat - m_one[:, None, None, :, None] - input_grouped * m_two[:, None, None, :, None]
    )
    input_grad = grad + dx.reshape(batch_images, row_count, column_count, channel_count)
    gain_grad = jnp.sum(second_moment, axis=0) * scale
    bias_grad = jnp.sum(first, axis=0) * scale
    conv_b_grad = jnp.sum(gsum, axis=0) * scale
    time_w_grad = jnp.dot(emb.astype(jnp.float32).T, gsum) * scale
    return (block_out, input_grad, conv_w_grad, gain_grad, bias_grad, conv_b_grad, time_w_grad)


def solution(mesh):
    return jax.shard_map(
        local,
        mesh=mesh,
        in_specs=(
            P(None, "row", "col", None),
            P(),
            P(),
            P(),
            P(),
            P(),
            P(),
            P(),
            P(),
            P(None, "row", "col", None),
        ),
        out_specs=(
            P(None, "row", "col", None),
            P(None, "row", "col", None),
            P("row", None, None, None),
            P(),
            P(),
            P(),
            P(),
        ),
        check_vma=False,
    )
```

profile of v0, /device:TPU:0, one launch (start us, length us, event | category | flops | bytes accessed | tf_op | source)
XLA Modules:
  0.0 327.4 jit_solution(4224257573681596242)
XLA Ops:
  7.2 0.9 fusion.168
  8.1 5.0 %collective-permute-start.4 = (bf16[2,1,8,320]{3,2,1,0:T(8,128)(2,1)S(1)}, bf16[2,1,8,320]{3,2,1,0:T(8,128)(2,1)S(1)}, u32[]{:S(2)}, u32[]{:S(2)}) collective-permute-start(bf16[2,1,8,320]{3,2,1,0:T(8,128)(2,1)S(1)} %get-tuple-element.33), channel_id=1, source_target_pairs={{0,16},{1,17},{2,18},{3,19},{4,20},{5,21},{6,22},{7,23},{8,24},{9,... | collective-permute-start | bytes 30728 | tf_op jit(solution)/shard_map/ppermute | solution.py:21
  13.1 1.3 collective-permute-start.5
  14.4 1.4 convert_reduce_fusion
  16.2 3.0 fusion.84
  19.2 41.6 %all-reduce.1 = (f32[2,32]{1,0:T(2,128)S(1)}, f32[2,32]{1,0:T(2,128)S(1)}) all-reduce(f32[2,32]{1,0:T(2,128)S(1)} %reduce_sum.109, f32[2,32]{1,0:T(2,128)S(1)} %reduce_sum.106), channel_id=1, replica_groups=mesh['row'=2,'col'=16] {'row','col'}, use_global_device_ids=true, to_apply=%region_5.6 | all-reduce | flops 128 | bytes 1024 | tf_op jit(solution)/shard_map/psum | solution.py:60
  60.8 0.1 fusion.133
  61.0 2.0 fusion.127
  63.0 1.5 fusion.172
  64.5 1.5 convert_reduce_fusion.1
  66.4 0.2 constant_dynamic-update-slice_fusion.1
  66.5 0.3 fusion.167
  66.8 1.3 collective-permute-start.7
  68.1 1.3 collective-permute-start.6
  69.4 0.6 fusion.42
  70.1 0.6 fusion.38
  70.7 3.2 collective-permute-done.6
  74.0 0.7 fusion.60
  74.6 0.7 fusion.53
  75.3 0.7 fusion.47
  76.0 0.7 fusion.50
  76.7 1.8 fusion.56
  78.5 4.0 %fusion.164 = (f32[2,320]{1,0:T(2,128)S(1)}, f32[2,320]{1,0:T(2,128)S(1)}, f32[2,64,8,320]{3,2,1,0:T(8,128)}) fusion(f32[2,320]{1,0:T(2,128)S(1)} %mul.138, f32[2,320]{1,0:T(2,128)S(1)} %sub.38, bf16[2,64,8,320]{3,2,1,0:T(8,128)(2,1)S(1)} %copy-done.8, f32[320]{0:T(512)S(1)} %copy-done.18, f32[320]{0:T(512)S(1)} %copy-done.17, ...), kind=kOutput, calls=%fused_computation.200 | convolution fusion | flops 218888960 | bytes 13470720 | tf_op jit(solution)/shard_map/bhwd,cd->bhwc/dot_general | solution.py:90
  82.5 43.4 %all-reduce = (f32[2,320]{1,0:T(2,128)S(1)}, f32[2,320]{1,0:T(2,128)S(1)}, f32[2,320]{1,0:T(2,128)S(1)}) all-reduce(f32[2,320]{1,0:T(2,128)S(1)} %get-tuple-element.8, f32[2,320]{1,0:T(2,128)S(1)} %get-tuple-element.7, f32[2,320]{1,0:T(2,128)S(1)} %convert_reduce_fusion.1), channel_id=1, replica_groups=mesh['row'=2,'col'=16] {'row','col'}, use_global_device_ids=true, to_apply=%region_10.11 | all-reduce | flops 1920 | bytes 15360 | tf_op jit(solution)/shard_map/psum | solution.py:116
  126.7 3.5 %convert_add_fusion.1 = (f32[2,64,8,320]{3,2,1,0:T(8,128)}, bf16[2,64,8,320]{3,2,1,0:T(8,128)(2,1)S(1)}) fusion(bf16[2,64,8,320]{3,2,1,0:T(8,128)(2,1)S(1)} %copy-done.6, bf16[2,64,8,320]{3,2,1,0:T(8,128)(2,1)S(1)} %copy-done.8, f32[2,64,8,320]{3,2,1,0:T(8,128)} %get-tuple-element.44, f32[2,320]{1,0:T(2,128)S(1)} %mul.158, f32[2,320]{1,0:T(2,128)S(1)} %sub.44, ...), kind=kLoop, calls=%fused_computation.11 | loop fusion | flops 5570560 | bytes 4600320 | tf_op jit(solution)/shard_map/add | solution.py:148
  130.2 3.0 fusion.86
  133.2 1.6 convolution_multiply_fusion
  134.8 1.3 collective-permute-start.1
  136.1 4.5 %collective-permute-start = (bf16[2,1,8,320]{3,2,1,0:T(8,128)(2,1)S(1)}, bf16[2,1,8,320]{3,2,1,0:T(8,128)(2,1)S(1)}, u32[]{:S(2)}, u32[]{:S(2)}) collective-permute-start(bf16[2,1,8,320]{3,2,1,0:T(8,128)(2,1)S(1)} %get-tuple-element.34), channel_id=1, source_target_pairs={{0,16},{1,17},{2,18},{3,19},{4,20},{5,21},{6,22},{7,23},{8,24},{9,... | collective-permute-start | bytes 30728 | tf_op jit(solution)/shard_map/ppermute | solution.py:21
  140.7 0.6 broadcast_multiply_fusion.5
  141.2 0.6 broadcast_multiply_fusion.4
  141.8 0.6 broadcast_multiply_fusion.3
  142.4 0.3 pad_maximum_fusion.9
  142.7 1.3 collective-permute-start.3
  144.0 3.0 collective-permute-start.2
  147.1 2.7 fusion.34
  149.8 2.7 fusion.30
  152.5 0.1 pad_maximum_fusion.1
  152.6 2.4 pad_maximum_fusion
  155.1 3.1 fusion.79
  158.2 0.2 fusion.166
  158.4 0.9 copy-done.7
  159.3 0.5 fusion.29
  159.8 0.3 fusion.165
  160.1 0.5 fusion.28
  160.6 0.5 fusion.27
  161.2 0.5 fusion.26
  161.7 0.6 copy-done.5
  162.3 0.5 fusion.25
  162.9 0.5 fusion.24
  163.4 0.5 fusion.23
  164.0 0.5 fusion.22
  164.5 0.5 fusion.21
  165.0 2.5 broadcast_multiply_fusion
  167.5 6.0 %copy.73 = f32[320,3,3,320]{3,0,2,1:T(8,128)} copy(f32[320,3,3,320]{0,3,2,1:T(8,128)} %bitcast.184) | data formatting | bytes 7372800 | tf_op jit(solution)/shard_map/mul | solution.py:109
  173.5 1.7 fusion.82
  175.2 1.7 fusion.89
  177.0 1.7 fusion.92
  178.7 1.8 fusion.97
  180.6 0.2 copy-done.3
  180.7 0.2 copy-done.9
  181.0 3.2 fusion.20
  184.2 133.3 %all-reduce.4.cloned.1.call-done = f32[320,3,3,320]{3,0,2,1:T(8,128)} async-done(((f32[320,3,3,320]{3,0,2,1:T(8,128)}), f32[320,3,3,320]{3,0,2,1:T(8,128)}) %all-reduce.4.cloned.1.call-update) | async-done | bytes 3686416 | tf_op jit(solution)/shard_map/psum | solution.py:108
  317.5 3.1 constant_dynamic-slice_fusion
  (71 shorter events, 1.8 us)
Async XLA Ops:
  7.2 53.8 %copy-start = (bf16[1280,1280]{1,0:T(8,128)(2,1)S(1)}, bf16[1280,1280]{1,0:T(8,128)(2,1)}, u32[]{:S(2)}) copy-start(bf16[1280,1280]{1,0:T(8,128)(2,1)} %param.17) | copy-start | bytes 9830404
  7.2 310.3 %all-reduce.4.cloned.1.call-start = ((), (), s32[]{:S(2)}) async-start(), calls=%async_computation | async-start | bytes 8847360 | tf_op jit(solution)/shard_map/psum | solution.py:108
  8.1 58.2 %collective-permute-start.4 = (bf16[2,1,8,320]{3,2,1,0:T(8,128)(2,1)S(1)}, bf16[2,1,8,320]{3,2,1,0:T(8,128)(2,1)S(1)}, u32[]{:S(2)}, u32[]{:S(2)}) collective-permute-start(bf16[2,1,8,320]{3,2,1,0:T(8,128)(2,1)S(1)} %get-tuple-element.33), channel_id=1, source_target_pairs={{0,16},{1,17},{2,18},{3,19},{4,20},{5,21},{6,22},{7,23},{8,24},{9,... | collective-permute-start | bytes 30728 | tf_op jit(solution)/shard_map/ppermute | solution.py:21
  13.1 53.4 %collective-permute-start.5 = (bf16[2,1,8,320]{3,2,1,0:T(8,128)(2,1)S(1)}, bf16[2,1,8,320]{3,2,1,0:T(8,128)(2,1)S(1)}, u32[]{:S(2)}, u32[]{:S(2)}) collective-permute-start(bf16[2,1,8,320]{3,2,1,0:T(8,128)(2,1)S(1)} %get-tuple-element.32), channel_id=1, source_target_pairs={{16,0},{17,1},{18,2},{19,3},{20,4},{21,5},{22,6},{23,7},{24,8},{25... | collective-permute-start | bytes 30728 | tf_op jit(solution)/shard_map/ppermute | solution.py:22
  14.4 4.8 %copy-start.19 = (s32[2]{0:T(128)S(1)}, s32[2]{0:T(128)}, u32[]{:S(2)}) copy-start(s32[2]{0:T(128)} %param.11) | copy-start | bytes 28
  62.9 3.4 %copy-start.6 = (bf16[2,64,8,320]{3,2,1,0:T(8,128)(2,1)S(1)}, bf16[2,64,8,320]{3,2,1,0:T(8,128)(2,1)}, u32[]{:S(2)}) copy-start(bf16[2,64,8,320]{3,2,1,0:T(8,128)(2,1)} %param.19) | copy-start | bytes 1966084
  64.5 5.0 %copy-start.12 = (bf16[3,3,320,320]{3,2,1,0:T(8,128)(2,1)S(1)}, bf16[3,3,320,320]{3,2,1,0:T(8,128)(2,1)}, u32[]{:S(2)}) copy-start(bf16[3,3,320,320]{3,2,1,0:T(8,128)(2,1)} %param.14) | copy-start | bytes 5529604
  66.8 8.5 %collective-permute-start.7 = (bf16[2,66,1,320]{3,2,1,0:T(2,128)(2,1)S(1)}, bf16[2,66,1,320]{3,2,1,0:T(2,128)(2,1)S(1)}, u32[]{:S(2)}, u32[]{:S(2)}) collective-permute-start(bf16[2,66,1,320]{3,2,1,0:T(2,128)(2,1)S(1)} %get-tuple-element.22), channel_id=1, source_target_pairs={{0,1},{1,2},{2,3},{3,4},{4,5},{5,6},{6,7},{7,8},{8,9},{9,10},{10,1... | collective-permute-start | bytes 253448 | tf_op jit(solution)/shard_map/ppermute | solution.py:21
  68.1 5.8 %collective-permute-start.6 = (bf16[2,66,1,320]{3,2,1,0:T(2,128)(2,1)S(1)}, bf16[2,66,1,320]{3,2,1,0:T(2,128)(2,1)S(1)}, u32[]{:S(2)}, u32[]{:S(2)}) collective-permute-start(bf16[2,66,1,320]{3,2,1,0:T(2,128)(2,1)S(1)} %get-tuple-element.23), channel_id=1, source_target_pairs={{1,0},{2,1},{3,2},{4,3},{5,4},{6,5},{7,6},{8,7},{9,8},{10,9},{11,1... | collective-permute-start | bytes 253448 | tf_op jit(solution)/shard_map/ppermute | solution.py:22
  76.6 1.8 copy-start.8
  76.7 1.8 copy-start.15
  76.7 1.8 copy-start.17
  76.7 1.8 copy-start.18
  130.2 22.3 %copy-start.4 = (bf16[2,64,8,320]{3,2,1,0:T(8,128)(2,1)}, bf16[2,64,8,320]{3,2,1,0:T(8,128)(2,1)S(1)}, u32[]{:S(2)}) copy-start(bf16[2,64,8,320]{3,2,1,0:T(8,128)(2,1)S(1)} %get-tuple-element.29) | copy-start | bytes 1966084
  134.8 7.6 %collective-permute-start.1 = (bf16[2,1,8,320]{3,2,1,0:T(8,128)(2,1)S(1)}, bf16[2,1,8,320]{3,2,1,0:T(8,128)(2,1)S(1)}, u32[]{:S(2)}, u32[]{:S(2)}) collective-permute-start(bf16[2,1,8,320]{3,2,1,0:T(8,128)(2,1)S(1)} %get-tuple-element.35), channel_id=1, source_target_pairs={{16,0},{17,1},{18,2},{19,3},{20,4},{21,5},{22,6},{23,7},{24,8},{25... | collective-permute-start | bytes 30728 | tf_op jit(solution)/shard_map/ppermute | solution.py:22
  136.1 6.3 %collective-permute-start = (bf16[2,1,8,320]{3,2,1,0:T(8,128)(2,1)S(1)}, bf16[2,1,8,320]{3,2,1,0:T(8,128)(2,1)S(1)}, u32[]{:S(2)}, u32[]{:S(2)}) collective-permute-start(bf16[2,1,8,320]{3,2,1,0:T(8,128)(2,1)S(1)} %get-tuple-element.34), channel_id=1, source_target_pairs={{0,16},{1,17},{2,18},{3,19},{4,20},{5,21},{6,22},{7,23},{8,24},{9,... | collective-permute-start | bytes 30728 | tf_op jit(solution)/shard_map/ppermute | solution.py:21
  142.7 9.9 %collective-permute-start.3 = (bf16[2,66,1,320]{3,2,1,0:T(2,128)(2,1)S(1)}, bf16[2,66,1,320]{3,2,1,0:T(2,128)(2,1)S(1)}, u32[]{:S(2)}, u32[]{:S(2)}) collective-permute-start(bf16[2,66,1,320]{3,2,1,0:T(2,128)(2,1)S(1)} %get-tuple-element.26), channel_id=1, source_target_pairs={{1,0},{2,1},{3,2},{4,3},{5,4},{6,5},{7,6},{8,7},{9,8},{10,9},{11,1... | collective-permute-start | bytes 253448 | tf_op jit(solution)/shard_map/ppermute | solution.py:22
  144.0 8.6 %collective-permute-start.2 = (bf16[2,66,1,320]{3,2,1,0:T(2,128)(2,1)S(1)}, bf16[2,66,1,320]{3,2,1,0:T(2,128)(2,1)S(1)}, u32[]{:S(2)}, u32[]{:S(2)}) collective-permute-start(bf16[2,66,1,320]{3,2,1,0:T(2,128)(2,1)S(1)} %get-tuple-element.27), channel_id=1, source_target_pairs={{0,1},{1,2},{2,3},{3,4},{4,5},{5,6},{6,7},{7,8},{8,9},{9,10},{10,1... | collective-permute-start | bytes 253448 | tf_op jit(solution)/shard_map/ppermute | solution.py:21
  155.1 21.9 %copy-start.2 = (bf16[2,66,9,320]{3,2,1,0:T(8,128)(2,1)}, bf16[2,66,9,320]{3,2,1,0:T(8,128)(2,1)S(1)}, u32[]{:S(2)}) copy-start(bf16[2,66,9,320]{3,2,1,0:T(8,128)(2,1)S(1)} %get-tuple-element.24) | copy-start | bytes 2280964
  158.2 1.1 copy-start.7
  161.2 1.1 copy-start.5
  173.5 7.0 %copy-start.14 = (f32[2,64,8,320]{3,2,1,0:T(8,128)S(1)}, f32[2,64,8,320]{3,2,1,0:T(8,128)}, u32[]{:S(2)}) copy-start(f32[2,64,8,320]{3,2,1,0:T(8,128)} %fusion.30) | copy-start | bytes 3932164
  175.2 5.3 %copy-start.11 = (f32[2,64,8,320]{3,2,1,0:T(8,128)S(1)}, f32[2,64,8,320]{3,2,1,0:T(8,128)}, u32[]{:S(2)}) copy-start(f32[2,64,8,320]{3,2,1,0:T(8,128)} %fusion.79) | copy-start | bytes 3932164
  175.2 5.3 %copy-start.13 = (f32[2,64,8,320]{3,2,1,0:T(8,128)S(1)}, f32[2,64,8,320]{3,2,1,0:T(8,128)}, u32[]{:S(2)}) copy-start(f32[2,64,8,320]{3,2,1,0:T(8,128)} %fusion.34) | copy-start | bytes 3932164
  177.0 3.6 %copy-start.10 = (f32[2,64,8,320]{3,2,1,0:T(8,128)S(1)}, f32[2,64,8,320]{3,2,1,0:T(8,128)}, u32[]{:S(2)}) copy-start(f32[2,64,8,320]{3,2,1,0:T(8,128)} %fusion.86) | copy-start | bytes 3932164
  178.7 2.1 copy-start.3
  178.7 2.3 copy-start.9
  178.7 2.3 copy-start.16
  181.0 139.6 %copy-start.1 = (bf16[1280,1280]{1,0:T(8,128)(2,1)S(1)}, bf16[1280,1280]{1,0:T(8,128)(2,1)}, u32[]{:S(2)}) copy-start(bf16[1280,1280]{1,0:T(8,128)(2,1)} %param.17) | copy-start | bytes 9830404
Sparse Core Ops, SparseCore 0:
  173.7 143.7 all-reduce.3
where the time goes:
time: 328 us; the launch traced here: 327 us
  waiting for transfers between devices  137 us (42%)
  blocking collectives  85.1 us (26%)
  matrix products  44.1 us (13%)
  starting transfers between devices  19.1 us (6%)
  between operations  14.7 us (4%)
  local copies, waits for them, and re-layouts  14 us (4%)
  other arithmetic  13.9 us (4%)
    psum x1, waiting for transfers between devices, local(): lax.psum(jnp.stack(pieces, axis=1).reshape(channel_count, 3, 3, channel_c...  133 us
    psum x1, blocking collectives, local(): lax.psum((jnp.sum(normed_gradient, axis=(1, 2)), jnp.sum(normed_gradient...  43.4 us
    psum x1, blocking collectives, local(): lax.psum((jnp.sum(grouped, axis=(1, 2, 4)), jnp.sum(grouped * grouped, ax...  41.6 us
    dot_general x9, matrix products, local(): jnp.einsum('bhwc,cd->bhwd', padded[:, kh:kh + row_count, kw:kw + column_c...  21.6 us
    ppermute x4, starting transfers between devices, with_halo(): before = lax.ppermute(last, axis, up)  13.9 us
    dot_general x9, matrix products, local(): jnp.einsum('bhwd,cd->bhwc', gpad[:, 2 - kh:2 - kh + row_count, 2 - kw:2 -...  12.6 us
  transfers between devices with their start and end apart: 9, of which 2 were waited for; matrix products, arithmetic and copies ran while one was open for 9% of the time, Pallas kernels for 0%

commit v1 on v0

v1 whole, which is shorter than its diff:
```python
import functools
import math

import jax
import jax.numpy as jnp
from jax import lax
from jax.experimental import pallas as pl
from jax.experimental.pallas import tpu as pltpu
from jax.sharding import PartitionSpec as P

NORM_GROUPS = 32
EPS = 1e-05
LANES = 128
F32 = jnp.float32
BF16 = jnp.bfloat16
AXES = ("row", "col")
VMEM_LIMIT = 48 * 1024 * 1024
HI = lax.Precision.HIGHEST


def iota(shape, dim):
    return lax.broadcasted_iota(jnp.int32, shape, dim)


def call(body, out_shape, scratch=(), flops=0, transcendentals=0, nbytes=4_000_000):
    return pl.pallas_call(
        body,
        out_shape=out_shape,
        scratch_shapes=list(scratch),
        compiler_params=pltpu.CompilerParams(vmem_limit_bytes=VMEM_LIMIT),
        cost_estimate=pl.CostEstimate(
            flops=flops, bytes_accessed=nbytes, transcendentals=transcendentals
        ),
    )


def group_matrix(channels, lanes):
    size = channels // NORM_GROUPS
    group = iota((channels, lanes), 1) & (NORM_GROUPS - 1)
    channel = iota((channels, lanes), 0)
    return jnp.where((channel >= group * size) & (channel < (group + 1) * size), 1.0, 0.0).astype(F32)


def group_sums(rows):
    lanes = LANES
    g = group_matrix(rows.shape[1], lanes)
    keep = iota((8, lanes), 1) < NORM_GROUPS
    s = jnp.dot(rows, g, precision=HI, preferred_element_type=F32)
    s = jnp.where(keep, s, 0.0)
    return lax.dot_general(
        s, g, (((1,), (1,)), ((), ())), precision=HI, preferred_element_type=F32
    )


def stack_rows(rows, channels):
    r = iota((8, channels), 0)
    out = jnp.zeros((8, channels), F32)
    for k, v in enumerate(rows):
        out = out + jnp.where(r == k, v, 0.0)
    return out


def stats_kernel(batch, x_ref, pay_ref):
    n, channels = x_ref.shape
    per = n // batch
    step = 64
    rows = []
    for b in range(batch):

        def add(i, c, b=b):
            start = pl.multiple_of(b * per + i * step, 16)
            v = x_ref[pl.ds(start, step), :].astype(F32).reshape(step // 8, 8, channels)
            return c[0] + jnp.sum(v, axis=0), c[1] + jnp.sum(v * v, axis=0)

        zero = jnp.zeros((8, channels), F32)
        s, q = lax.fori_loop(0, per // step, add, (zero, zero))
        rows.append((jnp.sum(s, axis=0, keepdims=True), jnp.sum(q, axis=0, keepdims=True)))
    stacked = stack_rows([r[0] for r in rows] + [r[1] for r in rows], channels)
    lanes = pay_ref.shape[-1]
    res = jnp.dot(
        stacked, group_matrix(channels, lanes), precision=HI, preferred_element_type=F32
    )
    first = iota((8, lanes), 0) * NORM_GROUPS
    lane = iota((8, lanes), 1)
    mine = (lane >= first) & (lane < first + NORM_GROUPS)
    row = jnp.sum(jnp.where(mine, res, 0.0), axis=0, keepdims=True)
    pay_ref[...] = jnp.broadcast_to(row[None], pay_ref.shape)


def affine_rows(st_ref, gain_ref, bias_ref, batch, count):
    channels = gain_ref.shape[-1]
    lanes = st_ref.shape[-1]
    total = jnp.sum(st_ref[...], axis=0)
    first = iota((8, lanes), 0) * NORM_GROUPS
    lane = iota((8, lanes), 1)
    mine = (lane >= first) & (lane < first + NORM_GROUPS)
    spread = jnp.where(mine, total, 0.0)
    sums = lax.dot_general(
        spread,
        group_matrix(channels, lanes),
        (((1,), (1,)), ((), ())),
        precision=HI,
        preferred_element_type=F32,
    )
    gain, bias = gain_ref[...], bias_ref[...]
    a, s, r, t = [], [], [], []
    for b in range(batch):
        mean = sums[b : b + 1] / count
        var = sums[batch + b : batch + b + 1] / count - mean * mean
        inv = lax.rsqrt(var + EPS)
        r.append(inv)
        t.append(-mean * inv)
        a.append(inv * gain)
        s.append(bias - mean * inv * gain)
    return stack_rows(a + s + r + t, channels)


def put_shifted(ap, b, h, v, left, right):
    t, w, c = v.shape
    j = iota((t, w, c), 1)
    ap[0, b, pl.ds(h, t)] = jnp.where(j == 0, left, pltpu.roll(v, 1, 1))
    ap[1, b, pl.ds(h, t)] = v
    ap[2, b, pl.ds(h, t)] = jnp.where(j == w - 1, right, pltpu.roll(v, w - 1, 1))


def fill_acts(ap, aff, x_ref, xt_ref, xb_ref, xl_ref, xr_ref):
    _, batch, tall, w, c = ap.shape
    high = tall - 2
    ri, rn = lax.axis_index("row"), lax.axis_size("row")
    ci, cn = lax.axis_index("col"), lax.axis_size("col")
    up = jnp.where(ri == 0, 0.0, 1.0)
    down = jnp.where(ri == rn - 1, 0.0, 1.0)
    west = jnp.where(ci == 0, 0.0, 1.0)
    east = jnp.where(ci == cn - 1, 0.0, 1.0)

    def silu(v):
        return v / (1.0 + jnp.exp(-v))

    t = 8
    for b in range(batch):
        a = aff[b : b + 1].reshape(1, 1, c)
        s = aff[batch + b : batch + b + 1].reshape(1, 1, c)

        def act(x, a=a, s=s):
            return silu(x * a + s)

        def body(i, _, b=b, act=act):
            start = pl.multiple_of(b * high * w + i * t * w, 16)
            v = act(x_ref[pl.ds(start, t * w), :].astype(F32).reshape(t, w, c))
            h = i * t + 1
            put_shifted(
                ap, b, h, v, act(xl_ref[b, pl.ds(h, t)]) * west, act(xr_ref[b, pl.ds(h, t)]) * east
            )
            return 0

        lax.fori_loop(0, high // t, body, 0)
        for ref, h, edge in ((xt_ref, 0, up), (xb_ref, tall - 1, down)):
            put_shifted(
                ap,
                b,
                h,
                act(ref[b * w : (b + 1) * w, :].reshape(1, w, c)) * edge,
                act(xl_ref[b, h : h + 1]) * (west * edge),
                act(xr_ref[b, h : h + 1]) * (east * edge),
            )


def tap_rows(ap, b, kh, kw):
    _, _, tall, w, c = ap.shape
    return ap[kw, b, kh : kh + tall - 2].reshape((tall - 2) * w, c).astype(BF16)


def wgrad_kernel(batch, count, scale, relative, *refs):
    (st_ref, gain_ref, bias_ref, x_ref, g_ref, xt_ref, xb_ref, xl_ref, xr_ref) = refs[:9]
    aff_ref, keep_ref, send_ref = refs[9:12]
    ap, gt, gp, part = refs[12:]
    channels = x_ref.shape[1]
    n = x_ref.shape[0]
    aff = affine_rows(st_ref, gain_ref, bias_ref, batch, count)
    aff_ref[...] = aff
    wide = gt.shape[0]
    step = LANES
    for i in range(n // step):
        v = g_ref[i * step : (i + 1) * step, :].astype(F32)
        v = jnp.concatenate([v, jnp.zeros((step, wide - channels), F32)], axis=1)
        gt[:, i * step : (i + 1) * step] = jnp.transpose(v).astype(BF16)
    _, rows, pieces, share, width = send_ref.shape
    if relative:
        me = lax.axis_index("row") * 2 + (lax.axis_index("col") & 1)
        for q in range(2 * rows):
            other = (me ^ ((q % rows) * 2 + q // rows)) * share
            gp[q * share : (q + 1) * share, :] = gt[pl.ds(pl.multiple_of(other, 16), share), :]
    else:
        gp[...] = gt[:channels, :]
    fill_acts(ap, aff, x_ref, xt_ref, xb_ref, xl_ref, xr_ref)
    part[:, 9 * channels :] = jnp.zeros((channels, part.shape[1] - 9 * channels), F32)
    per = n // batch
    for kh in range(3):
        for kw in range(3):
            tap = kh * 3 + kw
            acc = jnp.zeros((channels, channels), F32)
            for b in range(batch):
                acc = acc + jnp.dot(
                    gp[:, b * per : (b + 1) * per],
                    tap_rows(ap, b, kh, kw),
                    preferred_element_type=F32,
                )
            part[:, tap * channels : (tap + 1) * channels] = acc * scale
    for r in range(rows):
        for p in range(pieces):
            lane = slice(p * width, (p + 1) * width)
            keep_ref[r, p] = part[r * share : (r + 1) * share, lane]
            low = (rows + r) * share
            send_ref[0, r, p] = part[low : low + share, lane].astype(BF16)


def back_kernel(batch, *refs):
    aff_ref, x_ref, g_ref, gt_ref, gb_ref, gl_ref, gr_ref, w_ref = refs[:8]
    dn_ref, sums_ref, ap = refs[8:]
    _, _, tall, w, c = ap.shape
    high = tall - 2
    per = high * w
    t = 8
    rows = []
    totals = []
    for b in range(batch):

        def body(i, tot, b=b):
            start = pl.multiple_of(b * per + i * t * w, 16)
            v = g_ref[pl.ds(start, t * w), :].astype(F32).reshape(t, w, c)
            h = i * t + 1
            put_shifted(ap, b, h, v, gl_ref[b, pl.ds(h, t)], gr_ref[b, pl.ds(h, t)])
            return tot + jnp.sum(v, axis=0)

        tot = lax.fori_loop(0, high // t, body, jnp.zeros((w, c), F32))
        totals.append(jnp.sum(tot, axis=0, keepdims=True))
        for ref, h in ((gt_ref, 0), (gb_ref, tall - 1)):
            put_shifted(
                ap,
                b,
                h,
                ref[b * w : (b + 1) * w, :].reshape(1, w, c),
                gl_ref[b, h : h + 1],
                gr_ref[b, h : h + 1],
            )
    for b in range(batch):
        acc = jnp.zeros((per, c), F32)
        for kh in range(3):
            for kw in range(3):
                acc = acc + lax.dot_general(
                    tap_rows(ap, b, 2 - kh, 2 - kw),
                    w_ref[kh * 3 + kw],
                    (((1,), (1,)), ((), ())),
                    preferred_element_type=F32,
                )
        dn_ref[b * per : (b + 1) * per, :] = acc
    aff = aff_ref[...]
    for b in range(batch):
        a, s, r, o = (aff[k * batch + b : k * batch + b + 1] for k in range(4))

        def body(i, carry, b=b, a=a, s=s, r=r, o=o):
            rows_here = pl.ds(pl.multiple_of(b * per + i * 64, 16), 64)
            x = x_ref[rows_here, :].astype(F32)
            normed = x * a + s
            sig = 1.0 / (1.0 + jnp.exp(-normed))
            dn = dn_ref[rows_here, :] * sig * (1.0 + normed * (1.0 - sig))
            dn_ref[rows_here, :] = dn
            xhat = x * r + o
            return (
                carry[0] + jnp.sum(dn.reshape(8, 8, c), axis=0),
                carry[1] + jnp.sum((dn * xhat).reshape(8, 8, c), axis=0),
            )

        zero = jnp.zeros((8, c), F32)
        rows.append(lax.fori_loop(0, per // 64, body, (zero, zero)))
    sums_ref[...] = stack_rows(
        [jnp.sum(v[0], axis=0, keepdims=True) for v in rows]
        + [jnp.sum(v[1], axis=0, keepdims=True) for v in rows]
        + totals,
        c,
    )


def conv_kernel(batch, *refs):
    aff_ref, x_ref, xt_ref, xb_ref, xl_ref, xr_ref, w_ref, cb_ref, temb_ref = refs[:9]
    out_ref, ap = refs[9:]
    _, _, tall, w, c = ap.shape
    per = (tall - 2) * w
    fill_acts(ap, aff_ref[...], x_ref, xt_ref, xb_ref, xl_ref, xr_ref)
    for b in range(batch):
        acc = jnp.zeros((per, c), F32)
        for kh in range(3):
            for kw in range(3):
                acc = acc + jnp.dot(
                    tap_rows(ap, b, kh, kw), w_ref[kh * 3 + kw], preferred_element_type=F32
                )
        here = slice(b * per, (b + 1) * per)
        out = x_ref[here, :].astype(F32) + acc + cb_ref[...] + temb_ref[b : b + 1, :]
        out_ref[here, :] = out.astype(BF16)


def input_kernel(batch, count, scale, *refs):
    aff_ref, red_ref, gain_ref, x_ref, g_ref, dn_ref = refs[:6]
    out_ref, gain_out, bias_out, cb_out = refs[6:]
    n, c = x_ref.shape
    per = n // batch
    red = red_ref[...]
    aff = aff_ref[...]
    gain = gain_ref[...]
    m = group_sums(red * gain) / count
    total = lambda k: sum(red[k * batch + b : k * batch + b + 1] for b in range(batch)) * scale
    bias_out[...] = total(0)
    gain_out[...] = total(1)
    cb_out[...] = total(2)
    for b in range(batch):
        a, r, o = (aff[k * batch + b : k * batch + b + 1] for k in (0, 2, 3))
        m1 = r * m[b : b + 1]
        m2 = r * m[batch + b : batch + b + 1]

        def body(i, _, b=b, a=a, r=r, o=o, m1=m1, m2=m2):
            here = pl.ds(pl.multiple_of(b * per + i * 64, 16), 64)
            xhat = x_ref[here, :].astype(F32) * r + o
            out_ref[here, :] = g_ref[here, :].astype(F32) + (dn_ref[here, :] * a - m1 - xhat * m2)
            return 0

        lax.fori_loop(0, per // 64, body, 0)


def assemble_kernel(nz, own_ref, z_ref, x_ref, core_ref, out_ref, full):
    share, width = own_ref.shape[-2:]
    c = out_ref.shape[-1]
    col = lax.axis_index("col")
    core, xb, z = col & 1, (col >> 1) & 1, col >> 2

    def put(k, core, xb, z):
        row = pl.multiple_of(core * share, 16)
        lane = pl.multiple_of((xb * nz + z) * width, LANES)
        full[pl.ds(row, share), pl.ds(lane, width)] = k.astype(F32)

    put(own_ref[0], core, xb, z)
    for k in range(1, nz):
        put(z_ref[k - 1], core, xb, z ^ k)
    for k in range(nz):
        put(x_ref[k], core, 1 - xb, z ^ k)
    for half in range(2):
        for k in range(nz):
            put(core_ref[half * nz + k], 1 - core, xb ^ half, z ^ k)
    for tap in range(out_ref.shape[0]):
        out_ref[tap] = full[:, tap * c : (tap + 1) * c]


def embed(timestep, embed_in, embed_out):
    half = embed_in.shape[0] // 2
    freqs = jnp.exp(-math.log(10000.0) * jnp.arange(half, dtype=F32) / half)
    angles = timestep.astype(F32)[:, None] * freqs[None, :]
    sinus = jnp.concatenate([jnp.cos(angles), jnp.sin(angles)], axis=1).astype(BF16)
    first_hidden = jax.nn.silu(jnp.dot(sinus, embed_in, preferred_element_type=F32)).astype(BF16)
    return jax.nn.silu(jnp.dot(first_hidden, embed_out, preferred_element_type=F32)).astype(BF16)


def partner(value, bit):
    size = lax.axis_size("row") * lax.axis_size("col")
    return lax.ppermute(value, AXES, [(i, i ^ bit) for i in range(size)])


def halo(rows_last, rows_first, axis):
    devices = lax.axis_size(axis)
    up = [(i, i + 1) for i in range(devices - 1)]
    down = [(j, i) for i, j in up]
    return lax.ppermute(rows_last, axis, up), lax.ppermute(rows_first, axis, down)


def plus(*values):
    total = values[0].astype(F32)
    for v in values[1:]:
        total = total + v.astype(F32)
    return total


def reduce_weights(keep, send, nz):
    rows, pieces, share, width = keep.shape
    cols = lax.axis_size("col")
    col = lax.axis_index("col")
    xb, z = (col >> 1) & 1, col >> 2
    held = plus(keep, partner(send, 1)).reshape(rows, 2, nz, share, width)
    pick = lambda v, i, dim: lax.dynamic_index_in_dim(v, i, dim, keepdims=False)
    half = nz // 2
    a, b = held[:, :, :half], held[:, :, half:]
    a_in = partner(a[1].astype(BF16), cols)
    b_in = partner(pick(b, 1 - xb, 1).astype(BF16), 2)
    a = plus(a[0], a_in)
    b = plus(pick(b, xb, 1), b_in)
    a_in = partner(pick(a, 1 - xb, 0).astype(BF16), 2)
    b_in = partner(b[1].astype(BF16), cols)
    held = jnp.concatenate([plus(pick(a, xb, 0), a_in), plus(b[0], b_in)], axis=0)
    got = [partner(pick(held, z ^ k, 0).astype(BF16), 4 * k) for k in range(1, nz)]
    own = plus(pick(held, z, 0), *got).astype(BF16)[None]
    zs = jnp.concatenate([partner(own, 4 * k) for k in range(1, nz)], axis=0)
    chip = jnp.concatenate([own, zs], axis=0)
    xs = partner(chip, 2)
    others = partner(jnp.concatenate([chip, xs], axis=0), 1)
    return own, zs, xs, others


def local(
    latent,
    timestep,
    group_norm_gain,
    group_norm_bias,
    conv_w,
    conv_b,
    embed_in,
    embed_out,
    time_w,
    cotangent,
):
    batch, high, wide, channels = latent.shape
    rows, cols = lax.axis_size("row"), lax.axis_size("col")
    devices = rows * cols
    n = batch * high * wide
    count = high * rows * wide * cols * (channels // NORM_GROUPS)
    scale = 1.0 / math.sqrt(batch * high * rows * wide * cols)
    x2 = latent.reshape(n, channels)
    g2 = cotangent.reshape(n, channels)
    gain = group_norm_gain.reshape(1, channels)
    bias = group_norm_bias.reshape(1, channels)
    w9 = conv_w.reshape(9, channels, channels)

    lanes = -(-2 * batch * NORM_GROUPS // LANES) * LANES
    pay = call(
        functools.partial(stats_kernel, batch),
        jax.ShapeDtypeStruct((devices, 1, lanes), F32),
        flops=4 * n * channels,
    )(x2)
    stats = lax.all_to_all(pay, AXES, 0, 0)

    top, bottom = halo(
        jnp.concatenate([latent[:, -1:], cotangent[:, -1:]], axis=0),
        jnp.concatenate([latent[:, :1], cotangent[:, :1]], axis=0),
        "row",
    )
    tall = jnp.concatenate([top, jnp.concatenate([latent, cotangent], axis=0), bottom], axis=1)
    left, right = halo(tall[:, :, -1:], tall[:, :, :1], "col")
    top, bottom, left, right = (v.astype(F32) for v in (top, bottom, left, right))
    flat = lambda v: v.reshape(batch * wide, channels)
    xt, gt = flat(top[:batch]), flat(top[batch:])
    xb, gb = flat(bottom[:batch]), flat(bottom[batch:])
    xl, gl = left[:batch], left[batch:]
    xr, gr = right[:batch], right[batch:]

    shifted = pltpu.VMEM((3, batch, high + 2, wide, channels), F32)
    nz = cols // 4
    share = channels // (2 * rows)
    relative = rows == 2 and nz >= 2 and share % 16 == 0
    pieces = cols // 2 if relative else 1
    width = -(-9 * channels // (LANES * pieces)) * LANES
    padded = -(-channels // LANES) * LANES
    conv_flops = 2 * 9 * n * channels * channels
    if not relative:
        share = channels // 2
    keep_rows = rows if relative else 1
    aff, keep, send = call(
        functools.partial(wgrad_kernel, batch, count, scale, relative),
        (
            jax.ShapeDtypeStruct((8, channels), F32),
            jax.ShapeDtypeStruct((keep_rows, pieces, share, width), F32),
            jax.ShapeDtypeStruct((1, keep_rows, pieces, share, width), BF16),
        ),
        scratch=(
            shifted,
            pltpu.VMEM((padded, n), BF16),
            pltpu.VMEM((channels, n), BF16),
            pltpu.VMEM((channels, pieces * width), F32),
        ),
        flops=conv_flops,
    )(stats, gain, bias, x2, g2, xt, xb, xl, xr)

    dn, sums = call(
        functools.partial(back_kernel, batch),
        (
            jax.ShapeDtypeStruct((n, channels), F32),
            jax.ShapeDtypeStruct((8, channels), F32),
        ),
        scratch=(shifted,),
        flops=conv_flops,
    )(aff, x2, g2, gt, gb, gl, gr, w9)

    if relative:
        own, zs, xs, others = reduce_weights(keep, send[0], nz)
        grad = call(
            functools.partial(assemble_kernel, nz),
            jax.ShapeDtypeStruct((9, 2 * share, channels), F32),
            scratch=(pltpu.VMEM((2 * share, pieces * width), F32),),
        )(own, zs, xs, others)
    else:
        both = jnp.concatenate([keep[0, 0], send[0, 0, 0].astype(F32)], axis=0)
        both = lax.psum(both[:, : 9 * channels], AXES)
        mine = channels // rows
        grad = lax.dynamic_slice_in_dim(both, lax.axis_index("row") * mine, mine, 0)
        grad = jnp.transpose(grad.reshape(mine, 9, channels), (1, 0, 2))
    conv_w_grad = jnp.transpose(grad.reshape(3, 3, channels // rows, channels), (2, 0, 1, 3))

    bit = 1
    while bit < devices:
        sums = sums + partner(sums, bit)
        bit *= 2
    emb = embed(timestep, embed_in, embed_out)
    temb = jnp.dot(emb, time_w, preferred_element_type=F32)
    block_out = call(
        functools.partial(conv_kernel, batch),
        jax.ShapeDtypeStruct((n, channels), BF16),
        scratch=(shifted,),
        flops=conv_flops,
    )(aff, x2, xt, xb, xl, xr, w9, conv_b.reshape(1, channels), temb)

    vector = jax.ShapeDtypeStruct((1, channels), F32)
    input_grad, gain_grad, bias_grad, conv_b_grad = call(
        functools.partial(input_kernel, batch, count, scale),
        (jax.ShapeDtypeStruct((n, channels), F32), vector, vector, vector),
        flops=8 * n * channels,
    )(aff, sums, gain, x2, g2, dn)
    gsum = sums[2 * batch : 3 * batch]
    time_w_grad = jnp.dot(emb.astype(F32).T, gsum) * scale
    return (
        block_out.reshape(latent.shape),
        input_grad.reshape(latent.shape),
        conv_w_grad,
        gain_grad.reshape(channels),
        bias_grad.reshape(channels),
        conv_b_grad.reshape(channels),
        time_w_grad,
    )


def solution(mesh):
    return jax.shard_map(
        local,
        mesh=mesh,
        in_specs=(
            P(None, "row", "col", None),
            P(),
            P(),
            P(),
            P(),
            P(),
            P(),
            P(),
            P(),
            P(None, "row", "col", None),
        ),
        out_specs=(
            P(None, "row", "col", None),
            P(None, "row", "col", None),
            P("row", None, None, None),
            P(),
            P(),
            P(),
            P(),
        ),
        check_vma=False,
    )
```

time: 328 us -> 128 us (0.39)
  waiting for transfers between devices: 137 us -> 15 us
  blocking collectives: 85.1 us -> 0 us
  matrix products: 44.1 us -> 6.31 us
  starting transfers between devices: 19.1 us -> 44.9 us
  Pallas kernels: 0 us -> 24.9 us
  between operations: 14.7 us -> 1.02 us
  local copies, waits for them, and re-layouts: 14 us -> 21.7 us
    psum x1 -> x0, waiting for transfers between devices: 133 us -> none  [local(): lax.psum(jnp.stack(pieces, axis=1).reshape(channel_count, 3, 3, channel_c...]
    psum x2 -> x0, blocking collectives: 85.1 us -> none  [the longest x1 43.4 us: local(): lax.psum((jnp.sum(normed_gradient, axis=(1, 2)), jnp.sum(normed_gradient...]
    dot_general x30 -> x3, matrix products: 44.1 us -> 6.31 us  [the longest x1 2.58 us: embed(): jnp.dot(first_hidden, embed_out, preferred_element_type=F32)]
    pallas_call x0 -> x6, Pallas kernels: none -> 24.9 us  [the longest x1 6.98 us: local(): call(functools.partial(conv_kernel, batch), jax.ShapeDtypeStruct((n, chan...]
    ppermute x8 -> x22, starting transfers between devices: 19 us -> 37.6 us  [the longest x18 27.4 us: partner(): return lax.ppermute(value, AXES, [(i, i ^ bit) for i in range(size)])]
    ppermute x8 -> x22, waiting for transfers between devices: 3.25 us -> 15 us  [the longest x18 15 us: partner(): return lax.ppermute(value, AXES, [(i, i ^ bit) for i in range(size)])]
    unnamed x42 -> x67, local copies, waits for them, and re-layouts: 2.15 us -> 11.9 us
    all_to_all x0 -> x1, starting transfers between devices: none -> 7.3 us  [local(): stats = lax.all_to_all(pay, AXES, 0, 0)]
  transfers between devices with their start and end apart: 9 -> 23, of which waited for: 2 -> 9; matrix products, arithmetic and copies ran while one was open for 9% -> 24% of each run, Pallas kernels for 0% -> 12%
where the time goes in v1:
time: 128 us; the launch traced here: 127 us
  starting transfers between devices  44.9 us (35%)
  Pallas kernels  24.9 us (19%)
  local copies, waits for them, and re-layouts  21.7 us (17%)
  waiting for transfers between devices  15 us (12%)
  other arithmetic  12.8 us (10%)
  matrix products  6.31 us (5%)
    ppermute x18, starting transfers between devices, partner(): return lax.ppermute(value, AXES, [(i, i ^ bit) for i in range(size)])  27.4 us
    ppermute x18, waiting for transfers between devices, partner(): return lax.ppermute(value, AXES, [(i, i ^ bit) for i in range(size)])  15 us
    unnamed x67, local copies, waits for them, and re-layouts  11.9 us
    ppermute x2, starting transfers between devices, halo(): lax.ppermute(rows_last, axis, up)  7.6 us
    all_to_all x1, starting transfers between devices, local(): stats = lax.all_to_all(pay, AXES, 0, 0)  7.3 us
    pallas_call x1, Pallas kernels, local(): call(functools.partial(conv_kernel, batch), jax.ShapeDtypeStruct((n, chan...  6.98 us
    pallas_call x1, Pallas kernels, local(): call(functools.partial(back_kernel, batch), (jax.ShapeDtypeStruct((n, cha...  6.14 us
    pallas_call x1, Pallas kernels, local(): call(functools.partial(wgrad_kernel, batch, count, scale, relative), (jax...  5.42 us
  transfers between devices with their start and end apart: 23, of which 9 were waited for; matrix products, arithmetic and copies ran while one was open for 24% of the time, Pallas kernels for 12%

profile of v1, /device:TPU:0, one launch (start us, length us, event | category | flops | bytes accessed | tf_op | source)
XLA Modules:
  0.0 126.6 jit_solution(3325939490028589630)
XLA Ops:
  0.7 1.3 %copy-done.1 = bf16[2,64,8,320]{3,2,1,0:T(8,128)(2,1)S(1)} copy-done((bf16[2,64,8,320]{3,2,1,0:T(8,128)(2,1)S(1)}, bf16[2,64,8,320]{3,2,1,0:T(8,128)(2,1)}, u32[]{:S(2)}) %copy-start.1) | copy-done | bytes 655384
  1.9 1.2 shard_map.153
  3.1 7.3 %all-to-all-start = ((f32[32,1,128]{2,1,0:T(1,128)}), f32[32,1,128]{2,1,0:T(1,128)S(1)}, u32[]{:S(2)}, u32[]{:S(2)}) async-start(f32[32,1,128]{2,1,0:T(1,128)} %shard_map.153), calls=%async_computation | async-start | bytes 32768 | tf_op jit(solution)/shard_map/all_to_all | solution.py:435
  10.4 0.7 fusion.46
  11.1 0.7 fusion.47
  11.9 1.3 %collective-permute-start.1 = (bf16[4,1,8,320]{3,2,1,0:T(8,128)(2,1)S(1)}, bf16[4,1,8,320]{3,2,1,0:T(8,128)(2,1)S(1)}, u32[]{:S(2)}, u32[]{:S(2)}) collective-permute-start(bf16[4,1,8,320]{3,2,1,0:T(8,128)(2,1)S(1)} %pad_maximum_fusion.7), channel_id=1, source_target_pairs={{16,0},{17,1},{18,2},{19,3},{20,4},{21,5},{22,6},{23,7},{24,8},{25... | collective-permute-start | bytes 61448 | tf_op jit(solution)/shard_map/ppermute | solution.py:370
  13.2 4.5 %collective-permute-start = (bf16[4,1,8,320]{3,2,1,0:T(8,128)(2,1)S(1)}, bf16[4,1,8,320]{3,2,1,0:T(8,128)(2,1)S(1)}, u32[]{:S(2)}, u32[]{:S(2)}) collective-permute-start(bf16[4,1,8,320]{3,2,1,0:T(8,128)(2,1)S(1)} %pad_maximum_fusion.6), channel_id=1, source_target_pairs={{0,16},{1,17},{2,18},{3,19},{4,20},{5,21},{6,22},{7,23},{8,24},{9,... | collective-permute-start | bytes 61448 | tf_op jit(solution)/shard_map/ppermute | solution.py:370
  17.8 0.7 reshape.79.refs_1_.refs_2_
  18.4 0.7 reshape.80.refs_2_
  19.7 2.8 %pad_maximum_fusion = (bf16[4,66,1,320]{3,2,1,0:T(2,128)(2,1)S(1)}, bf16[4,66,1,320]{3,2,1,0:T(2,128)(2,1)S(1)}) fusion(bf16[4,1,8,320]{3,2,1,0:T(8,128)(2,1)S(1)} %collective-permute-done.1, bf16[4,1,8,320]{3,2,1,0:T(8,128)(2,1)S(1)} %collective-permute-done, bf16[2,64,8,320]{3,2,1,0:T(8,128)(2,1)} %param.19, bf16[2,64,8,320]{3,2,1,0:T(8,128)(2,1)} %param.10), kind=kLoop, calls=%fused_computation.15 | loop fusion | flops 1351680 | bytes 1689600 | tf_op jit(solution)/shard_map/concatenate | solution.py:442
  22.6 1.3 %collective-permute-start.3 = (bf16[4,66,1,320]{3,2,1,0:T(2,128)(2,1)S(1)}, bf16[4,66,1,320]{3,2,1,0:T(2,128)(2,1)S(1)}, u32[]{:S(2)}, u32[]{:S(2)}) collective-permute-start(bf16[4,66,1,320]{3,2,1,0:T(2,128)(2,1)S(1)} %get-tuple-element.27), channel_id=1, source_target_pairs={{1,0},{2,1},{3,2},{4,3},{5,4},{6,5},{7,6},{8,7},{9,8},{10,9},{11,1... | collective-permute-start | bytes 506888 | tf_op jit(solution)/shard_map/ppermute | solution.py:370
  23.9 3.1 %collective-permute-start.2 = (bf16[4,66,1,320]{3,2,1,0:T(2,128)(2,1)S(1)}, bf16[4,66,1,320]{3,2,1,0:T(2,128)(2,1)S(1)}, u32[]{:S(2)}, u32[]{:S(2)}) collective-permute-start(bf16[4,66,1,320]{3,2,1,0:T(2,128)(2,1)S(1)} %get-tuple-element.28), channel_id=1, source_target_pairs={{0,1},{1,2},{2,3},{3,4},{4,5},{5,6},{6,7},{7,8},{8,9},{9,10},{10,1... | collective-permute-start | bytes 506888 | tf_op jit(solution)/shard_map/ppermute | solution.py:370
  27.6 1.1 fusion.48
  28.7 1.2 fusion.49
  29.9 1.1 copy-done.2
  31.0 1.1 copy-done.5
  32.2 0.9 copy-done.14
  33.2 5.4 %shard_map.154 = (f32[8,320]{1,0:T(8,128)S(1)}, f32[2,8,80,384]{3,2,1,0:T(8,128)S(1)}, bf16[1,2,8,80,384]{4,3,2,1,0:T(8,128)(2,1)S(1)}) custom-call(f32[32,1,128]{2,1,0:T(1,128)S(1)} %all-to-all-done.refs_0_, f32[1,320]{1,0:T(1,128)S(1)} %reshape.79.refs_1_.refs_2_, f32[1,320]{1,0:T(1,128)S(1)} %reshape.80.refs_2_, bf16[1024,320]{1,0:T(8,128)(2,1)S(1)} %bitcast.72, ...), custom_call_target="tpu_custom_call" | custom-call | flops 1887436800 | bytes 4000000 | tf_op jit(solution)/shard_map/pallas_call | solution.py:462
  38.6 7.6 %collective-permute-start.9 = (bf16[2,8,80,384]{3,2,1,0:T(8,128)(2,1)S(1)}, bf16[2,8,80,384]{3,2,1,0:T(8,128)(2,1)S(1)}, u32[]{:S(2)}, u32[]{:S(2)}) collective-permute-start(bf16[2,8,80,384]{3,2,1,0:T(8,128)(2,1)S(1)} %bitcast.81), channel_id=1, source_target_pairs={{0,1},{1,0},{2,3},{3,2},{4,5},{5,4},{6,7},{7,6},{8,9},{9,8},{10,11... | collective-permute-start | bytes 2949128 | tf_op jit(solution)/shard_map/ppermute | solution.py:363
  46.2 6.1 %shard_map.156 = (f32[1024,320]{1,0:T(8,128)S(1)}, f32[8,320]{1,0:T(8,128)S(1)}) custom-call(f32[8,320]{1,0:T(8,128)S(1)} %get-tuple-element.16.refs_0_, bf16[1024,320]{1,0:T(8,128)(2,1)S(1)} %bitcast.73, bf16[1024,320]{1,0:T(8,128)(2,1)S(1)} %bitcast.77, f32[16,320]{1,0:T(8,128)S(1)} %copy-done.21, f32[16,320]{1,0:T(8,128)S(1)} %copy-done.20, ...), custom_call_target="tpu_custom_call" | custom-call | flops 1887436800 | bytes 4000000 | tf_op jit(solution)/shard_map/pallas_call | solution.py:478
  52.5 1.1 collective-permute-done.4
  54.2 2.5 %collective-permute-start.5 = (f32[8,320]{1,0:T(8,128)}, f32[8,320]{1,0:T(8,128)}, u32[]{:S(2)}, u32[]{:S(2)}) collective-permute-start(f32[8,320]{1,0:T(8,128)} %add.72), channel_id=1, source_target_pairs={{0,2},{1,3},{2,0},{3,1},{4,6},{5,7},{6,4},{7,5},{8,10},{9,11},{10,... | collective-permute-start | bytes 30728 | tf_op jit(solution)/shard_map/ppermute | solution.py:363
  57.0 1.3 copy-done.26
  58.3 0.7 fusion.2
  59.0 1.2 collective-permute-start.10
  60.2 0.7 fusion.30
  60.9 1.3 %add.73 = f32[8,320]{1,0:T(8,128)} add(f32[8,320]{1,0:T(8,128)} %add.72, f32[8,320]{1,0:T(8,128)} %collective-permute-done.5) | non-fusion elementwise | flops 2560 | bytes 30720 | tf_op jit(solution)/shard_map/add | solution.py:505
  62.2 1.5 %collective-permute-start.6 = (f32[8,320]{1,0:T(8,128)}, f32[8,320]{1,0:T(8,128)}, u32[]{:S(2)}, u32[]{:S(2)}) collective-permute-start(f32[8,320]{1,0:T(8,128)} %add.73), channel_id=1, source_target_pairs={{0,4},{1,5},{2,6},{3,7},{4,0},{5,1},{6,2},{7,3},{8,12},{9,13},{10,... | collective-permute-start | bytes 30728 | tf_op jit(solution)/shard_map/ppermute | solution.py:363
  63.7 1.3 slice.95
  65.0 1.4 %collective-permute-start.12 = (bf16[2,2,80,384]{3,2,1,0:T(8,128)(2,1)S(1)}, bf16[2,2,80,384]{3,2,1,0:T(8,128)(2,1)S(1)}, u32[]{:S(2)}, u32[]{:S(2)}) collective-permute-start(bf16[2,2,80,384]{3,2,1,0:T(8,128)(2,1)S(1)} %fusion.1), channel_id=1, source_target_pairs={{0,2},{1,3},{2,0},{3,1},{4,6},{5,7},{6,4},{7,5},{8,10},{9,11},{10,... | collective-permute-start | bytes 737288 | tf_op jit(solution)/shard_map/ppermute | solution.py:363
  66.4 0.7 collective-permute-done.10
  67.2 1.1 fusion
  68.6 5.1 %collective-permute-done.12 = bf16[2,2,80,384]{3,2,1,0:T(8,128)(2,1)S(1)} collective-permute-done((bf16[2,2,80,384]{3,2,1,0:T(8,128)(2,1)S(1)}, bf16[2,2,80,384]{3,2,1,0:T(8,128)(2,1)S(1)}, u32[]{:S(2)}, u32[]{:S(2)}) %collective-permute-start.12) | collective-permute-done | bytes 245792 | tf_op jit(solution)/shard_map/ppermute | solution.py:363
  73.8 0.9 collective-permute-start.13
  75.1 3.7 %collective-permute-done.13 = bf16[2,80,384]{2,1,0:T(8,128)(2,1)S(1)} collective-permute-done((bf16[2,80,384]{2,1,0:T(8,128)(2,1)S(1)}, bf16[2,80,384]{2,1,0:T(8,128)(2,1)S(1)}, u32[]{:S(2)}, u32[]{:S(2)}) %collective-permute-start.13) | collective-permute-done | bytes 122912 | tf_op jit(solution)/shard_map/ppermute | solution.py:363
  78.8 0.7 copy-done.27
  79.5 0.7 fusion.19
  80.7 2.4 %collective-permute-start.15 = (bf16[80,384]{1,0:T(8,128)(2,1)}, bf16[80,384]{1,0:T(8,128)(2,1)}, u32[]{:S(2)}, u32[]{:S(2)}) collective-permute-start(bf16[80,384]{1,0:T(8,128)(2,1)} %get-tuple-element.34), channel_id=1, source_target_pairs={{0,8},{1,9},{2,10},{3,11},{4,12},{5,13},{6,14},{7,15},{8,0},{9,1},... | collective-permute-start | bytes 184328 | tf_op jit(solution)/shard_map/ppermute | solution.py:363
  83.2 1.4 %collective-permute-start.16 = (bf16[80,384]{1,0:T(8,128)(2,1)}, bf16[80,384]{1,0:T(8,128)(2,1)}, u32[]{:S(2)}, u32[]{:S(2)}) collective-permute-start(bf16[80,384]{1,0:T(8,128)(2,1)} %get-tuple-element.35), channel_id=1, source_target_pairs={{0,12},{1,13},{2,14},{3,15},{4,8},{5,9},{6,10},{7,11},{8,4},{9,5},... | collective-permute-start | bytes 184328 | tf_op jit(solution)/shard_map/ppermute | solution.py:363
  84.6 2.6 %fusion.23 = bf16[2,1280]{1,0:T(2,128)(2,1)} fusion(bf16[1280,1280]{1,0:T(8,128)(2,1)S(1)} %copy-done, bf16[320,1280]{1,0:T(8,128)(2,1)} %param.16, bf16[2,160]{1,0:T(2,128)(2,1)} %get-tuple-element.45, bf16[2,160]{1,0:T(2,128)(2,1)S(1)} %get-tuple-element.44), kind=kOutput, calls=%fused_computation.60 | convolution fusion | flops 8220160 | bytes 4102400 | tf_op jit(solution)/shard_map/dot_general | solution.py:358
  87.2 0.9 add.74
  88.0 1.0 collective-permute-start.7
  89.5 1.6 %constant_dynamic-update-slice_fusion.4 = (bf16[8,80,384]{2,1,0:T(8,128)(2,1)}, bf16[1,80,384]{2,1,0:T(8,128)(2,1)S(1)}) fusion(bf16[80,384]{1,0:T(8,128)(2,1)} %collective-permute-done.16, bf16[80,384]{1,0:T(8,128)(2,1)} %collective-permute-done.15, bf16[80,384]{1,0:T(8,128)(2,1)} %collective-permute-done.14, s32[]{:T(128)S(6)} %select_n.25, ...), kind=kLoop, calls=%fused_computation.56 | loop fusion | flops 245759 | bytes 798724
  91.1 1.6 %collective-permute-start.19 = (bf16[1,80,384]{2,1,0:T(8,128)(2,1)S(1)}, bf16[1,80,384]{2,1,0:T(8,128)(2,1)S(1)}, u32[]{:S(2)}, u32[]{:S(2)}) collective-permute-start(bf16[1,80,384]{2,1,0:T(8,128)(2,1)S(1)} %get-tuple-element.26.own_ref), channel_id=1, source_target_pairs={{0,12},{1,13},{2,14},{3,15},{4,8},{5,9},{6,10},{7,11},{8,4},{9,5},... | collective-permute-start | bytes 184328 | tf_op jit(solution)/shard_map/ppermute | solution.py:363
  92.7 1.4 %collective-permute-start.18 = (bf16[1,80,384]{2,1,0:T(8,128)(2,1)S(1)}, bf16[1,80,384]{2,1,0:T(8,128)(2,1)S(1)}, u32[]{:S(2)}, u32[]{:S(2)}) collective-permute-start(bf16[1,80,384]{2,1,0:T(8,128)(2,1)S(1)} %get-tuple-element.26.own_ref), channel_id=1, source_target_pairs={{0,8},{1,9},{2,10},{3,11},{4,12},{5,13},{6,14},{7,15},{8,0},{9,1},... | collective-permute-start | bytes 184328 | tf_op jit(solution)/shard_map/ppermute | solution.py:363
  94.1 1.4 %collective-permute-start.17 = (bf16[1,80,384]{2,1,0:T(8,128)(2,1)S(1)}, bf16[1,80,384]{2,1,0:T(8,128)(2,1)S(1)}, u32[]{:S(2)}, u32[]{:S(2)}) collective-permute-start(bf16[1,80,384]{2,1,0:T(8,128)(2,1)S(1)} %get-tuple-element.26.own_ref), channel_id=1, source_target_pairs={{0,4},{1,5},{2,6},{3,7},{4,0},{5,1},{6,2},{7,3},{8,12},{9,13},{10,... | collective-permute-start | bytes 184328 | tf_op jit(solution)/shard_map/ppermute | solution.py:363
  95.4 1.4 %fusion.50.refs_8_ = f32[2,320]{1,0:T(2,128)S(1)} fusion(bf16[2,1280]{1,0:T(2,128)(2,1)} %fusion.23, bf16[1280,320]{0,1:T(8,128)(2,1)} %param.18), kind=kOutput, calls=%fused_computation.79 | convolution fusion | flops 1638400 | bytes 826880 | tf_op jit(solution)/shard_map/dot_general | solution.py:508
  96.9 0.7 reshape.85.refs_7_
  97.6 0.9 collective-permute-start.8
  98.9 1.2 collective-permute-start.20
  100.2 0.6 constant_dynamic-update-slice_fusion.3
  100.8 0.6 constant_dynamic-update-slice_fusion.2
  101.4 0.6 constant_dynamic-update-slice_fusion.1
  102.1 3.1 %collective-permute-done.20.x_ref = bf16[4,80,384]{2,1,0:T(8,128)(2,1)S(1)} collective-permute-done((bf16[4,80,384]{2,1,0:T(8,128)(2,1)S(1)}, bf16[4,80,384]{2,1,0:T(8,128)(2,1)S(1)}, u32[]{:S(2)}, u32[]{:S(2)}) %collective-permute-start.20) | collective-permute-done | bytes 245792 | tf_op jit(solution)/shard_map/ppermute | solution.py:363
  105.2 0.7 constant_dynamic-update-slice_fusion
  106.0 1.1 copy-done.13
  107.1 0.9 copy-done.15
  108.0 0.7 copy-done.19
  108.7 0.7 copy-done.23
  109.4 7.0 %shard_map.155 = bf16[1024,320]{1,0:T(8,128)(2,1)} custom-call(f32[8,320]{1,0:T(8,128)S(1)} %copy-done.23, bf16[1024,320]{1,0:T(8,128)(2,1)S(1)} %bitcast.74, f32[16,320]{1,0:T(8,128)S(1)} %copy-done.19, f32[16,320]{1,0:T(8,128)S(1)} %get-tuple-element.41.refs_6_.refs_3_, f32[2,66,1,320]{3,2,1,0:T(1,128)S(1)} %copy-done.15, ...), custom_call_target="tpu_custom_call" | custom-call | flops 1887436800 | bytes 4000000 | tf_op jit(solution)/shard_map/pallas_call | solution.py:509
  116.4 2.3 %shard_map.157 = (f32[1024,320]{1,0:T(8,128)}, f32[1,320]{1,0:T(1,128)S(1)}, f32[1,320]{1,0:T(1,128)S(1)}, f32[1,320]{1,0:T(1,128)S(1)}) custom-call(f32[8,320]{1,0:T(8,128)S(1)} %copy-done.23, f32[8,320]{1,0:T(8,128)S(1)} %add.76.refs_1_, f32[1,320]{1,0:T(1,128)S(1)} %reshape.79.refs_1_.refs_2_, bf16[1024,320]{1,0:T(8,128)(2,1)S(1)} %bitcast.75, ...), custom_call_target="tpu_custom_call" | custom-call | flops 2621440 | bytes 4000000 | tf_op jit(solution)/shard_map/pallas_call | solution.py:517
  120.5 2.3 %convolution_multiply_fusion = f32[1280,320]{0,1:T(8,128)} fusion(bf16[2,1280]{1,0:T(2,128)(2,1)} %fusion.23, f32[8,320]{1,0:T(8,128)S(1)} %add.76.refs_1_), kind=kOutput, calls=%fused_computation | convolution fusion | flops 2048000 | bytes 1645056 | tf_op jit(solution)/shard_map/dot_general | solution.py:523
  122.8 0.9 pad_maximum_fusion.5.z_ref
  123.7 2.9 %shard_map.158 = f32[9,160,320]{2,1,0:T(8,128)} custom-call(bf16[1,80,384]{2,1,0:T(8,128)(2,1)S(1)} %copy-done.11, bf16[3,80,384]{2,1,0:T(8,128)(2,1)S(1)} %pad_maximum_fusion.5.z_ref, bf16[4,80,384]{2,1,0:T(8,128)(2,1)S(1)} %collective-permute-done.20.x_ref, bf16[8,80,384]{2,1,0:T(8,128)(2,1)} %collective-permute-done.21.core_ref), custom_call_target="tpu_custom_call" | custom-call | bytes 4000000 | tf_op jit(solution)/shard_map/pallas_call | solution.py:490
  (98 shorter events, 6.4 us)
Async XLA Ops:
  0.6 84.0 %copy-start = (bf16[1280,1280]{1,0:T(8,128)(2,1)S(1)}, bf16[1280,1280]{1,0:T(8,128)(2,1)}, u32[]{:S(2)}) copy-start(bf16[1280,1280]{1,0:T(8,128)(2,1)} %param.17) | copy-start | bytes 9830404
  0.6 1.3 %copy-start.1 = (bf16[2,64,8,320]{3,2,1,0:T(8,128)(2,1)S(1)}, bf16[2,64,8,320]{3,2,1,0:T(8,128)(2,1)}, u32[]{:S(2)}) copy-start(bf16[2,64,8,320]{3,2,1,0:T(8,128)(2,1)} %param.10) | copy-start | bytes 1966084
  3.1 26.8 %all-to-all-start = ((f32[32,1,128]{2,1,0:T(1,128)}), f32[32,1,128]{2,1,0:T(1,128)S(1)}, u32[]{:S(2)}, u32[]{:S(2)}) async-start(f32[32,1,128]{2,1,0:T(1,128)} %shard_map.153), calls=%async_computation | async-start | bytes 32768 | tf_op jit(solution)/shard_map/all_to_all | solution.py:435
  11.9 7.2 %collective-permute-start.1 = (bf16[4,1,8,320]{3,2,1,0:T(8,128)(2,1)S(1)}, bf16[4,1,8,320]{3,2,1,0:T(8,128)(2,1)S(1)}, u32[]{:S(2)}, u32[]{:S(2)}) collective-permute-start(bf16[4,1,8,320]{3,2,1,0:T(8,128)(2,1)S(1)} %pad_maximum_fusion.7), channel_id=1, source_target_pairs={{16,0},{17,1},{18,2},{19,3},{20,4},{21,5},{22,6},{23,7},{24,8},{25... | collective-permute-start | bytes 61448 | tf_op jit(solution)/shard_map/ppermute | solution.py:370
  13.2 6.5 %collective-permute-start = (bf16[4,1,8,320]{3,2,1,0:T(8,128)(2,1)S(1)}, bf16[4,1,8,320]{3,2,1,0:T(8,128)(2,1)S(1)}, u32[]{:S(2)}, u32[]{:S(2)}) collective-permute-start(bf16[4,1,8,320]{3,2,1,0:T(8,128)(2,1)S(1)} %pad_maximum_fusion.6), channel_id=1, source_target_pairs={{0,16},{1,17},{2,18},{3,19},{4,20},{5,21},{6,22},{7,23},{8,24},{9,... | collective-permute-start | bytes 61448 | tf_op jit(solution)/shard_map/ppermute | solution.py:370
  22.6 5.0 %collective-permute-start.3 = (bf16[4,66,1,320]{3,2,1,0:T(2,128)(2,1)S(1)}, bf16[4,66,1,320]{3,2,1,0:T(2,128)(2,1)S(1)}, u32[]{:S(2)}, u32[]{:S(2)}) collective-permute-start(bf16[4,66,1,320]{3,2,1,0:T(2,128)(2,1)S(1)} %get-tuple-element.27), channel_id=1, source_target_pairs={{1,0},{2,1},{3,2},{4,3},{5,4},{6,5},{7,6},{8,7},{9,8},{10,9},{11,1... | collective-permute-start | bytes 506888 | tf_op jit(solution)/shard_map/ppermute | solution.py:370
  23.9 4.8 %collective-permute-start.2 = (bf16[4,66,1,320]{3,2,1,0:T(2,128)(2,1)S(1)}, bf16[4,66,1,320]{3,2,1,0:T(2,128)(2,1)S(1)}, u32[]{:S(2)}, u32[]{:S(2)}) collective-permute-start(bf16[4,66,1,320]{3,2,1,0:T(2,128)(2,1)S(1)} %get-tuple-element.28), channel_id=1, source_target_pairs={{0,1},{1,2},{2,3},{3,4},{4,5},{5,6},{6,7},{7,8},{8,9},{9,10},{10,1... | collective-permute-start | bytes 506888 | tf_op jit(solution)/shard_map/ppermute | solution.py:370
  27.6 11.0 %copy-start.18 = (f32[16,320]{1,0:T(8,128)}, f32[16,320]{1,0:T(8,128)S(1)}, u32[]{:S(2)}) copy-start(f32[16,320]{1,0:T(8,128)S(1)} %get-tuple-element.43.refs_5_.refs_2_) | copy-start | bytes 61444
  28.7 9.9 %copy-start.12 = (f32[2,66,1,320]{3,2,1,0:T(1,128)}, f32[2,66,1,320]{3,2,1,0:T(1,128)S(1)}, u32[]{:S(2)}) copy-start(f32[2,66,1,320]{3,2,1,0:T(1,128)S(1)} %get-tuple-element.37.refs_8_.refs_5_) | copy-start | bytes 506884
  29.9 1.1 copy-start.2
  31.0 1.1 copy-start.5
  32.2 0.9 copy-start.14
  33.1 13.1 %copy-start.3 = (bf16[2,64,8,320]{3,2,1,0:T(8,128)(2,1)S(1)}, bf16[2,64,8,320]{3,2,1,0:T(8,128)(2,1)}, u32[]{:S(2)}) copy-start(bf16[2,64,8,320]{3,2,1,0:T(8,128)(2,1)} %param.10) | copy-start | bytes 1966084
  33.1 13.1 %copy-start.6 = (bf16[2,64,8,320]{3,2,1,0:T(8,128)(2,1)S(1)}, bf16[2,64,8,320]{3,2,1,0:T(8,128)(2,1)}, u32[]{:S(2)}) copy-start(bf16[2,64,8,320]{3,2,1,0:T(8,128)(2,1)} %param.19) | copy-start | bytes 1966084
  33.1 13.1 %copy-start.16 = (f32[2,66,1,320]{3,2,1,0:T(1,128)S(1)}, f32[2,66,1,320]{3,2,1,0:T(1,128)}, u32[]{:S(2)}) copy-start(f32[2,66,1,320]{3,2,1,0:T(1,128)} %get-tuple-element.36.refs_6_) | copy-start | bytes 506884
  33.1 13.1 %copy-start.17 = (f32[2,66,1,320]{3,2,1,0:T(1,128)S(1)}, f32[2,66,1,320]{3,2,1,0:T(1,128)}, u32[]{:S(2)}) copy-start(f32[2,66,1,320]{3,2,1,0:T(1,128)} %get-tuple-element.38.refs_5_) | copy-start | bytes 506884
  33.1 13.1 %copy-start.20 = (f32[16,320]{1,0:T(8,128)S(1)}, f32[16,320]{1,0:T(8,128)}, u32[]{:S(2)}) copy-start(f32[16,320]{1,0:T(8,128)} %get-tuple-element.40.refs_4_) | copy-start | bytes 61444
  33.1 13.1 %copy-start.21 = (f32[16,320]{1,0:T(8,128)S(1)}, f32[16,320]{1,0:T(8,128)}, u32[]{:S(2)}) copy-start(f32[16,320]{1,0:T(8,128)} %get-tuple-element.42.refs_3_) | copy-start | bytes 61444
  33.1 13.1 %copy-start.24 = (bf16[3,3,320,320]{3,2,1,0:T(8,128)(2,1)S(1)}, bf16[3,3,320,320]{3,2,1,0:T(8,128)(2,1)}, u32[]{:S(2)}) copy-start(bf16[3,3,320,320]{3,2,1,0:T(8,128)(2,1)} %param.14) | copy-start | bytes 5529604
  38.6 13.8 %copy-start.22 = (f32[8,320]{1,0:T(8,128)}, f32[8,320]{1,0:T(8,128)S(1)}, u32[]{:S(2)}) copy-start(f32[8,320]{1,0:T(8,128)S(1)} %get-tuple-element.16.refs_0_) | copy-start | bytes 30724
  38.6 18.1 %collective-permute-start.9 = (bf16[2,8,80,384]{3,2,1,0:T(8,128)(2,1)S(1)}, bf16[2,8,80,384]{3,2,1,0:T(8,128)(2,1)S(1)}, u32[]{:S(2)}, u32[]{:S(2)}) collective-permute-start(bf16[2,8,80,384]{3,2,1,0:T(8,128)(2,1)S(1)} %bitcast.81), channel_id=1, source_target_pairs={{0,1},{1,0},{2,3},{3,2},{4,5},{5,4},{6,7},{7,6},{8,9},{9,8},{10,11... | collective-permute-start | bytes 2949128 | tf_op jit(solution)/shard_map/ppermute | solution.py:363
  46.2 6.3 %copy-start.31 = (s32[2]{0:T(128)S(1)}, s32[2]{0:T(128)}, u32[]{:S(2)}) copy-start(s32[2]{0:T(128)} %param.11) | copy-start | bytes 28
  52.4 4.6 %copy-start.8 = (f32[1024,320]{1,0:T(8,128)}, f32[1024,320]{1,0:T(8,128)S(1)}, u32[]{:S(2)}) copy-start(f32[1024,320]{1,0:T(8,128)S(1)} %get-tuple-element.18.refs_5_) | copy-start | bytes 3932164
  52.4 1.2 collective-permute-start.4
  54.2 6.6 %collective-permute-start.5 = (f32[8,320]{1,0:T(8,128)}, f32[8,320]{1,0:T(8,128)}, u32[]{:S(2)}, u32[]{:S(2)}) collective-permute-start(f32[8,320]{1,0:T(8,128)} %add.72), channel_id=1, source_target_pairs={{0,2},{1,3},{2,0},{3,1},{4,6},{5,7},{6,4},{7,5},{8,10},{9,11},{10,... | collective-permute-start | bytes 30728 | tf_op jit(solution)/shard_map/ppermute | solution.py:363
  57.0 1.3 %copy-start.26 = (f32[2,8,80,384]{3,2,1,0:T(8,128)}, f32[2,8,80,384]{3,2,1,0:T(8,128)S(1)}, u32[]{:S(2)}) copy-start(f32[2,8,80,384]{3,2,1,0:T(8,128)S(1)} %convert_add_fusion) | copy-start | bytes 5898244
  59.0 8.1 %collective-permute-start.10 = (bf16[2,2,80,384]{3,2,1,0:T(8,128)(2,1)}, bf16[2,2,80,384]{3,2,1,0:T(8,128)(2,1)S(1)}, u32[]{:S(2)}, u32[]{:S(2)}) collective-permute-start(bf16[2,2,80,384]{3,2,1,0:T(8,128)(2,1)} %fusion.2), channel_id=1, source_target_pairs={{0,16},{1,17},{2,18},{3,19},{4,20},{5,21},{6,22},{7,23},{8,24},{9,... | collective-permute-start | bytes 737288 | tf_op jit(solution)/shard_map/ppermute | solution.py:363
  62.2 25.0 %collective-permute-start.6 = (f32[8,320]{1,0:T(8,128)}, f32[8,320]{1,0:T(8,128)}, u32[]{:S(2)}, u32[]{:S(2)}) collective-permute-start(f32[8,320]{1,0:T(8,128)} %add.73), channel_id=1, source_target_pairs={{0,4},{1,5},{2,6},{3,7},{4,0},{5,1},{6,2},{7,3},{8,12},{9,13},{10,... | collective-permute-start | bytes 30728 | tf_op jit(solution)/shard_map/ppermute | solution.py:363
  65.0 8.7 %collective-permute-start.12 = (bf16[2,2,80,384]{3,2,1,0:T(8,128)(2,1)S(1)}, bf16[2,2,80,384]{3,2,1,0:T(8,128)(2,1)S(1)}, u32[]{:S(2)}, u32[]{:S(2)}) collective-permute-start(bf16[2,2,80,384]{3,2,1,0:T(8,128)(2,1)S(1)} %fusion.1), channel_id=1, source_target_pairs={{0,2},{1,3},{2,0},{3,1},{4,6},{5,7},{6,4},{7,5},{8,10},{9,11},{10,... | collective-permute-start | bytes 737288 | tf_op jit(solution)/shard_map/ppermute | solution.py:363
  68.3 6.8 %collective-permute-start.11 = (bf16[2,80,384]{2,1,0:T(8,128)(2,1)S(1)}, bf16[2,80,384]{2,1,0:T(8,128)(2,1)S(1)}, u32[]{:S(2)}, u32[]{:S(2)}) collective-permute-start(bf16[2,80,384]{2,1,0:T(8,128)(2,1)S(1)} %fusion.4), channel_id=1, source_target_pairs={{0,2},{1,3},{2,0},{3,1},{4,6},{5,7},{6,4},{7,5},{8,10},{9,11},{10,... | collective-permute-start | bytes 368648 | tf_op jit(solution)/shard_map/ppermute | solution.py:363
  73.8 4.9 %collective-permute-start.13 = (bf16[2,80,384]{2,1,0:T(8,128)(2,1)S(1)}, bf16[2,80,384]{2,1,0:T(8,128)(2,1)S(1)}, u32[]{:S(2)}, u32[]{:S(2)}) collective-permute-start(bf16[2,80,384]{2,1,0:T(8,128)(2,1)S(1)} %fusion.5), channel_id=1, source_target_pairs={{0,16},{1,17},{2,18},{3,19},{4,20},{5,21},{6,22},{7,23},{8,24},{9,... | collective-permute-start | bytes 368648 | tf_op jit(solution)/shard_map/ppermute | solution.py:363
  78.8 0.7 copy-start.27
  80.2 8.8 %collective-permute-start.14 = (bf16[80,384]{1,0:T(8,128)(2,1)}, bf16[80,384]{1,0:T(8,128)(2,1)}, u32[]{:S(2)}, u32[]{:S(2)}) collective-permute-start(bf16[80,384]{1,0:T(8,128)(2,1)} %get-tuple-element.33), channel_id=1, source_target_pairs={{0,4},{1,5},{2,6},{3,7},{4,0},{5,1},{6,2},{7,3},{8,12},{9,13},{10,... | collective-permute-start | bytes 184328 | tf_op jit(solution)/shard_map/ppermute | solution.py:363
  80.7 8.3 %collective-permute-start.15 = (bf16[80,384]{1,0:T(8,128)(2,1)}, bf16[80,384]{1,0:T(8,128)(2,1)}, u32[]{:S(2)}, u32[]{:S(2)}) collective-permute-start(bf16[80,384]{1,0:T(8,128)(2,1)} %get-tuple-element.34), channel_id=1, source_target_pairs={{0,8},{1,9},{2,10},{3,11},{4,12},{5,13},{6,14},{7,15},{8,0},{9,1},... | collective-permute-start | bytes 184328 | tf_op jit(solution)/shard_map/ppermute | solution.py:363
  83.2 6.3 %collective-permute-start.16 = (bf16[80,384]{1,0:T(8,128)(2,1)}, bf16[80,384]{1,0:T(8,128)(2,1)}, u32[]{:S(2)}, u32[]{:S(2)}) collective-permute-start(bf16[80,384]{1,0:T(8,128)(2,1)} %get-tuple-element.35), channel_id=1, source_target_pairs={{0,12},{1,13},{2,14},{3,15},{4,8},{5,9},{6,10},{7,11},{8,4},{9,5},... | collective-permute-start | bytes 184328 | tf_op jit(solution)/shard_map/ppermute | solution.py:363
  87.2 18.8 %copy-start.4 = (bf16[2,64,8,320]{3,2,1,0:T(8,128)(2,1)S(1)}, bf16[2,64,8,320]{3,2,1,0:T(8,128)(2,1)}, u32[]{:S(2)}) copy-start(bf16[2,64,8,320]{3,2,1,0:T(8,128)(2,1)} %param.10) | copy-start | bytes 1966084
  87.2 18.8 %copy-start.25 = (bf16[3,3,320,320]{3,2,1,0:T(8,128)(2,1)S(1)}, bf16[3,3,320,320]{3,2,1,0:T(8,128)(2,1)}, u32[]{:S(2)}) copy-start(bf16[3,3,320,320]{3,2,1,0:T(8,128)(2,1)} %param.14) | copy-start | bytes 5529604
  88.0 9.6 %collective-permute-start.7 = (f32[8,320]{1,0:T(8,128)S(1)}, f32[8,320]{1,0:T(8,128)S(1)}, u32[]{:S(2)}, u32[]{:S(2)}) collective-permute-start(f32[8,320]{1,0:T(8,128)S(1)} %add.74), channel_id=1, source_target_pairs={{0,8},{1,9},{2,10},{3,11},{4,12},{5,13},{6,14},{7,15},{8,0},{9,1},... | collective-permute-start | bytes 30728 | tf_op jit(solution)/shard_map/ppermute | solution.py:363
  91.1 14.2 %copy-start.10 = (bf16[1,80,384]{2,1,0:T(8,128)(2,1)}, bf16[1,80,384]{2,1,0:T(8,128)(2,1)S(1)}, u32[]{:S(2)}) copy-start(bf16[1,80,384]{2,1,0:T(8,128)(2,1)S(1)} %get-tuple-element.26.own_ref) | copy-start | bytes 184324
  91.1 7.4 %collective-permute-start.19 = (bf16[1,80,384]{2,1,0:T(8,128)(2,1)S(1)}, bf16[1,80,384]{2,1,0:T(8,128)(2,1)S(1)}, u32[]{:S(2)}, u32[]{:S(2)}) collective-permute-start(bf16[1,80,384]{2,1,0:T(8,128)(2,1)S(1)} %get-tuple-element.26.own_ref), channel_id=1, source_target_pairs={{0,12},{1,13},{2,14},{3,15},{4,8},{5,9},{6,10},{7,11},{8,4},{9,5},... | collective-permute-start | bytes 184328 | tf_op jit(solution)/shard_map/ppermute | solution.py:363
  92.7 5.9 %collective-permute-start.18 = (bf16[1,80,384]{2,1,0:T(8,128)(2,1)S(1)}, bf16[1,80,384]{2,1,0:T(8,128)(2,1)S(1)}, u32[]{:S(2)}, u32[]{:S(2)}) collective-permute-start(bf16[1,80,384]{2,1,0:T(8,128)(2,1)S(1)} %get-tuple-element.26.own_ref), channel_id=1, source_target_pairs={{0,8},{1,9},{2,10},{3,11},{4,12},{5,13},{6,14},{7,15},{8,0},{9,1},... | collective-permute-start | bytes 184328 | tf_op jit(solution)/shard_map/ppermute | solution.py:363
  94.1 4.8 %collective-permute-start.17 = (bf16[1,80,384]{2,1,0:T(8,128)(2,1)S(1)}, bf16[1,80,384]{2,1,0:T(8,128)(2,1)S(1)}, u32[]{:S(2)}, u32[]{:S(2)}) collective-permute-start(bf16[1,80,384]{2,1,0:T(8,128)(2,1)S(1)} %get-tuple-element.26.own_ref), channel_id=1, source_target_pairs={{0,4},{1,5},{2,6},{3,7},{4,0},{5,1},{6,2},{7,3},{8,12},{9,13},{10,... | collective-permute-start | bytes 184328 | tf_op jit(solution)/shard_map/ppermute | solution.py:363
  97.6 18.8 %collective-permute-start.8 = (f32[8,320]{1,0:T(8,128)S(1)}, f32[8,320]{1,0:T(8,128)S(1)}, u32[]{:S(2)}, u32[]{:S(2)}) collective-permute-start(f32[8,320]{1,0:T(8,128)S(1)} %add.75), channel_id=1, source_target_pairs={{0,16},{1,17},{2,18},{3,19},{4,20},{5,21},{6,22},{7,23},{8,24},{9,... | collective-permute-start | bytes 30728 | tf_op jit(solution)/shard_map/ppermute | solution.py:363
  98.5 6.7 %copy-start.28 = (bf16[1,80,384]{2,1,0:T(8,128)(2,1)}, bf16[1,80,384]{2,1,0:T(8,128)(2,1)S(1)}, u32[]{:S(2)}) copy-start(bf16[1,80,384]{2,1,0:T(8,128)(2,1)S(1)} %collective-permute-done.19) | copy-start | bytes 184324
  98.6 6.7 %copy-start.29 = (bf16[1,80,384]{2,1,0:T(8,128)(2,1)}, bf16[1,80,384]{2,1,0:T(8,128)(2,1)S(1)}, u32[]{:S(2)}) copy-start(bf16[1,80,384]{2,1,0:T(8,128)(2,1)S(1)} %collective-permute-done.18) | copy-start | bytes 184324
  98.9 6.3 %copy-start.30 = (bf16[1,80,384]{2,1,0:T(8,128)(2,1)}, bf16[1,80,384]{2,1,0:T(8,128)(2,1)S(1)}, u32[]{:S(2)}) copy-start(bf16[1,80,384]{2,1,0:T(8,128)(2,1)S(1)} %collective-permute-done.17) | copy-start | bytes 184324
  98.9 6.3 %collective-permute-start.20 = (bf16[4,80,384]{2,1,0:T(8,128)(2,1)S(1)}, bf16[4,80,384]{2,1,0:T(8,128)(2,1)S(1)}, u32[]{:S(2)}, u32[]{:S(2)}) collective-permute-start(bf16[4,80,384]{2,1,0:T(8,128)(2,1)S(1)} %pad_maximum_fusion.4), channel_id=1, source_target_pairs={{0,2},{1,3},{2,0},{3,1},{4,6},{5,7},{6,4},{7,5},{8,10},{9,11},{10,... | collective-permute-start | bytes 737288 | tf_op jit(solution)/shard_map/ppermute | solution.py:363
  106.0 10.5 %copy-start.7 = (bf16[2,64,8,320]{3,2,1,0:T(8,128)(2,1)S(1)}, bf16[2,64,8,320]{3,2,1,0:T(8,128)(2,1)}, u32[]{:S(2)}) copy-start(bf16[2,64,8,320]{3,2,1,0:T(8,128)(2,1)} %param.19) | copy-start | bytes 1966084
  106.0 10.5 %copy-start.9 = (f32[1024,320]{1,0:T(8,128)S(1)}, f32[1024,320]{1,0:T(8,128)}, u32[]{:S(2)}) copy-start(f32[1024,320]{1,0:T(8,128)} %copy-done.8) | copy-start | bytes 3932164
  106.0 17.8 %collective-permute-start.21 = (bf16[8,80,384]{2,1,0:T(8,128)(2,1)}, bf16[8,80,384]{2,1,0:T(8,128)(2,1)}, u32[]{:S(2)}, u32[]{:S(2)}) collective-permute-start(bf16[8,80,384]{2,1,0:T(8,128)(2,1)} %constant_dynamic-update-slice_fusion), channel_id=1, source_target_pairs={{0,1},{1,0},{2,3},{3,2},{4,5},{5,4},{6,7},{7,6},{8,9},{9,8},{10,11... | collective-permute-start | bytes 1474568 | tf_op jit(solution)/shard_map/ppermute | solution.py:363
  106.0 1.1 copy-start.13
  107.1 0.9 copy-start.15
  108.0 0.7 copy-start.19
  108.7 0.7 copy-start.23
  120.5 3.2 %copy-start.11 = (bf16[1,80,384]{2,1,0:T(8,128)(2,1)S(1)}, bf16[1,80,384]{2,1,0:T(8,128)(2,1)}, u32[]{:S(2)}) copy-start(bf16[1,80,384]{2,1,0:T(8,128)(2,1)} %copy-done.10) | copy-start | bytes 184324

commit v2 on v1

v2 whole, which is shorter than its diff:
```python
import functools
import math

import jax
import jax.numpy as jnp
from jax import lax
from jax.experimental import pallas as pl
from jax.experimental.pallas import tpu as pltpu
from jax.sharding import PartitionSpec as P

NORM_GROUPS = 32
EPS = 1e-05
LANES = 128
F32 = jnp.float32
BF16 = jnp.bfloat16
AXES = ("row", "col")
VMEM_LIMIT = 32 * 1024 * 1024
HI = lax.Precision.HIGHEST


def iota(shape, dim):
    return lax.broadcasted_iota(jnp.int32, shape, dim)


def call(body, out_shape, operands, after=(), scratch=(), flops=0, nbytes=2_000_000):
    used, waits = len(operands), len(after)

    def kernel(*refs):
        body(*refs[:used], *refs[used + waits :])

    vmem = pl.BlockSpec(memory_space=pltpu.VMEM)
    return pl.pallas_call(
        kernel,
        out_shape=out_shape,
        in_specs=[vmem] * used + [pl.BlockSpec(memory_space=pl.ANY)] * waits,
        out_specs=jax.tree.map(lambda _: vmem, out_shape),
        scratch_shapes=list(scratch),
        compiler_params=pltpu.CompilerParams(vmem_limit_bytes=VMEM_LIMIT),
        cost_estimate=pl.CostEstimate(flops=flops, bytes_accessed=nbytes, transcendentals=0),
    )(*operands, *after)


def group_matrix(channels, lanes):
    size = channels // NORM_GROUPS
    group = iota((channels, lanes), 1) & (NORM_GROUPS - 1)
    channel = iota((channels, lanes), 0)
    return jnp.where((channel >= group * size) & (channel < (group + 1) * size), 1.0, 0.0).astype(F32)


def group_sums(rows):
    lanes = LANES
    g = group_matrix(rows.shape[1], lanes)
    keep = iota((8, lanes), 1) < NORM_GROUPS
    s = jnp.dot(rows, g, precision=HI, preferred_element_type=F32)
    s = jnp.where(keep, s, 0.0)
    return lax.dot_general(
        s, g, (((1,), (1,)), ((), ())), precision=HI, preferred_element_type=F32
    )


def stack_rows(rows, channels):
    r = iota((8, channels), 0)
    out = jnp.zeros((8, channels), F32)
    for k, v in enumerate(rows):
        out = out + jnp.where(r == k, v, 0.0)
    return out


def stats_kernel(batch, w, rows, x_ref, g_ref, pay_ref, west_ref, east_ref, *edge_refs):
    n, channels = x_ref.shape
    per = n // batch
    step = 64
    t = step // w
    sums = []
    for k, ref in enumerate((x_ref, g_ref)):
        for b in range(batch):

            def add(i, c, b=b, k=k, ref=ref):
                start = pl.multiple_of(b * per + i * step, 16)
                v = ref[pl.ds(start, step), :].astype(F32).reshape(t, w, channels)
                west_ref[k * batch + b, pl.ds(i * t, t)] = v[:, :1]
                east_ref[k * batch + b, pl.ds(i * t, t)] = v[:, w - 1 :]
                if k:
                    return c
                return c[0] + jnp.sum(v, axis=0), c[1] + jnp.sum(v * v, axis=0)

            zero = jnp.zeros((w, channels), F32)
            s, q = lax.fori_loop(0, per // step, add, (zero, zero))
            if not k:
                sums.append((jnp.sum(s, axis=0, keepdims=True), jnp.sum(q, axis=0, keepdims=True)))
            last = ref[(b + 1) * per - 16 : (b + 1) * per, :].astype(F32)[16 - w :]
            first = ref[b * per : b * per + 16, :].astype(F32)[:w]
            if rows == 2:
                edges = (jnp.where(lax.axis_index("row") == 0, last, first),)
            else:
                edges = (last, first)
            for e, v in enumerate(edges):
                line, corner_w, corner_e = edge_refs[3 * e : 3 * e + 3]
                at = k * batch + b
                line[at * w : (at + 1) * w, :] = v
                corner_w[at] = v[:1]
                corner_e[at] = v[w - 1 :]
    stacked = stack_rows([r[0] for r in sums] + [r[1] for r in sums], channels)
    lanes = pay_ref.shape[-1]
    res = jnp.dot(
        stacked, group_matrix(channels, lanes), precision=HI, preferred_element_type=F32
    )
    first = iota((8, lanes), 0) * NORM_GROUPS
    lane = iota((8, lanes), 1)
    mine = (lane >= first) & (lane < first + NORM_GROUPS)
    row = jnp.sum(jnp.where(mine, res, 0.0), axis=0, keepdims=True)
    pay_ref[...] = jnp.broadcast_to(row[None], pay_ref.shape)


def affine_rows(st_ref, gain_ref, bias_ref, batch, count):
    channels = gain_ref.shape[-1]
    lanes = st_ref.shape[-1]
    total = jnp.sum(st_ref[...], axis=0)
    first = iota((8, lanes), 0) * NORM_GROUPS
    lane = iota((8, lanes), 1)
    mine = (lane >= first) & (lane < first + NORM_GROUPS)
    spread = jnp.where(mine, total, 0.0)
    sums = lax.dot_general(
        spread,
        group_matrix(channels, lanes),
        (((1,), (1,)), ((), ())),
        precision=HI,
        preferred_element_type=F32,
    )
    gain, bias = gain_ref[...].reshape(1, channels), bias_ref[...].reshape(1, channels)
    a, s, r, t = [], [], [], []
    for b in range(batch):
        mean = sums[b : b + 1] / count
        var = sums[batch + b : batch + b + 1] / count - mean * mean
        inv = lax.rsqrt(var + EPS)
        r.append(inv)
        t.append(-mean * inv)
        a.append(inv * gain)
        s.append(bias - mean * inv * gain)
    return stack_rows(a + s + r + t, channels)


def put_shifted(ap, b, h, v, left, right):
    t, w, c = v.shape
    j = iota((t, w, c), 1)
    ap[0, b, pl.ds(h, t)] = jnp.where(j == 0, left, pltpu.roll(v, 1, 1))
    ap[1, b, pl.ds(h, t)] = v
    ap[2, b, pl.ds(h, t)] = jnp.where(j == w - 1, right, pltpu.roll(v, w - 1, 1))


def edge_masks():
    ri, rn = lax.axis_index("row"), lax.axis_size("row")
    ci, cn = lax.axis_index("col"), lax.axis_size("col")
    flags = (ri == 0, ri == rn - 1, ci == 0, ci == cn - 1)
    return tuple(jnp.where(f, 0.0, 1.0) for f in flags)


def fill(ap, part, batch, fn, src_ref, halo, visit=None):
    _, _, tall, w, c = ap.shape
    high = tall - 2
    up, down, west, east = edge_masks()
    left, right, top, top_w, top_e, low, low_w, low_e = halo
    t = 8
    first = part * batch
    for b in range(batch):

        def body(i, carry, b=b):
            start = pl.multiple_of(b * high * w + i * t * w, 16)
            v = src_ref[pl.ds(start, t * w), :].astype(F32).reshape(t, w, c)
            h = i * t
            put_shifted(
                ap,
                b,
                h + 1,
                fn(b, v),
                fn(b, left[first + b, pl.ds(h, t)]) * west,
                fn(b, right[first + b, pl.ds(h, t)]) * east,
            )
            return carry if visit is None else visit(carry, v)

        out = lax.fori_loop(0, high // t, body, jnp.zeros((w, c), F32))
        if visit is not None:
            yield out
        for line, wc, ec, h, edge in (
            (top, top_w, top_e, 0, up),
            (low, low_w, low_e, tall - 1, down),
        ):
            at = first + b
            put_shifted(
                ap,
                b,
                h,
                fn(b, line[at * w : (at + 1) * w, :].reshape(1, w, c)) * edge,
                fn(b, wc[at : at + 1]) * (west * edge),
                fn(b, ec[at : at + 1]) * (east * edge),
            )


def fill_acts(ap, aff, batch, x_ref, halo):
    c = ap.shape[-1]

    def act(b, x):
        v = x * aff[b : b + 1].reshape(1, 1, c) + aff[batch + b : batch + b + 1].reshape(1, 1, c)
        return v / (1.0 + jnp.exp(-v))

    for _ in fill(ap, 0, batch, act, x_ref, halo):
        pass


def tap_rows(ap, b, kh, kw):
    _, _, tall, w, c = ap.shape
    return ap[kw, b, kh : kh + tall - 2].reshape((tall - 2) * w, c).astype(BF16)


def wgrad_kernel(batch, count, scale, relative, *refs):
    st_ref, gain_ref, bias_ref, x_ref, g_ref = refs[:5]
    halo = refs[5:13]
    aff_ref, keep_ref, send_ref = refs[13:16]
    ap, gt, gp, part = refs[16:]
    channels = x_ref.shape[1]
    n = x_ref.shape[0]
    aff = affine_rows(st_ref, gain_ref, bias_ref, batch, count)
    aff_ref[...] = aff
    wide = gt.shape[0]
    step = LANES
    for i in range(n // step):
        v = g_ref[i * step : (i + 1) * step, :].astype(F32)
        v = jnp.concatenate([v, jnp.zeros((step, wide - channels), F32)], axis=1)
        gt[:, i * step : (i + 1) * step] = jnp.transpose(v).astype(BF16)
    _, rows, pieces, share, width = send_ref.shape
    if relative:
        me = lax.axis_index("row") * 2 + (lax.axis_index("col") & 1)
        for q in range(2 * rows):
            other = (me ^ ((q % rows) * 2 + q // rows)) * share
            gp[q * share : (q + 1) * share, :] = gt[pl.ds(pl.multiple_of(other, 16), share), :]
    else:
        gp[...] = gt[:channels, :]
    fill_acts(ap, aff, batch, x_ref, halo)
    part[:, 9 * channels :] = jnp.zeros((channels, part.shape[1] - 9 * channels), F32)
    per = n // batch
    for kh in range(3):
        for kw in range(3):
            tap = kh * 3 + kw
            acc = jnp.zeros((channels, channels), F32)
            for b in range(batch):
                acc = acc + jnp.dot(
                    gp[:, b * per : (b + 1) * per],
                    tap_rows(ap, b, kh, kw),
                    preferred_element_type=F32,
                )
            part[:, tap * channels : (tap + 1) * channels] = acc * scale
    for r in range(rows):
        for p in range(pieces):
            lane = slice(p * width, (p + 1) * width)
            keep_ref[r, p] = part[r * share : (r + 1) * share, lane]
            low = (rows + r) * share
            send_ref[0, r, p] = part[low : low + share, lane].astype(BF16)


def back_kernel(batch, *refs):
    aff_ref, x_ref, g_ref = refs[:3]
    halo = refs[3:11]
    w_ref, dn_ref, sums_ref, ap = refs[11:]
    _, _, tall, w, c = ap.shape
    per = (tall - 2) * w
    rows = []
    totals = fill(
        ap, 1, batch, lambda b, v: v, g_ref, halo, lambda tot, v: tot + jnp.sum(v, axis=0)
    )
    totals = [jnp.sum(v, axis=0, keepdims=True) for v in totals]
    for b in range(batch):
        acc = jnp.zeros((per, c), F32)
        for kh in range(3):
            for kw in range(3):
                acc = acc + lax.dot_general(
                    tap_rows(ap, b, 2 - kh, 2 - kw),
                    w_ref[kh * 3 + kw],
                    (((1,), (1,)), ((), ())),
                    preferred_element_type=F32,
                )
        dn_ref[b * per : (b + 1) * per, :] = acc
    aff = aff_ref[...]
    for b in range(batch):
        a, s, r, o = (aff[k * batch + b : k * batch + b + 1] for k in range(4))

        def body(i, carry, b=b, a=a, s=s, r=r, o=o):
            rows_here = pl.ds(pl.multiple_of(b * per + i * 64, 16), 64)
            x = x_ref[rows_here, :].astype(F32)
            normed = x * a + s
            sig = 1.0 / (1.0 + jnp.exp(-normed))
            dn = dn_ref[rows_here, :] * sig * (1.0 + normed * (1.0 - sig))
            dn_ref[rows_here, :] = dn
            xhat = x * r + o
            return (
                carry[0] + jnp.sum(dn.reshape(8, 8, c), axis=0),
                carry[1] + jnp.sum((dn * xhat).reshape(8, 8, c), axis=0),
            )

        zero = jnp.zeros((8, c), F32)
        rows.append(lax.fori_loop(0, per // 64, body, (zero, zero)))
    sums_ref[...] = stack_rows(
        [jnp.sum(v[0], axis=0, keepdims=True) for v in rows]
        + [jnp.sum(v[1], axis=0, keepdims=True) for v in rows]
        + totals,
        c,
    )


def conv_kernel(batch, *refs):
    aff_ref, x_ref = refs[:2]
    halo = refs[2:10]
    w_ref, cb_ref, temb_ref, out_ref, ap = refs[10:]
    _, _, tall, w, c = ap.shape
    per = (tall - 2) * w
    fill_acts(ap, aff_ref[...], batch, x_ref, halo)
    bias = cb_ref[...].reshape(1, c)
    for b in range(batch):
        acc = jnp.zeros((per, c), F32)
        for kh in range(3):
            for kw in range(3):
                acc = acc + jnp.dot(
                    tap_rows(ap, b, kh, kw), w_ref[kh * 3 + kw], preferred_element_type=F32
                )
        here = slice(b * per, (b + 1) * per)
        out = x_ref[here, :].astype(F32) + acc + bias + temb_ref[b : b + 1, :]
        out_ref[here, :] = out.astype(BF16)


def input_kernel(batch, count, scale, *refs):
    aff_ref, red_ref, gain_ref, x_ref, g_ref, dn_ref, emb_ref = refs[:7]
    out_ref, gain_out, bias_out, cb_out, tw_out = refs[7:]
    n, c = x_ref.shape
    per = n // batch
    red = red_ref[...]
    aff = aff_ref[...]
    gain = gain_ref[...].reshape(1, c)
    m = group_sums(red * gain) / count
    total = lambda k: sum(red[k * batch + b : k * batch + b + 1] for b in range(batch)) * scale
    bias_out[...] = total(0).reshape(c)
    gain_out[...] = total(1).reshape(c)
    cb_out[...] = total(2).reshape(c)
    rest = red[2 * batch : 3 * batch] * scale
    parts = []
    for _ in range(3):
        parts.append(rest.astype(BF16))
        rest = rest - parts[-1].astype(F32)
    emb = emb_ref[...]
    tw_out[...] = sum(
        lax.dot_general(p, emb, (((0,), (0,)), ((), ())), preferred_element_type=F32)
        for p in reversed(parts)
    )
    for b in range(batch):
        a, r, o = (aff[k * batch + b : k * batch + b + 1] for k in (0, 2, 3))
        m1 = r * m[b : b + 1]
        m2 = r * m[batch + b : batch + b + 1]

        def body(i, _, b=b, a=a, r=r, o=o, m1=m1, m2=m2):
            here = pl.ds(pl.multiple_of(b * per + i * 64, 16), 64)
            xhat = x_ref[here, :].astype(F32) * r + o
            out_ref[here, :] = g_ref[here, :].astype(F32) + (dn_ref[here, :] * a - m1 - xhat * m2)
            return 0

        lax.fori_loop(0, per // 64, body, 0)


def place():
    col = lax.axis_index("col")
    return col & 1, (col >> 1) & 1, col >> 2


def step_one(nz, keep_ref, got_ref, a_send, a_keep, b_send, b_keep):
    _, xb, _ = place()
    half = nz // 2
    total = lambda r, p: keep_ref[r, p] + got_ref[r, p].astype(F32)
    for x in range(2):
        for z in range(half):
            p = x * nz + z
            a_send[x, z] = total(1, p).astype(BF16)
            a_keep[x, z] = total(0, p)
    for r in range(2):
        for z in range(half):
            b_send[r, z] = total(r, (1 - xb) * nz + half + z).astype(BF16)
            b_keep[r, z] = total(r, xb * nz + half + z)


def step_two(nz, a_got, a_keep, b_got, b_keep, a_send, a_next, b_send, b_next):
    _, xb, _ = place()
    for z in range(nz // 2):
        a_send[z] = (a_keep[1 - xb, z] + a_got[1 - xb, z].astype(F32)).astype(BF16)
        a_next[z] = a_keep[xb, z] + a_got[xb, z].astype(F32)
        b_send[z] = (b_keep[1, z] + b_got[1, z].astype(F32)).astype(BF16)
        b_next[z] = b_keep[0, z] + b_got[0, z].astype(F32)


def step_three(nz, a_got, a_keep, b_got, b_keep, own_ref, *refs):
    sends, held = refs[: nz - 1], refs[nz - 1]
    _, _, zb = place()
    half = nz // 2
    for z in range(half):
        held[z] = a_keep[z] + a_got[z].astype(F32)
        held[half + z] = b_keep[z] + b_got[z].astype(F32)
    own_ref[...] = held[zb]
    for k in range(1, nz):
        sends[k - 1][...] = held[zb ^ k].astype(BF16)


def step_four(own_ref, *refs):
    total = own_ref[...]
    for g in refs[:-1]:
        total = total + g[...].astype(F32)
    refs[-1][...] = total.astype(BF16)


def step_five(nz, *refs):
    out = refs[-1]
    width = refs[0].shape[-1]
    _, xb, zb = place()
    for k, ref in enumerate(refs[:-1]):
        p = (xb ^ (k % 2)) * nz + (zb ^ (k // 2))
        out[:, pl.ds(pl.multiple_of(p * width, LANES), width)] = ref[...]


def step_six(mine_ref, other_ref, out_ref, full):
    core, _, _ = place()
    share = mine_ref.shape[0]
    c = out_ref.shape[-1]
    full[pl.ds(pl.multiple_of(core * share, 16), share), :] = mine_ref[...].astype(F32)
    full[pl.ds(pl.multiple_of((1 - core) * share, 16), share), :] = other_ref[...].astype(F32)
    for tap in range(out_ref.shape[0]):
        out_ref[tap] = full[:, tap * c : (tap + 1) * c]


def embed(timestep, embed_in, embed_out):
    half = embed_in.shape[0] // 2
    freqs = jnp.exp(-math.log(10000.0) * jnp.arange(half, dtype=F32) / half)
    angles = timestep.astype(F32)[:, None] * freqs[None, :]
    sinus = jnp.concatenate([jnp.cos(angles), jnp.sin(angles)], axis=1).astype(BF16)
    first_hidden = jax.nn.silu(jnp.dot(sinus, embed_in, preferred_element_type=F32)).astype(BF16)
    return jax.nn.silu(jnp.dot(first_hidden, embed_out, preferred_element_type=F32)).astype(BF16)


def partner(value, bit):
    size = lax.axis_size("row") * lax.axis_size("col")
    return lax.ppermute(value, AXES, [(i, i ^ bit) for i in range(size)])


def shift(value, down, right):
    rows, cols = lax.axis_size("row"), lax.axis_size("col")
    pairs = []
    for r in range(rows):
        for c in range(cols):
            to = (r + down, c + right)
            if 0 <= to[0] < rows and 0 <= to[1] < cols:
                pairs.append((r * cols + c, to[0] * cols + to[1]))
    return lax.ppermute(value, AXES, pairs)


def swap(value, right):
    cols = lax.axis_size("col")
    pairs = []
    for r in range(2):
        for c in range(cols):
            if 0 <= c + right < cols:
                pairs.append((r * cols + c, (1 - r) * cols + c + right))
    return lax.ppermute(value, AXES, pairs)


def local(
    latent,
    timestep,
    group_norm_gain,
    group_norm_bias,
    conv_w,
    conv_b,
    embed_in,
    embed_out,
    time_w,
    cotangent,
):
    batch, high, wide, channels = latent.shape
    rows, cols = lax.axis_size("row"), lax.axis_size("col")
    devices = rows * cols
    n = batch * high * wide
    count = high * rows * wide * cols * (channels // NORM_GROUPS)
    scale = 1.0 / math.sqrt(batch * high * rows * wide * cols)
    x2 = latent.reshape(n, channels)
    g2 = cotangent.reshape(n, channels)
    w9 = conv_w.reshape(9, channels, channels)
    of = jax.ShapeDtypeStruct

    lanes = -(-2 * batch * NORM_GROUPS // LANES) * LANES
    column = of((2 * batch, high, 1, channels), F32)
    edge = (
        of((2 * batch * wide, channels), F32),
        of((2 * batch, 1, channels), F32),
        of((2 * batch, 1, channels), F32),
    )
    pay, west, east, *edges = call(
        functools.partial(stats_kernel, batch, wide, rows),
        (of((devices, 1, lanes), F32), column, column, *(edge * (1 if rows == 2 else 2))),
        (x2, g2),
    )
    left, right = shift(east, 0, 1), shift(west, 0, -1)
    if rows == 2:
        line, corner_w, corner_e = edges
        top = (swap(line, 0), swap(corner_e, 1), swap(corner_w, -1))
        low = top
    else:
        line, corner_w, corner_e = edges[:3]
        top = (shift(line, 1, 0), shift(corner_e, 1, 1), shift(corner_w, 1, -1))
        line, corner_w, corner_e = edges[3:]
        low = (shift(line, -1, 0), shift(corner_e, -1, 1), shift(corner_w, -1, -1))
    stats = lax.all_to_all(pay, AXES, 0, 0)
    halo = (left, right, *top, *low)

    shifted = pltpu.VMEM((3, batch, high + 2, wide, channels), F32)
    nz = cols // 4
    share = channels // (2 * rows)
    relative = rows == 2 and nz >= 2 and share % 16 == 0
    pieces = cols // 2 if relative else 1
    width = -(-9 * channels // (LANES * pieces)) * LANES
    padded = -(-channels // LANES) * LANES
    conv_flops = 2 * 9 * n * channels * channels
    if not relative:
        share = channels // 2
    keep_rows = rows if relative else 1
    aff, keep, send = call(
        functools.partial(wgrad_kernel, batch, count, scale, relative),
        (
            of((8, channels), F32),
            of((keep_rows, pieces, share, width), F32),
            of((1, keep_rows, pieces, share, width), BF16),
        ),
        (stats, group_norm_gain, group_norm_bias, x2, g2, *halo),
        scratch=(
            shifted,
            pltpu.VMEM((padded, n), BF16),
            pltpu.VMEM((channels, n), BF16),
            pltpu.VMEM((channels, pieces * width), F32),
        ),
        flops=conv_flops,
    )

    if relative:
        half = nz // 2
        many = lambda k, dtype: of((*k, share, width), dtype)
        got = partner(send[0], 1)
        a_send, a_keep, b_send, b_keep = call(
            functools.partial(step_one, nz),
            (many((2, half), BF16), many((2, half), F32)) * 2,
            (keep, got),
        )
        a_got, b_got = partner(a_send, cols), partner(b_send, 2)
        first = (a_send, b_send)
    else:
        first = ()

    dn, sums = call(
        functools.partial(back_kernel, batch),
        (of((n, channels), F32), of((8, channels), F32)),
        (aff, x2, g2, *halo, w9),
        after=first,
        scratch=(shifted,),
        flops=conv_flops,
    )
    emb = embed(timestep, embed_in, embed_out)
    temb = jnp.dot(emb, time_w, preferred_element_type=F32)

    if relative:
        a_send, a_keep, b_send, b_keep = call(
            functools.partial(step_two, nz),
            (many((half,), BF16), many((half,), F32)) * 2,
            (a_got, a_keep, b_got, b_keep),
            after=(sums,),
        )
        a_got, b_got = partner(a_send, 2), partner(b_send, cols)
        own, *sends = call(
            functools.partial(step_three, nz),
            (many((), F32), *[many((), BF16)] * (nz - 1)),
            (a_got, a_keep, b_got, b_keep),
            scratch=(pltpu.VMEM((nz, share, width), F32),),
        )
        gots = [partner(v, 4 * (k + 1)) for k, v in enumerate(sends)]
        second = tuple(sends)
    else:
        second = ()

    block_out = call(
        functools.partial(conv_kernel, batch),
        of((n, channels), BF16),
        (aff, x2, *halo, w9, conv_b, temb),
        after=second,
        scratch=(shifted,),
        flops=conv_flops,
    )
    bit = 1
    while bit < devices:
        sums = sums + partner(sums, bit)
        bit *= 2

    if relative:
        own = call(step_four, many((), BF16), (own, *gots), after=(block_out,))
        others = [partner(own, 2 * k) for k in range(1, pieces)]
        third = (own,)
    else:
        third = ()

    vector = of((channels,), F32)
    input_grad, gain_grad, bias_grad, conv_b_grad, time_grad = call(
        functools.partial(input_kernel, batch, count, scale),
        (of((n, channels), F32), vector, vector, vector, of((channels, emb.shape[1]), F32)),
        (aff, sums, group_norm_gain, x2, g2, dn, emb),
        after=third,
        flops=8 * n * channels,
    )

    if relative:
        mine = call(
            functools.partial(step_five, nz),
            of((share, pieces * width), BF16),
            (own, *others),
            after=(input_grad,),
        )
        grad = call(
            step_six,
            of((9, 2 * share, channels), F32),
            (mine, partner(mine, 1)),
            scratch=(pltpu.VMEM((2 * share, pieces * width), F32),),
        )
    else:
        both = jnp.concatenate([keep[0, 0], send[0, 0, 0].astype(F32)], axis=0)
        both = lax.psum(both[:, : 9 * channels], AXES)
        mine = channels // rows
        grad = lax.dynamic_slice_in_dim(both, lax.axis_index("row") * mine, mine, 0)
        grad = jnp.transpose(grad.reshape(mine, 9, channels), (1, 0, 2))
    conv_w_grad = jnp.transpose(grad.reshape(3, 3, channels // rows, channels), (2, 0, 1, 3))
    return (
        block_out.reshape(latent.shape),
        input_grad.reshape(latent.shape),
        conv_w_grad,
        gain_grad,
        bias_grad,
        conv_b_grad,
        time_grad.T,
    )


def solution(mesh):
    return jax.shard_map(
        local,
        mesh=mesh,
        in_specs=(
            P(None, "row", "col", None),
            P(),
            P(),
            P(),
            P(),
            P(),
            P(),
            P(),
            P(),
            P(None, "row", "col", None),
        ),
        out_specs=(
            P(None, "row", "col", None),
            P(None, "row", "col", None),
            P("row", None, None, None),
            P(),
            P(),
            P(),
            P(),
        ),
        check_vma=False,
    )
```

time: 128 us -> 118 us (0.922)
  other arithmetic: 12.8 us -> 0.72 us
  waiting for transfers between devices: 15 us -> 23.3 us
  Pallas kernels: 24.9 us -> 31.3 us
  local copies, waits for them, and re-layouts: 21.7 us -> 15.6 us
  matrix products: 6.31 us -> 2.26 us
  starting transfers between devices: 44.9 us -> 42.9 us
    pallas_call x6 -> x11, Pallas kernels: 24.9 us -> 31.3 us  [call(): pl.pallas_call(kernel, out_shape=out_shape, in_specs=[vmem] * used + [pl....]
    slice x5 -> x0, local copies, waits for them, and re-layouts: 5.04 us -> none  [the longest x1 1.27 us: reduce_weights(): a, b = (held[:, :, :half], held[:, :, half:])]
    ppermute x18 -> x21, waiting for transfers between devices: 15 us -> 19.7 us  [partner(): return lax.ppermute(value, AXES, [(i, i ^ bit) for i in range(size)])]
    concatenate x5 -> x0, other arithmetic: 3.82 us -> none  [the longest x1 2.84 us: local(): jnp.concatenate([top, jnp.concatenate([latent, cotangent], axis=0), botto...]
    unnamed x67 -> x54, local copies, waits for them, and re-layouts: 11.9 us -> 15.6 us
    ppermute x4 -> x5, waiting for transfers between devices: 0.01 us -> 3.66 us  [the longest x3 3.65 us: swap(): return lax.ppermute(value, AXES, pairs)]
    reshape x5 -> x0, local copies, waits for them, and re-layouts: 3.32 us -> none  [the longest x2 1.22 us: local(): flat = lambda v: v.reshape(batch * wide, channels)]
    add x5, other arithmetic: 2.8 us -> 0.02 us  [local(): sums = sums + partner(sums, bit)]
  transfers between devices with their start and end apart: 23 -> 27, of which waited for: 9 -> 10; matrix products, arithmetic and copies ran while one was open for 24% -> 3% of each run, Pallas kernels for 12% -> 16%
where the time goes in v2:
time: 118 us; the launch traced here: 117 us
  starting transfers between devices  42.9 us (36%)
  Pallas kernels  31.3 us (27%)
  waiting for transfers between devices  23.3 us (20%)
  local copies, waits for them, and re-layouts  15.6 us (13%)
  matrix products  2.26 us (2%)
    pallas_call x11, Pallas kernels, call(): pl.pallas_call(kernel, out_shape=out_shape, in_specs=[vmem] * used + [pl....  31.3 us
    ppermute x21, starting transfers between devices, partner(): return lax.ppermute(value, AXES, [(i, i ^ bit) for i in range(size)])  24.7 us
    ppermute x21, waiting for transfers between devices, partner(): return lax.ppermute(value, AXES, [(i, i ^ bit) for i in range(size)])  19.7 us
    unnamed x54, local copies, waits for them, and re-layouts  15.6 us
    ppermute x3, starting transfers between devices, swap(): return lax.ppermute(value, AXES, pairs)  7.13 us
    all_to_all x1, starting transfers between devices, local(): stats = lax.all_to_all(pay, AXES, 0, 0)  6.69 us
    ppermute x2, starting transfers between devices, shift(): return lax.ppermute(value, AXES, pairs)  4.39 us
    ppermute x3, waiting for transfers between devices, swap(): return lax.ppermute(value, AXES, pairs)  3.65 us
  transfers between devices with their start and end apart: 27, of which 10 were waited for; matrix products, arithmetic and copies ran while one was open for 3% of the time, Pallas kernels for 16%

profile of v2, /device:TPU:0, one launch (start us, length us, event | category | flops | bytes accessed | tf_op | source)
XLA Modules:
  0.0 117.0 jit_solution(8168233001895478919)
XLA Ops:
  0.7 1.3 %copy-done.1 = bf16[2,64,8,320]{3,2,1,0:T(8,128)(2,1)S(1)} copy-done((bf16[2,64,8,320]{3,2,1,0:T(8,128)(2,1)S(1)}, bf16[2,64,8,320]{3,2,1,0:T(8,128)(2,1)}, u32[]{:S(2)}) %copy-start.1) | copy-done | bytes 655384
  1.9 1.1 copy-done.5
  3.1 1.8 %shard_map.153 = (f32[32,1,128]{2,1,0:T(1,128)}, f32[4,64,1,320]{3,2,1,0:T(1,128)}, f32[4,64,1,320]{3,2,1,0:T(1,128)}, f32[32,320]{1,0:T(8,128)S(1)}, f32[4,1,32...) custom-call(bf16[1024,320]{1,0:T(8,128)(2,1)S(1)} %bitcast.14, bf16[1024,320]{1,0:T(8,128)(2,1)S(1)} %bitcast.19), custom_call_target="tpu_custom_call" | custom-call | bytes 2000000 | tf_op jit(solution)/shard_map/pallas_call | solution.py:32
  4.9 3.1 %collective-permute-start = (f32[4,64,1,320]{3,2,1,0:T(1,128)}, f32[4,64,1,320]{3,2,1,0:T(1,128)}, u32[]{:S(2)}, u32[]{:S(2)}) collective-permute-start(f32[4,64,1,320]{3,2,1,0:T(1,128)} %get-tuple-element.36), channel_id=1, source_target_pairs={{0,1},{1,2},{2,3},{3,4},{4,5},{5,6},{6,7},{7,8},{8,9},{9,10},{10,1... | collective-permute-start | bytes 983048 | tf_op jit(solution)/shard_map/ppermute | solution.py:455
  8.0 1.3 %collective-permute-start.1 = (f32[4,64,1,320]{3,2,1,0:T(1,128)}, f32[4,64,1,320]{3,2,1,0:T(1,128)}, u32[]{:S(2)}, u32[]{:S(2)}) collective-permute-start(f32[4,64,1,320]{3,2,1,0:T(1,128)} %get-tuple-element.37), channel_id=1, source_target_pairs={{1,0},{2,1},{3,2},{4,3},{5,4},{6,5},{7,6},{8,7},{9,8},{10,9},{11,1... | collective-permute-start | bytes 983048 | tf_op jit(solution)/shard_map/ppermute | solution.py:455
  9.2 2.4 %collective-permute-start.2 = (f32[32,320]{1,0:T(8,128)S(1)}, f32[32,320]{1,0:T(8,128)S(1)}, u32[]{:S(2)}, u32[]{:S(2)}) collective-permute-start(f32[32,320]{1,0:T(8,128)S(1)} %get-tuple-element.38), channel_id=1, source_target_pairs={{0,16},{1,17},{2,18},{3,19},{4,20},{5,21},{6,22},{7,23},{8,24},{9,... | collective-permute-start | bytes 122888 | tf_op jit(solution)/shard_map/ppermute | solution.py:465
  11.7 6.7 %all-to-all-start = ((f32[32,1,128]{2,1,0:T(1,128)}), f32[32,1,128]{2,1,0:T(1,128)S(1)}, u32[]{:S(2)}, u32[]{:S(2)}) async-start(f32[32,1,128]{2,1,0:T(1,128)} %get-tuple-element.35), calls=%async_computation | async-start | bytes 32768 | tf_op jit(solution)/shard_map/all_to_all | solution.py:513
  18.4 3.4 %collective-permute-start.3 = (f32[4,1,320]{2,1,0:T(1,128)S(1)}, f32[4,1,320]{2,1,0:T(1,128)S(1)}, u32[]{:S(2)}, u32[]{:S(2)}) collective-permute-start(f32[4,1,320]{2,1,0:T(1,128)S(1)} %get-tuple-element.39), channel_id=1, source_target_pairs={{0,17},{1,18},{2,19},{3,20},{4,21},{5,22},{6,23},{7,24},{8,25},{9,... | collective-permute-start | bytes 15368 | tf_op jit(solution)/shard_map/ppermute | solution.py:465
  21.8 1.3 %collective-permute-start.4 = (f32[4,1,320]{2,1,0:T(1,128)S(1)}, f32[4,1,320]{2,1,0:T(1,128)S(1)}, u32[]{:S(2)}, u32[]{:S(2)}) collective-permute-start(f32[4,1,320]{2,1,0:T(1,128)S(1)} %get-tuple-element.40), channel_id=1, source_target_pairs={{1,16},{2,17},{3,18},{4,19},{5,20},{6,21},{7,22},{8,23},{9,24},{10... | collective-permute-start | bytes 15368 | tf_op jit(solution)/shard_map/ppermute | solution.py:465
  23.1 0.0 collective-permute-done.3.refs_8_.refs_11_.refs_6_.refs_9_.refs_5_
  23.1 3.6 %collective-permute-done.4.refs_9_.refs_12_.refs_7_.refs_10_.refs_6_ = f32[4,1,320]{2,1,0:T(1,128)S(1)} collective-permute-done((f32[4,1,320]{2,1,0:T(1,128)S(1)}, f32[4,1,320]{2,1,0:T(1,128)S(1)}, u32[]{:S(2)}, u32[]{:S(2)}) %collective-permute-start.4) | collective-permute-done | bytes 5152 | tf_op jit(solution)/shard_map/ppermute | solution.py:465
  26.8 1.1 copy-done.2
  27.9 1.1 copy-done.6
  29.1 0.7 copy-done.15
  29.7 0.7 copy-done.23
  30.4 6.4 %shard_map.154 = (f32[8,320]{1,0:T(8,128)S(1)}, f32[2,8,80,384]{3,2,1,0:T(8,128)S(1)}, bf16[1,2,8,80,384]{4,3,2,1,0:T(8,128)(2,1)S(1)}) custom-call(f32[32,1,128]{2,1,0:T(1,128)S(1)} %all-to-all-done.refs_0_, f32[320]{0:T(512)S(1)} %copy-done.15, f32[320]{0:T(512)S(1)} %copy-done.23, bf16[1024,320]{1,0:T(8,128)(2,1)S(1)} %bitcast.15, ...), custom_call_target="tpu_custom_call" | custom-call | flops 1887436800 | bytes 2000000 | tf_op jit(solution)/shard_map/pallas_call | solution.py:32
  36.8 2.2 %collective-permute-start.5 = (bf16[2,8,80,384]{3,2,1,0:T(8,128)(2,1)S(1)}, bf16[2,8,80,384]{3,2,1,0:T(8,128)(2,1)S(1)}, u32[]{:S(2)}, u32[]{:S(2)}) collective-permute-start(bf16[2,8,80,384]{3,2,1,0:T(8,128)(2,1)S(1)} %bitcast.27), channel_id=1, source_target_pairs={{0,1},{1,0},{2,3},{3,2},{4,5},{5,4},{6,7},{7,6},{8,9},{9,8},{10,11... | collective-permute-start | bytes 2949128 | tf_op jit(solution)/shard_map/ppermute | solution.py:444
  39.1 0.7 fusion.7
  39.8 1.5 %collective-permute-done.5.refs_1_ = bf16[2,8,80,384]{3,2,1,0:T(8,128)(2,1)S(1)} collective-permute-done((bf16[2,8,80,384]{3,2,1,0:T(8,128)(2,1)S(1)}, bf16[2,8,80,384]{3,2,1,0:T(8,128)(2,1)S(1)}, u32[]{:S(2)}, u32[]{:S(2)}) %collective-permute-start.5) | collective-permute-done | bytes 983072 | tf_op jit(solution)/shard_map/ppermute | solution.py:444
  41.2 0.9 shard_map.155
  42.2 0.8 copy-done.11
  43.0 0.8 copy-done.13
  43.7 0.6 collective-permute-start.6
  44.3 2.4 %collective-permute-start.7 = (bf16[2,2,80,384]{3,2,1,0:T(8,128)(2,1)}, bf16[2,2,80,384]{3,2,1,0:T(8,128)(2,1)}, u32[]{:S(2)}, u32[]{:S(2)}) collective-permute-start(bf16[2,2,80,384]{3,2,1,0:T(8,128)(2,1)} %get-tuple-element.46.refs_13_), channel_id=1, source_target_pairs={{0,2},{1,3},{2,0},{3,1},{4,6},{5,7},{6,4},{7,5},{8,10},{9,11},{10,... | collective-permute-start | bytes 737288 | tf_op jit(solution)/shard_map/ppermute | solution.py:444
  46.7 2.0 %fusion.1.refs_6_ = bf16[2,1280]{1,0:T(2,128)(2,1)S(1)} fusion(bf16[1280,1280]{1,0:T(8,128)(2,1)S(1)} %copy-done, bf16[320,1280]{1,0:T(8,128)(2,1)} %param.16, bf16[2,160]{1,0:T(2,128)(2,1)} %get-tuple-element.64, bf16[2,160]{1,0:T(2,128)(2,1)S(1)} %get-tuple-element.63), kind=kOutput, calls=%fused_computation.3 | convolution fusion | flops 8220160 | bytes 4102400 | tf_op jit(solution)/shard_map/dot_general | solution.py:439
  48.7 1.1 copy-done.3
  49.8 1.1 copy-done.7
  50.9 1.6 %copy-done.17 = bf16[3,3,320,320]{3,2,1,0:T(8,128)(2,1)S(1)} copy-done((bf16[3,3,320,320]{3,2,1,0:T(8,128)(2,1)S(1)}, bf16[3,3,320,320]{3,2,1,0:T(8,128)(2,1)}, u32[]{:S(2)}) %copy-start.17) | copy-done | bytes 1843224
  52.6 0.8 copy-done.20
  53.4 0.7 copy-done.22
  54.1 7.5 %shard_map.156 = (f32[1024,320]{1,0:T(8,128)S(1)}, f32[8,320]{1,0:T(8,128)S(1)}) custom-call(f32[8,320]{1,0:T(8,128)S(1)} %get-tuple-element.41.refs_0_, bf16[1024,320]{1,0:T(8,128)(2,1)S(1)} %bitcast.16, bf16[1024,320]{1,0:T(8,128)(2,1)S(1)} %bitcast.21, f32[4,64,1,320]{3,2,1,0:T(1,128)} %collective-permute-done.refs_5_.refs_3_.refs_2_, ...), custom_call_target="tpu_custom_call" | custom-call | flops 1887436800 | bytes 2000000 | tf_op jit(solution)/shard_map/pallas_call | solution.py:32
  61.6 1.2 %shard_map.157 = (bf16[2,80,384]{2,1,0:T(8,128)(2,1)S(1)}, f32[2,80,384]{2,1,0:T(8,128)S(1)}, bf16[2,80,384]{2,1,0:T(8,128)(2,1)S(1)}, f32[2,80,384]{2,1,0:T(8,128)S(1)}) custom-call(bf16[2,2,80,384]{3,2,1,0:T(8,128)(2,1)S(1)} %collective-permute-done.6.refs_0_, f32[2,2,80,384]{3,2,1,0:T(8,128)S(1)} %copy-done.12, ...), custom_call_target="tpu_custom_call" | custom-call | bytes 2000000 | tf_op jit(solution)/shard_map/pallas_call | solution.py:32
  62.8 0.1 collective-permute-start.8
  62.9 1.5 %collective-permute-start.9 = (bf16[2,80,384]{2,1,0:T(8,128)(2,1)S(1)}, bf16[2,80,384]{2,1,0:T(8,128)(2,1)S(1)}, u32[]{:S(2)}, u32[]{:S(2)}) collective-permute-start(bf16[2,80,384]{2,1,0:T(8,128)(2,1)S(1)} %get-tuple-element.51), channel_id=1, source_target_pairs={{0,16},{1,17},{2,18},{3,19},{4,20},{5,21},{6,22},{7,23},{8,24},{9,... | collective-permute-start | bytes 368648 | tf_op jit(solution)/shard_map/ppermute | solution.py:444
  64.5 0.3 fusion.22.refs_12_
  64.7 3.2 %collective-permute-done.8.refs_0_ = bf16[2,80,384]{2,1,0:T(8,128)(2,1)S(1)} collective-permute-done((bf16[2,80,384]{2,1,0:T(8,128)(2,1)S(1)}, bf16[2,80,384]{2,1,0:T(8,128)(2,1)S(1)}, u32[]{:S(2)}, u32[]{:S(2)}) %collective-permute-start.8) | collective-permute-done | bytes 122912 | tf_op jit(solution)/shard_map/ppermute | solution.py:444
  67.9 0.1 collective-permute-done.9.refs_2_
  68.0 0.1 shard_map.158
  68.1 1.5 %collective-permute-start.15 = (bf16[80,384]{1,0:T(8,128)(2,1)S(1)}, bf16[80,384]{1,0:T(8,128)(2,1)S(1)}, u32[]{:S(2)}, u32[]{:S(2)}) collective-permute-start(bf16[80,384]{1,0:T(8,128)(2,1)S(1)} %get-tuple-element.53.refs_13_), channel_id=1, source_target_pairs={{0,4},{1,5},{2,6},{3,7},{4,0},{5,1},{6,2},{7,3},{8,12},{9,13},{10,... | collective-permute-start | bytes 184328 | tf_op jit(solution)/shard_map/ppermute | solution.py:444
  69.6 1.9 %collective-permute-start.16 = (bf16[80,384]{1,0:T(8,128)(2,1)S(1)}, bf16[80,384]{1,0:T(8,128)(2,1)S(1)}, u32[]{:S(2)}, u32[]{:S(2)}) collective-permute-start(bf16[80,384]{1,0:T(8,128)(2,1)S(1)} %get-tuple-element.54.refs_14_), channel_id=1, source_target_pairs={{0,8},{1,9},{2,10},{3,11},{4,12},{5,13},{6,14},{7,15},{8,0},{9,1},... | collective-permute-start | bytes 184328 | tf_op jit(solution)/shard_map/ppermute | solution.py:444
  71.5 1.1 collective-permute-start.17
  72.6 8.0 %shard_map.159.refs_4_ = bf16[1024,320]{1,0:T(8,128)(2,1)} custom-call(f32[8,320]{1,0:T(8,128)S(1)} %get-tuple-element.41.refs_0_, bf16[1024,320]{1,0:T(8,128)(2,1)S(1)} %bitcast.17, f32[4,64,1,320]{3,2,1,0:T(1,128)} %collective-permute-done.refs_5_.refs_3_.refs_2_, f32[4,64,1,320]{3,2,1,0:T(1,128)} %collective-permute-done.1.refs_6_.refs_4_.refs_3_, ...), custom_call_target="tpu_custom_call" | custom-call | flops 1887436800 | bytes 2000000 | tf_op jit(solution)/shard_map/pallas_call | solution.py:32
  80.6 1.1 copy-done.10
  81.8 3.2 %collective-permute-start.24 = (bf16[80,384]{1,0:T(8,128)(2,1)S(1)}, bf16[80,384]{1,0:T(8,128)(2,1)S(1)}, u32[]{:S(2)}, u32[]{:S(2)}) collective-permute-start(bf16[80,384]{1,0:T(8,128)(2,1)S(1)} %shard_map.160.refs_7_.refs_0_), channel_id=1, source_target_pairs={{0,14},{1,15},{2,12},{3,13},{4,10},{5,11},{6,8},{7,9},{8,6},{9,7},... | collective-permute-start | bytes 184328 | tf_op jit(solution)/shard_map/ppermute | solution.py:444
  85.0 1.9 %collective-permute-start.23 = (bf16[80,384]{1,0:T(8,128)(2,1)S(1)}, bf16[80,384]{1,0:T(8,128)(2,1)S(1)}, u32[]{:S(2)}, u32[]{:S(2)}) collective-permute-start(bf16[80,384]{1,0:T(8,128)(2,1)S(1)} %shard_map.160.refs_7_.refs_0_), channel_id=1, source_target_pairs={{0,12},{1,13},{2,14},{3,15},{4,8},{5,9},{6,10},{7,11},{8,4},{9,5},... | collective-permute-start | bytes 184328 | tf_op jit(solution)/shard_map/ppermute | solution.py:444
  86.9 1.2 %collective-permute-done.10 = f32[8,320]{1,0:T(8,128)S(1)} collective-permute-done((f32[8,320]{1,0:T(8,128)S(1)}, f32[8,320]{1,0:T(8,128)S(1)}, u32[]{:S(2)}, u32[]{:S(2)}) %collective-permute-start.10) | collective-permute-done | bytes 10272 | tf_op jit(solution)/shard_map/ppermute | solution.py:444
  88.1 0.2 collective-permute-start.11
  88.3 3.5 %collective-permute-done.11 = f32[8,320]{1,0:T(8,128)S(1)} collective-permute-done((f32[8,320]{1,0:T(8,128)S(1)}, f32[8,320]{1,0:T(8,128)S(1)}, u32[]{:S(2)}, u32[]{:S(2)}) %collective-permute-start.11) | collective-permute-done | bytes 10272 | tf_op jit(solution)/shard_map/ppermute | solution.py:444
  91.8 3.7 %collective-permute-done.12 = f32[8,320]{1,0:T(8,128)S(1)} collective-permute-done((f32[8,320]{1,0:T(8,128)S(1)}, f32[8,320]{1,0:T(8,128)S(1)}, u32[]{:S(2)}, u32[]{:S(2)}) %collective-permute-start.12) | collective-permute-done | bytes 10272 | tf_op jit(solution)/shard_map/ppermute | solution.py:444
  95.5 0.5 collective-permute-start.13
  96.0 4.1 %collective-permute-done.13 = f32[8,320]{1,0:T(8,128)S(1)} collective-permute-done((f32[8,320]{1,0:T(8,128)S(1)}, f32[8,320]{1,0:T(8,128)S(1)}, u32[]{:S(2)}, u32[]{:S(2)}) %collective-permute-start.13) | collective-permute-done | bytes 10272 | tf_op jit(solution)/shard_map/ppermute | solution.py:444
  100.1 1.5 %collective-permute-start.14 = (f32[8,320]{1,0:T(8,128)S(1)}, f32[8,320]{1,0:T(8,128)S(1)}, u32[]{:S(2)}, u32[]{:S(2)}) collective-permute-start(f32[8,320]{1,0:T(8,128)S(1)} %add.27), channel_id=1, source_target_pairs={{0,16},{1,17},{2,18},{3,19},{4,20},{5,21},{6,22},{7,23},{8,24},{9,... | collective-permute-start | bytes 30728 | tf_op jit(solution)/shard_map/ppermute | solution.py:444
  101.6 1.0 collective-permute-start.22
  102.6 1.6 %collective-permute-start.21 = (bf16[80,384]{1,0:T(8,128)(2,1)S(1)}, bf16[80,384]{1,0:T(8,128)(2,1)S(1)}, u32[]{:S(2)}, u32[]{:S(2)}) collective-permute-start(bf16[80,384]{1,0:T(8,128)(2,1)S(1)} %shard_map.160.refs_7_.refs_0_), channel_id=1, source_target_pairs={{0,8},{1,9},{2,10},{3,11},{4,12},{5,13},{6,14},{7,15},{8,0},{9,1},... | collective-permute-start | bytes 184328 | tf_op jit(solution)/shard_map/ppermute | solution.py:444
  104.2 1.2 %collective-permute-start.20 = (bf16[80,384]{1,0:T(8,128)(2,1)S(1)}, bf16[80,384]{1,0:T(8,128)(2,1)S(1)}, u32[]{:S(2)}, u32[]{:S(2)}) collective-permute-start(bf16[80,384]{1,0:T(8,128)(2,1)S(1)} %shard_map.160.refs_7_.refs_0_), channel_id=1, source_target_pairs={{0,6},{1,7},{2,4},{3,5},{4,2},{5,3},{6,0},{7,1},{8,14},{9,15},{10,... | collective-permute-start | bytes 184328 | tf_op jit(solution)/shard_map/ppermute | solution.py:444
  105.4 2.0 %collective-permute-start.19 = (bf16[80,384]{1,0:T(8,128)(2,1)S(1)}, bf16[80,384]{1,0:T(8,128)(2,1)S(1)}, u32[]{:S(2)}, u32[]{:S(2)}) collective-permute-start(bf16[80,384]{1,0:T(8,128)(2,1)S(1)} %shard_map.160.refs_7_.refs_0_), channel_id=1, source_target_pairs={{0,4},{1,5},{2,6},{3,7},{4,0},{5,1},{6,2},{7,3},{8,12},{9,13},{10,... | collective-permute-start | bytes 184328 | tf_op jit(solution)/shard_map/ppermute | solution.py:444
  107.4 0.2 collective-permute-start.18
  107.7 3.4 %shard_map.161 = (f32[1024,320]{1,0:T(8,128)}, f32[320]{0:T(512)}, f32[320]{0:T(512)}, f32[320]{0:T(512)}, f32[320,1280]{1,0:T(8,128)}) custom-call(f32[8,320]{1,0:T(8,128)S(1)} %get-tuple-element.41.refs_0_, f32[8,320]{1,0:T(8,128)S(1)} %add.28.refs_1_, f32[320]{0:T(512)S(1)} %copy-done.16, bf16[1024,320]{1,0:T(8,128)(2,1)S(1)} %bitcast.18, ...), custom_call_target="tpu_custom_call" | custom-call | flops 2621440 | bytes 2000000 | tf_op jit(solution)/shard_map/pallas_call | solution.py:32
  111.1 0.6 collective-permute-done.18.refs_1_
  111.7 1.4 %copy-done.9 = f32[1024,320]{1,0:T(8,128)S(1)} copy-done((f32[1024,320]{1,0:T(8,128)S(1)}, f32[1024,320]{1,0:T(8,128)}, u32[]{:S(2)}) %copy-start.9) | copy-done | bytes 1310744
  113.1 0.1 shard_map.162.refs_0_
  113.1 0.1 collective-permute-start.25
  113.2 1.9 %collective-permute-done.25.refs_1_ = bf16[80,3072]{1,0:T(8,128)(2,1)S(1)} collective-permute-done((bf16[80,3072]{1,0:T(8,128)(2,1)S(1)}, bf16[80,3072]{1,0:T(8,128)(2,1)S(1)}, u32[]{:S(2)}, u32[]{:S(2)}) %collective-permute-start.25) | collective-permute-done | bytes 491552 | tf_op jit(solution)/shard_map/ppermute | solution.py:444
  115.1 1.9 %shard_map.163 = f32[9,160,320]{2,1,0:T(8,128)} custom-call(bf16[80,3072]{1,0:T(8,128)(2,1)S(1)} %shard_map.162.refs_0_, bf16[80,3072]{1,0:T(8,128)(2,1)S(1)} %collective-permute-done.25.refs_1_), custom_call_target="tpu_custom_call" | custom-call | bytes 2000000 | tf_op jit(solution)/shard_map/pallas_call | solution.py:32
  (65 shorter events, 0.2 us)
Async XLA Ops:
  0.6 46.1 %copy-start = (bf16[1280,1280]{1,0:T(8,128)(2,1)S(1)}, bf16[1280,1280]{1,0:T(8,128)(2,1)}, u32[]{:S(2)}) copy-start(bf16[1280,1280]{1,0:T(8,128)(2,1)} %param.17) | copy-start | bytes 9830404
  0.6 1.3 %copy-start.1 = (bf16[2,64,8,320]{3,2,1,0:T(8,128)(2,1)S(1)}, bf16[2,64,8,320]{3,2,1,0:T(8,128)(2,1)}, u32[]{:S(2)}) copy-start(bf16[2,64,8,320]{3,2,1,0:T(8,128)(2,1)} %param.10) | copy-start | bytes 1966084
  1.9 1.1 copy-start.5
  4.9 21.9 %collective-permute-start = (f32[4,64,1,320]{3,2,1,0:T(1,128)}, f32[4,64,1,320]{3,2,1,0:T(1,128)}, u32[]{:S(2)}, u32[]{:S(2)}) collective-permute-start(f32[4,64,1,320]{3,2,1,0:T(1,128)} %get-tuple-element.36), channel_id=1, source_target_pairs={{0,1},{1,2},{2,3},{3,4},{4,5},{5,6},{6,7},{7,8},{8,9},{9,10},{10,1... | collective-permute-start | bytes 983048 | tf_op jit(solution)/shard_map/ppermute | solution.py:455
  8.0 18.8 %collective-permute-start.1 = (f32[4,64,1,320]{3,2,1,0:T(1,128)}, f32[4,64,1,320]{3,2,1,0:T(1,128)}, u32[]{:S(2)}, u32[]{:S(2)}) collective-permute-start(f32[4,64,1,320]{3,2,1,0:T(1,128)} %get-tuple-element.37), channel_id=1, source_target_pairs={{1,0},{2,1},{3,2},{4,3},{5,4},{6,5},{7,6},{8,7},{9,8},{10,9},{11,1... | collective-permute-start | bytes 983048 | tf_op jit(solution)/shard_map/ppermute | solution.py:455
  9.2 17.5 %collective-permute-start.2 = (f32[32,320]{1,0:T(8,128)S(1)}, f32[32,320]{1,0:T(8,128)S(1)}, u32[]{:S(2)}, u32[]{:S(2)}) collective-permute-start(f32[32,320]{1,0:T(8,128)S(1)} %get-tuple-element.38), channel_id=1, source_target_pairs={{0,16},{1,17},{2,18},{3,19},{4,20},{5,21},{6,22},{7,23},{8,24},{9,... | collective-permute-start | bytes 122888 | tf_op jit(solution)/shard_map/ppermute | solution.py:465
  11.7 15.1 %all-to-all-start = ((f32[32,1,128]{2,1,0:T(1,128)}), f32[32,1,128]{2,1,0:T(1,128)S(1)}, u32[]{:S(2)}, u32[]{:S(2)}) async-start(f32[32,1,128]{2,1,0:T(1,128)} %get-tuple-element.35), calls=%async_computation | async-start | bytes 32768 | tf_op jit(solution)/shard_map/all_to_all | solution.py:513
  18.4 4.8 %collective-permute-start.3 = (f32[4,1,320]{2,1,0:T(1,128)S(1)}, f32[4,1,320]{2,1,0:T(1,128)S(1)}, u32[]{:S(2)}, u32[]{:S(2)}) collective-permute-start(f32[4,1,320]{2,1,0:T(1,128)S(1)} %get-tuple-element.39), channel_id=1, source_target_pairs={{0,17},{1,18},{2,19},{3,20},{4,21},{5,22},{6,23},{7,24},{8,25},{9,... | collective-permute-start | bytes 15368 | tf_op jit(solution)/shard_map/ppermute | solution.py:465
  21.8 17.3 %copy-start.26 = (s32[2]{0:T(128)S(1)}, s32[2]{0:T(128)}, u32[]{:S(2)}) copy-start(s32[2]{0:T(128)} %param.11) | copy-start | bytes 28
  21.8 4.9 %collective-permute-start.4 = (f32[4,1,320]{2,1,0:T(1,128)S(1)}, f32[4,1,320]{2,1,0:T(1,128)S(1)}, u32[]{:S(2)}, u32[]{:S(2)}) collective-permute-start(f32[4,1,320]{2,1,0:T(1,128)S(1)} %get-tuple-element.40), channel_id=1, source_target_pairs={{1,16},{2,17},{3,18},{4,19},{5,20},{6,21},{7,22},{8,23},{9,24},{10... | collective-permute-start | bytes 15368 | tf_op jit(solution)/shard_map/ppermute | solution.py:465
  26.8 10.0 %copy-start.21 = (f32[4,1,320]{2,1,0:T(1,128)}, f32[4,1,320]{2,1,0:T(1,128)S(1)}, u32[]{:S(2)}) copy-start(f32[4,1,320]{2,1,0:T(1,128)S(1)} %collective-permute-done.4.refs_9_.refs_12_.refs_7_.refs_10_.refs_6_) | copy-start | bytes 15364
  26.8 10.0 %copy-start.19 = (f32[32,320]{1,0:T(8,128)}, f32[32,320]{1,0:T(8,128)S(1)}, u32[]{:S(2)}) copy-start(f32[32,320]{1,0:T(8,128)S(1)} %collective-permute-done.2.refs_7_.refs_10_.refs_5_.refs_8_.refs_4_) | copy-start | bytes 122884
  26.8 1.1 copy-start.2
  27.9 1.1 copy-start.6
  29.1 0.7 copy-start.15
  29.7 0.7 copy-start.23
  36.8 4.4 %collective-permute-start.5 = (bf16[2,8,80,384]{3,2,1,0:T(8,128)(2,1)S(1)}, bf16[2,8,80,384]{3,2,1,0:T(8,128)(2,1)S(1)}, u32[]{:S(2)}, u32[]{:S(2)}) collective-permute-start(bf16[2,8,80,384]{3,2,1,0:T(8,128)(2,1)S(1)} %bitcast.27), channel_id=1, source_target_pairs={{0,1},{1,0},{2,3},{3,2},{4,5},{5,4},{6,7},{7,6},{8,9},{9,8},{10,11... | collective-permute-start | bytes 2949128 | tf_op jit(solution)/shard_map/ppermute | solution.py:444
  42.2 0.8 copy-start.11
  43.0 0.8 copy-start.13
  43.7 17.9 %collective-permute-start.6 = (bf16[2,2,80,384]{3,2,1,0:T(8,128)(2,1)}, bf16[2,2,80,384]{3,2,1,0:T(8,128)(2,1)S(1)}, u32[]{:S(2)}, u32[]{:S(2)}) collective-permute-start(bf16[2,2,80,384]{3,2,1,0:T(8,128)(2,1)} %get-tuple-element.44.refs_12_), channel_id=1, source_target_pairs={{0,16},{1,17},{2,18},{3,19},{4,20},{5,21},{6,22},{7,23},{8,24},{9,... | collective-permute-start | bytes 737288 | tf_op jit(solution)/shard_map/ppermute | solution.py:444
  44.3 17.3 %collective-permute-start.7 = (bf16[2,2,80,384]{3,2,1,0:T(8,128)(2,1)}, bf16[2,2,80,384]{3,2,1,0:T(8,128)(2,1)}, u32[]{:S(2)}, u32[]{:S(2)}) collective-permute-start(bf16[2,2,80,384]{3,2,1,0:T(8,128)(2,1)} %get-tuple-element.46.refs_13_), channel_id=1, source_target_pairs={{0,2},{1,3},{2,0},{3,1},{4,6},{5,7},{6,4},{7,5},{8,10},{9,11},{10,... | collective-permute-start | bytes 737288 | tf_op jit(solution)/shard_map/ppermute | solution.py:444
  48.7 1.1 copy-start.3
  49.8 1.1 copy-start.7
  50.9 1.6 %copy-start.17 = (bf16[3,3,320,320]{3,2,1,0:T(8,128)(2,1)S(1)}, bf16[3,3,320,320]{3,2,1,0:T(8,128)(2,1)}, u32[]{:S(2)}) copy-start(bf16[3,3,320,320]{3,2,1,0:T(8,128)(2,1)} %param.14) | copy-start | bytes 5529604
  52.6 0.8 copy-start.20
  53.4 0.7 copy-start.22
  54.1 7.6 %copy-start.12 = (f32[2,2,80,384]{3,2,1,0:T(8,128)S(1)}, f32[2,2,80,384]{3,2,1,0:T(8,128)}, u32[]{:S(2)}) copy-start(f32[2,2,80,384]{3,2,1,0:T(8,128)} %copy-done.11) | copy-start | bytes 1474564
  54.1 7.6 %copy-start.14 = (f32[2,2,80,384]{3,2,1,0:T(8,128)S(1)}, f32[2,2,80,384]{3,2,1,0:T(8,128)}, u32[]{:S(2)}) copy-start(f32[2,2,80,384]{3,2,1,0:T(8,128)} %copy-done.13) | copy-start | bytes 1474564
  54.1 10.4 %copy-start.25 = (bf16[1280,320]{0,1:T(8,128)(2,1)S(1)}, bf16[1280,320]{0,1:T(8,128)(2,1)}, u32[]{:S(2)}) copy-start(bf16[1280,320]{0,1:T(8,128)(2,1)} %param.18) | copy-start | bytes 2457604
  61.6 11.0 %copy-start.4 = (bf16[2,64,8,320]{3,2,1,0:T(8,128)(2,1)S(1)}, bf16[2,64,8,320]{3,2,1,0:T(8,128)(2,1)}, u32[]{:S(2)}) copy-start(bf16[2,64,8,320]{3,2,1,0:T(8,128)(2,1)} %param.10) | copy-start | bytes 1966084
  61.6 11.0 %copy-start.18 = (bf16[3,3,320,320]{3,2,1,0:T(8,128)(2,1)S(1)}, bf16[3,3,320,320]{3,2,1,0:T(8,128)(2,1)}, u32[]{:S(2)}) copy-start(bf16[3,3,320,320]{3,2,1,0:T(8,128)(2,1)} %param.14) | copy-start | bytes 5529604
  61.6 11.0 %copy-start.24 = (f32[320]{0:T(512)S(1)}, f32[320]{0:T(512)}, u32[]{:S(2)}) copy-start(f32[320]{0:T(512)} %refs_11_.1) | copy-start | bytes 3844
  62.8 5.1 %collective-permute-start.8 = (bf16[2,80,384]{2,1,0:T(8,128)(2,1)S(1)}, bf16[2,80,384]{2,1,0:T(8,128)(2,1)S(1)}, u32[]{:S(2)}, u32[]{:S(2)}) collective-permute-start(bf16[2,80,384]{2,1,0:T(8,128)(2,1)S(1)} %get-tuple-element.49), channel_id=1, source_target_pairs={{0,2},{1,3},{2,0},{3,1},{4,6},{5,7},{6,4},{7,5},{8,10},{9,11},{10,... | collective-permute-start | bytes 368648 | tf_op jit(solution)/shard_map/ppermute | solution.py:444
  62.9 5.1 %collective-permute-start.9 = (bf16[2,80,384]{2,1,0:T(8,128)(2,1)S(1)}, bf16[2,80,384]{2,1,0:T(8,128)(2,1)S(1)}, u32[]{:S(2)}, u32[]{:S(2)}) collective-permute-start(bf16[2,80,384]{2,1,0:T(8,128)(2,1)S(1)} %get-tuple-element.51), channel_id=1, source_target_pairs={{0,16},{1,17},{2,18},{3,19},{4,20},{5,21},{6,22},{7,23},{8,24},{9,... | collective-permute-start | bytes 368648 | tf_op jit(solution)/shard_map/ppermute | solution.py:444
  68.1 12.5 %collective-permute-start.15 = (bf16[80,384]{1,0:T(8,128)(2,1)S(1)}, bf16[80,384]{1,0:T(8,128)(2,1)S(1)}, u32[]{:S(2)}, u32[]{:S(2)}) collective-permute-start(bf16[80,384]{1,0:T(8,128)(2,1)S(1)} %get-tuple-element.53.refs_13_), channel_id=1, source_target_pairs={{0,4},{1,5},{2,6},{3,7},{4,0},{5,1},{6,2},{7,3},{8,12},{9,13},{10,... | collective-permute-start | bytes 184328 | tf_op jit(solution)/shard_map/ppermute | solution.py:444
  69.6 11.0 %collective-permute-start.16 = (bf16[80,384]{1,0:T(8,128)(2,1)S(1)}, bf16[80,384]{1,0:T(8,128)(2,1)S(1)}, u32[]{:S(2)}, u32[]{:S(2)}) collective-permute-start(bf16[80,384]{1,0:T(8,128)(2,1)S(1)} %get-tuple-element.54.refs_14_), channel_id=1, source_target_pairs={{0,8},{1,9},{2,10},{3,11},{4,12},{5,13},{6,14},{7,15},{8,0},{9,1},... | collective-permute-start | bytes 184328 | tf_op jit(solution)/shard_map/ppermute | solution.py:444
  71.5 36.2 %copy-start.8 = (bf16[2,64,8,320]{3,2,1,0:T(8,128)(2,1)S(1)}, bf16[2,64,8,320]{3,2,1,0:T(8,128)(2,1)}, u32[]{:S(2)}) copy-start(bf16[2,64,8,320]{3,2,1,0:T(8,128)(2,1)} %param.19) | copy-start | bytes 1966084
  71.5 36.2 %copy-start.16 = (f32[320]{0:T(512)S(1)}, f32[320]{0:T(512)}, u32[]{:S(2)}) copy-start(f32[320]{0:T(512)} %refs_2_.3) | copy-start | bytes 3844
  71.5 9.1 %collective-permute-start.17 = (bf16[80,384]{1,0:T(8,128)(2,1)S(1)}, bf16[80,384]{1,0:T(8,128)(2,1)S(1)}, u32[]{:S(2)}, u32[]{:S(2)}) collective-permute-start(bf16[80,384]{1,0:T(8,128)(2,1)S(1)} %get-tuple-element.55.refs_15_), channel_id=1, source_target_pairs={{0,12},{1,13},{2,14},{3,15},{4,8},{5,9},{6,10},{7,11},{8,4},{9,5},... | collective-permute-start | bytes 184328 | tf_op jit(solution)/shard_map/ppermute | solution.py:444
  80.6 1.1 copy-start.10
  81.8 23.6 %collective-permute-start.24 = (bf16[80,384]{1,0:T(8,128)(2,1)S(1)}, bf16[80,384]{1,0:T(8,128)(2,1)S(1)}, u32[]{:S(2)}, u32[]{:S(2)}) collective-permute-start(bf16[80,384]{1,0:T(8,128)(2,1)S(1)} %shard_map.160.refs_7_.refs_0_), channel_id=1, source_target_pairs={{0,14},{1,15},{2,12},{3,13},{4,10},{5,11},{6,8},{7,9},{8,6},{9,7},... | collective-permute-start | bytes 184328 | tf_op jit(solution)/shard_map/ppermute | solution.py:444
  85.0 22.4 %collective-permute-start.23 = (bf16[80,384]{1,0:T(8,128)(2,1)S(1)}, bf16[80,384]{1,0:T(8,128)(2,1)S(1)}, u32[]{:S(2)}, u32[]{:S(2)}) collective-permute-start(bf16[80,384]{1,0:T(8,128)(2,1)S(1)} %shard_map.160.refs_7_.refs_0_), channel_id=1, source_target_pairs={{0,12},{1,13},{2,14},{3,15},{4,8},{5,9},{6,10},{7,11},{8,4},{9,5},... | collective-permute-start | bytes 184328 | tf_op jit(solution)/shard_map/ppermute | solution.py:444
  86.9 1.2 %collective-permute-start.10 = (f32[8,320]{1,0:T(8,128)S(1)}, f32[8,320]{1,0:T(8,128)S(1)}, u32[]{:S(2)}, u32[]{:S(2)}) collective-permute-start(f32[8,320]{1,0:T(8,128)S(1)} %get-tuple-element.48.refs_4_), channel_id=1, source_target_pairs={{0,1},{1,0},{2,3},{3,2},{4,5},{5,4},{6,7},{7,6},{8,9},{9,8},{10,11... | collective-permute-start | bytes 30728 | tf_op jit(solution)/shard_map/ppermute | solution.py:444
  88.1 3.7 %collective-permute-start.11 = (f32[8,320]{1,0:T(8,128)S(1)}, f32[8,320]{1,0:T(8,128)S(1)}, u32[]{:S(2)}, u32[]{:S(2)}) collective-permute-start(f32[8,320]{1,0:T(8,128)S(1)} %add.24), channel_id=1, source_target_pairs={{0,2},{1,3},{2,0},{3,1},{4,6},{5,7},{6,4},{7,5},{8,10},{9,11},{10,... | collective-permute-start | bytes 30728 | tf_op jit(solution)/shard_map/ppermute | solution.py:444
  91.8 3.7 %collective-permute-start.12 = (f32[8,320]{1,0:T(8,128)S(1)}, f32[8,320]{1,0:T(8,128)S(1)}, u32[]{:S(2)}, u32[]{:S(2)}) collective-permute-start(f32[8,320]{1,0:T(8,128)S(1)} %add.25), channel_id=1, source_target_pairs={{0,4},{1,5},{2,6},{3,7},{4,0},{5,1},{6,2},{7,3},{8,12},{9,13},{10,... | collective-permute-start | bytes 30728 | tf_op jit(solution)/shard_map/ppermute | solution.py:444
  95.5 4.6 %collective-permute-start.13 = (f32[8,320]{1,0:T(8,128)S(1)}, f32[8,320]{1,0:T(8,128)S(1)}, u32[]{:S(2)}, u32[]{:S(2)}) collective-permute-start(f32[8,320]{1,0:T(8,128)S(1)} %add.26), channel_id=1, source_target_pairs={{0,8},{1,9},{2,10},{3,11},{4,12},{5,13},{6,14},{7,15},{8,0},{9,1},... | collective-permute-start | bytes 30728 | tf_op jit(solution)/shard_map/ppermute | solution.py:444
  100.1 4.1 %collective-permute-start.14 = (f32[8,320]{1,0:T(8,128)S(1)}, f32[8,320]{1,0:T(8,128)S(1)}, u32[]{:S(2)}, u32[]{:S(2)}) collective-permute-start(f32[8,320]{1,0:T(8,128)S(1)} %add.27), channel_id=1, source_target_pairs={{0,16},{1,17},{2,18},{3,19},{4,20},{5,21},{6,22},{7,23},{8,24},{9,... | collective-permute-start | bytes 30728 | tf_op jit(solution)/shard_map/ppermute | solution.py:444
  101.6 9.5 %collective-permute-start.22 = (bf16[80,384]{1,0:T(8,128)(2,1)S(1)}, bf16[80,384]{1,0:T(8,128)(2,1)S(1)}, u32[]{:S(2)}, u32[]{:S(2)}) collective-permute-start(bf16[80,384]{1,0:T(8,128)(2,1)S(1)} %shard_map.160.refs_7_.refs_0_), channel_id=1, source_target_pairs={{0,10},{1,11},{2,8},{3,9},{4,14},{5,15},{6,12},{7,13},{8,2},{9,3},... | collective-permute-start | bytes 184328 | tf_op jit(solution)/shard_map/ppermute | solution.py:444
  102.6 8.5 %collective-permute-start.21 = (bf16[80,384]{1,0:T(8,128)(2,1)S(1)}, bf16[80,384]{1,0:T(8,128)(2,1)S(1)}, u32[]{:S(2)}, u32[]{:S(2)}) collective-permute-start(bf16[80,384]{1,0:T(8,128)(2,1)S(1)} %shard_map.160.refs_7_.refs_0_), channel_id=1, source_target_pairs={{0,8},{1,9},{2,10},{3,11},{4,12},{5,13},{6,14},{7,15},{8,0},{9,1},... | collective-permute-start | bytes 184328 | tf_op jit(solution)/shard_map/ppermute | solution.py:444
  104.2 6.9 %collective-permute-start.20 = (bf16[80,384]{1,0:T(8,128)(2,1)S(1)}, bf16[80,384]{1,0:T(8,128)(2,1)S(1)}, u32[]{:S(2)}, u32[]{:S(2)}) collective-permute-start(bf16[80,384]{1,0:T(8,128)(2,1)S(1)} %shard_map.160.refs_7_.refs_0_), channel_id=1, source_target_pairs={{0,6},{1,7},{2,4},{3,5},{4,2},{5,3},{6,0},{7,1},{8,14},{9,15},{10,... | collective-permute-start | bytes 184328 | tf_op jit(solution)/shard_map/ppermute | solution.py:444
  105.4 5.7 %collective-permute-start.19 = (bf16[80,384]{1,0:T(8,128)(2,1)S(1)}, bf16[80,384]{1,0:T(8,128)(2,1)S(1)}, u32[]{:S(2)}, u32[]{:S(2)}) collective-permute-start(bf16[80,384]{1,0:T(8,128)(2,1)S(1)} %shard_map.160.refs_7_.refs_0_), channel_id=1, source_target_pairs={{0,4},{1,5},{2,6},{3,7},{4,0},{5,1},{6,2},{7,3},{8,12},{9,13},{10,... | collective-permute-start | bytes 184328 | tf_op jit(solution)/shard_map/ppermute | solution.py:444
  107.4 4.2 %collective-permute-start.18 = (bf16[80,384]{1,0:T(8,128)(2,1)S(1)}, bf16[80,384]{1,0:T(8,128)(2,1)S(1)}, u32[]{:S(2)}, u32[]{:S(2)}) collective-permute-start(bf16[80,384]{1,0:T(8,128)(2,1)S(1)} %shard_map.160.refs_7_.refs_0_), channel_id=1, source_target_pairs={{0,2},{1,3},{2,0},{3,1},{4,6},{5,7},{6,4},{7,5},{8,10},{9,11},{10,... | collective-permute-start | bytes 184328 | tf_op jit(solution)/shard_map/ppermute | solution.py:444
  111.7 1.4 %copy-start.9 = (f32[1024,320]{1,0:T(8,128)S(1)}, f32[1024,320]{1,0:T(8,128)}, u32[]{:S(2)}) copy-start(f32[1024,320]{1,0:T(8,128)} %get-tuple-element.58.refs_8_) | copy-start | bytes 3932164
  113.1 1.9 %collective-permute-start.25 = (bf16[80,3072]{1,0:T(8,128)(2,1)S(1)}, bf16[80,3072]{1,0:T(8,128)(2,1)S(1)}, u32[]{:S(2)}, u32[]{:S(2)}) collective-permute-start(bf16[80,3072]{1,0:T(8,128)(2,1)S(1)} %shard_map.162.refs_0_), channel_id=1, source_target_pairs={{0,1},{1,0},{2,3},{3,2},{4,5},{5,4},{6,7},{7,6},{8,9},{9,8},{10,11... | collective-permute-start | bytes 1474568 | tf_op jit(solution)/shard_map/ppermute | solution.py:444

commit v3 on v2

--- a/solution.py
+++ b/solution.py
@@ -14,7 +14,7 @@
 F32 = jnp.float32
 BF16 = jnp.bfloat16
 AXES = ("row", "col")
-VMEM_LIMIT = 32 * 1024 * 1024
+VMEM_LIMIT = 20 * 1024 * 1024
 HI = lax.Precision.HIGHEST
 
 
@@ -22,22 +22,46 @@
     return lax.broadcasted_iota(jnp.int32, shape, dim)
 
 
-def call(body, out_shape, operands, after=(), scratch=(), flops=0, nbytes=2_000_000):
-    used, waits = len(operands), len(after)
+def call(body, out_shape, operands, far=(), after=(), scratch=(), flops=0, nbytes=2_000_000):
+    count, used, waits = len(far), len(operands), len(after)
 
     def kernel(*refs):
-        body(*refs[:used], *refs[used + waits :])
+        ins = refs[:count]
+        rest = refs[count : count + used] + refs[count + used + waits :]
+        if not count:
+            return body(*rest)
+        holds, sems = rest[-1 - count : -1], rest[-1]
+        copies = [
+            pltpu.make_async_copy(ins[i], holds[i], sems.at[i]) for i in range(count)
+        ]
+        for c in copies:
+            c.start()
+
+        def loader(i):
+            def load():
+                copies[i].wait()
+                return holds[i]
+
+            return load
+
+        body(*[loader(i) for i in range(count)], *rest[: -1 - count])
 
     vmem = pl.BlockSpec(memory_space=pltpu.VMEM)
+    scratch = list(scratch)
+    if count:
+        scratch += [pltpu.VMEM(v.shape, v.dtype) for v in far]
+        scratch.append(pltpu.SemaphoreType.DMA((count,)))
     return pl.pallas_call(
         kernel,
         out_shape=out_shape,
-        in_specs=[vmem] * used + [pl.BlockSpec(memory_space=pl.ANY)] * waits,
+        in_specs=[pl.BlockSpec(memory_space=pltpu.HBM)] * count
+        + [vmem] * used
+        + [pl.BlockSpec(memory_space=pl.ANY)] * waits,
         out_specs=jax.tree.map(lambda _: vmem, out_shape),
-        scratch_shapes=list(scratch),
+        scratch_shapes=scratch,
         compiler_params=pltpu.CompilerParams(vmem_limit_bytes=VMEM_LIMIT),
         cost_estimate=pl.CostEstimate(flops=flops, bytes_accessed=nbytes, transcendentals=0),
-    )(*operands, *after)
+    )(*far, *operands, *after)
 
 
 def group_matrix(channels, lanes):
@@ -66,20 +90,24 @@
     return out
 
 
-def stats_kernel(batch, w, rows, x_ref, g_ref, pay_ref, west_ref, east_ref, *edge_refs):
-    n, channels = x_ref.shape
-    per = n // batch
+def stats_kernel(batch, w, x_load, g_load, top_ref, low_ref, pay_ref, west_ref, east_ref):
+    sums = []
     step = 64
     t = step // w
-    sums = []
-    for k, ref in enumerate((x_ref, g_ref)):
+    top, low = top_ref[...].astype(F32), low_ref[...].astype(F32)
+    for k, load in enumerate((x_load, g_load)):
+        ref = load()
+        n, channels = ref.shape
+        per = n // batch
+        high = per // w
         for b in range(batch):
-
-            def add(i, c, b=b, k=k, ref=ref):
+            at = k * batch + b
+
+            def add(i, c, b=b, k=k, ref=ref, at=at):
                 start = pl.multiple_of(b * per + i * step, 16)
                 v = ref[pl.ds(start, step), :].astype(F32).reshape(t, w, channels)
-                west_ref[k * batch + b, pl.ds(i * t, t)] = v[:, :1]
-                east_ref[k * batch + b, pl.ds(i * t, t)] = v[:, w - 1 :]
+                west_ref[at, pl.ds(i * t + 1, t)] = v[:, :1]
+                east_ref[at, pl.ds(i * t + 1, t)] = v[:, w - 1 :]
                 if k:
                     return c
                 return c[0] + jnp.sum(v, axis=0), c[1] + jnp.sum(v * v, axis=0)
@@ -88,18 +116,9 @@
             s, q = lax.fori_loop(0, per // step, add, (zero, zero))
             if not k:
                 sums.append((jnp.sum(s, axis=0, keepdims=True), jnp.sum(q, axis=0, keepdims=True)))
-            last = ref[(b + 1) * per - 16 : (b + 1) * per, :].astype(F32)[16 - w :]
-            first = ref[b * per : b * per + 16, :].astype(F32)[:w]
-            if rows == 2:
-                edges = (jnp.where(lax.axis_index("row") == 0, last, first),)
-            else:
-                edges = (last, first)
-            for e, v in enumerate(edges):
-                line, corner_w, corner_e = edge_refs[3 * e : 3 * e + 3]
-                at = k * batch + b
-                line[at * w : (at + 1) * w, :] = v
-                corner_w[at] = v[:1]
-                corner_e[at] = v[w - 1 :]
+            for v, h in ((top, 0), (low, high + 1)):
+                west_ref[at, h] = v[at * w : at * w + 1]
+                east_ref[at, h] = v[(at + 1) * w - 1 : (at + 1) * w]
     stacked = stack_rows([r[0] for r in sums] + [r[1] for r in sums], channels)
     lanes = pay_ref.shape[-1]
     res = jnp.dot(
@@ -159,7 +178,8 @@
     _, _, tall, w, c = ap.shape
     high = tall - 2
     up, down, west, east = edge_masks()
-    left, right, top, top_w, top_e, low, low_w, low_e = halo
+    left, right, top, low = halo
+    top, low = top[...].astype(F32), low[...].astype(F32)
     t = 8
     first = part * batch
     for b in range(batch):
@@ -173,26 +193,23 @@
                 b,
                 h + 1,
                 fn(b, v),
-                fn(b, left[first + b, pl.ds(h, t)]) * west,
-                fn(b, right[first + b, pl.ds(h, t)]) * east,
+                fn(b, left[first + b, pl.ds(h + 1, t)]) * west,
+                fn(b, right[first + b, pl.ds(h + 1, t)]) * east,
             )
             return carry if visit is None else visit(carry, v)
 
         out = lax.fori_loop(0, high // t, body, jnp.zeros((w, c), F32))
         if visit is not None:
             yield out
-        for line, wc, ec, h, edge in (
-            (top, top_w, top_e, 0, up),
-            (low, low_w, low_e, tall - 1, down),
-        ):
+        for line, h, edge in ((top, 0, up), (low, tall - 1, down)):
             at = first + b
             put_shifted(
                 ap,
                 b,
                 h,
-                fn(b, line[at * w : (at + 1) * w, :].reshape(1, w, c)) * edge,
-                fn(b, wc[at : at + 1]) * (west * edge),
-                fn(b, ec[at : at + 1]) * (east * edge),
+                fn(b, line[at * w : (at + 1) * w].reshape(1, w, c)) * edge,
+                fn(b, left[at, h : h + 1]) * (west * edge),
+                fn(b, right[at, h : h + 1]) * (east * edge),
             )
 
 
@@ -213,10 +230,12 @@
 
 
 def wgrad_kernel(batch, count, scale, relative, *refs):
-    st_ref, gain_ref, bias_ref, x_ref, g_ref = refs[:5]
-    halo = refs[5:13]
-    aff_ref, keep_ref, send_ref = refs[13:16]
-    ap, gt, gp, part = refs[16:]
+    x_load, g_load, gain_load, bias_load, st_ref = refs[:5]
+    halo = refs[5:9]
+    aff_ref, keep_ref, send_ref = refs[9:12]
+    ap, gt, gp, part = refs[12:]
+    gain_ref, bias_ref = gain_load(), bias_load()
+    x_ref, g_ref = x_load(), g_load()
     channels = x_ref.shape[1]
     n = x_ref.shape[0]
     aff = affine_rows(st_ref, gain_ref, bias_ref, batch, count)
@@ -258,9 +277,10 @@
 
 
 def back_kernel(batch, *refs):
-    aff_ref, x_ref, g_ref = refs[:3]
-    halo = refs[3:11]
-    w_ref, dn_ref, sums_ref, ap = refs[11:]
+    g_load, w_load, x_load, aff_ref = refs[:4]
+    halo = refs[4:8]
+    dn_ref, sums_ref, ap = refs[8:]
+    g_ref = g_load()
     _, _, tall, w, c = ap.shape
     per = (tall - 2) * w
     rows = []
@@ -268,6 +288,7 @@
         ap, 1, batch, lambda b, v: v, g_ref, halo, lambda tot, v: tot + jnp.sum(v, axis=0)
     )
     totals = [jnp.sum(v, axis=0, keepdims=True) for v in totals]
+    w_ref = w_load()
     for b in range(batch):
         acc = jnp.zeros((per, c), F32)
         for kh in range(3):
@@ -280,6 +301,7 @@
                 )
         dn_ref[b * per : (b + 1) * per, :] = acc
     aff = aff_ref[...]
+    x_ref = x_load()
     for b in range(batch):
         a, s, r, o = (aff[k * batch + b : k * batch + b + 1] for k in range(4))
 
@@ -307,13 +329,16 @@
 
 
 def conv_kernel(batch, *refs):
-    aff_ref, x_ref = refs[:2]
-    halo = refs[2:10]
-    w_ref, cb_ref, temb_ref, out_ref, ap = refs[10:]
+    x_load, w_load, cb_load, aff_ref = refs[:4]
+    halo = refs[4:8]
+    temb_ref, out_ref, done_ref, ap = refs[8:]
+    x_ref = x_load()
+    done_ref[...] = jnp.zeros_like(done_ref)
     _, _, tall, w, c = ap.shape
     per = (tall - 2) * w
     fill_acts(ap, aff_ref[...], batch, x_ref, halo)
-    bias = cb_ref[...].reshape(1, c)
+    w_ref = w_load()
+    bias = cb_load()[...].reshape(1, c)
     for b in range(batch):
         acc = jnp.zeros((per, c), F32)
         for kh in range(3):
@@ -327,11 +352,13 @@
 
 
 def input_kernel(batch, count, scale, *refs):
-    aff_ref, red_ref, gain_ref, x_ref, g_ref, dn_ref, emb_ref = refs[:7]
-    out_ref, gain_out, bias_out, cb_out, tw_out = refs[7:]
-    n, c = x_ref.shape
+    x_load, g_load, dn_load, gain_load, aff_ref, part_ref, other_ref, emb_ref = refs[:8]
+    out_ref, gain_out, bias_out, cb_out, tw_out, done_ref = refs[8:]
+    done_ref[...] = jnp.zeros_like(done_ref)
+    gain_ref = gain_load()
+    n, c = out_ref.shape
     per = n // batch
-    red = red_ref[...]
+    red = part_ref[...] + other_ref[...]
     aff = aff_ref[...]
     gain = gain_ref[...].reshape(1, c)
     m = group_sums(red * gain) / count
@@ -349,6 +376,7 @@
         lax.dot_general(p, emb, (((0,), (0,)), ((), ())), preferred_element_type=F32)
         for p in reversed(parts)
     )
+    x_ref, g_ref, dn_ref = x_load(), g_load(), dn_load()
     for b in range(batch):
         a, r, o = (aff[k * batch + b : k * batch + b + 1] for k in (0, 2, 3))
         m1 = r * m[b : b + 1]
@@ -383,8 +411,9 @@
             b_keep[r, z] = total(r, xb * nz + half + z)
 
 
-def step_two(nz, a_got, a_keep, b_got, b_keep, a_send, a_next, b_send, b_next):
+def step_two(nz, a_got, a_keep, b_got, b_keep, s, s_got, a_send, a_next, b_send, b_next, s_next):
     _, xb, _ = place()
+    s_next[...] = s[...] + s_got[...]
     for z in range(nz // 2):
         a_send[z] = (a_keep[1 - xb, z] + a_got[1 - xb, z].astype(F32)).astype(BF16)
         a_next[z] = a_keep[xb, z] + a_got[xb, z].astype(F32)
@@ -392,7 +421,8 @@
         b_next[z] = b_keep[0, z] + b_got[0, z].astype(F32)
 
 
-def step_three(nz, a_got, a_keep, b_got, b_keep, own_ref, *refs):
+def step_three(nz, a_got, a_keep, b_got, b_keep, s, s_got, own_ref, s_next, *refs):
+    s_next[...] = s[...] + s_got[...]
     sends, held = refs[: nz - 1], refs[nz - 1]
     _, _, zb = place()
     half = nz // 2
@@ -404,11 +434,13 @@
         sends[k - 1][...] = held[zb ^ k].astype(BF16)
 
 
-def step_four(own_ref, *refs):
-    total = own_ref[...]
-    for g in refs[:-1]:
-        total = total + g[...].astype(F32)
-    refs[-1][...] = total.astype(BF16)
+def step_four(nz, own_ref, s, *refs):
+    total, sums = own_ref[...], s[...]
+    for k in range(nz - 1):
+        total = total + refs[k][...].astype(F32)
+        sums = sums + refs[nz - 1 + k][...]
+    refs[-2][...] = total.astype(BF16)
+    refs[-1][...] = sums
 
 
 def step_five(nz, *refs):
@@ -455,14 +487,8 @@
     return lax.ppermute(value, AXES, pairs)
 
 
-def swap(value, right):
-    cols = lax.axis_size("col")
-    pairs = []
-    for r in range(2):
-        for c in range(cols):
-            if 0 <= c + right < cols:
-                pairs.append((r * cols + c, (1 - r) * cols + c + right))
-    return lax.ppermute(value, AXES, pairs)
+def swap(value):
+    return partner(value, lax.axis_size("col"))
 
 
 def local(
@@ -489,29 +515,27 @@
     of = jax.ShapeDtypeStruct
 
     lanes = -(-2 * batch * NORM_GROUPS // LANES) * LANES
-    column = of((2 * batch, high, 1, channels), F32)
-    edge = (
-        of((2 * batch * wide, channels), F32),
-        of((2 * batch, 1, channels), F32),
-        of((2 * batch, 1, channels), F32),
-    )
-    pay, west, east, *edges = call(
-        functools.partial(stats_kernel, batch, wide, rows),
-        (of((devices, 1, lanes), F32), column, column, *(edge * (1 if rows == 2 else 2))),
-        (x2, g2),
-    )
-    left, right = shift(east, 0, 1), shift(west, 0, -1)
+    column = of((2 * batch, high + 2, 1, channels), F32)
+    row = lax.axis_index("row")
+
+    def edge(at):
+        lines = [lax.dynamic_slice_in_dim(v, at, 1, 1) for v in (latent, cotangent)]
+        return jnp.concatenate(lines, axis=0).reshape(2 * batch * wide, channels)
+
     if rows == 2:
-        line, corner_w, corner_e = edges
-        top = (swap(line, 0), swap(corner_e, 1), swap(corner_w, -1))
+        top = swap(edge(jnp.where(row == 0, high - 1, 0)))
         low = top
     else:
-        line, corner_w, corner_e = edges[:3]
-        top = (shift(line, 1, 0), shift(corner_e, 1, 1), shift(corner_w, 1, -1))
-        line, corner_w, corner_e = edges[3:]
-        low = (shift(line, -1, 0), shift(corner_e, -1, 1), shift(corner_w, -1, -1))
+        top, low = shift(edge(high - 1), 1, 0), shift(edge(0), -1, 0)
+    pay, west, east = call(
+        functools.partial(stats_kernel, batch, wide),
+        (of((devices, 1, lanes), F32), column, column),
+        (top, low),
+        far=(x2, g2),
+    )
+    left, right = shift(east, 0, 1), shift(west, 0, -1)
     stats = lax.all_to_all(pay, AXES, 0, 0)
-    halo = (left, right, *top, *low)
+    halo = (left, right, top, low)
 
     shifted = pltpu.VMEM((3, batch, high + 2, wide, channels), F32)
     nz = cols // 4
@@ -531,7 +555,8 @@
             of((keep_rows, pieces, share, width), F32),
             of((1, keep_rows, pieces, share, width), BF16),
         ),
-        (stats, group_norm_gain, group_norm_bias, x2, g2, *halo),
+        (stats, *halo),
+        far=(x2, g2, group_norm_gain, group_norm_bias),
         scratch=(
             shifted,
             pltpu.VMEM((padded, n), BF16),
@@ -558,7 +583,8 @@
     dn, sums = call(
         functools.partial(back_kernel, batch),
         (of((n, channels), F32), of((8, channels), F32)),
-        (aff, x2, g2, *halo, w9),
+        (aff, *halo),
+        far=(g2, w9, x2),
         after=first,
         scratch=(shifted,),
         flops=conv_flops,
@@ -567,49 +593,58 @@
     temb = jnp.dot(emb, time_w, preferred_element_type=F32)
 
     if relative:
-        a_send, a_keep, b_send, b_keep = call(
+        s_shape = of(sums.shape, F32)
+        a_send, a_keep, b_send, b_keep, sums = call(
             functools.partial(step_two, nz),
-            (many((half,), BF16), many((half,), F32)) * 2,
-            (a_got, a_keep, b_got, b_keep),
-            after=(sums,),
+            (many((half,), BF16), many((half,), F32)) * 2 + (s_shape,),
+            (a_got, a_keep, b_got, b_keep, sums, partner(sums, 1)),
         )
         a_got, b_got = partner(a_send, 2), partner(b_send, cols)
-        own, *sends = call(
+        own, sums, *sends = call(
             functools.partial(step_three, nz),
-            (many((), F32), *[many((), BF16)] * (nz - 1)),
-            (a_got, a_keep, b_got, b_keep),
+            (many((), F32), s_shape, *[many((), BF16)] * (nz - 1)),
+            (a_got, a_keep, b_got, b_keep, sums, partner(sums, 2)),
             scratch=(pltpu.VMEM((nz, share, width), F32),),
         )
         gots = [partner(v, 4 * (k + 1)) for k, v in enumerate(sends)]
+        gots += [partner(sums, 4 * k) for k in range(1, nz)]
         second = tuple(sends)
     else:
         second = ()
 
-    block_out = call(
+    token = of((8, LANES), F32)
+    block_out, done = call(
         functools.partial(conv_kernel, batch),
-        of((n, channels), BF16),
-        (aff, x2, *halo, w9, conv_b, temb),
+        (of((n, channels), BF16), token),
+        (aff, *halo, temb),
+        far=(x2, w9, conv_b),
         after=second,
         scratch=(shifted,),
         flops=conv_flops,
     )
-    bit = 1
-    while bit < devices:
-        sums = sums + partner(sums, bit)
-        bit *= 2
 
     if relative:
-        own = call(step_four, many((), BF16), (own, *gots), after=(block_out,))
+        own, sums = call(
+            functools.partial(step_four, nz),
+            (many((), BF16), s_shape),
+            (own, sums, *gots),
+            after=(done,),
+        )
         others = [partner(own, 2 * k) for k in range(1, pieces)]
         third = (own,)
     else:
+        bit = 1
+        while 2 * bit < devices:
+            sums = sums + partner(sums, bit)
+            bit *= 2
         third = ()
 
     vector = of((channels,), F32)
-    input_grad, gain_grad, bias_grad, conv_b_grad, time_grad = call(
+    input_grad, gain_grad, bias_grad, conv_b_grad, time_grad, done = call(
         functools.partial(input_kernel, batch, count, scale),
-        (of((n, channels), F32), vector, vector, vector, of((channels, emb.shape[1]), F32)),
-        (aff, sums, group_norm_gain, x2, g2, dn, emb),
+        (of((n, channels), F32), *[vector] * 3, of((channels, emb.shape[1]), F32), token),
+        (aff, sums, partner(sums, cols if relative else bit), emb),
+        far=(x2, g2, dn, group_norm_gain),
         after=third,
         flops=8 * n * channels,
     )
@@ -619,7 +654,7 @@
             functools.partial(step_five, nz),
             of((share, pieces * width), BF16),
             (own, *others),
-            after=(input_grad,),
+            after=(done,),
         )
         grad = call(
             step_six,

time: 118 us -> 107 us (0.907)
  blocking collectives: 0 us -> 16.3 us
  waiting for transfers between devices: 23.3 us -> 8.45 us
  starting transfers between devices: 42.9 us -> 32 us
  Pallas kernels: 31.3 us -> 28.2 us
    all_to_all x0 -> x1, blocking collectives: none -> 16.3 us  [local(): stats = lax.all_to_all(pay, AXES, 0, 0)]
    ppermute x21 -> x23, waiting for transfers between devices: 19.7 us -> 8.45 us  [partner(): return lax.ppermute(value, AXES, [(i, i ^ bit) for i in range(size)])]
    ppermute x3 -> x0, starting transfers between devices: 7.13 us -> none  [swap(): return lax.ppermute(value, AXES, pairs)]
    all_to_all x1 -> x0, starting transfers between devices: 6.69 us -> none  [local(): stats = lax.all_to_all(pay, AXES, 0, 0)]
    ppermute x21 -> x23, starting transfers between devices: 24.7 us -> 29.4 us  [partner(): return lax.ppermute(value, AXES, [(i, i ^ bit) for i in range(size)])]
    ppermute x3 -> x0, waiting for transfers between devices: 3.65 us -> none  [swap(): return lax.ppermute(value, AXES, pairs)]
    pallas_call x11, Pallas kernels: 31.3 us -> 28.2 us  [call(): pl.pallas_call(kernel, out_shape=out_shape, in_specs=[pl.BlockSpec(memory...]
    ppermute x2, starting transfers between devices: 4.39 us -> 2.61 us  [shift(): return lax.ppermute(value, AXES, pairs)]
  transfers between devices with their start and end apart: 27 -> 25, of which waited for: 10 -> 6; matrix products, arithmetic and copies ran while one was open for 3% -> 4% of each run, Pallas kernels for 16% -> 17%
where the time goes in v3:
time: 107 us; the launch traced here: 106 us
  starting transfers between devices  32 us (30%)
  Pallas kernels  28.2 us (26%)
  blocking collectives  16.3 us (15%)
  local copies, waits for them, and re-layouts  15.9 us (15%)
  waiting for transfers between devices  8.45 us (8%)
  matrix products  3.42 us (3%)
    ppermute x23, starting transfers between devices, partner(): return lax.ppermute(value, AXES, [(i, i ^ bit) for i in range(size)])  29.4 us
    pallas_call x11, Pallas kernels, call(): pl.pallas_call(kernel, out_shape=out_shape, in_specs=[pl.BlockSpec(memory...  28.2 us
    all_to_all x1, blocking collectives, local(): stats = lax.all_to_all(pay, AXES, 0, 0)  16.3 us
    unnamed x54, local copies, waits for them, and re-layouts  15 us
    ppermute x23, waiting for transfers between devices, partner(): return lax.ppermute(value, AXES, [(i, i ^ bit) for i in range(size)])  8.45 us
    ppermute x2, starting transfers between devices, shift(): return lax.ppermute(value, AXES, pairs)  2.61 us
  transfers between devices with their start and end apart: 25, of which 6 were waited for; matrix products, arithmetic and copies ran while one was open for 4% of the time, Pallas kernels for 17%

profile of v3, /device:TPU:0, one launch (start us, length us, event | category | flops | bytes accessed | tf_op | source)
XLA Modules:
  0.0 105.9 jit_solution(15893154237396715018)
XLA Ops:
  0.6 0.0 copy-start
  0.7 0.9 constant_dynamic-slice_fusion
  1.6 3.0 %collective-permute-start = (bf16[32,320]{1,0:T(8,128)(2,1)S(1)}, bf16[32,320]{1,0:T(8,128)(2,1)S(1)}, u32[]{:S(2)}, u32[]{:S(2)}) collective-permute-start(bf16[32,320]{1,0:T(8,128)(2,1)S(1)} %maximum_bitcast_fusion), channel_id=1, source_target_pairs={{0,16},{1,17},{2,18},{3,19},{4,20},{5,21},{6,22},{7,23},{8,24},{9,... | collective-permute-start | bytes 61448 | tf_op jit(solution)/shard_map/ppermute | solution.py:476
  4.6 1.8 %collective-permute-done.refs_2_.refs_3_.refs_7_.refs_8_.refs_6_ = bf16[32,320]{1,0:T(8,128)(2,1)S(1)} collective-permute-done((bf16[32,320]{1,0:T(8,128)(2,1)S(1)}, bf16[32,320]{1,0:T(8,128)(2,1)S(1)}, u32[]{:S(2)}, u32[]{:S(2)}) %collective-permute-start) | collective-permute-done | bytes 20512 | tf_op jit(solution)/shard_map/ppermute | solution.py:476
  6.4 1.1 %copy-done.1 = bf16[2,64,8,320]{3,2,1,0:T(8,128)(2,1)S(1)} copy-done((bf16[2,64,8,320]{3,2,1,0:T(8,128)(2,1)S(1)}, bf16[2,64,8,320]{3,2,1,0:T(8,128)(2,1)}, u32[]{:S(2)}) %copy-start.1) | copy-done | bytes 655384
  7.5 1.1 %copy-done.6 = bf16[2,64,8,320]{3,2,1,0:T(8,128)(2,1)S(1)} copy-done((bf16[2,64,8,320]{3,2,1,0:T(8,128)(2,1)S(1)}, bf16[2,64,8,320]{3,2,1,0:T(8,128)(2,1)}, u32[]{:S(2)}) %copy-start.6) | copy-done | bytes 655384
  8.7 1.3 %shard_map.153 = (f32[32,1,128]{2,1,0:T(1,128)S(1)}, f32[4,66,1,320]{3,2,1,0:T(1,128)S(1)}, f32[4,66,1,320]{3,2,1,0:T(1,128)S(1)}) custom-call(bf16[1024,320]{1,0:T(8,128)(2,1)S(1)} %bitcast.16, bf16[1024,320]{1,0:T(8,128)(2,1)S(1)} %bitcast.21, bf16[32,320]{1,0:T(8,128)(2,1)S(1)} %collective-permute-done.refs_2_.refs_3_.refs_7_.refs_8_.refs_6_, ...), custom_call_target="tpu_custom_call" | custom-call | bytes 2000000 | tf_op jit(solution)/shard_map/pallas_call | solution.py:54
  9.9 1.3 %collective-permute-start.1 = (f32[4,66,1,320]{3,2,1,0:T(1,128)S(1)}, f32[4,66,1,320]{3,2,1,0:T(1,128)S(1)}, u32[]{:S(2)}, u32[]{:S(2)}) collective-permute-start(f32[4,66,1,320]{3,2,1,0:T(1,128)S(1)} %get-tuple-element.40), channel_id=1, source_target_pairs={{0,1},{1,2},{2,3},{3,4},{4,5},{5,6},{6,7},{7,8},{8,9},{9,10},{10,1... | collective-permute-start | bytes 1013768 | tf_op jit(solution)/shard_map/ppermute | solution.py:487
  11.3 1.3 %collective-permute-start.2 = (f32[4,66,1,320]{3,2,1,0:T(1,128)S(1)}, f32[4,66,1,320]{3,2,1,0:T(1,128)S(1)}, u32[]{:S(2)}, u32[]{:S(2)}) collective-permute-start(f32[4,66,1,320]{3,2,1,0:T(1,128)S(1)} %get-tuple-element.41), channel_id=1, source_target_pairs={{1,0},{2,1},{3,2},{4,3},{5,4},{6,5},{7,6},{8,7},{9,8},{10,9},{11,1... | collective-permute-start | bytes 1013768 | tf_op jit(solution)/shard_map/ppermute | solution.py:487
  12.6 0.0 copy-start.26
  12.6 16.3 %all_to_all.5.refs_4_ = f32[32,1,128]{2,1,0:T(1,128)S(1)} all-to-all(f32[32,1,128]{2,1,0:T(1,128)S(1)} %get-tuple-element.39), channel_id=1, replica_groups=mesh['row'=2,'col'=16] {'row','col'}, dimensions={0} | all-to-all | bytes 32768 | tf_op jit(solution)/shard_map/all_to_all | solution.py:537
  28.8 0.0 copy-start.2
  28.9 1.3 %copy-done.2 = bf16[2,64,8,320]{3,2,1,0:T(8,128)(2,1)S(1)} copy-done((bf16[2,64,8,320]{3,2,1,0:T(8,128)(2,1)S(1)}, bf16[2,64,8,320]{3,2,1,0:T(8,128)(2,1)}, u32[]{:S(2)}) %copy-start.2) | copy-done | bytes 655384
  30.1 1.1 %copy-done.7 = bf16[2,64,8,320]{3,2,1,0:T(8,128)(2,1)S(1)} copy-done((bf16[2,64,8,320]{3,2,1,0:T(8,128)(2,1)S(1)}, bf16[2,64,8,320]{3,2,1,0:T(8,128)(2,1)}, u32[]{:S(2)}) %copy-start.7) | copy-done | bytes 655384
  31.3 0.7 copy-done.16
  31.9 0.7 copy-done.24
  32.6 5.4 %shard_map.154 = (f32[8,320]{1,0:T(8,128)S(1)}, f32[2,8,80,384]{3,2,1,0:T(8,128)S(1)}, bf16[1,2,8,80,384]{4,3,2,1,0:T(8,128)(2,1)S(1)}) custom-call(bf16[1024,320]{1,0:T(8,128)(2,1)S(1)} %bitcast.17, bf16[1024,320]{1,0:T(8,128)(2,1)S(1)} %bitcast.22, f32[320]{0:T(512)S(1)} %copy-done.16, f32[320]{0:T(512)S(1)} %copy-done.24, ...), custom_call_target="tpu_custom_call" | custom-call | flops 1887436800 | bytes 2000000 | tf_op jit(solution)/shard_map/pallas_call | solution.py:54
  38.1 0.0 copy-start.3
  38.1 0.0 copy-start.8
  38.1 0.1 collective-permute-start.3
  38.2 2.5 %collective-permute-done.3.refs_1_ = bf16[2,8,80,384]{3,2,1,0:T(8,128)(2,1)S(1)} collective-permute-done((bf16[2,8,80,384]{3,2,1,0:T(8,128)(2,1)S(1)}, bf16[2,8,80,384]{3,2,1,0:T(8,128)(2,1)S(1)}, u32[]{:S(2)}, u32[]{:S(2)}) %collective-permute-start.3) | collective-permute-done | bytes 983072 | tf_op jit(solution)/shard_map/ppermute | solution.py:476
  40.7 0.2 shard_map.155
  40.9 0.7 collective-permute-start.4
  41.5 0.5 collective-permute-start.5
  42.1 6.7 %shard_map.156 = (f32[1024,320]{1,0:T(8,128)S(1)}, f32[8,320]{1,0:T(8,128)S(1)}) custom-call(bf16[1024,320]{1,0:T(8,128)(2,1)S(1)} %bitcast.23, bf16[9,320,320]{2,1,0:T(8,128)(2,1)S(1)} %bitcast.25, bf16[1024,320]{1,0:T(8,128)(2,1)S(1)} %bitcast.18, f32[8,320]{1,0:T(8,128)S(1)} %get-tuple-element.42.refs_3_.refs_4_, ...), custom_call_target="tpu_custom_call" | custom-call | flops 1887436800 | bytes 2000000 | tf_op jit(solution)/shard_map/pallas_call | solution.py:54
  48.8 0.0 copy-start.10
  48.8 1.1 %copy-done.10 = f32[1024,320]{1,0:T(8,128)} copy-done((f32[1024,320]{1,0:T(8,128)}, f32[1024,320]{1,0:T(8,128)S(1)}, u32[]{:S(2)}) %copy-start.10) | copy-done | bytes 1310744
  49.9 0.7 fusion.7
  50.6 0.5 collective-permute-done.6.refs_5_
  51.1 0.8 shard_map.157
  51.9 0.7 copy-done.12
  52.6 1.5 %collective-permute-start.9 = (f32[8,320]{1,0:T(8,128)}, f32[8,320]{1,0:T(8,128)}, u32[]{:S(2)}, u32[]{:S(2)}) collective-permute-start(f32[8,320]{1,0:T(8,128)} %get-tuple-element.54.refs_4_), channel_id=1, source_target_pairs={{0,2},{1,3},{2,0},{3,1},{4,6},{5,7},{6,4},{7,5},{8,10},{9,11},{10,... | collective-permute-start | bytes 30728 | tf_op jit(solution)/shard_map/ppermute | solution.py:476
  54.1 0.5 collective-permute-start.7
  54.6 1.4 %collective-permute-start.8 = (bf16[2,80,384]{2,1,0:T(8,128)(2,1)}, bf16[2,80,384]{2,1,0:T(8,128)(2,1)}, u32[]{:S(2)}, u32[]{:S(2)}) collective-permute-start(bf16[2,80,384]{2,1,0:T(8,128)(2,1)} %get-tuple-element.52), channel_id=1, source_target_pairs={{0,16},{1,17},{2,18},{3,19},{4,20},{5,21},{6,22},{7,23},{8,24},{9,... | collective-permute-start | bytes 368648 | tf_op jit(solution)/shard_map/ppermute | solution.py:476
  56.0 2.0 %fusion.1.refs_7_ = bf16[2,1280]{1,0:T(2,128)(2,1)S(1)} fusion(bf16[1280,1280]{1,0:T(8,128)(2,1)S(1)} %copy-done, bf16[320,1280]{1,0:T(8,128)(2,1)} %param.16, bf16[2,160]{1,0:T(2,128)(2,1)} %get-tuple-element.72, bf16[2,160]{1,0:T(2,128)(2,1)} %get-tuple-element.71), kind=kOutput, calls=%fused_computation.4 | convolution fusion | flops 8220160 | bytes 4102400 | tf_op jit(solution)/shard_map/dot_general | solution.py:471
  58.0 1.4 %collective-permute-done.7.refs_0_ = bf16[2,80,384]{2,1,0:T(8,128)(2,1)} collective-permute-done((bf16[2,80,384]{2,1,0:T(8,128)(2,1)}, bf16[2,80,384]{2,1,0:T(8,128)(2,1)}, u32[]{:S(2)}, u32[]{:S(2)}) %collective-permute-start.7) | collective-permute-done | bytes 122912 | tf_op jit(solution)/shard_map/ppermute | solution.py:476
  59.5 0.3 collective-permute-done.8.refs_2_
  59.8 0.9 copy-done.13
  60.7 1.0 shard_map.158
  61.8 0.6 collective-permute-start.15
  62.4 1.4 %fusion.22.refs_8_ = f32[2,320]{1,0:T(2,128)S(1)} fusion(bf16[2,1280]{1,0:T(2,128)(2,1)S(1)} %fusion.1.refs_7_, bf16[1280,320]{0,1:T(8,128)(2,1)} %param.18), kind=kOutput, calls=%fused_computation.20 | convolution fusion | flops 1638400 | bytes 826880 | tf_op jit(solution)/shard_map/dot_general | solution.py:593
  63.8 1.5 %collective-permute-start.14 = (f32[8,320]{1,0:T(8,128)S(1)}, f32[8,320]{1,0:T(8,128)S(1)}, u32[]{:S(2)}, u32[]{:S(2)}) collective-permute-start(f32[8,320]{1,0:T(8,128)S(1)} %get-tuple-element.61.refs_1_), channel_id=1, source_target_pairs={{0,8},{1,9},{2,10},{3,11},{4,12},{5,13},{6,14},{7,15},{8,0},{9,1},... | collective-permute-start | bytes 30728 | tf_op jit(solution)/shard_map/ppermute | solution.py:476
  65.4 2.3 %collective-permute-start.13 = (f32[8,320]{1,0:T(8,128)S(1)}, f32[8,320]{1,0:T(8,128)S(1)}, u32[]{:S(2)}, u32[]{:S(2)}) collective-permute-start(f32[8,320]{1,0:T(8,128)S(1)} %get-tuple-element.61.refs_1_), channel_id=1, source_target_pairs={{0,4},{1,5},{2,6},{3,7},{4,0},{5,1},{6,2},{7,3},{8,12},{9,13},{10,... | collective-permute-start | bytes 30728 | tf_op jit(solution)/shard_map/ppermute | solution.py:476
  67.7 0.0 collective-permute-start.10
  67.7 1.1 %collective-permute-start.11 = (bf16[80,384]{1,0:T(8,128)(2,1)S(1)}, bf16[80,384]{1,0:T(8,128)(2,1)S(1)}, u32[]{:S(2)}, u32[]{:S(2)}) collective-permute-start(bf16[80,384]{1,0:T(8,128)(2,1)S(1)} %get-tuple-element.56.refs_10_), channel_id=1, source_target_pairs={{0,8},{1,9},{2,10},{3,11},{4,12},{5,13},{6,14},{7,15},{8,0},{9,1},... | collective-permute-start | bytes 184328 | tf_op jit(solution)/shard_map/ppermute | solution.py:476
  68.8 3.3 %collective-permute-start.12 = (bf16[80,384]{1,0:T(8,128)(2,1)S(1)}, bf16[80,384]{1,0:T(8,128)(2,1)S(1)}, u32[]{:S(2)}, u32[]{:S(2)}) collective-permute-start(bf16[80,384]{1,0:T(8,128)(2,1)S(1)} %get-tuple-element.57.refs_11_), channel_id=1, source_target_pairs={{0,12},{1,13},{2,14},{3,15},{4,8},{5,9},{6,10},{7,11},{8,4},{9,5},... | collective-permute-start | bytes 184328 | tf_op jit(solution)/shard_map/ppermute | solution.py:476
  72.1 1.1 %copy-done.4 = bf16[2,64,8,320]{3,2,1,0:T(8,128)(2,1)S(1)} copy-done((bf16[2,64,8,320]{3,2,1,0:T(8,128)(2,1)S(1)}, bf16[2,64,8,320]{3,2,1,0:T(8,128)(2,1)}, u32[]{:S(2)}) %copy-start.4) | copy-done | bytes 655384
  73.2 0.7 copy-done.15
  73.9 1.6 %copy-done.19 = bf16[3,3,320,320]{3,2,1,0:T(8,128)(2,1)S(1)} copy-done((bf16[3,3,320,320]{3,2,1,0:T(8,128)(2,1)S(1)}, bf16[3,3,320,320]{3,2,1,0:T(8,128)(2,1)}, u32[]{:S(2)}) %copy-start.19) | copy-done | bytes 1843224
  75.6 1.0 copy-done.21
  76.6 1.0 copy-done.23
  77.6 0.7 copy-done.25
  78.3 7.2 %shard_map.159 = (bf16[1024,320]{1,0:T(8,128)(2,1)}, f32[8,128]{1,0:T(8,128)S(1)}) custom-call(bf16[1024,320]{1,0:T(8,128)(2,1)S(1)} %bitcast.19, bf16[9,320,320]{2,1,0:T(8,128)(2,1)S(1)} %bitcast.26, f32[320]{0:T(512)S(1)} %copy-done.25, f32[8,320]{1,0:T(8,128)S(1)} %copy-done.15, f32[4,66,1,320]{3,2,1,0:T(1,128)S(1)} %copy-done.21, ...), custom_call_target="tpu_custom_call" | custom-call | flops 1887436800 | bytes 2000000 | tf_op jit(solution)/shard_map/pallas_call | solution.py:54
  85.6 1.7 %collective-permute-start.23 = (bf16[80,384]{1,0:T(8,128)(2,1)S(1)}, bf16[80,384]{1,0:T(8,128)(2,1)S(1)}, u32[]{:S(2)}, u32[]{:S(2)}) collective-permute-start(bf16[80,384]{1,0:T(8,128)(2,1)S(1)} %get-tuple-element.64.refs_8_.refs_0_), channel_id=1, source_target_pairs={{0,14},{1,15},{2,12},{3,13},{4,10},{5,11},{6,8},{7,9},{8,6},{9,7},... | collective-permute-start | bytes 184328 | tf_op jit(solution)/shard_map/ppermute | solution.py:476
  87.3 3.1 %collective-permute-start.22 = (bf16[80,384]{1,0:T(8,128)(2,1)S(1)}, bf16[80,384]{1,0:T(8,128)(2,1)S(1)}, u32[]{:S(2)}, u32[]{:S(2)}) collective-permute-start(bf16[80,384]{1,0:T(8,128)(2,1)S(1)} %get-tuple-element.64.refs_8_.refs_0_), channel_id=1, source_target_pairs={{0,12},{1,13},{2,14},{3,15},{4,8},{5,9},{6,10},{7,11},{8,4},{9,5},... | collective-permute-start | bytes 184328 | tf_op jit(solution)/shard_map/ppermute | solution.py:476
  90.4 1.4 %collective-permute-start.16 = (f32[8,320]{1,0:T(8,128)S(1)}, f32[8,320]{1,0:T(8,128)S(1)}, u32[]{:S(2)}, u32[]{:S(2)}) collective-permute-start(f32[8,320]{1,0:T(8,128)S(1)} %get-tuple-element.63.refs_5_), channel_id=1, source_target_pairs={{0,16},{1,17},{2,18},{3,19},{4,20},{5,21},{6,22},{7,23},{8,24},{9,... | collective-permute-start | bytes 30728 | tf_op jit(solution)/shard_map/ppermute | solution.py:476
  91.9 2.9 %collective-permute-start.20 = (bf16[80,384]{1,0:T(8,128)(2,1)S(1)}, bf16[80,384]{1,0:T(8,128)(2,1)S(1)}, u32[]{:S(2)}, u32[]{:S(2)}) collective-permute-start(bf16[80,384]{1,0:T(8,128)(2,1)S(1)} %get-tuple-element.64.refs_8_.refs_0_), channel_id=1, source_target_pairs={{0,8},{1,9},{2,10},{3,11},{4,12},{5,13},{6,14},{7,15},{8,0},{9,1},... | collective-permute-start | bytes 184328 | tf_op jit(solution)/shard_map/ppermute | solution.py:476
  94.8 2.9 %collective-permute-start.18 = (bf16[80,384]{1,0:T(8,128)(2,1)S(1)}, bf16[80,384]{1,0:T(8,128)(2,1)S(1)}, u32[]{:S(2)}, u32[]{:S(2)}) collective-permute-start(bf16[80,384]{1,0:T(8,128)(2,1)S(1)} %get-tuple-element.64.refs_8_.refs_0_), channel_id=1, source_target_pairs={{0,4},{1,5},{2,6},{3,7},{4,0},{5,1},{6,2},{7,3},{8,12},{9,13},{10,... | collective-permute-start | bytes 184328 | tf_op jit(solution)/shard_map/ppermute | solution.py:476
  97.7 0.5 collective-permute-start.17
  98.3 3.6 %shard_map.161 = (f32[1024,320]{1,0:T(8,128)}, f32[320]{0:T(512)}, f32[320]{0:T(512)}, f32[320]{0:T(512)}, f32[320,1280]{1,0:T(8,128)}, /*index=5*/f32[8,128]{1,0:T(8,128)S(1)}) custom-call(bf16[1024,320]{1,0:T(8,128)(2,1)S(1)} %bitcast.20, bf16[1024,320]{1,0:T(8,128)(2,1)S(1)} %bitcast.24, f32[1024,320]{1,0:T(8,128)S(1)} %copy-done.11, f32[320]{0:T(512)S(1)} %copy-done.17, ...), custom_call_target="tpu_custom_call" | custom-call | flops 2621440 | bytes 2000000 | tf_op jit(solution)/shard_map/pallas_call | solution.py:54
  102.0 0.1 shard_map.162.refs_0_
  102.0 0.1 collective-permute-start.24
  102.1 1.9 %collective-permute-done.24.refs_1_ = bf16[80,3072]{1,0:T(8,128)(2,1)S(1)} collective-permute-done((bf16[80,3072]{1,0:T(8,128)(2,1)S(1)}, bf16[80,3072]{1,0:T(8,128)(2,1)S(1)}, u32[]{:S(2)}, u32[]{:S(2)}) %collective-permute-start.24) | collective-permute-done | bytes 491552 | tf_op jit(solution)/shard_map/ppermute | solution.py:476
  104.0 1.9 %shard_map.163 = f32[9,160,320]{2,1,0:T(8,128)} custom-call(bf16[80,3072]{1,0:T(8,128)(2,1)S(1)} %shard_map.162.refs_0_, bf16[80,3072]{1,0:T(8,128)(2,1)S(1)} %collective-permute-done.24.refs_1_), custom_call_target="tpu_custom_call" | custom-call | bytes 2000000 | tf_op jit(solution)/shard_map/pallas_call | solution.py:54
  (59 shorter events, 0.2 us)
Async XLA Ops:
  0.6 55.4 %copy-start = (bf16[1280,1280]{1,0:T(8,128)(2,1)S(1)}, bf16[1280,1280]{1,0:T(8,128)(2,1)}, u32[]{:S(2)}) copy-start(bf16[1280,1280]{1,0:T(8,128)(2,1)} %param.17) | copy-start | bytes 9830404
  1.6 4.8 %collective-permute-start = (bf16[32,320]{1,0:T(8,128)(2,1)S(1)}, bf16[32,320]{1,0:T(8,128)(2,1)S(1)}, u32[]{:S(2)}, u32[]{:S(2)}) collective-permute-start(bf16[32,320]{1,0:T(8,128)(2,1)S(1)} %maximum_bitcast_fusion), channel_id=1, source_target_pairs={{0,16},{1,17},{2,18},{3,19},{4,20},{5,21},{6,22},{7,23},{8,24},{9,... | collective-permute-start | bytes 61448 | tf_op jit(solution)/shard_map/ppermute | solution.py:476
  6.4 1.1 %copy-start.1 = (bf16[2,64,8,320]{3,2,1,0:T(8,128)(2,1)S(1)}, bf16[2,64,8,320]{3,2,1,0:T(8,128)(2,1)}, u32[]{:S(2)}) copy-start(bf16[2,64,8,320]{3,2,1,0:T(8,128)(2,1)} %param.10) | copy-start | bytes 1966084
  7.5 1.1 %copy-start.6 = (bf16[2,64,8,320]{3,2,1,0:T(8,128)(2,1)S(1)}, bf16[2,64,8,320]{3,2,1,0:T(8,128)(2,1)}, u32[]{:S(2)}) copy-start(bf16[2,64,8,320]{3,2,1,0:T(8,128)(2,1)} %param.19) | copy-start | bytes 1966084
  9.9 18.9 %collective-permute-start.1 = (f32[4,66,1,320]{3,2,1,0:T(1,128)S(1)}, f32[4,66,1,320]{3,2,1,0:T(1,128)S(1)}, u32[]{:S(2)}, u32[]{:S(2)}) collective-permute-start(f32[4,66,1,320]{3,2,1,0:T(1,128)S(1)} %get-tuple-element.40), channel_id=1, source_target_pairs={{0,1},{1,2},{2,3},{3,4},{4,5},{5,6},{6,7},{7,8},{8,9},{9,10},{10,1... | collective-permute-start | bytes 1013768 | tf_op jit(solution)/shard_map/ppermute | solution.py:487
  11.3 17.6 %collective-permute-start.2 = (f32[4,66,1,320]{3,2,1,0:T(1,128)S(1)}, f32[4,66,1,320]{3,2,1,0:T(1,128)S(1)}, u32[]{:S(2)}, u32[]{:S(2)}) collective-permute-start(f32[4,66,1,320]{3,2,1,0:T(1,128)S(1)} %get-tuple-element.41), channel_id=1, source_target_pairs={{1,0},{2,1},{3,2},{4,3},{5,4},{6,5},{7,6},{8,7},{9,8},{10,9},{11,1... | collective-permute-start | bytes 1013768 | tf_op jit(solution)/shard_map/ppermute | solution.py:487
  12.6 25.6 %copy-start.26 = (s32[2]{0:T(128)S(1)}, s32[2]{0:T(128)}, u32[]{:S(2)}) copy-start(s32[2]{0:T(128)} %param.11) | copy-start | bytes 28
  28.8 13.2 %copy-start.20 = (f32[4,66,1,320]{3,2,1,0:T(1,128)}, f32[4,66,1,320]{3,2,1,0:T(1,128)S(1)}, u32[]{:S(2)}) copy-start(f32[4,66,1,320]{3,2,1,0:T(1,128)S(1)} %collective-permute-done.1.refs_5_.refs_4_) | copy-start | bytes 1013764
  28.8 1.3 %copy-start.2 = (bf16[2,64,8,320]{3,2,1,0:T(8,128)(2,1)S(1)}, bf16[2,64,8,320]{3,2,1,0:T(8,128)(2,1)}, u32[]{:S(2)}) copy-start(bf16[2,64,8,320]{3,2,1,0:T(8,128)(2,1)} %param.10) | copy-start | bytes 1966084
  30.1 1.1 %copy-start.7 = (bf16[2,64,8,320]{3,2,1,0:T(8,128)(2,1)S(1)}, bf16[2,64,8,320]{3,2,1,0:T(8,128)(2,1)}, u32[]{:S(2)}) copy-start(bf16[2,64,8,320]{3,2,1,0:T(8,128)(2,1)} %param.19) | copy-start | bytes 1966084
  31.3 0.7 copy-start.16
  31.9 0.7 copy-start.24
  32.6 9.4 %copy-start.22 = (f32[4,66,1,320]{3,2,1,0:T(1,128)}, f32[4,66,1,320]{3,2,1,0:T(1,128)S(1)}, u32[]{:S(2)}) copy-start(f32[4,66,1,320]{3,2,1,0:T(1,128)S(1)} %collective-permute-done.2.refs_6_.refs_5_) | copy-start | bytes 1013764
  32.6 9.4 %copy-start.18 = (bf16[3,3,320,320]{3,2,1,0:T(8,128)(2,1)S(1)}, bf16[3,3,320,320]{3,2,1,0:T(8,128)(2,1)}, u32[]{:S(2)}) copy-start(bf16[3,3,320,320]{3,2,1,0:T(8,128)(2,1)} %param.14) | copy-start | bytes 5529604
  38.0 10.7 %copy-start.14 = (f32[8,320]{1,0:T(8,128)}, f32[8,320]{1,0:T(8,128)S(1)}, u32[]{:S(2)}) copy-start(f32[8,320]{1,0:T(8,128)S(1)} %get-tuple-element.42.refs_3_.refs_4_) | copy-start | bytes 30724
  38.1 4.0 %copy-start.3 = (bf16[2,64,8,320]{3,2,1,0:T(8,128)(2,1)S(1)}, bf16[2,64,8,320]{3,2,1,0:T(8,128)(2,1)}, u32[]{:S(2)}) copy-start(bf16[2,64,8,320]{3,2,1,0:T(8,128)(2,1)} %param.10) | copy-start | bytes 1966084
  38.1 4.0 %copy-start.8 = (bf16[2,64,8,320]{3,2,1,0:T(8,128)(2,1)S(1)}, bf16[2,64,8,320]{3,2,1,0:T(8,128)(2,1)}, u32[]{:S(2)}) copy-start(bf16[2,64,8,320]{3,2,1,0:T(8,128)(2,1)} %param.19) | copy-start | bytes 1966084
  38.1 2.6 %collective-permute-start.3 = (bf16[2,8,80,384]{3,2,1,0:T(8,128)(2,1)S(1)}, bf16[2,8,80,384]{3,2,1,0:T(8,128)(2,1)S(1)}, u32[]{:S(2)}, u32[]{:S(2)}) collective-permute-start(bf16[2,8,80,384]{3,2,1,0:T(8,128)(2,1)S(1)} %bitcast.27), channel_id=1, source_target_pairs={{0,1},{1,0},{2,3},{3,2},{4,5},{5,4},{6,7},{7,6},{8,9},{9,8},{10,11... | collective-permute-start | bytes 2949128 | tf_op jit(solution)/shard_map/ppermute | solution.py:476
  40.9 10.2 %collective-permute-start.4 = (bf16[2,2,80,384]{3,2,1,0:T(8,128)(2,1)S(1)}, bf16[2,2,80,384]{3,2,1,0:T(8,128)(2,1)S(1)}, u32[]{:S(2)}, u32[]{:S(2)}) collective-permute-start(bf16[2,2,80,384]{3,2,1,0:T(8,128)(2,1)S(1)} %get-tuple-element.45.refs_8_), channel_id=1, source_target_pairs={{0,16},{1,17},{2,18},{3,19},{4,20},{5,21},{6,22},{7,23},{8,24},{9,... | collective-permute-start | bytes 737288 | tf_op jit(solution)/shard_map/ppermute | solution.py:476
  41.5 9.6 %collective-permute-start.5 = (bf16[2,2,80,384]{3,2,1,0:T(8,128)(2,1)S(1)}, bf16[2,2,80,384]{3,2,1,0:T(8,128)(2,1)S(1)}, u32[]{:S(2)}, u32[]{:S(2)}) collective-permute-start(bf16[2,2,80,384]{3,2,1,0:T(8,128)(2,1)S(1)} %get-tuple-element.47.refs_9_), channel_id=1, source_target_pairs={{0,2},{1,3},{2,0},{3,1},{4,6},{5,7},{6,4},{7,5},{8,10},{9,11},{10,... | collective-permute-start | bytes 737288 | tf_op jit(solution)/shard_map/ppermute | solution.py:476
  48.8 1.1 %copy-start.10 = (f32[1024,320]{1,0:T(8,128)}, f32[1024,320]{1,0:T(8,128)S(1)}, u32[]{:S(2)}) copy-start(f32[1024,320]{1,0:T(8,128)S(1)} %get-tuple-element.59.refs_2_) | copy-start | bytes 3932164
  49.9 1.2 %collective-permute-start.6 = (f32[8,320]{1,0:T(8,128)S(1)}, f32[8,320]{1,0:T(8,128)S(1)}, u32[]{:S(2)}, u32[]{:S(2)}) collective-permute-start(f32[8,320]{1,0:T(8,128)S(1)} %get-tuple-element.49.refs_4_), channel_id=1, source_target_pairs={{0,1},{1,0},{2,3},{3,2},{4,5},{5,4},{6,7},{7,6},{8,9},{9,8},{10,11... | collective-permute-start | bytes 30728 | tf_op jit(solution)/shard_map/ppermute | solution.py:476
  51.9 0.7 copy-start.12
  52.6 5.5 %collective-permute-start.9 = (f32[8,320]{1,0:T(8,128)}, f32[8,320]{1,0:T(8,128)}, u32[]{:S(2)}, u32[]{:S(2)}) collective-permute-start(f32[8,320]{1,0:T(8,128)} %get-tuple-element.54.refs_4_), channel_id=1, source_target_pairs={{0,2},{1,3},{2,0},{3,1},{4,6},{5,7},{6,4},{7,5},{8,10},{9,11},{10,... | collective-permute-start | bytes 30728 | tf_op jit(solution)/shard_map/ppermute | solution.py:476
  54.1 5.4 %collective-permute-start.7 = (bf16[2,80,384]{2,1,0:T(8,128)(2,1)}, bf16[2,80,384]{2,1,0:T(8,128)(2,1)}, u32[]{:S(2)}, u32[]{:S(2)}) collective-permute-start(bf16[2,80,384]{2,1,0:T(8,128)(2,1)} %get-tuple-element.50), channel_id=1, source_target_pairs={{0,2},{1,3},{2,0},{3,1},{4,6},{5,7},{6,4},{7,5},{8,10},{9,11},{10,... | collective-permute-start | bytes 368648 | tf_op jit(solution)/shard_map/ppermute | solution.py:476
  54.6 5.2 %collective-permute-start.8 = (bf16[2,80,384]{2,1,0:T(8,128)(2,1)}, bf16[2,80,384]{2,1,0:T(8,128)(2,1)}, u32[]{:S(2)}, u32[]{:S(2)}) collective-permute-start(bf16[2,80,384]{2,1,0:T(8,128)(2,1)} %get-tuple-element.52), channel_id=1, source_target_pairs={{0,16},{1,17},{2,18},{3,19},{4,20},{5,21},{6,22},{7,23},{8,24},{9,... | collective-permute-start | bytes 368648 | tf_op jit(solution)/shard_map/ppermute | solution.py:476
  59.8 0.9 copy-start.13
  61.8 7.1 %collective-permute-start.15 = (f32[8,320]{1,0:T(8,128)S(1)}, f32[8,320]{1,0:T(8,128)S(1)}, u32[]{:S(2)}, u32[]{:S(2)}) collective-permute-start(f32[8,320]{1,0:T(8,128)S(1)} %get-tuple-element.61.refs_1_), channel_id=1, source_target_pairs={{0,12},{1,13},{2,14},{3,15},{4,8},{5,9},{6,10},{7,11},{8,4},{9,5},... | collective-permute-start | bytes 30728 | tf_op jit(solution)/shard_map/ppermute | solution.py:476
  63.8 21.7 %collective-permute-start.14 = (f32[8,320]{1,0:T(8,128)S(1)}, f32[8,320]{1,0:T(8,128)S(1)}, u32[]{:S(2)}, u32[]{:S(2)}) collective-permute-start(f32[8,320]{1,0:T(8,128)S(1)} %get-tuple-element.61.refs_1_), channel_id=1, source_target_pairs={{0,8},{1,9},{2,10},{3,11},{4,12},{5,13},{6,14},{7,15},{8,0},{9,1},... | collective-permute-start | bytes 30728 | tf_op jit(solution)/shard_map/ppermute | solution.py:476
  65.4 20.1 %collective-permute-start.13 = (f32[8,320]{1,0:T(8,128)S(1)}, f32[8,320]{1,0:T(8,128)S(1)}, u32[]{:S(2)}, u32[]{:S(2)}) collective-permute-start(f32[8,320]{1,0:T(8,128)S(1)} %get-tuple-element.61.refs_1_), channel_id=1, source_target_pairs={{0,4},{1,5},{2,6},{3,7},{4,0},{5,1},{6,2},{7,3},{8,12},{9,13},{10,... | collective-permute-start | bytes 30728 | tf_op jit(solution)/shard_map/ppermute | solution.py:476
  67.7 17.8 %collective-permute-start.10 = (bf16[80,384]{1,0:T(8,128)(2,1)S(1)}, bf16[80,384]{1,0:T(8,128)(2,1)S(1)}, u32[]{:S(2)}, u32[]{:S(2)}) collective-permute-start(bf16[80,384]{1,0:T(8,128)(2,1)S(1)} %get-tuple-element.55.refs_9_), channel_id=1, source_target_pairs={{0,4},{1,5},{2,6},{3,7},{4,0},{5,1},{6,2},{7,3},{8,12},{9,13},{10,... | collective-permute-start | bytes 184328 | tf_op jit(solution)/shard_map/ppermute | solution.py:476
  67.7 17.8 %collective-permute-start.11 = (bf16[80,384]{1,0:T(8,128)(2,1)S(1)}, bf16[80,384]{1,0:T(8,128)(2,1)S(1)}, u32[]{:S(2)}, u32[]{:S(2)}) collective-permute-start(bf16[80,384]{1,0:T(8,128)(2,1)S(1)} %get-tuple-element.56.refs_10_), channel_id=1, source_target_pairs={{0,8},{1,9},{2,10},{3,11},{4,12},{5,13},{6,14},{7,15},{8,0},{9,1},... | collective-permute-start | bytes 184328 | tf_op jit(solution)/shard_map/ppermute | solution.py:476
  68.8 16.7 %collective-permute-start.12 = (bf16[80,384]{1,0:T(8,128)(2,1)S(1)}, bf16[80,384]{1,0:T(8,128)(2,1)S(1)}, u32[]{:S(2)}, u32[]{:S(2)}) collective-permute-start(bf16[80,384]{1,0:T(8,128)(2,1)S(1)} %get-tuple-element.57.refs_11_), channel_id=1, source_target_pairs={{0,12},{1,13},{2,14},{3,15},{4,8},{5,9},{6,10},{7,11},{8,4},{9,5},... | collective-permute-start | bytes 184328 | tf_op jit(solution)/shard_map/ppermute | solution.py:476
  72.1 1.1 %copy-start.4 = (bf16[2,64,8,320]{3,2,1,0:T(8,128)(2,1)S(1)}, bf16[2,64,8,320]{3,2,1,0:T(8,128)(2,1)}, u32[]{:S(2)}) copy-start(bf16[2,64,8,320]{3,2,1,0:T(8,128)(2,1)} %param.10) | copy-start | bytes 1966084
  73.2 0.7 copy-start.15
  73.9 1.6 %copy-start.19 = (bf16[3,3,320,320]{3,2,1,0:T(8,128)(2,1)S(1)}, bf16[3,3,320,320]{3,2,1,0:T(8,128)(2,1)}, u32[]{:S(2)}) copy-start(bf16[3,3,320,320]{3,2,1,0:T(8,128)(2,1)} %param.14) | copy-start | bytes 5529604
  75.6 1.0 copy-start.21
  76.6 1.0 copy-start.23
  77.6 0.7 copy-start.25
  78.2 20.0 %copy-start.5 = (bf16[2,64,8,320]{3,2,1,0:T(8,128)(2,1)S(1)}, bf16[2,64,8,320]{3,2,1,0:T(8,128)(2,1)}, u32[]{:S(2)}) copy-start(bf16[2,64,8,320]{3,2,1,0:T(8,128)(2,1)} %param.10) | copy-start | bytes 1966084
  78.3 20.0 %copy-start.9 = (bf16[2,64,8,320]{3,2,1,0:T(8,128)(2,1)S(1)}, bf16[2,64,8,320]{3,2,1,0:T(8,128)(2,1)}, u32[]{:S(2)}) copy-start(bf16[2,64,8,320]{3,2,1,0:T(8,128)(2,1)} %param.19) | copy-start | bytes 1966084
  78.3 20.0 %copy-start.11 = (f32[1024,320]{1,0:T(8,128)S(1)}, f32[1024,320]{1,0:T(8,128)}, u32[]{:S(2)}) copy-start(f32[1024,320]{1,0:T(8,128)} %copy-done.10) | copy-start | bytes 3932164
  78.3 20.0 %copy-start.17 = (f32[320]{0:T(512)S(1)}, f32[320]{0:T(512)}, u32[]{:S(2)}) copy-start(f32[320]{0:T(512)} %refs_3_.3) | copy-start | bytes 3844
  85.6 9.2 %collective-permute-start.23 = (bf16[80,384]{1,0:T(8,128)(2,1)S(1)}, bf16[80,384]{1,0:T(8,128)(2,1)S(1)}, u32[]{:S(2)}, u32[]{:S(2)}) collective-permute-start(bf16[80,384]{1,0:T(8,128)(2,1)S(1)} %get-tuple-element.64.refs_8_.refs_0_), channel_id=1, source_target_pairs={{0,14},{1,15},{2,12},{3,13},{4,10},{5,11},{6,8},{7,9},{8,6},{9,7},... | collective-permute-start | bytes 184328 | tf_op jit(solution)/shard_map/ppermute | solution.py:476
  87.3 10.4 %collective-permute-start.22 = (bf16[80,384]{1,0:T(8,128)(2,1)S(1)}, bf16[80,384]{1,0:T(8,128)(2,1)S(1)}, u32[]{:S(2)}, u32[]{:S(2)}) collective-permute-start(bf16[80,384]{1,0:T(8,128)(2,1)S(1)} %get-tuple-element.64.refs_8_.refs_0_), channel_id=1, source_target_pairs={{0,12},{1,13},{2,14},{3,15},{4,8},{5,9},{6,10},{7,11},{8,4},{9,5},... | collective-permute-start | bytes 184328 | tf_op jit(solution)/shard_map/ppermute | solution.py:476
  90.4 4.3 %collective-permute-start.16 = (f32[8,320]{1,0:T(8,128)S(1)}, f32[8,320]{1,0:T(8,128)S(1)}, u32[]{:S(2)}, u32[]{:S(2)}) collective-permute-start(f32[8,320]{1,0:T(8,128)S(1)} %get-tuple-element.63.refs_5_), channel_id=1, source_target_pairs={{0,16},{1,17},{2,18},{3,19},{4,20},{5,21},{6,22},{7,23},{8,24},{9,... | collective-permute-start | bytes 30728 | tf_op jit(solution)/shard_map/ppermute | solution.py:476
  91.9 10.1 %collective-permute-start.21 = (bf16[80,384]{1,0:T(8,128)(2,1)S(1)}, bf16[80,384]{1,0:T(8,128)(2,1)S(1)}, u32[]{:S(2)}, u32[]{:S(2)}) collective-permute-start(bf16[80,384]{1,0:T(8,128)(2,1)S(1)} %get-tuple-element.64.refs_8_.refs_0_), channel_id=1, source_target_pairs={{0,10},{1,11},{2,8},{3,9},{4,14},{5,15},{6,12},{7,13},{8,2},{9,3},... | collective-permute-start | bytes 184328 | tf_op jit(solution)/shard_map/ppermute | solution.py:476
  91.9 10.1 %collective-permute-start.20 = (bf16[80,384]{1,0:T(8,128)(2,1)S(1)}, bf16[80,384]{1,0:T(8,128)(2,1)S(1)}, u32[]{:S(2)}, u32[]{:S(2)}) collective-permute-start(bf16[80,384]{1,0:T(8,128)(2,1)S(1)} %get-tuple-element.64.refs_8_.refs_0_), channel_id=1, source_target_pairs={{0,8},{1,9},{2,10},{3,11},{4,12},{5,13},{6,14},{7,15},{8,0},{9,1},... | collective-permute-start | bytes 184328 | tf_op jit(solution)/shard_map/ppermute | solution.py:476
  94.8 7.2 %collective-permute-start.19 = (bf16[80,384]{1,0:T(8,128)(2,1)S(1)}, bf16[80,384]{1,0:T(8,128)(2,1)S(1)}, u32[]{:S(2)}, u32[]{:S(2)}) collective-permute-start(bf16[80,384]{1,0:T(8,128)(2,1)S(1)} %get-tuple-element.64.refs_8_.refs_0_), channel_id=1, source_target_pairs={{0,6},{1,7},{2,4},{3,5},{4,2},{5,3},{6,0},{7,1},{8,14},{9,15},{10,... | collective-permute-start | bytes 184328 | tf_op jit(solution)/shard_map/ppermute | solution.py:476
  94.8 7.2 %collective-permute-start.18 = (bf16[80,384]{1,0:T(8,128)(2,1)S(1)}, bf16[80,384]{1,0:T(8,128)(2,1)S(1)}, u32[]{:S(2)}, u32[]{:S(2)}) collective-permute-start(bf16[80,384]{1,0:T(8,128)(2,1)S(1)} %get-tuple-element.64.refs_8_.refs_0_), channel_id=1, source_target_pairs={{0,4},{1,5},{2,6},{3,7},{4,0},{5,1},{6,2},{7,3},{8,12},{9,13},{10,... | collective-permute-start | bytes 184328 | tf_op jit(solution)/shard_map/ppermute | solution.py:476
  97.7 4.2 %collective-permute-start.17 = (bf16[80,384]{1,0:T(8,128)(2,1)S(1)}, bf16[80,384]{1,0:T(8,128)(2,1)S(1)}, u32[]{:S(2)}, u32[]{:S(2)}) collective-permute-start(bf16[80,384]{1,0:T(8,128)(2,1)S(1)} %get-tuple-element.64.refs_8_.refs_0_), channel_id=1, source_target_pairs={{0,2},{1,3},{2,0},{3,1},{4,6},{5,7},{6,4},{7,5},{8,10},{9,11},{10,... | collective-permute-start | bytes 184328 | tf_op jit(solution)/shard_map/ppermute | solution.py:476
  102.0 1.9 %collective-permute-start.24 = (bf16[80,3072]{1,0:T(8,128)(2,1)S(1)}, bf16[80,3072]{1,0:T(8,128)(2,1)S(1)}, u32[]{:S(2)}, u32[]{:S(2)}) collective-permute-start(bf16[80,3072]{1,0:T(8,128)(2,1)S(1)} %shard_map.162.refs_0_), channel_id=1, source_target_pairs={{0,1},{1,0},{2,3},{3,2},{4,5},{5,4},{6,7},{7,6},{8,9},{9,8},{10,11... | collective-permute-start | bytes 1474568 | tf_op jit(solution)/shard_map/ppermute | solution.py:476

commit v4 on v3

--- a/solution.py
+++ b/solution.py
@@ -14,7 +14,7 @@
 F32 = jnp.float32
 BF16 = jnp.bfloat16
 AXES = ("row", "col")
-VMEM_LIMIT = 20 * 1024 * 1024
+VMEM_LIMIT = 64 * 1024 * 1024
 HI = lax.Precision.HIGHEST
 
 
@@ -23,45 +23,53 @@
 
 
 def call(body, out_shape, operands, far=(), after=(), scratch=(), flops=0, nbytes=2_000_000):
-    count, used, waits = len(far), len(operands), len(after)
+    outs, tree = jax.tree.flatten(out_shape)
+    ins = (*far, *operands)
+    waits, own = len(after), len(scratch)
 
     def kernel(*refs):
-        ins = refs[:count]
-        rest = refs[count : count + used] + refs[count + used + waits :]
-        if not count:
-            return body(*rest)
-        holds, sems = rest[-1 - count : -1], rest[-1]
-        copies = [
-            pltpu.make_async_copy(ins[i], holds[i], sems.at[i]) for i in range(count)
-        ]
-        for c in copies:
+        src, refs = refs[: len(ins)], refs[len(ins) + waits :]
+        dst, refs = refs[: len(outs)], refs[len(outs) :]
+        mine, refs = refs[:own], refs[own:]
+        held, refs = refs[: len(ins)], refs[len(ins) :]
+        made, (sem_in, sem_out) = refs[: len(outs)], refs[len(outs) :]
+        copies = [pltpu.make_async_copy(a, b, sem_in.at[i]) for i, (a, b) in enumerate(zip(src, held))]
+        for c in (*copies[len(far) :], *copies[: len(far)]):
             c.start()
 
         def loader(i):
             def load():
                 copies[i].wait()
-                return holds[i]
+                return held[i]
 
             return load
 
-        body(*[loader(i) for i in range(count)], *rest[: -1 - count])
-
-    vmem = pl.BlockSpec(memory_space=pltpu.VMEM)
-    scratch = list(scratch)
-    if count:
-        scratch += [pltpu.VMEM(v.shape, v.dtype) for v in far]
-        scratch.append(pltpu.SemaphoreType.DMA((count,)))
-    return pl.pallas_call(
+        for c in copies[len(far) :]:
+            c.wait()
+        body(*[loader(i) for i in range(len(far))], *held[len(far) :], *made, *mine)
+        copies = [pltpu.make_async_copy(a, b, sem_out.at[i]) for i, (a, b) in enumerate(zip(made, dst))]
+        for c in copies:
+            c.start()
+        for c in copies:
+            c.wait()
+
+    hbm = pl.BlockSpec(memory_space=pltpu.HBM)
+    results = pl.pallas_call(
         kernel,
-        out_shape=out_shape,
-        in_specs=[pl.BlockSpec(memory_space=pltpu.HBM)] * count
-        + [vmem] * used
-        + [pl.BlockSpec(memory_space=pl.ANY)] * waits,
-        out_specs=jax.tree.map(lambda _: vmem, out_shape),
-        scratch_shapes=scratch,
+        out_shape=tuple(outs),
+        in_specs=[hbm] * len(ins) + [pl.BlockSpec(memory_space=pl.ANY)] * waits,
+        out_specs=(hbm,) * len(outs),
+        scratch_shapes=[
+            *scratch,
+            *[pltpu.VMEM(v.shape, v.dtype) for v in ins],
+            *[pltpu.VMEM(v.shape, v.dtype) for v in outs],
+            pltpu.SemaphoreType.DMA((max(len(ins), 1),)),
+            pltpu.SemaphoreType.DMA((len(outs),)),
+        ],
         compiler_params=pltpu.CompilerParams(vmem_limit_bytes=VMEM_LIMIT),
         cost_estimate=pl.CostEstimate(flops=flops, bytes_accessed=nbytes, transcendentals=0),
-    )(*far, *operands, *after)
+    )(*ins, *after)
+    return jax.tree.unflatten(tree, results)
 
 
 def group_matrix(channels, lanes):
@@ -229,34 +237,60 @@
     return ap[kw, b, kh : kh + tall - 2].reshape((tall - 2) * w, c).astype(BF16)
 
 
-def wgrad_kernel(batch, count, scale, relative, *refs):
-    x_load, g_load, gain_load, bias_load, st_ref = refs[:5]
-    halo = refs[5:9]
-    aff_ref, keep_ref, send_ref = refs[9:12]
-    ap, gt, gp, part = refs[12:]
-    gain_ref, bias_ref = gain_load(), bias_load()
-    x_ref, g_ref = x_load(), g_load()
-    channels = x_ref.shape[1]
-    n = x_ref.shape[0]
-    aff = affine_rows(st_ref, gain_ref, bias_ref, batch, count)
-    aff_ref[...] = aff
+def dacts_kernel(batch, relative, share, *refs):
+    g_load, w_load = refs[:2]
+    halo = refs[2:6]
+    da_ref, gsum_ref, gp_ref, ap, gt = refs[6:]
+    g_ref = g_load()
+    n, c = g_ref.shape
+    _, _, tall, w, _ = ap.shape
+    per = (tall - 2) * w
+    totals = fill(
+        ap, 1, batch, lambda b, v: v, g_ref, halo, lambda tot, v: tot + jnp.sum(v, axis=0)
+    )
+    totals = [jnp.sum(v, axis=0, keepdims=True) for v in totals]
+    gsum_ref[...] = stack_rows([jnp.zeros((1, c), F32)] * (2 * batch) + totals, c)
+    w_ref = w_load()
+    for b in range(batch):
+        acc = jnp.zeros((per, c), F32)
+        for kh in range(3):
+            for kw in range(3):
+                acc = acc + lax.dot_general(
+                    tap_rows(ap, b, 2 - kh, 2 - kw),
+                    w_ref[kh * 3 + kw],
+                    (((1,), (1,)), ((), ())),
+                    preferred_element_type=F32,
+                )
+        da_ref[b * per : (b + 1) * per, :] = acc
     wide = gt.shape[0]
     step = LANES
     for i in range(n // step):
         v = g_ref[i * step : (i + 1) * step, :].astype(F32)
-        v = jnp.concatenate([v, jnp.zeros((step, wide - channels), F32)], axis=1)
+        v = jnp.concatenate([v, jnp.zeros((step, wide - c), F32)], axis=1)
         gt[:, i * step : (i + 1) * step] = jnp.transpose(v).astype(BF16)
-    _, rows, pieces, share, width = send_ref.shape
     if relative:
         me = lax.axis_index("row") * 2 + (lax.axis_index("col") & 1)
-        for q in range(2 * rows):
-            other = (me ^ ((q % rows) * 2 + q // rows)) * share
-            gp[q * share : (q + 1) * share, :] = gt[pl.ds(pl.multiple_of(other, 16), share), :]
+        for q in range(4):
+            other = (me ^ ((q % 2) * 2 + q // 2)) * share
+            gp_ref[q * share : (q + 1) * share, :] = gt[pl.ds(pl.multiple_of(other, 16), share), :]
     else:
-        gp[...] = gt[:channels, :]
+        gp_ref[...] = gt[:c, :]
+
+
+def wgrad_kernel(batch, count, scale, *refs):
+    x_load, gp_load, gain_ref, bias_ref, st_ref = refs[:5]
+    halo = refs[5:9]
+    aff_ref, keep_ref, send_ref = refs[9:12]
+    ap, part = refs[12:]
+    aff = affine_rows(st_ref, gain_ref, bias_ref, batch, count)
+    aff_ref[...] = aff
+    x_ref = x_load()
+    n, channels = x_ref.shape
+    _, rows, pieces, share, width = send_ref.shape
     fill_acts(ap, aff, batch, x_ref, halo)
     part[:, 9 * channels :] = jnp.zeros((channels, part.shape[1] - 9 * channels), F32)
     per = n // batch
+    gp = gp_load()
     for kh in range(3):
         for kw in range(3):
             tap = kh * 3 + kw
@@ -277,31 +311,12 @@
 
 
 def back_kernel(batch, *refs):
-    g_load, w_load, x_load, aff_ref = refs[:4]
-    halo = refs[4:8]
-    dn_ref, sums_ref, ap = refs[8:]
-    g_ref = g_load()
-    _, _, tall, w, c = ap.shape
-    per = (tall - 2) * w
+    x_load, da_load, aff_ref, gsum_ref, dn_ref, sums_ref = refs
+    n, c = dn_ref.shape
+    per = n // batch
     rows = []
-    totals = fill(
-        ap, 1, batch, lambda b, v: v, g_ref, halo, lambda tot, v: tot + jnp.sum(v, axis=0)
-    )
-    totals = [jnp.sum(v, axis=0, keepdims=True) for v in totals]
-    w_ref = w_load()
-    for b in range(batch):
-        acc = jnp.zeros((per, c), F32)
-        for kh in range(3):
-            for kw in range(3):
-                acc = acc + lax.dot_general(
-                    tap_rows(ap, b, 2 - kh, 2 - kw),
-                    w_ref[kh * 3 + kw],
-                    (((1,), (1,)), ((), ())),
-                    preferred_element_type=F32,
-                )
-        dn_ref[b * per : (b + 1) * per, :] = acc
     aff = aff_ref[...]
-    x_ref = x_load()
+    x_ref, da_ref = x_load(), da_load()
     for b in range(batch):
         a, s, r, o = (aff[k * batch + b : k * batch + b + 1] for k in range(4))
 
@@ -310,7 +325,7 @@
             x = x_ref[rows_here, :].astype(F32)
             normed = x * a + s
             sig = 1.0 / (1.0 + jnp.exp(-normed))
-            dn = dn_ref[rows_here, :] * sig * (1.0 + normed * (1.0 - sig))
+            dn = da_ref[rows_here, :] * sig * (1.0 + normed * (1.0 - sig))
             dn_ref[rows_here, :] = dn
             xhat = x * r + o
             return (
@@ -320,10 +335,9 @@
 
         zero = jnp.zeros((8, c), F32)
         rows.append(lax.fori_loop(0, per // 64, body, (zero, zero)))
-    sums_ref[...] = stack_rows(
+    sums_ref[...] = gsum_ref[...] + stack_rows(
         [jnp.sum(v[0], axis=0, keepdims=True) for v in rows]
-        + [jnp.sum(v[1], axis=0, keepdims=True) for v in rows]
-        + totals,
+        + [jnp.sum(v[1], axis=0, keepdims=True) for v in rows],
         c,
     )
 
@@ -548,21 +562,24 @@
     if not relative:
         share = channels // 2
     keep_rows = rows if relative else 1
+    dacts, gsum, flipped = call(
+        functools.partial(dacts_kernel, batch, relative, share),
+        (of((n, channels), F32), of((8, channels), F32), of((channels, n), BF16)),
+        halo,
+        far=(g2, w9),
+        scratch=(shifted, pltpu.VMEM((padded, n), BF16)),
+        flops=conv_flops,
+    )
     aff, keep, send = call(
-        functools.partial(wgrad_kernel, batch, count, scale, relative),
+        functools.partial(wgrad_kernel, batch, count, scale),
         (
             of((8, channels), F32),
             of((keep_rows, pieces, share, width), F32),
             of((1, keep_rows, pieces, share, width), BF16),
         ),
-        (stats, *halo),
-        far=(x2, g2, group_norm_gain, group_norm_bias),
-        scratch=(
-            shifted,
-            pltpu.VMEM((padded, n), BF16),
-            pltpu.VMEM((channels, n), BF16),
-            pltpu.VMEM((channels, pieces * width), F32),
-        ),
+        (group_norm_gain, group_norm_bias, stats, *halo),
+        far=(x2, flipped),
+        scratch=(shifted, pltpu.VMEM((channels, pieces * width), F32)),
         flops=conv_flops,
     )
 
@@ -583,11 +600,10 @@
     dn, sums = call(
         functools.partial(back_kernel, batch),
         (of((n, channels), F32), of((8, channels), F32)),
-        (aff, *halo),
-        far=(g2, w9, x2),
+        (aff, gsum),
+        far=(x2, dacts),
         after=first,
-        scratch=(shifted,),
-        flops=conv_flops,
+        flops=20 * n * channels,
     )
     emb = embed(timestep, embed_in, embed_out)
     temb = jnp.dot(emb, time_w, preferred_element_type=F32)

time: 107 us -> 115 us (1.075)
  Pallas kernels: 28.2 us -> 51.4 us
  blocking collectives: 16.3 us -> 0 us
  local copies, waits for them, and re-layouts: 15.9 us -> 0.73 us
  starting transfers between devices: 32 us -> 44.1 us
  other arithmetic: 0.71 us -> 3.11 us
  matrix products: 3.42 us -> 5.69 us
    pallas_call x11 -> x12, Pallas kernels: 28.2 us -> 51.4 us  [call(): pl.pallas_call(kernel, out_shape=tuple(outs), in_specs=[hbm] * len(ins) +...]
    all_to_all x1 -> x0, blocking collectives: 16.3 us -> none  [local(): stats = lax.all_to_all(pay, AXES, 0, 0)]
    unnamed x54 -> x0, local copies, waits for them, and re-layouts: 15 us -> none
    all_to_all x0 -> x1, starting transfers between devices: none -> 8.72 us  [local(): stats = lax.all_to_all(pay, AXES, 0, 0)]
    ppermute x23, starting transfers between devices: 29.4 us -> 32 us  [partner(): return lax.ppermute(value, AXES, [(i, i ^ bit) for i in range(size)])]
    dot_general x1, matrix products: 1.99 us -> 3.63 us  [embed(): jnp.dot(first_hidden, embed_out, preferred_element_type=F32)]
    convert_element_type x1, other arithmetic: 0.01 us -> 1.16 us  [embed(): angles = timestep.astype(F32)[:, None] * freqs[None, :]]
  transfers between devices with their start and end apart: 25 -> 26, of which waited for: 6 -> 7; matrix products, arithmetic and copies ran while one was open for 4% -> 8% of each run, Pallas kernels for 17% -> 22%
where the time goes in v4:
time: 115 us
  Pallas kernels  51.4 us (45%)
  starting transfers between devices  44.1 us (38%)
  waiting for transfers between devices  8.46 us (7%)
  matrix products  5.69 us (5%)
  other arithmetic  3.11 us (3%)
    pallas_call x12, Pallas kernels, call(): pl.pallas_call(kernel, out_shape=tuple(outs), in_specs=[hbm] * len(ins) +...  51.4 us
    ppermute x23, starting transfers between devices, partner(): return lax.ppermute(value, AXES, [(i, i ^ bit) for i in range(size)])  32 us
    all_to_all x1, starting transfers between devices, local(): stats = lax.all_to_all(pay, AXES, 0, 0)  8.72 us
    ppermute x23, waiting for transfers between devices, partner(): return lax.ppermute(value, AXES, [(i, i ^ bit) for i in range(size)])  8.45 us
    dot_general x1, matrix products, embed(): jnp.dot(first_hidden, embed_out, preferred_element_type=F32)  3.63 us
    ppermute x2, starting transfers between devices, shift(): return lax.ppermute(value, AXES, pairs)  3.34 us
  transfers between devices with their start and end apart: 26, of which 7 were waited for; matrix products, arithmetic and copies ran while one was open for 8% of the time, Pallas kernels for 22%

profile of v4, /device:TPU:0, one launch (start us, length us, event | category | flops | bytes accessed | tf_op | source)
XLA Modules:
  0.0 114.5 jit_solution(11829139066146822410)
XLA Ops:
  0.6 0.7 constant_dynamic-slice_fusion
  1.4 3.0 %collective-permute-start = (bf16[32,320]{1,0:T(8,128)(2,1)S(1)}, bf16[32,320]{1,0:T(8,128)(2,1)}, u32[]{:S(2)}, u32[]{:S(2)}) collective-permute-start(bf16[32,320]{1,0:T(8,128)(2,1)S(1)} %maximum_bitcast_fusion), channel_id=1, source_target_pairs={{0,16},{1,17},{2,18},{3,19},{4,20},{5,21},{6,22},{7,23},{8,24},{9,... | collective-permute-start | bytes 61448 | tf_op jit(solution)/shard_map/ppermute | solution.py:490
  4.4 1.9 %collective-permute-done.refs_2_.refs_3_.refs_4_.refs_5_.refs_7_.refs_8_.refs_6_ = bf16[32,320]{1,0:T(8,128)(2,1)} collective-permute-done((bf16[32,320]{1,0:T(8,128)(2,1)S(1)}, bf16[32,320]{1,0:T(8,128)(2,1)}, u32[]{:S(2)}, u32[]{:S(2)}) %collective-permute-start) | collective-permute-done | bytes 20512 | tf_op jit(solution)/shard_map/ppermute | solution.py:490
  6.3 3.3 %shard_map.153 = (f32[32,1,128]{2,1,0:T(1,128)}, f32[4,66,1,320]{3,2,1,0:T(1,128)}, f32[4,66,1,320]{3,2,1,0:T(1,128)}) custom-call(bf16[1024,320]{1,0:T(8,128)(2,1)} %bitcast.16, bf16[1024,320]{1,0:T(8,128)(2,1)} %bitcast.21, bf16[32,320]{1,0:T(8,128)(2,1)} %collective-permute-done.refs_2_.refs_3_.refs_4_.refs_5_.refs_7_.refs_8_.refs_6_, ...), custom_call_target="tpu_custom_call" | custom-call | bytes 2000000 | tf_op jit(solution)/shard_map/pallas_call | solution.py:57
  9.6 2.1 %collective-permute-start.1 = (f32[4,66,1,320]{3,2,1,0:T(1,128)}, f32[4,66,1,320]{3,2,1,0:T(1,128)}, u32[]{:S(2)}, u32[]{:S(2)}) collective-permute-start(f32[4,66,1,320]{3,2,1,0:T(1,128)} %get-tuple-element.42), channel_id=1, source_target_pairs={{0,1},{1,2},{2,3},{3,4},{4,5},{5,6},{6,7},{7,8},{8,9},{9,10},{10,1... | collective-permute-start | bytes 1013768 | tf_op jit(solution)/shard_map/ppermute | solution.py:501
  11.7 1.3 %collective-permute-start.2 = (f32[4,66,1,320]{3,2,1,0:T(1,128)}, f32[4,66,1,320]{3,2,1,0:T(1,128)}, u32[]{:S(2)}, u32[]{:S(2)}) collective-permute-start(f32[4,66,1,320]{3,2,1,0:T(1,128)} %get-tuple-element.43), channel_id=1, source_target_pairs={{1,0},{2,1},{3,2},{4,3},{5,4},{6,5},{7,6},{8,7},{9,8},{10,9},{11,1... | collective-permute-start | bytes 1013768 | tf_op jit(solution)/shard_map/ppermute | solution.py:501
  12.9 8.7 %all-to-all-start = ((f32[32,1,128]{2,1,0:T(1,128)}), f32[32,1,128]{2,1,0:T(1,128)}, u32[]{:S(2)}, u32[]{:S(2)}) async-start(f32[32,1,128]{2,1,0:T(1,128)} %get-tuple-element.45), calls=%async_computation | async-start | bytes 32768 | tf_op jit(solution)/shard_map/all_to_all | solution.py:551
  21.7 0.0 collective-permute-done.1.refs_2_.refs_5_.refs_4_
  21.7 0.0 collective-permute-done.2.refs_3_.refs_6_.refs_5_
  21.7 8.1 %shard_map.154 = (f32[1024,320]{1,0:T(8,128)}, f32[8,320]{1,0:T(8,128)}, bf16[320,1024]{1,0:T(8,128)(2,1)}) custom-call(bf16[1024,320]{1,0:T(8,128)(2,1)} %bitcast.22, bf16[9,320,320]{2,1,0:T(8,128)(2,1)} %bitcast.25, f32[4,66,1,320]{3,2,1,0:T(1,128)} %collective-permute-done.1.refs_2_.refs_5_.refs_4_, ...), custom_call_target="tpu_custom_call" | custom-call | flops 1887436800 | bytes 2000000 | tf_op jit(solution)/shard_map/pallas_call | solution.py:57
  29.7 0.0 all-to-all-done.refs_4_
  29.8 8.3 %shard_map.155 = (f32[8,320]{1,0:T(8,128)}, f32[2,8,80,384]{3,2,1,0:T(8,128)}, bf16[1,2,8,80,384]{4,3,2,1,0:T(8,128)(2,1)}) custom-call(bf16[1024,320]{1,0:T(8,128)(2,1)} %bitcast.17, bf16[320,1024]{1,0:T(8,128)(2,1)} %get-tuple-element.44.refs_1_, f32[320]{0:T(512)} %refs_3_.3, f32[320]{0:T(512)} %refs_3_.2, f32[32,1,128]{2,1,0:T(1,128)} %all-to-all-done.refs_4_, ...), custom_call_target="tpu_custom_call" | custom-call | flops 1887436800 | bytes 2000000 | tf_op jit(solution)/shard_map/pallas_call | solution.py:57
  38.0 1.5 %collective-permute-start.3 = (bf16[2,8,80,384]{3,2,1,0:T(8,128)(2,1)}, bf16[2,8,80,384]{3,2,1,0:T(8,128)(2,1)}, u32[]{:S(2)}, u32[]{:S(2)}) collective-permute-start(bf16[2,8,80,384]{3,2,1,0:T(8,128)(2,1)} %bitcast.29), channel_id=1, source_target_pairs={{0,1},{1,0},{2,3},{3,2},{4,5},{5,4},{6,7},{7,6},{8,9},{9,8},{10,11... | collective-permute-start | bytes 2949128 | tf_op jit(solution)/shard_map/ppermute | solution.py:490
  39.6 2.5 %collective-permute-done.3.refs_1_ = bf16[2,8,80,384]{3,2,1,0:T(8,128)(2,1)} collective-permute-done((bf16[2,8,80,384]{3,2,1,0:T(8,128)(2,1)}, bf16[2,8,80,384]{3,2,1,0:T(8,128)(2,1)}, u32[]{:S(2)}, u32[]{:S(2)}) %collective-permute-start.3) | collective-permute-done | bytes 983072 | tf_op jit(solution)/shard_map/ppermute | solution.py:490
  42.1 3.0 %shard_map.156 = (bf16[2,2,80,384]{3,2,1,0:T(8,128)(2,1)}, f32[2,2,80,384]{3,2,1,0:T(8,128)}, bf16[2,2,80,384]{3,2,1,0:T(8,128)(2,1)}, f32[2,2,80,384]{3,2,1,0:T(8,128)}) custom-call(f32[2,8,80,384]{3,2,1,0:T(8,128)} %get-tuple-element.47.refs_0_, bf16[2,8,80,384]{3,2,1,0:T(8,128)(2,1)} %collective-permute-done.3.refs_1_), custom_call_target="tpu_custom_call" | custom-call | bytes 2000000 | tf_op jit(solution)/shard_map/pallas_call | solution.py:57
  45.1 1.7 %collective-permute-start.4 = (bf16[2,2,80,384]{3,2,1,0:T(8,128)(2,1)}, bf16[2,2,80,384]{3,2,1,0:T(8,128)(2,1)}, u32[]{:S(2)}, u32[]{:S(2)}) collective-permute-start(bf16[2,2,80,384]{3,2,1,0:T(8,128)(2,1)} %get-tuple-element.49.refs_4_), channel_id=1, source_target_pairs={{0,16},{1,17},{2,18},{3,19},{4,20},{5,21},{6,22},{7,23},{8,24},{9,... | collective-permute-start | bytes 737288 | tf_op jit(solution)/shard_map/ppermute | solution.py:490
  46.8 2.6 %collective-permute-start.5 = (bf16[2,2,80,384]{3,2,1,0:T(8,128)(2,1)}, bf16[2,2,80,384]{3,2,1,0:T(8,128)(2,1)}, u32[]{:S(2)}, u32[]{:S(2)}) collective-permute-start(bf16[2,2,80,384]{3,2,1,0:T(8,128)(2,1)} %get-tuple-element.51.refs_5_), channel_id=1, source_target_pairs={{0,2},{1,3},{2,0},{3,1},{4,6},{5,7},{6,4},{7,5},{8,10},{9,11},{10,... | collective-permute-start | bytes 737288 | tf_op jit(solution)/shard_map/ppermute | solution.py:490
  49.4 0.6 multiply_exponential_fusion
  50.0 1.2 %convert_element_type.10 = f32[2]{0:T(128)} convert(s32[2]{0:T(128)} %param.11) | non-fusion elementwise | flops 2 | bytes 16 | tf_op jit(solution)/shard_map/convert_element_type | solution.py:482
  51.2 4.0 %shard_map.157 = (f32[1024,320]{1,0:T(8,128)}, f32[8,320]{1,0:T(8,128)}) custom-call(bf16[1024,320]{1,0:T(8,128)(2,1)} %bitcast.18, f32[1024,320]{1,0:T(8,128)} %get-tuple-element.53.refs_1_, f32[8,320]{1,0:T(8,128)} %get-tuple-element.46.refs_2_.refs_3_.refs_4_, f32[8,320]{1,0:T(8,128)} %get-tuple-element.54.refs_3_, ...), custom_call_target="tpu_custom_call" | custom-call | flops 6553600 | bytes 2000000 | tf_op jit(solution)/shard_map/pallas_call | solution.py:57
  55.2 0.1 collective-permute-start.6
  55.3 1.4 %fusion.7 = (bf16[2,160]{1,0:T(2,128)(2,1)}, bf16[2,160]{1,0:T(2,128)(2,1)}) fusion(f32[160]{0:T(256)} %multiply_exponential_fusion, f32[2]{0:T(128)} %convert_element_type.10), kind=kLoop, calls=%fused_computation.9 | loop fusion | flops 960 | bytes 1928 | tf_op jit(solution)/shard_map/convert
  56.7 0.1 collective-permute-done.6.refs_5_
  56.8 0.0 collective-permute-done.4.refs_0_
  56.8 0.0 collective-permute-done.5.refs_2_
  56.8 2.4 %shard_map.158 = (bf16[2,80,384]{2,1,0:T(8,128)(2,1)}, f32[2,80,384]{2,1,0:T(8,128)}, bf16[2,80,384]{2,1,0:T(8,128)(2,1)}, f32[2,80,384]{2,1,0:T(8,128)}, f32[8,320]{1,0:T(8,128)}) custom-call(bf16[2,2,80,384]{3,2,1,0:T(8,128)(2,1)} %collective-permute-done.4.refs_0_, f32[2,2,80,384]{3,2,1,0:T(8,128)} %get-tuple-element.50.refs_1_, ...), custom_call_target="tpu_custom_call" | custom-call | bytes 2000000 | tf_op jit(solution)/shard_map/pallas_call | solution.py:57
  59.2 0.9 collective-permute-start.9
  60.1 1.2 %collective-permute-start.7 = (bf16[2,80,384]{2,1,0:T(8,128)(2,1)}, bf16[2,80,384]{2,1,0:T(8,128)(2,1)}, u32[]{:S(2)}, u32[]{:S(2)}) collective-permute-start(bf16[2,80,384]{2,1,0:T(8,128)(2,1)} %get-tuple-element.56), channel_id=1, source_target_pairs={{0,2},{1,3},{2,0},{3,1},{4,6},{5,7},{6,4},{7,5},{8,10},{9,11},{10,... | collective-permute-start | bytes 368648 | tf_op jit(solution)/shard_map/ppermute | solution.py:490
  61.3 0.3 collective-permute-start.8
  61.5 3.6 %fusion.1.refs_7_ = bf16[2,1280]{1,0:T(2,128)(2,1)} fusion(bf16[1280,1280]{1,0:T(8,128)(2,1)} %param.17, bf16[320,1280]{1,0:T(8,128)(2,1)} %param.16, bf16[2,160]{1,0:T(2,128)(2,1)} %get-tuple-element.78, bf16[2,160]{1,0:T(2,128)(2,1)} %get-tuple-element.77), kind=kOutput, calls=%fused_computation.4 | convolution fusion | flops 8220160 | bytes 4102400 | tf_op jit(solution)/shard_map/dot_general | solution.py:485
  65.2 0.2 collective-permute-done.7.refs_0_
  65.4 1.2 %collective-permute-done.8.refs_2_ = bf16[2,80,384]{2,1,0:T(8,128)(2,1)} collective-permute-done((bf16[2,80,384]{2,1,0:T(8,128)(2,1)}, bf16[2,80,384]{2,1,0:T(8,128)(2,1)}, u32[]{:S(2)}, u32[]{:S(2)}) %collective-permute-start.8) | collective-permute-done | bytes 122912 | tf_op jit(solution)/shard_map/ppermute | solution.py:490
  66.6 2.0 %shard_map.159 = (f32[80,384]{1,0:T(8,128)}, f32[8,320]{1,0:T(8,128)}, bf16[80,384]{1,0:T(8,128)(2,1)}, bf16[80,384]{1,0:T(8,128)(2,1)}, bf16[80,384]{1,0:T(8,128)(2,1)}) custom-call(bf16[2,80,384]{2,1,0:T(8,128)(2,1)} %collective-permute-done.7.refs_0_, f32[2,80,384]{2,1,0:T(8,128)} %get-tuple-element.57.refs_1_, ...), custom_call_target="tpu_custom_call" | custom-call | bytes 2000000 | tf_op jit(solution)/shard_map/pallas_call | solution.py:57
  68.7 3.5 %collective-permute-start.15 = (f32[8,320]{1,0:T(8,128)}, f32[8,320]{1,0:T(8,128)}, u32[]{:S(2)}, u32[]{:S(2)}) collective-permute-start(f32[8,320]{1,0:T(8,128)} %get-tuple-element.67.refs_1_), channel_id=1, source_target_pairs={{0,12},{1,13},{2,14},{3,15},{4,8},{5,9},{6,10},{7,11},{8,4},{9,5},... | collective-permute-start | bytes 30728 | tf_op jit(solution)/shard_map/ppermute | solution.py:490
  72.1 2.1 %fusion.22.refs_8_ = f32[2,320]{1,0:T(2,128)} fusion(bf16[2,1280]{1,0:T(2,128)(2,1)} %fusion.1.refs_7_, bf16[1280,320]{0,1:T(8,128)(2,1)} %param.18), kind=kOutput, calls=%fused_computation.20 | convolution fusion | flops 1638400 | bytes 826880 | tf_op jit(solution)/shard_map/dot_general | solution.py:609
  74.2 0.0 collective-permute-start.14
  74.2 1.0 collective-permute-start.13
  75.2 1.0 collective-permute-start.10
  76.2 2.9 %collective-permute-start.11 = (bf16[80,384]{1,0:T(8,128)(2,1)}, bf16[80,384]{1,0:T(8,128)(2,1)}, u32[]{:S(2)}, u32[]{:S(2)}) collective-permute-start(bf16[80,384]{1,0:T(8,128)(2,1)} %get-tuple-element.62.refs_10_), channel_id=1, source_target_pairs={{0,8},{1,9},{2,10},{3,11},{4,12},{5,13},{6,14},{7,15},{8,0},{9,1},... | collective-permute-start | bytes 184328 | tf_op jit(solution)/shard_map/ppermute | solution.py:490
  79.2 0.4 collective-permute-start.12
  79.6 8.4 %shard_map.160 = (bf16[1024,320]{1,0:T(8,128)(2,1)}, f32[8,128]{1,0:T(8,128)}) custom-call(bf16[1024,320]{1,0:T(8,128)(2,1)} %bitcast.19, bf16[9,320,320]{2,1,0:T(8,128)(2,1)} %bitcast.26, f32[320]{0:T(512)} %refs_2_.3, f32[8,320]{1,0:T(8,128)} %get-tuple-element.46.refs_2_.refs_3_.refs_4_, f32[4,66,1,320]{3,2,1,0:T(1,128)} %collective-permute-done.1.refs_2_.refs_5_.refs_4_, ...), custom_call_target="tpu_custom_call" | custom-call | flops 1887436800 | bytes 2000000 | tf_op jit(solution)/shard_map/pallas_call | solution.py:57
  88.0 0.0 collective-permute-done.14.refs_6_
  88.0 0.0 collective-permute-done.13.refs_5_
  88.0 0.0 collective-permute-done.11.refs_3_
  88.0 0.0 collective-permute-done.12.refs_4_
  88.0 1.7 %shard_map.161 = (bf16[80,384]{1,0:T(8,128)(2,1)}, f32[8,320]{1,0:T(8,128)}) custom-call(f32[80,384]{1,0:T(8,128)} %get-tuple-element.66.refs_0_, f32[8,320]{1,0:T(8,128)} %get-tuple-element.67.refs_1_, bf16[80,384]{1,0:T(8,128)(2,1)} %collective-permute-done.10.refs_2_, bf16[80,384]{1,0:T(8,128)(2,1)} %collective-permute-done.11.refs_3_, ...), custom_call_target="tpu_custom_call" | custom-call | bytes 2000000 | tf_op jit(solution)/shard_map/pallas_call | solution.py:57
  89.8 4.2 %collective-permute-start.23 = (bf16[80,384]{1,0:T(8,128)(2,1)}, bf16[80,384]{1,0:T(8,128)(2,1)}, u32[]{:S(2)}, u32[]{:S(2)}) collective-permute-start(bf16[80,384]{1,0:T(8,128)(2,1)} %get-tuple-element.70.refs_8_.refs_0_), channel_id=1, source_target_pairs={{0,14},{1,15},{2,12},{3,13},{4,10},{5,11},{6,8},{7,9},{8,6},{9,7},... | collective-permute-start | bytes 184328 | tf_op jit(solution)/shard_map/ppermute | solution.py:490
  94.0 0.0 collective-permute-start.22
  94.0 0.7 collective-permute-start.16
  94.7 0.0 collective-permute-start.21
  94.7 3.1 %collective-permute-start.20 = (bf16[80,384]{1,0:T(8,128)(2,1)}, bf16[80,384]{1,0:T(8,128)(2,1)}, u32[]{:S(2)}, u32[]{:S(2)}) collective-permute-start(bf16[80,384]{1,0:T(8,128)(2,1)} %get-tuple-element.70.refs_8_.refs_0_), channel_id=1, source_target_pairs={{0,8},{1,9},{2,10},{3,11},{4,12},{5,13},{6,14},{7,15},{8,0},{9,1},... | collective-permute-start | bytes 184328 | tf_op jit(solution)/shard_map/ppermute | solution.py:490
  97.8 0.2 collective-permute-done.16.refs_6_
  98.0 2.0 %collective-permute-start.19 = (bf16[80,384]{1,0:T(8,128)(2,1)}, bf16[80,384]{1,0:T(8,128)(2,1)}, u32[]{:S(2)}, u32[]{:S(2)}) collective-permute-start(bf16[80,384]{1,0:T(8,128)(2,1)} %get-tuple-element.70.refs_8_.refs_0_), channel_id=1, source_target_pairs={{0,6},{1,7},{2,4},{3,5},{4,2},{5,3},{6,0},{7,1},{8,14},{9,15},{10,... | collective-permute-start | bytes 184328 | tf_op jit(solution)/shard_map/ppermute | solution.py:490
  99.9 0.7 collective-permute-start.18
  100.6 0.0 collective-permute-done.22.refs_6_
  100.6 1.1 collective-permute-start.17
  101.7 5.2 %shard_map.162 = (f32[1024,320]{1,0:T(8,128)}, f32[320]{0:T(512)}, f32[320]{0:T(512)}, f32[320]{0:T(512)}, f32[320,1280]{1,0:T(8,128)}, /*index=5*/f32[8,128]{1,0:T(8,128)}) custom-call(bf16[1024,320]{1,0:T(8,128)(2,1)} %bitcast.20, bf16[1024,320]{1,0:T(8,128)(2,1)} %bitcast.23, f32[1024,320]{1,0:T(8,128)} %get-tuple-element.65.refs_2_, f32[320]{0:T(512)} %refs_3_.3, ...), custom_call_target="tpu_custom_call" | custom-call | flops 2621440 | bytes 2000000 | tf_op jit(solution)/shard_map/pallas_call | solution.py:57
  107.0 0.0 collective-permute-done.21.refs_5_
  107.0 0.0 collective-permute-done.19.refs_3_
  107.0 0.0 collective-permute-done.18.refs_2_
  107.0 2.0 %shard_map.163.refs_0_ = bf16[80,3072]{1,0:T(8,128)(2,1)} custom-call(bf16[80,384]{1,0:T(8,128)(2,1)} %get-tuple-element.70.refs_8_.refs_0_, bf16[80,384]{1,0:T(8,128)(2,1)} %collective-permute-done.17.refs_1_, bf16[80,384]{1,0:T(8,128)(2,1)} %collective-permute-done.18.refs_2_, bf16[80,384]{1,0:T(8,128)(2,1)} %collective-permute-done.19.refs_3_, ...), custom_call_target="tpu_custom_call" | custom-call | bytes 2000000 | tf_op jit(solution)/shard_map/pallas_call | solution.py:57
  109.0 0.1 collective-permute-start.24
  109.0 2.2 %collective-permute-done.24.refs_1_ = bf16[80,3072]{1,0:T(8,128)(2,1)} collective-permute-done((bf16[80,3072]{1,0:T(8,128)(2,1)}, bf16[80,3072]{1,0:T(8,128)(2,1)}, u32[]{:S(2)}, u32[]{:S(2)}) %collective-permute-start.24) | collective-permute-done | bytes 491552 | tf_op jit(solution)/shard_map/ppermute | solution.py:490
  111.2 3.1 %shard_map.164 = f32[9,160,320]{2,1,0:T(8,128)} custom-call(bf16[80,3072]{1,0:T(8,128)(2,1)} %shard_map.163.refs_0_, bf16[80,3072]{1,0:T(8,128)(2,1)} %collective-permute-done.24.refs_1_), custom_call_target="tpu_custom_call" | custom-call | bytes 2000000 | tf_op jit(solution)/shard_map/pallas_call | solution.py:57
  (7 shorter events, 0.0 us)
Async XLA Ops:
  1.4 4.9 %collective-permute-start = (bf16[32,320]{1,0:T(8,128)(2,1)S(1)}, bf16[32,320]{1,0:T(8,128)(2,1)}, u32[]{:S(2)}, u32[]{:S(2)}) collective-permute-start(bf16[32,320]{1,0:T(8,128)(2,1)S(1)} %maximum_bitcast_fusion), channel_id=1, source_target_pairs={{0,16},{1,17},{2,18},{3,19},{4,20},{5,21},{6,22},{7,23},{8,24},{9,... | collective-permute-start | bytes 61448 | tf_op jit(solution)/shard_map/ppermute | solution.py:490
  9.6 12.1 %collective-permute-start.1 = (f32[4,66,1,320]{3,2,1,0:T(1,128)}, f32[4,66,1,320]{3,2,1,0:T(1,128)}, u32[]{:S(2)}, u32[]{:S(2)}) collective-permute-start(f32[4,66,1,320]{3,2,1,0:T(1,128)} %get-tuple-element.42), channel_id=1, source_target_pairs={{0,1},{1,2},{2,3},{3,4},{4,5},{5,6},{6,7},{7,8},{8,9},{9,10},{10,1... | collective-permute-start | bytes 1013768 | tf_op jit(solution)/shard_map/ppermute | solution.py:501
  11.7 10.0 %collective-permute-start.2 = (f32[4,66,1,320]{3,2,1,0:T(1,128)}, f32[4,66,1,320]{3,2,1,0:T(1,128)}, u32[]{:S(2)}, u32[]{:S(2)}) collective-permute-start(f32[4,66,1,320]{3,2,1,0:T(1,128)} %get-tuple-element.43), channel_id=1, source_target_pairs={{1,0},{2,1},{3,2},{4,3},{5,4},{6,5},{7,6},{8,7},{9,8},{10,9},{11,1... | collective-permute-start | bytes 1013768 | tf_op jit(solution)/shard_map/ppermute | solution.py:501
  12.9 16.8 %all-to-all-start = ((f32[32,1,128]{2,1,0:T(1,128)}), f32[32,1,128]{2,1,0:T(1,128)}, u32[]{:S(2)}, u32[]{:S(2)}) async-start(f32[32,1,128]{2,1,0:T(1,128)} %get-tuple-element.45), calls=%async_computation | async-start | bytes 32768 | tf_op jit(solution)/shard_map/all_to_all | solution.py:551
  38.0 4.1 %collective-permute-start.3 = (bf16[2,8,80,384]{3,2,1,0:T(8,128)(2,1)}, bf16[2,8,80,384]{3,2,1,0:T(8,128)(2,1)}, u32[]{:S(2)}, u32[]{:S(2)}) collective-permute-start(bf16[2,8,80,384]{3,2,1,0:T(8,128)(2,1)} %bitcast.29), channel_id=1, source_target_pairs={{0,1},{1,0},{2,3},{3,2},{4,5},{5,4},{6,7},{7,6},{8,9},{9,8},{10,11... | collective-permute-start | bytes 2949128 | tf_op jit(solution)/shard_map/ppermute | solution.py:490
  45.1 11.7 %collective-permute-start.4 = (bf16[2,2,80,384]{3,2,1,0:T(8,128)(2,1)}, bf16[2,2,80,384]{3,2,1,0:T(8,128)(2,1)}, u32[]{:S(2)}, u32[]{:S(2)}) collective-permute-start(bf16[2,2,80,384]{3,2,1,0:T(8,128)(2,1)} %get-tuple-element.49.refs_4_), channel_id=1, source_target_pairs={{0,16},{1,17},{2,18},{3,19},{4,20},{5,21},{6,22},{7,23},{8,24},{9,... | collective-permute-start | bytes 737288 | tf_op jit(solution)/shard_map/ppermute | solution.py:490
  46.8 10.0 %collective-permute-start.5 = (bf16[2,2,80,384]{3,2,1,0:T(8,128)(2,1)}, bf16[2,2,80,384]{3,2,1,0:T(8,128)(2,1)}, u32[]{:S(2)}, u32[]{:S(2)}) collective-permute-start(bf16[2,2,80,384]{3,2,1,0:T(8,128)(2,1)} %get-tuple-element.51.refs_5_), channel_id=1, source_target_pairs={{0,2},{1,3},{2,0},{3,1},{4,6},{5,7},{6,4},{7,5},{8,10},{9,11},{10,... | collective-permute-start | bytes 737288 | tf_op jit(solution)/shard_map/ppermute | solution.py:490
  55.2 1.6 %collective-permute-start.6 = (f32[8,320]{1,0:T(8,128)}, f32[8,320]{1,0:T(8,128)}, u32[]{:S(2)}, u32[]{:S(2)}) collective-permute-start(f32[8,320]{1,0:T(8,128)} %get-tuple-element.55.refs_4_), channel_id=1, source_target_pairs={{0,1},{1,0},{2,3},{3,2},{4,5},{5,4},{6,7},{7,6},{8,9},{9,8},{10,11... | collective-permute-start | bytes 30728 | tf_op jit(solution)/shard_map/ppermute | solution.py:490
  59.2 6.0 %collective-permute-start.9 = (f32[8,320]{1,0:T(8,128)}, f32[8,320]{1,0:T(8,128)}, u32[]{:S(2)}, u32[]{:S(2)}) collective-permute-start(f32[8,320]{1,0:T(8,128)} %get-tuple-element.60.refs_4_), channel_id=1, source_target_pairs={{0,2},{1,3},{2,0},{3,1},{4,6},{5,7},{6,4},{7,5},{8,10},{9,11},{10,... | collective-permute-start | bytes 30728 | tf_op jit(solution)/shard_map/ppermute | solution.py:490
  60.1 5.3 %collective-permute-start.7 = (bf16[2,80,384]{2,1,0:T(8,128)(2,1)}, bf16[2,80,384]{2,1,0:T(8,128)(2,1)}, u32[]{:S(2)}, u32[]{:S(2)}) collective-permute-start(bf16[2,80,384]{2,1,0:T(8,128)(2,1)} %get-tuple-element.56), channel_id=1, source_target_pairs={{0,2},{1,3},{2,0},{3,1},{4,6},{5,7},{6,4},{7,5},{8,10},{9,11},{10,... | collective-permute-start | bytes 368648 | tf_op jit(solution)/shard_map/ppermute | solution.py:490
  61.3 5.3 %collective-permute-start.8 = (bf16[2,80,384]{2,1,0:T(8,128)(2,1)}, bf16[2,80,384]{2,1,0:T(8,128)(2,1)}, u32[]{:S(2)}, u32[]{:S(2)}) collective-permute-start(bf16[2,80,384]{2,1,0:T(8,128)(2,1)} %get-tuple-element.58), channel_id=1, source_target_pairs={{0,16},{1,17},{2,18},{3,19},{4,20},{5,21},{6,22},{7,23},{8,24},{9,... | collective-permute-start | bytes 368648 | tf_op jit(solution)/shard_map/ppermute | solution.py:490
  68.7 10.5 %collective-permute-start.15 = (f32[8,320]{1,0:T(8,128)}, f32[8,320]{1,0:T(8,128)}, u32[]{:S(2)}, u32[]{:S(2)}) collective-permute-start(f32[8,320]{1,0:T(8,128)} %get-tuple-element.67.refs_1_), channel_id=1, source_target_pairs={{0,12},{1,13},{2,14},{3,15},{4,8},{5,9},{6,10},{7,11},{8,4},{9,5},... | collective-permute-start | bytes 30728 | tf_op jit(solution)/shard_map/ppermute | solution.py:490
  74.2 13.8 %collective-permute-start.14 = (f32[8,320]{1,0:T(8,128)}, f32[8,320]{1,0:T(8,128)}, u32[]{:S(2)}, u32[]{:S(2)}) collective-permute-start(f32[8,320]{1,0:T(8,128)} %get-tuple-element.67.refs_1_), channel_id=1, source_target_pairs={{0,8},{1,9},{2,10},{3,11},{4,12},{5,13},{6,14},{7,15},{8,0},{9,1},... | collective-permute-start | bytes 30728 | tf_op jit(solution)/shard_map/ppermute | solution.py:490
  74.2 13.8 %collective-permute-start.13 = (f32[8,320]{1,0:T(8,128)}, f32[8,320]{1,0:T(8,128)}, u32[]{:S(2)}, u32[]{:S(2)}) collective-permute-start(f32[8,320]{1,0:T(8,128)} %get-tuple-element.67.refs_1_), channel_id=1, source_target_pairs={{0,4},{1,5},{2,6},{3,7},{4,0},{5,1},{6,2},{7,3},{8,12},{9,13},{10,... | collective-permute-start | bytes 30728 | tf_op jit(solution)/shard_map/ppermute | solution.py:490
  75.2 12.8 %collective-permute-start.10 = (bf16[80,384]{1,0:T(8,128)(2,1)}, bf16[80,384]{1,0:T(8,128)(2,1)}, u32[]{:S(2)}, u32[]{:S(2)}) collective-permute-start(bf16[80,384]{1,0:T(8,128)(2,1)} %get-tuple-element.61.refs_9_), channel_id=1, source_target_pairs={{0,4},{1,5},{2,6},{3,7},{4,0},{5,1},{6,2},{7,3},{8,12},{9,13},{10,... | collective-permute-start | bytes 184328 | tf_op jit(solution)/shard_map/ppermute | solution.py:490
  76.2 11.8 %collective-permute-start.11 = (bf16[80,384]{1,0:T(8,128)(2,1)}, bf16[80,384]{1,0:T(8,128)(2,1)}, u32[]{:S(2)}, u32[]{:S(2)}) collective-permute-start(bf16[80,384]{1,0:T(8,128)(2,1)} %get-tuple-element.62.refs_10_), channel_id=1, source_target_pairs={{0,8},{1,9},{2,10},{3,11},{4,12},{5,13},{6,14},{7,15},{8,0},{9,1},... | collective-permute-start | bytes 184328 | tf_op jit(solution)/shard_map/ppermute | solution.py:490
  79.2 8.9 %collective-permute-start.12 = (bf16[80,384]{1,0:T(8,128)(2,1)}, bf16[80,384]{1,0:T(8,128)(2,1)}, u32[]{:S(2)}, u32[]{:S(2)}) collective-permute-start(bf16[80,384]{1,0:T(8,128)(2,1)} %get-tuple-element.63.refs_11_), channel_id=1, source_target_pairs={{0,12},{1,13},{2,14},{3,15},{4,8},{5,9},{6,10},{7,11},{8,4},{9,5},... | collective-permute-start | bytes 184328 | tf_op jit(solution)/shard_map/ppermute | solution.py:490
  89.8 10.2 %collective-permute-start.23 = (bf16[80,384]{1,0:T(8,128)(2,1)}, bf16[80,384]{1,0:T(8,128)(2,1)}, u32[]{:S(2)}, u32[]{:S(2)}) collective-permute-start(bf16[80,384]{1,0:T(8,128)(2,1)} %get-tuple-element.70.refs_8_.refs_0_), channel_id=1, source_target_pairs={{0,14},{1,15},{2,12},{3,13},{4,10},{5,11},{6,8},{7,9},{8,6},{9,7},... | collective-permute-start | bytes 184328 | tf_op jit(solution)/shard_map/ppermute | solution.py:490
  94.0 6.7 %collective-permute-start.22 = (bf16[80,384]{1,0:T(8,128)(2,1)}, bf16[80,384]{1,0:T(8,128)(2,1)}, u32[]{:S(2)}, u32[]{:S(2)}) collective-permute-start(bf16[80,384]{1,0:T(8,128)(2,1)} %get-tuple-element.70.refs_8_.refs_0_), channel_id=1, source_target_pairs={{0,12},{1,13},{2,14},{3,15},{4,8},{5,9},{6,10},{7,11},{8,4},{9,5},... | collective-permute-start | bytes 184328 | tf_op jit(solution)/shard_map/ppermute | solution.py:490
  94.0 4.0 %collective-permute-start.16 = (f32[8,320]{1,0:T(8,128)}, f32[8,320]{1,0:T(8,128)}, u32[]{:S(2)}, u32[]{:S(2)}) collective-permute-start(f32[8,320]{1,0:T(8,128)} %get-tuple-element.69.refs_5_), channel_id=1, source_target_pairs={{0,16},{1,17},{2,18},{3,19},{4,20},{5,21},{6,22},{7,23},{8,24},{9,... | collective-permute-start | bytes 30728 | tf_op jit(solution)/shard_map/ppermute | solution.py:490
  94.7 12.3 %collective-permute-start.21 = (bf16[80,384]{1,0:T(8,128)(2,1)}, bf16[80,384]{1,0:T(8,128)(2,1)}, u32[]{:S(2)}, u32[]{:S(2)}) collective-permute-start(bf16[80,384]{1,0:T(8,128)(2,1)} %get-tuple-element.70.refs_8_.refs_0_), channel_id=1, source_target_pairs={{0,10},{1,11},{2,8},{3,9},{4,14},{5,15},{6,12},{7,13},{8,2},{9,3},... | collective-permute-start | bytes 184328 | tf_op jit(solution)/shard_map/ppermute | solution.py:490
  94.7 12.3 %collective-permute-start.20 = (bf16[80,384]{1,0:T(8,128)(2,1)}, bf16[80,384]{1,0:T(8,128)(2,1)}, u32[]{:S(2)}, u32[]{:S(2)}) collective-permute-start(bf16[80,384]{1,0:T(8,128)(2,1)} %get-tuple-element.70.refs_8_.refs_0_), channel_id=1, source_target_pairs={{0,8},{1,9},{2,10},{3,11},{4,12},{5,13},{6,14},{7,15},{8,0},{9,1},... | collective-permute-start | bytes 184328 | tf_op jit(solution)/shard_map/ppermute | solution.py:490
  98.0 9.0 %collective-permute-start.19 = (bf16[80,384]{1,0:T(8,128)(2,1)}, bf16[80,384]{1,0:T(8,128)(2,1)}, u32[]{:S(2)}, u32[]{:S(2)}) collective-permute-start(bf16[80,384]{1,0:T(8,128)(2,1)} %get-tuple-element.70.refs_8_.refs_0_), channel_id=1, source_target_pairs={{0,6},{1,7},{2,4},{3,5},{4,2},{5,3},{6,0},{7,1},{8,14},{9,15},{10,... | collective-permute-start | bytes 184328 | tf_op jit(solution)/shard_map/ppermute | solution.py:490
  99.9 7.0 %collective-permute-start.18 = (bf16[80,384]{1,0:T(8,128)(2,1)}, bf16[80,384]{1,0:T(8,128)(2,1)}, u32[]{:S(2)}, u32[]{:S(2)}) collective-permute-start(bf16[80,384]{1,0:T(8,128)(2,1)} %get-tuple-element.70.refs_8_.refs_0_), channel_id=1, source_target_pairs={{0,4},{1,5},{2,6},{3,7},{4,0},{5,1},{6,2},{7,3},{8,12},{9,13},{10,... | collective-permute-start | bytes 184328 | tf_op jit(solution)/shard_map/ppermute | solution.py:490
  100.6 6.4 %collective-permute-start.17 = (bf16[80,384]{1,0:T(8,128)(2,1)}, bf16[80,384]{1,0:T(8,128)(2,1)}, u32[]{:S(2)}, u32[]{:S(2)}) collective-permute-start(bf16[80,384]{1,0:T(8,128)(2,1)} %get-tuple-element.70.refs_8_.refs_0_), channel_id=1, source_target_pairs={{0,2},{1,3},{2,0},{3,1},{4,6},{5,7},{6,4},{7,5},{8,10},{9,11},{10,... | collective-permute-start | bytes 184328 | tf_op jit(solution)/shard_map/ppermute | solution.py:490
  109.0 2.3 %collective-permute-start.24 = (bf16[80,3072]{1,0:T(8,128)(2,1)}, bf16[80,3072]{1,0:T(8,128)(2,1)}, u32[]{:S(2)}, u32[]{:S(2)}) collective-permute-start(bf16[80,3072]{1,0:T(8,128)(2,1)} %shard_map.163.refs_0_), channel_id=1, source_target_pairs={{0,1},{1,0},{2,3},{3,2},{4,5},{5,4},{6,7},{7,6},{8,9},{9,8},{10,11... | collective-permute-start | bytes 1474568 | tf_op jit(solution)/shard_map/ppermute | solution.py:490

commit v5 on v4

--- a/solution.py
+++ b/solution.py
@@ -14,7 +14,6 @@
 F32 = jnp.float32
 BF16 = jnp.bfloat16
 AXES = ("row", "col")
-VMEM_LIMIT = 64 * 1024 * 1024
 HI = lax.Precision.HIGHEST
 
 
@@ -22,54 +21,46 @@
     return lax.broadcasted_iota(jnp.int32, shape, dim)
 
 
-def call(body, out_shape, operands, far=(), after=(), scratch=(), flops=0, nbytes=2_000_000):
-    outs, tree = jax.tree.flatten(out_shape)
-    ins = (*far, *operands)
-    waits, own = len(after), len(scratch)
+def call(body, out_shape, operands, far=(), after=(), scratch=(), vmem=20, flops=0):
+    count, used, waits = len(far), len(operands), len(after)
 
     def kernel(*refs):
-        src, refs = refs[: len(ins)], refs[len(ins) + waits :]
-        dst, refs = refs[: len(outs)], refs[len(outs) :]
-        mine, refs = refs[:own], refs[own:]
-        held, refs = refs[: len(ins)], refs[len(ins) :]
-        made, (sem_in, sem_out) = refs[: len(outs)], refs[len(outs) :]
-        copies = [pltpu.make_async_copy(a, b, sem_in.at[i]) for i, (a, b) in enumerate(zip(src, held))]
-        for c in (*copies[len(far) :], *copies[: len(far)]):
+        ins = refs[:count]
+        rest = refs[count : count + used] + refs[count + used + waits :]
+        if not count:
+            return body(*rest)
+        holds, sems = rest[-1 - count : -1], rest[-1]
+        copies = [
+            pltpu.make_async_copy(ins[i], holds[i], sems.at[i]) for i in range(count)
+        ]
+        for c in copies:
             c.start()
 
         def loader(i):
             def load():
                 copies[i].wait()
-                return held[i]
+                return holds[i]
 
             return load
 
-        for c in copies[len(far) :]:
-            c.wait()
-        body(*[loader(i) for i in range(len(far))], *held[len(far) :], *made, *mine)
-        copies = [pltpu.make_async_copy(a, b, sem_out.at[i]) for i, (a, b) in enumerate(zip(made, dst))]
-        for c in copies:
-            c.start()
-        for c in copies:
-            c.wait()
-
-    hbm = pl.BlockSpec(memory_space=pltpu.HBM)
-    results = pl.pallas_call(
+        body(*[loader(i) for i in range(count)], *rest[: -1 - count])
+
+    near = pl.BlockSpec(memory_space=pltpu.VMEM)
+    scratch = list(scratch)
+    if count:
+        scratch += [pltpu.VMEM(v.shape, v.dtype) for v in far]
+        scratch.append(pltpu.SemaphoreType.DMA((count,)))
+    return pl.pallas_call(
         kernel,
-        out_shape=tuple(outs),
-        in_specs=[hbm] * len(ins) + [pl.BlockSpec(memory_space=pl.ANY)] * waits,
-        out_specs=(hbm,) * len(outs),
-        scratch_shapes=[
-            *scratch,
-            *[pltpu.VMEM(v.shape, v.dtype) for v in ins],
-            *[pltpu.VMEM(v.shape, v.dtype) for v in outs],
-            pltpu.SemaphoreType.DMA((max(len(ins), 1),)),
-            pltpu.SemaphoreType.DMA((len(outs),)),
-        ],
-        compiler_params=pltpu.CompilerParams(vmem_limit_bytes=VMEM_LIMIT),
-        cost_estimate=pl.CostEstimate(flops=flops, bytes_accessed=nbytes, transcendentals=0),
-    )(*ins, *after)
-    return jax.tree.unflatten(tree, results)
+        out_shape=out_shape,
+        in_specs=[pl.BlockSpec(memory_space=pltpu.HBM)] * count
+        + [near] * used
+        + [near] * waits,
+        out_specs=jax.tree.map(lambda _: near, out_shape),
+        scratch_shapes=scratch,
+        compiler_params=pltpu.CompilerParams(vmem_limit_bytes=vmem * 2**20),
+        cost_estimate=pl.CostEstimate(flops=flops, bytes_accessed=2_000_000, transcendentals=0),
+    )(*far, *operands, *after)
 
 
 def group_matrix(channels, lanes):
@@ -278,11 +269,11 @@
 
 
 def wgrad_kernel(batch, count, scale, *refs):
-    x_load, gp_load, gain_ref, bias_ref, st_ref = refs[:5]
+    x_load, gp_load, gain_load, bias_load, st_ref = refs[:5]
     halo = refs[5:9]
     aff_ref, keep_ref, send_ref = refs[9:12]
     ap, part = refs[12:]
-    aff = affine_rows(st_ref, gain_ref, bias_ref, batch, count)
+    aff = affine_rows(st_ref, gain_load(), bias_load(), batch, count)
     aff_ref[...] = aff
     x_ref = x_load()
     n, channels = x_ref.shape
@@ -410,9 +401,10 @@
     return col & 1, (col >> 1) & 1, col >> 2
 
 
-def step_one(nz, keep_ref, got_ref, a_send, a_keep, b_send, b_keep):
+def step_one(nz, keep_ref, got_ref, a_send, a_keep, b_send, b_keep, done_ref):
     _, xb, _ = place()
     half = nz // 2
+    done_ref[...] = jnp.zeros_like(done_ref)
     total = lambda r, p: keep_ref[r, p] + got_ref[r, p].astype(F32)
     for x in range(2):
         for z in range(half):
@@ -546,6 +538,7 @@
         (of((devices, 1, lanes), F32), column, column),
         (top, low),
         far=(x2, g2),
+        vmem=64,
     )
     left, right = shift(east, 0, 1), shift(west, 0, -1)
     stats = lax.all_to_all(pay, AXES, 0, 0)
@@ -567,6 +560,7 @@
         (of((n, channels), F32), of((8, channels), F32), of((channels, n), BF16)),
         halo,
         far=(g2, w9),
+        vmem=64,
         scratch=(shifted, pltpu.VMEM((padded, n), BF16)),
         flops=conv_flops,
     )
@@ -577,23 +571,25 @@
             of((keep_rows, pieces, share, width), F32),
             of((1, keep_rows, pieces, share, width), BF16),
         ),
-        (group_norm_gain, group_norm_bias, stats, *halo),
-        far=(x2, flipped),
+        (stats, *halo),
+        far=(x2, flipped, group_norm_gain, group_norm_bias),
+        vmem=56,
         scratch=(shifted, pltpu.VMEM((channels, pieces * width), F32)),
         flops=conv_flops,
     )
 
+    token = of((8, LANES), F32)
     if relative:
         half = nz // 2
         many = lambda k, dtype: of((*k, share, width), dtype)
         got = partner(send[0], 1)
-        a_send, a_keep, b_send, b_keep = call(
+        a_send, a_keep, b_send, b_keep, done = call(
             functools.partial(step_one, nz),
-            (many((2, half), BF16), many((2, half), F32)) * 2,
+            (many((2, half), BF16), many((2, half), F32)) * 2 + (token,),
             (keep, got),
         )
         a_got, b_got = partner(a_send, cols), partner(b_send, 2)
-        first = (a_send, b_send)
+        first = (done,)
     else:
         first = ()
 
@@ -602,11 +598,23 @@
         (of((n, channels), F32), of((8, channels), F32)),
         (aff, gsum),
         far=(x2, dacts),
+        vmem=58,
         after=first,
         flops=20 * n * channels,
     )
     emb = embed(timestep, embed_in, embed_out)
     temb = jnp.dot(emb, time_w, preferred_element_type=F32)
+
+    block_out, done = call(
+        functools.partial(conv_kernel, batch),
+        (of((n, channels), BF16), token),
+        (aff, *halo, temb),
+        far=(x2, w9, conv_b),
+        after=(sums,),
+        vmem=58,
+        scratch=(shifted,),
+        flops=conv_flops,
+    )
 
     if relative:
         s_shape = of(sums.shape, F32)
@@ -614,6 +622,7 @@
             functools.partial(step_two, nz),
             (many((half,), BF16), many((half,), F32)) * 2 + (s_shape,),
             (a_got, a_keep, b_got, b_keep, sums, partner(sums, 1)),
+            after=(done,),
         )
         a_got, b_got = partner(a_send, 2), partner(b_send, cols)
         own, sums, *sends = call(
@@ -624,36 +633,19 @@
         )
         gots = [partner(v, 4 * (k + 1)) for k, v in enumerate(sends)]
         gots += [partner(sums, 4 * k) for k in range(1, nz)]
-        second = tuple(sends)
-    else:
-        second = ()
-
-    token = of((8, LANES), F32)
-    block_out, done = call(
-        functools.partial(conv_kernel, batch),
-        (of((n, channels), BF16), token),
-        (aff, *halo, temb),
-        far=(x2, w9, conv_b),
-        after=second,
-        scratch=(shifted,),
-        flops=conv_flops,
-    )
 
     if relative:
         own, sums = call(
             functools.partial(step_four, nz),
             (many((), BF16), s_shape),
             (own, sums, *gots),
-            after=(done,),
         )
         others = [partner(own, 2 * k) for k in range(1, pieces)]
-        third = (own,)
     else:
         bit = 1
         while 2 * bit < devices:
             sums = sums + partner(sums, bit)
             bit *= 2
-        third = ()
 
     vector = of((channels,), F32)
     input_grad, gain_grad, bias_grad, conv_b_grad, time_grad, done = call(
@@ -661,7 +653,7 @@
         (of((n, channels), F32), *[vector] * 3, of((channels, emb.shape[1]), F32), token),
         (aff, sums, partner(sums, cols if relative else bit), emb),
         far=(x2, g2, dn, group_norm_gain),
-        after=third,
+        vmem=60,
         flops=8 * n * channels,
     )
 

time: 115 us -> 110 us (0.957)
  Pallas kernels: 51.4 us -> 43.8 us
  waiting for transfers between devices: 8.46 us -> 13.5 us
  other arithmetic: 3.11 us -> 0.15 us
  local copies, waits for them, and re-layouts: 0.73 us -> 2.71 us
  matrix products: 5.69 us -> 3.92 us
    pallas_call x12, Pallas kernels: 51.4 us -> 43.8 us  [call(): pl.pallas_call(kernel, out_shape=out_shape, in_specs=[pl.BlockSpec(memory...]
    ppermute x23, waiting for transfers between devices: 8.45 us -> 13.5 us  [partner(): return lax.ppermute(value, AXES, [(i, i ^ bit) for i in range(size)])]
    unnamed x0 -> x20, local copies, waits for them, and re-layouts: none -> 1.97 us
    another operation x1, other arithmetic: 1.37 us -> 0.12 us
    convert_element_type x1, other arithmetic: 1.16 us -> 0.01 us  [embed(): angles = timestep.astype(F32)[:, None] * freqs[None, :]]
  transfers between devices with their start and end apart: 26 -> 26, of which waited for: 7 -> 6; matrix products, arithmetic and copies ran while one was open for 8% -> 4% of each run, Pallas kernels for 22% -> 26%
where the time goes in v5:
time: 110 us; the launch traced here: 109 us
  starting transfers between devices  44 us (40%)
  Pallas kernels  43.8 us (40%)
  waiting for transfers between devices  13.5 us (12%)
  matrix products  3.92 us (4%)
  local copies, waits for them, and re-layouts  2.71 us (2%)
    pallas_call x12, Pallas kernels, call(): pl.pallas_call(kernel, out_shape=out_shape, in_specs=[pl.BlockSpec(memory...  43.8 us
    ppermute x23, starting transfers between devices, partner(): return lax.ppermute(value, AXES, [(i, i ^ bit) for i in range(size)])  31.9 us
    ppermute x23, waiting for transfers between devices, partner(): return lax.ppermute(value, AXES, [(i, i ^ bit) for i in range(size)])  13.5 us
    all_to_all x1, starting transfers between devices, local(): stats = lax.all_to_all(pay, AXES, 0, 0)  8.74 us
    ppermute x2, starting transfers between devices, shift(): return lax.ppermute(value, AXES, pairs)  3.32 us
    dot_general x1, matrix products, embed(): jnp.dot(first_hidden, embed_out, preferred_element_type=F32)  3 us
  transfers between devices with their start and end apart: 26, of which 6 were waited for; matrix products, arithmetic and copies ran while one was open for 4% of the time, Pallas kernels for 26%

profile of v5, /device:TPU:0, one launch (start us, length us, event | category | flops | bytes accessed | tf_op | source)
XLA Modules:
  0.0 109.0 jit_solution(5095205742662802130)
XLA Ops:
  0.6 0.7 constant_dynamic-slice_fusion
  1.4 3.0 %collective-permute-start = (bf16[32,320]{1,0:T(8,128)(2,1)S(1)}, bf16[32,320]{1,0:T(8,128)(2,1)}, u32[]{:S(2)}, u32[]{:S(2)}) collective-permute-start(bf16[32,320]{1,0:T(8,128)(2,1)S(1)} %maximum_bitcast_fusion), channel_id=1, source_target_pairs={{0,16},{1,17},{2,18},{3,19},{4,20},{5,21},{6,22},{7,23},{8,24},{9,... | collective-permute-start | bytes 61448 | tf_op jit(solution)/shard_map/ppermute | solution.py:482
  4.4 1.9 %collective-permute-done.refs_2_.refs_3_.refs_4_.refs_5_.refs_7_.refs_8_.refs_6_ = bf16[32,320]{1,0:T(8,128)(2,1)} collective-permute-done((bf16[32,320]{1,0:T(8,128)(2,1)S(1)}, bf16[32,320]{1,0:T(8,128)(2,1)}, u32[]{:S(2)}, u32[]{:S(2)}) %collective-permute-start) | collective-permute-done | bytes 20512 | tf_op jit(solution)/shard_map/ppermute | solution.py:482
  6.3 3.9 %shard_map.153 = (f32[32,1,128]{2,1,0:T(1,128)}, f32[4,66,1,320]{3,2,1,0:T(1,128)}, f32[4,66,1,320]{3,2,1,0:T(1,128)}) custom-call(bf16[1024,320]{1,0:T(8,128)(2,1)} %bitcast.16, bf16[1024,320]{1,0:T(8,128)(2,1)} %bitcast.21, bf16[32,320]{1,0:T(8,128)(2,1)} %collective-permute-done.refs_2_.refs_3_.refs_4_.refs_5_.refs_7_.refs_8_.refs_6_, ...), custom_call_target="tpu_custom_call" | custom-call | bytes 2000000 | tf_op jit(solution)/shard_map/pallas_call | solution.py:53
  10.2 2.0 %collective-permute-start.1 = (f32[4,66,1,320]{3,2,1,0:T(1,128)}, f32[4,66,1,320]{3,2,1,0:T(1,128)}, u32[]{:S(2)}, u32[]{:S(2)}) collective-permute-start(f32[4,66,1,320]{3,2,1,0:T(1,128)} %get-tuple-element.43), channel_id=1, source_target_pairs={{0,1},{1,2},{2,3},{3,4},{4,5},{5,6},{6,7},{7,8},{8,9},{9,10},{10,1... | collective-permute-start | bytes 1013768 | tf_op jit(solution)/shard_map/ppermute | solution.py:493
  12.2 1.3 %collective-permute-start.2 = (f32[4,66,1,320]{3,2,1,0:T(1,128)}, f32[4,66,1,320]{3,2,1,0:T(1,128)}, u32[]{:S(2)}, u32[]{:S(2)}) collective-permute-start(f32[4,66,1,320]{3,2,1,0:T(1,128)} %get-tuple-element.44), channel_id=1, source_target_pairs={{1,0},{2,1},{3,2},{4,3},{5,4},{6,5},{7,6},{8,7},{9,8},{10,9},{11,1... | collective-permute-start | bytes 1013768 | tf_op jit(solution)/shard_map/ppermute | solution.py:493
  13.5 8.7 %all-to-all-start = ((f32[32,1,128]{2,1,0:T(1,128)}), f32[32,1,128]{2,1,0:T(1,128)}, u32[]{:S(2)}, u32[]{:S(2)}) async-start(f32[32,1,128]{2,1,0:T(1,128)} %get-tuple-element.46), calls=%async_computation | async-start | bytes 32768 | tf_op jit(solution)/shard_map/all_to_all | solution.py:544
  22.3 0.0 collective-permute-done.1.refs_2_.refs_5_.refs_4_
  22.3 0.0 collective-permute-done.2.refs_3_.refs_6_.refs_5_
  22.3 8.8 %shard_map.154 = (f32[1024,320]{1,0:T(8,128)}, f32[8,320]{1,0:T(8,128)}, bf16[320,1024]{1,0:T(8,128)(2,1)}) custom-call(bf16[1024,320]{1,0:T(8,128)(2,1)} %bitcast.22, bf16[9,320,320]{2,1,0:T(8,128)(2,1)} %bitcast.25, f32[4,66,1,320]{3,2,1,0:T(1,128)} %collective-permute-done.1.refs_2_.refs_5_.refs_4_, ...), custom_call_target="tpu_custom_call" | custom-call | flops 1887436800 | bytes 2000000 | tf_op jit(solution)/shard_map/pallas_call | solution.py:53
  31.1 0.0 all-to-all-done.refs_4_
  31.1 0.0 copy-start.9
  31.1 9.1 %shard_map.155 = (f32[8,320]{1,0:T(8,128)}, f32[2,8,80,384]{3,2,1,0:T(8,128)}, bf16[1,2,8,80,384]{4,3,2,1,0:T(8,128)(2,1)}) custom-call(bf16[1024,320]{1,0:T(8,128)(2,1)} %bitcast.17, bf16[320,1024]{1,0:T(8,128)(2,1)} %get-tuple-element.45.refs_1_, f32[320]{0:T(512)} %refs_3_.3, f32[320]{0:T(512)} %refs_3_.2, f32[32,1,128]{2,1,0:T(1,128)} %all-to-all-done.refs_4_, ...), custom_call_target="tpu_custom_call" | custom-call | flops 1887436800 | bytes 2000000 | tf_op jit(solution)/shard_map/pallas_call | solution.py:53
  40.2 0.0 copy-start
  40.2 1.5 %collective-permute-start.3 = (bf16[2,8,80,384]{3,2,1,0:T(8,128)(2,1)}, bf16[2,8,80,384]{3,2,1,0:T(8,128)(2,1)S(1)}, u32[]{:S(2)}, u32[]{:S(2)}) collective-permute-start(bf16[2,8,80,384]{3,2,1,0:T(8,128)(2,1)} %bitcast.29), channel_id=1, source_target_pairs={{0,1},{1,0},{2,3},{3,2},{4,5},{5,4},{6,7},{7,6},{8,9},{9,8},{10,11... | collective-permute-start | bytes 2949128 | tf_op jit(solution)/shard_map/ppermute | solution.py:482
  41.8 0.1 fusion.7
  41.9 3.0 %fusion.1.refs_7_ = bf16[2,1280]{1,0:T(2,128)(2,1)S(1)} fusion(bf16[1280,1280]{1,0:T(8,128)(2,1)} %param.17, bf16[320,1280]{1,0:T(8,128)(2,1)} %param.16, bf16[2,160]{1,0:T(2,128)(2,1)S(1)} %get-tuple-element.80, bf16[2,160]{1,0:T(2,128)(2,1)S(1)} %get-tuple-element.79), kind=kOutput, calls=%fused_computation.4 | convolution fusion | flops 8220160 | bytes 4102400 | tf_op jit(solution)/shard_map/dot_general | solution.py:477
  44.9 0.0 copy-start.6
  45.0 0.2 shard_map.156
  45.1 0.0 copy-start.5
  45.1 0.6 copy-done.5
  45.7 1.7 %collective-permute-start.4 = (bf16[2,2,80,384]{3,2,1,0:T(8,128)(2,1)S(1)}, bf16[2,2,80,384]{3,2,1,0:T(8,128)(2,1)S(1)}, u32[]{:S(2)}, u32[]{:S(2)}) collective-permute-start(bf16[2,2,80,384]{3,2,1,0:T(8,128)(2,1)S(1)} %get-tuple-element.56), channel_id=1, source_target_pairs={{0,16},{1,17},{2,18},{3,19},{4,20},{5,21},{6,22},{7,23},{8,24},{9,... | collective-permute-start | bytes 737288 | tf_op jit(solution)/shard_map/ppermute | solution.py:482
  47.4 2.4 %collective-permute-start.5 = (bf16[2,2,80,384]{3,2,1,0:T(8,128)(2,1)S(1)}, bf16[2,2,80,384]{3,2,1,0:T(8,128)(2,1)S(1)}, u32[]{:S(2)}, u32[]{:S(2)}) collective-permute-start(bf16[2,2,80,384]{3,2,1,0:T(8,128)(2,1)S(1)} %get-tuple-element.58), channel_id=1, source_target_pairs={{0,2},{1,3},{2,0},{3,1},{4,6},{5,7},{6,4},{7,5},{8,10},{9,11},{10,... | collective-permute-start | bytes 737288 | tf_op jit(solution)/shard_map/ppermute | solution.py:482
  49.9 0.9 fusion.22.refs_8_
  50.8 4.7 %shard_map.157 = (f32[1024,320]{1,0:T(8,128)}, f32[8,320]{1,0:T(8,128)}) custom-call(bf16[1024,320]{1,0:T(8,128)(2,1)} %bitcast.18, f32[1024,320]{1,0:T(8,128)} %get-tuple-element.48.refs_1_, f32[8,320]{1,0:T(8,128)} %get-tuple-element.47.refs_2_.refs_3_.refs_4_, f32[8,320]{1,0:T(8,128)} %get-tuple-element.49.refs_3_, f32[8,128]{1,0:T(8,128)} %copy-done.5), custom_call_target="tpu_custom_call" | custom-call | flops 6553600 | bytes 2000000 | tf_op jit(solution)/shard_map/pallas_call | solution.py:53
  55.5 0.0 copy-start.2
  55.5 0.1 collective-permute-start.6
  55.6 9.2 %shard_map.158 = (bf16[1024,320]{1,0:T(8,128)(2,1)}, f32[8,128]{1,0:T(8,128)}) custom-call(bf16[1024,320]{1,0:T(8,128)(2,1)} %bitcast.19, bf16[9,320,320]{2,1,0:T(8,128)(2,1)} %bitcast.26, f32[320]{0:T(512)} %refs_2_.3, f32[8,320]{1,0:T(8,128)} %get-tuple-element.47.refs_2_.refs_3_.refs_4_, f32[4,66,1,320]{3,2,1,0:T(1,128)} %collective-permute-done.1.refs_2_.refs_5_.refs_4_, ...), custom_call_target="tpu_custom_call" | custom-call | flops 1887436800 | bytes 2000000 | tf_op jit(solution)/shard_map/pallas_call | solution.py:53
  64.8 0.0 collective-permute-done.4.refs_0_
  64.8 0.0 copy-start.4
  64.9 0.7 copy-done.4
  65.5 0.1 shard_map.159
  65.6 0.1 collective-permute-start.7
  65.7 0.5 collective-permute-start.8
  66.2 1.9 %collective-permute-start.9 = (f32[8,320]{1,0:T(8,128)S(1)}, f32[8,320]{1,0:T(8,128)S(1)}, u32[]{:S(2)}, u32[]{:S(2)}) collective-permute-start(f32[8,320]{1,0:T(8,128)S(1)} %get-tuple-element.65.refs_4_), channel_id=1, source_target_pairs={{0,2},{1,3},{2,0},{3,1},{4,6},{5,7},{6,4},{7,5},{8,10},{9,11},{10,... | collective-permute-start | bytes 30728 | tf_op jit(solution)/shard_map/ppermute | solution.py:482
  68.1 3.6 %collective-permute-done.9.refs_5_ = f32[8,320]{1,0:T(8,128)S(1)} collective-permute-done((f32[8,320]{1,0:T(8,128)S(1)}, f32[8,320]{1,0:T(8,128)S(1)}, u32[]{:S(2)}, u32[]{:S(2)}) %collective-permute-start.9) | collective-permute-done | bytes 10272 | tf_op jit(solution)/shard_map/ppermute | solution.py:482
  71.7 0.1 shard_map.160
  71.8 2.4 %collective-permute-start.10 = (bf16[80,384]{1,0:T(8,128)(2,1)S(1)}, bf16[80,384]{1,0:T(8,128)(2,1)S(1)}, u32[]{:S(2)}, u32[]{:S(2)}) collective-permute-start(bf16[80,384]{1,0:T(8,128)(2,1)S(1)} %get-tuple-element.68), channel_id=1, source_target_pairs={{0,4},{1,5},{2,6},{3,7},{4,0},{5,1},{6,2},{7,3},{8,12},{9,13},{10,... | collective-permute-start | bytes 184328 | tf_op jit(solution)/shard_map/ppermute | solution.py:482
  74.1 2.6 %collective-permute-start.11 = (bf16[80,384]{1,0:T(8,128)(2,1)S(1)}, bf16[80,384]{1,0:T(8,128)(2,1)S(1)}, u32[]{:S(2)}, u32[]{:S(2)}) collective-permute-start(bf16[80,384]{1,0:T(8,128)(2,1)S(1)} %get-tuple-element.69), channel_id=1, source_target_pairs={{0,8},{1,9},{2,10},{3,11},{4,12},{5,13},{6,14},{7,15},{8,0},{9,1},... | collective-permute-start | bytes 184328 | tf_op jit(solution)/shard_map/ppermute | solution.py:482
  76.7 3.8 %collective-permute-start.15 = (f32[8,320]{1,0:T(8,128)S(1)}, f32[8,320]{1,0:T(8,128)S(1)}, u32[]{:S(2)}, u32[]{:S(2)}) collective-permute-start(f32[8,320]{1,0:T(8,128)S(1)} %get-tuple-element.67.refs_1_), channel_id=1, source_target_pairs={{0,12},{1,13},{2,14},{3,15},{4,8},{5,9},{6,10},{7,11},{8,4},{9,5},... | collective-permute-start | bytes 30728 | tf_op jit(solution)/shard_map/ppermute | solution.py:482
  80.6 2.4 %collective-permute-done.15.refs_7_ = f32[8,320]{1,0:T(8,128)S(1)} collective-permute-done((f32[8,320]{1,0:T(8,128)S(1)}, f32[8,320]{1,0:T(8,128)S(1)}, u32[]{:S(2)}, u32[]{:S(2)}) %collective-permute-start.15) | collective-permute-done | bytes 10272 | tf_op jit(solution)/shard_map/ppermute | solution.py:482
  83.0 0.0 collective-permute-start.13
  83.0 2.2 %collective-permute-done.14.refs_6_ = f32[8,320]{1,0:T(8,128)S(1)} collective-permute-done((f32[8,320]{1,0:T(8,128)S(1)}, f32[8,320]{1,0:T(8,128)S(1)}, u32[]{:S(2)}, u32[]{:S(2)}) %collective-permute-start.14) | collective-permute-done | bytes 10272 | tf_op jit(solution)/shard_map/ppermute | solution.py:482
  85.2 1.5 %collective-permute-done.13.refs_5_ = f32[8,320]{1,0:T(8,128)S(1)} collective-permute-done((f32[8,320]{1,0:T(8,128)S(1)}, f32[8,320]{1,0:T(8,128)S(1)}, u32[]{:S(2)}, u32[]{:S(2)}) %collective-permute-start.13) | collective-permute-done | bytes 10272 | tf_op jit(solution)/shard_map/ppermute | solution.py:482
  86.6 0.0 collective-permute-done.11.refs_3_
  86.7 0.0 collective-permute-done.12.refs_4_
  86.7 3.2 %collective-permute-start.23 = (bf16[80,384]{1,0:T(8,128)(2,1)S(1)}, bf16[80,384]{1,0:T(8,128)(2,1)S(1)}, u32[]{:S(2)}, u32[]{:S(2)}) collective-permute-start(bf16[80,384]{1,0:T(8,128)(2,1)S(1)} %get-tuple-element.73.refs_0_), channel_id=1, source_target_pairs={{0,14},{1,15},{2,12},{3,13},{4,10},{5,11},{6,8},{7,9},{8,6},{9,7},... | collective-permute-start | bytes 184328 | tf_op jit(solution)/shard_map/ppermute | solution.py:482
  89.9 0.8 collective-permute-start.22
  90.6 0.6 collective-permute-start.16
  91.2 0.7 collective-permute-start.21
  91.9 3.1 %collective-permute-start.20 = (bf16[80,384]{1,0:T(8,128)(2,1)S(1)}, bf16[80,384]{1,0:T(8,128)(2,1)S(1)}, u32[]{:S(2)}, u32[]{:S(2)}) collective-permute-start(bf16[80,384]{1,0:T(8,128)(2,1)S(1)} %get-tuple-element.73.refs_0_), channel_id=1, source_target_pairs={{0,8},{1,9},{2,10},{3,11},{4,12},{5,13},{6,14},{7,15},{8,0},{9,1},... | collective-permute-start | bytes 184328 | tf_op jit(solution)/shard_map/ppermute | solution.py:482
  95.0 0.8 collective-permute-start.19
  95.8 1.4 %collective-permute-start.18 = (bf16[80,384]{1,0:T(8,128)(2,1)S(1)}, bf16[80,384]{1,0:T(8,128)(2,1)S(1)}, u32[]{:S(2)}, u32[]{:S(2)}) collective-permute-start(bf16[80,384]{1,0:T(8,128)(2,1)S(1)} %get-tuple-element.73.refs_0_), channel_id=1, source_target_pairs={{0,4},{1,5},{2,6},{3,7},{4,0},{5,1},{6,2},{7,3},{8,12},{9,13},{10,... | collective-permute-start | bytes 184328 | tf_op jit(solution)/shard_map/ppermute | solution.py:482
  97.2 0.0 collective-permute-done.22.refs_6_
  97.2 1.3 %collective-permute-start.17 = (bf16[80,384]{1,0:T(8,128)(2,1)S(1)}, bf16[80,384]{1,0:T(8,128)(2,1)S(1)}, u32[]{:S(2)}, u32[]{:S(2)}) collective-permute-start(bf16[80,384]{1,0:T(8,128)(2,1)S(1)} %get-tuple-element.73.refs_0_), channel_id=1, source_target_pairs={{0,2},{1,3},{2,0},{3,1},{4,6},{5,7},{6,4},{7,5},{8,10},{9,11},{10,... | collective-permute-start | bytes 184328 | tf_op jit(solution)/shard_map/ppermute | solution.py:482
  98.5 5.8 %shard_map.162 = (f32[1024,320]{1,0:T(8,128)}, f32[320]{0:T(512)}, f32[320]{0:T(512)}, f32[320]{0:T(512)}, f32[320,1280]{1,0:T(8,128)}, /*index=5*/f32[8,128]{1,0:T(8,128)}) custom-call(bf16[1024,320]{1,0:T(8,128)(2,1)} %bitcast.20, bf16[1024,320]{1,0:T(8,128)(2,1)} %bitcast.23, f32[1024,320]{1,0:T(8,128)} %get-tuple-element.55.refs_2_, f32[320]{0:T(512)} %refs_3_.3, ...), custom_call_target="tpu_custom_call" | custom-call | flops 2621440 | bytes 2000000 | tf_op jit(solution)/shard_map/pallas_call | solution.py:53
  104.3 0.0 collective-permute-done.20.refs_4_
  104.3 0.0 collective-permute-done.19.refs_3_
  104.4 0.0 collective-permute-done.17.refs_1_
  104.4 0.7 copy-done.3
  105.1 0.1 shard_map.163.refs_0_
  105.1 0.1 collective-permute-start.24
  105.2 1.9 %collective-permute-done.24.refs_1_ = bf16[80,3072]{1,0:T(8,128)(2,1)S(1)} collective-permute-done((bf16[80,3072]{1,0:T(8,128)(2,1)S(1)}, bf16[80,3072]{1,0:T(8,128)(2,1)S(1)}, u32[]{:S(2)}, u32[]{:S(2)}) %collective-permute-start.24) | collective-permute-done | bytes 491552 | tf_op jit(solution)/shard_map/ppermute | solution.py:482
  107.0 1.9 %shard_map.164 = f32[9,160,320]{2,1,0:T(8,128)} custom-call(bf16[80,3072]{1,0:T(8,128)(2,1)S(1)} %shard_map.163.refs_0_, bf16[80,3072]{1,0:T(8,128)(2,1)S(1)} %collective-permute-done.24.refs_1_), custom_call_target="tpu_custom_call" | custom-call | bytes 2000000 | tf_op jit(solution)/shard_map/pallas_call | solution.py:53
  (27 shorter events, 0.1 us)
Async XLA Ops:
  1.4 4.9 %collective-permute-start = (bf16[32,320]{1,0:T(8,128)(2,1)S(1)}, bf16[32,320]{1,0:T(8,128)(2,1)}, u32[]{:S(2)}, u32[]{:S(2)}) collective-permute-start(bf16[32,320]{1,0:T(8,128)(2,1)S(1)} %maximum_bitcast_fusion), channel_id=1, source_target_pairs={{0,16},{1,17},{2,18},{3,19},{4,20},{5,21},{6,22},{7,23},{8,24},{9,... | collective-permute-start | bytes 61448 | tf_op jit(solution)/shard_map/ppermute | solution.py:482
  10.2 12.1 %collective-permute-start.1 = (f32[4,66,1,320]{3,2,1,0:T(1,128)}, f32[4,66,1,320]{3,2,1,0:T(1,128)}, u32[]{:S(2)}, u32[]{:S(2)}) collective-permute-start(f32[4,66,1,320]{3,2,1,0:T(1,128)} %get-tuple-element.43), channel_id=1, source_target_pairs={{0,1},{1,2},{2,3},{3,4},{4,5},{5,6},{6,7},{7,8},{8,9},{9,10},{10,1... | collective-permute-start | bytes 1013768 | tf_op jit(solution)/shard_map/ppermute | solution.py:493
  12.2 10.0 %collective-permute-start.2 = (f32[4,66,1,320]{3,2,1,0:T(1,128)}, f32[4,66,1,320]{3,2,1,0:T(1,128)}, u32[]{:S(2)}, u32[]{:S(2)}) collective-permute-start(f32[4,66,1,320]{3,2,1,0:T(1,128)} %get-tuple-element.44), channel_id=1, source_target_pairs={{1,0},{2,1},{3,2},{4,3},{5,4},{6,5},{7,6},{8,7},{9,8},{10,9},{11,1... | collective-permute-start | bytes 1013768 | tf_op jit(solution)/shard_map/ppermute | solution.py:493
  13.5 17.6 %all-to-all-start = ((f32[32,1,128]{2,1,0:T(1,128)}), f32[32,1,128]{2,1,0:T(1,128)}, u32[]{:S(2)}, u32[]{:S(2)}) async-start(f32[32,1,128]{2,1,0:T(1,128)} %get-tuple-element.46), calls=%async_computation | async-start | bytes 32768 | tf_op jit(solution)/shard_map/all_to_all | solution.py:544
  31.1 10.6 %copy-start.9 = (s32[2]{0:T(128)S(1)}, s32[2]{0:T(128)}, u32[]{:S(2)}) copy-start(s32[2]{0:T(128)} %param.11) | copy-start | bytes 28
  40.2 4.7 %copy-start = (f32[2,8,80,384]{3,2,1,0:T(8,128)S(1)}, f32[2,8,80,384]{3,2,1,0:T(8,128)}, u32[]{:S(2)}) copy-start(f32[2,8,80,384]{3,2,1,0:T(8,128)} %get-tuple-element.50.refs_0_) | copy-start | bytes 5898244
  40.2 4.7 %collective-permute-start.3 = (bf16[2,8,80,384]{3,2,1,0:T(8,128)(2,1)}, bf16[2,8,80,384]{3,2,1,0:T(8,128)(2,1)S(1)}, u32[]{:S(2)}, u32[]{:S(2)}) collective-permute-start(bf16[2,8,80,384]{3,2,1,0:T(8,128)(2,1)} %bitcast.29), channel_id=1, source_target_pairs={{0,1},{1,0},{2,3},{3,2},{4,5},{5,4},{6,7},{7,6},{8,9},{9,8},{10,11... | collective-permute-start | bytes 2949128 | tf_op jit(solution)/shard_map/ppermute | solution.py:482
  44.9 10.6 %copy-start.7 = (bf16[2,1280]{1,0:T(2,128)(2,1)}, bf16[2,1280]{1,0:T(2,128)(2,1)S(1)}, u32[]{:S(2)}) copy-start(bf16[2,1280]{1,0:T(2,128)(2,1)S(1)} %fusion.1.refs_7_) | copy-start | bytes 15364
  44.9 5.0 %copy-start.6 = (bf16[1280,320]{0,1:T(8,128)(2,1)S(1)}, bf16[1280,320]{0,1:T(8,128)(2,1)}, u32[]{:S(2)}) copy-start(bf16[1280,320]{0,1:T(8,128)(2,1)} %param.18) | copy-start | bytes 2457604
  45.1 0.6 copy-start.5
  45.7 19.1 %collective-permute-start.4 = (bf16[2,2,80,384]{3,2,1,0:T(8,128)(2,1)S(1)}, bf16[2,2,80,384]{3,2,1,0:T(8,128)(2,1)S(1)}, u32[]{:S(2)}, u32[]{:S(2)}) collective-permute-start(bf16[2,2,80,384]{3,2,1,0:T(8,128)(2,1)S(1)} %get-tuple-element.56), channel_id=1, source_target_pairs={{0,16},{1,17},{2,18},{3,19},{4,20},{5,21},{6,22},{7,23},{8,24},{9,... | collective-permute-start | bytes 737288 | tf_op jit(solution)/shard_map/ppermute | solution.py:482
  47.4 17.4 %collective-permute-start.5 = (bf16[2,2,80,384]{3,2,1,0:T(8,128)(2,1)S(1)}, bf16[2,2,80,384]{3,2,1,0:T(8,128)(2,1)S(1)}, u32[]{:S(2)}, u32[]{:S(2)}) collective-permute-start(bf16[2,2,80,384]{3,2,1,0:T(8,128)(2,1)S(1)} %get-tuple-element.58), channel_id=1, source_target_pairs={{0,2},{1,3},{2,0},{3,1},{4,6},{5,7},{6,4},{7,5},{8,10},{9,11},{10,... | collective-permute-start | bytes 737288 | tf_op jit(solution)/shard_map/ppermute | solution.py:482
  55.5 9.3 %copy-start.2 = (f32[8,320]{1,0:T(8,128)S(1)}, f32[8,320]{1,0:T(8,128)}, u32[]{:S(2)}) copy-start(f32[8,320]{1,0:T(8,128)} %get-tuple-element.53.refs_9_.refs_4_) | copy-start | bytes 30724
  55.5 9.3 %collective-permute-start.6 = (f32[8,320]{1,0:T(8,128)}, f32[8,320]{1,0:T(8,128)S(1)}, u32[]{:S(2)}, u32[]{:S(2)}) collective-permute-start(f32[8,320]{1,0:T(8,128)} %get-tuple-element.53.refs_9_.refs_4_), channel_id=1, source_target_pairs={{0,1},{1,0},{2,3},{3,2},{4,5},{5,4},{6,7},{7,6},{8,9},{9,8},{10,11... | collective-permute-start | bytes 30728 | tf_op jit(solution)/shard_map/ppermute | solution.py:482
  64.8 0.7 copy-start.4
  65.6 6.0 %collective-permute-start.7 = (bf16[2,80,384]{2,1,0:T(8,128)(2,1)S(1)}, bf16[2,80,384]{2,1,0:T(8,128)(2,1)S(1)}, u32[]{:S(2)}, u32[]{:S(2)}) collective-permute-start(bf16[2,80,384]{2,1,0:T(8,128)(2,1)S(1)} %get-tuple-element.61), channel_id=1, source_target_pairs={{0,2},{1,3},{2,0},{3,1},{4,6},{5,7},{6,4},{7,5},{8,10},{9,11},{10,... | collective-permute-start | bytes 368648 | tf_op jit(solution)/shard_map/ppermute | solution.py:482
  65.7 6.0 %collective-permute-start.8 = (bf16[2,80,384]{2,1,0:T(8,128)(2,1)S(1)}, bf16[2,80,384]{2,1,0:T(8,128)(2,1)S(1)}, u32[]{:S(2)}, u32[]{:S(2)}) collective-permute-start(bf16[2,80,384]{2,1,0:T(8,128)(2,1)S(1)} %get-tuple-element.63), channel_id=1, source_target_pairs={{0,16},{1,17},{2,18},{3,19},{4,20},{5,21},{6,22},{7,23},{8,24},{9,... | collective-permute-start | bytes 368648 | tf_op jit(solution)/shard_map/ppermute | solution.py:482
  66.2 5.5 %collective-permute-start.9 = (f32[8,320]{1,0:T(8,128)S(1)}, f32[8,320]{1,0:T(8,128)S(1)}, u32[]{:S(2)}, u32[]{:S(2)}) collective-permute-start(f32[8,320]{1,0:T(8,128)S(1)} %get-tuple-element.65.refs_4_), channel_id=1, source_target_pairs={{0,2},{1,3},{2,0},{3,1},{4,6},{5,7},{6,4},{7,5},{8,10},{9,11},{10,... | collective-permute-start | bytes 30728 | tf_op jit(solution)/shard_map/ppermute | solution.py:482
  71.8 14.9 %collective-permute-start.10 = (bf16[80,384]{1,0:T(8,128)(2,1)S(1)}, bf16[80,384]{1,0:T(8,128)(2,1)S(1)}, u32[]{:S(2)}, u32[]{:S(2)}) collective-permute-start(bf16[80,384]{1,0:T(8,128)(2,1)S(1)} %get-tuple-element.68), channel_id=1, source_target_pairs={{0,4},{1,5},{2,6},{3,7},{4,0},{5,1},{6,2},{7,3},{8,12},{9,13},{10,... | collective-permute-start | bytes 184328 | tf_op jit(solution)/shard_map/ppermute | solution.py:482
  74.1 12.5 %collective-permute-start.11 = (bf16[80,384]{1,0:T(8,128)(2,1)S(1)}, bf16[80,384]{1,0:T(8,128)(2,1)S(1)}, u32[]{:S(2)}, u32[]{:S(2)}) collective-permute-start(bf16[80,384]{1,0:T(8,128)(2,1)S(1)} %get-tuple-element.69), channel_id=1, source_target_pairs={{0,8},{1,9},{2,10},{3,11},{4,12},{5,13},{6,14},{7,15},{8,0},{9,1},... | collective-permute-start | bytes 184328 | tf_op jit(solution)/shard_map/ppermute | solution.py:482
  76.7 9.9 %collective-permute-start.12 = (bf16[80,384]{1,0:T(8,128)(2,1)S(1)}, bf16[80,384]{1,0:T(8,128)(2,1)S(1)}, u32[]{:S(2)}, u32[]{:S(2)}) collective-permute-start(bf16[80,384]{1,0:T(8,128)(2,1)S(1)} %get-tuple-element.70), channel_id=1, source_target_pairs={{0,12},{1,13},{2,14},{3,15},{4,8},{5,9},{6,10},{7,11},{8,4},{9,5},... | collective-permute-start | bytes 184328 | tf_op jit(solution)/shard_map/ppermute | solution.py:482
  76.7 6.2 %collective-permute-start.15 = (f32[8,320]{1,0:T(8,128)S(1)}, f32[8,320]{1,0:T(8,128)S(1)}, u32[]{:S(2)}, u32[]{:S(2)}) collective-permute-start(f32[8,320]{1,0:T(8,128)S(1)} %get-tuple-element.67.refs_1_), channel_id=1, source_target_pairs={{0,12},{1,13},{2,14},{3,15},{4,8},{5,9},{6,10},{7,11},{8,4},{9,5},... | collective-permute-start | bytes 30728 | tf_op jit(solution)/shard_map/ppermute | solution.py:482
  80.6 4.6 %collective-permute-start.14 = (f32[8,320]{1,0:T(8,128)S(1)}, f32[8,320]{1,0:T(8,128)S(1)}, u32[]{:S(2)}, u32[]{:S(2)}) collective-permute-start(f32[8,320]{1,0:T(8,128)S(1)} %get-tuple-element.67.refs_1_), channel_id=1, source_target_pairs={{0,8},{1,9},{2,10},{3,11},{4,12},{5,13},{6,14},{7,15},{8,0},{9,1},... | collective-permute-start | bytes 30728 | tf_op jit(solution)/shard_map/ppermute | solution.py:482
  83.0 3.7 %collective-permute-start.13 = (f32[8,320]{1,0:T(8,128)S(1)}, f32[8,320]{1,0:T(8,128)S(1)}, u32[]{:S(2)}, u32[]{:S(2)}) collective-permute-start(f32[8,320]{1,0:T(8,128)S(1)} %get-tuple-element.67.refs_1_), channel_id=1, source_target_pairs={{0,4},{1,5},{2,6},{3,7},{4,0},{5,1},{6,2},{7,3},{8,12},{9,13},{10,... | collective-permute-start | bytes 30728 | tf_op jit(solution)/shard_map/ppermute | solution.py:482
  86.7 11.8 %copy-start.1 = (f32[8,320]{1,0:T(8,128)}, f32[8,320]{1,0:T(8,128)S(1)}, u32[]{:S(2)}) copy-start(f32[8,320]{1,0:T(8,128)S(1)} %get-tuple-element.71.refs_5_) | copy-start | bytes 30724
  86.7 9.1 %collective-permute-start.23 = (bf16[80,384]{1,0:T(8,128)(2,1)S(1)}, bf16[80,384]{1,0:T(8,128)(2,1)S(1)}, u32[]{:S(2)}, u32[]{:S(2)}) collective-permute-start(bf16[80,384]{1,0:T(8,128)(2,1)S(1)} %get-tuple-element.73.refs_0_), channel_id=1, source_target_pairs={{0,14},{1,15},{2,12},{3,13},{4,10},{5,11},{6,8},{7,9},{8,6},{9,7},... | collective-permute-start | bytes 184328 | tf_op jit(solution)/shard_map/ppermute | solution.py:482
  89.9 7.4 %collective-permute-start.22 = (bf16[80,384]{1,0:T(8,128)(2,1)S(1)}, bf16[80,384]{1,0:T(8,128)(2,1)S(1)}, u32[]{:S(2)}, u32[]{:S(2)}) collective-permute-start(bf16[80,384]{1,0:T(8,128)(2,1)S(1)} %get-tuple-element.73.refs_0_), channel_id=1, source_target_pairs={{0,12},{1,13},{2,14},{3,15},{4,8},{5,9},{6,10},{7,11},{8,4},{9,5},... | collective-permute-start | bytes 184328 | tf_op jit(solution)/shard_map/ppermute | solution.py:482
  90.6 4.4 %collective-permute-start.16 = (f32[8,320]{1,0:T(8,128)S(1)}, f32[8,320]{1,0:T(8,128)S(1)}, u32[]{:S(2)}, u32[]{:S(2)}) collective-permute-start(f32[8,320]{1,0:T(8,128)S(1)} %get-tuple-element.71.refs_5_), channel_id=1, source_target_pairs={{0,16},{1,17},{2,18},{3,19},{4,20},{5,21},{6,22},{7,23},{8,24},{9,... | collective-permute-start | bytes 30728 | tf_op jit(solution)/shard_map/ppermute | solution.py:482
  91.2 13.1 %collective-permute-start.21 = (bf16[80,384]{1,0:T(8,128)(2,1)S(1)}, bf16[80,384]{1,0:T(8,128)(2,1)S(1)}, u32[]{:S(2)}, u32[]{:S(2)}) collective-permute-start(bf16[80,384]{1,0:T(8,128)(2,1)S(1)} %get-tuple-element.73.refs_0_), channel_id=1, source_target_pairs={{0,10},{1,11},{2,8},{3,9},{4,14},{5,15},{6,12},{7,13},{8,2},{9,3},... | collective-permute-start | bytes 184328 | tf_op jit(solution)/shard_map/ppermute | solution.py:482
  91.9 12.4 %collective-permute-start.20 = (bf16[80,384]{1,0:T(8,128)(2,1)S(1)}, bf16[80,384]{1,0:T(8,128)(2,1)S(1)}, u32[]{:S(2)}, u32[]{:S(2)}) collective-permute-start(bf16[80,384]{1,0:T(8,128)(2,1)S(1)} %get-tuple-element.73.refs_0_), channel_id=1, source_target_pairs={{0,8},{1,9},{2,10},{3,11},{4,12},{5,13},{6,14},{7,15},{8,0},{9,1},... | collective-permute-start | bytes 184328 | tf_op jit(solution)/shard_map/ppermute | solution.py:482
  95.0 3.5 %copy-start.8 = (f32[8,320]{1,0:T(8,128)}, f32[8,320]{1,0:T(8,128)S(1)}, u32[]{:S(2)}) copy-start(f32[8,320]{1,0:T(8,128)S(1)} %collective-permute-done.16.refs_6_) | copy-start | bytes 30724
  95.0 9.3 %collective-permute-start.19 = (bf16[80,384]{1,0:T(8,128)(2,1)S(1)}, bf16[80,384]{1,0:T(8,128)(2,1)S(1)}, u32[]{:S(2)}, u32[]{:S(2)}) collective-permute-start(bf16[80,384]{1,0:T(8,128)(2,1)S(1)} %get-tuple-element.73.refs_0_), channel_id=1, source_target_pairs={{0,6},{1,7},{2,4},{3,5},{4,2},{5,3},{6,0},{7,1},{8,14},{9,15},{10,... | collective-permute-start | bytes 184328 | tf_op jit(solution)/shard_map/ppermute | solution.py:482
  95.8 8.5 %collective-permute-start.18 = (bf16[80,384]{1,0:T(8,128)(2,1)S(1)}, bf16[80,384]{1,0:T(8,128)(2,1)S(1)}, u32[]{:S(2)}, u32[]{:S(2)}) collective-permute-start(bf16[80,384]{1,0:T(8,128)(2,1)S(1)} %get-tuple-element.73.refs_0_), channel_id=1, source_target_pairs={{0,4},{1,5},{2,6},{3,7},{4,0},{5,1},{6,2},{7,3},{8,12},{9,13},{10,... | collective-permute-start | bytes 184328 | tf_op jit(solution)/shard_map/ppermute | solution.py:482
  97.2 7.1 %collective-permute-start.17 = (bf16[80,384]{1,0:T(8,128)(2,1)S(1)}, bf16[80,384]{1,0:T(8,128)(2,1)S(1)}, u32[]{:S(2)}, u32[]{:S(2)}) collective-permute-start(bf16[80,384]{1,0:T(8,128)(2,1)S(1)} %get-tuple-element.73.refs_0_), channel_id=1, source_target_pairs={{0,2},{1,3},{2,0},{3,1},{4,6},{5,7},{6,4},{7,5},{8,10},{9,11},{10,... | collective-permute-start | bytes 184328 | tf_op jit(solution)/shard_map/ppermute | solution.py:482
  104.4 0.7 copy-start.3
  105.1 1.9 %collective-permute-start.24 = (bf16[80,3072]{1,0:T(8,128)(2,1)S(1)}, bf16[80,3072]{1,0:T(8,128)(2,1)S(1)}, u32[]{:S(2)}, u32[]{:S(2)}) collective-permute-start(bf16[80,3072]{1,0:T(8,128)(2,1)S(1)} %shard_map.163.refs_0_), channel_id=1, source_target_pairs={{0,1},{1,0},{2,3},{3,2},{4,5},{5,4},{6,7},{7,6},{8,9},{9,8},{10,11... | collective-permute-start | bytes 1474568 | tf_op jit(solution)/shard_map/ppermute | solution.py:482

commit v6 on v5

--- a/solution.py
+++ b/solution.py
@@ -63,6 +63,69 @@
     )(*far, *operands, *after)
 
 
+def call_far(body, out_shape, operands, far=(), after=(), scratch=(), vmem=58, flops=0):
+    outs, tree = jax.tree.flatten(out_shape)
+    ins = (*far, *operands)
+    waits, own = len(after), len(scratch)
+    slots = len(outs) + 4
+
+    def kernel(*refs):
+        src, refs = refs[: len(ins)], refs[len(ins) + waits :]
+        dst, refs = refs[: len(outs)], refs[len(outs) :]
+        mine, refs = refs[:own], refs[own:]
+        held, refs = refs[: len(ins)], refs[len(ins) :]
+        made, (sem_in, sem_out) = refs[: len(outs)], refs[len(outs) :]
+        copies = [pltpu.make_async_copy(a, b, sem_in.at[i]) for i, (a, b) in enumerate(zip(src, held))]
+        for c in (*copies[len(far) :], *copies[: len(far)]):
+            c.start()
+
+        def loader(i):
+            def load():
+                copies[i].wait()
+                return held[i]
+
+            return load
+
+        sent = {}
+
+        def emit(i, start=None, size=None):
+            a, b = made[i], dst[i]
+            if start is not None:
+                a, b = a.at[pl.ds(start, size)], b.at[pl.ds(start, size)]
+            c = pltpu.make_async_copy(a, b, sem_out.at[sum(map(len, sent.values()))])
+            c.start()
+            sent.setdefault(i, []).append(c)
+
+        for c in copies[len(far) :]:
+            c.wait()
+        body(emit, *[loader(i) for i in range(len(far))], *held[len(far) :], *made, *mine)
+        for i in range(len(outs)):
+            if i not in sent:
+                emit(i)
+        for parts in sent.values():
+            for c in parts:
+                c.wait()
+
+    hbm = pl.BlockSpec(memory_space=pltpu.HBM)
+    near = pl.BlockSpec(memory_space=pltpu.VMEM)
+    results = pl.pallas_call(
+        kernel,
+        out_shape=tuple(outs),
+        in_specs=[hbm] * len(ins) + [near] * waits,
+        out_specs=(hbm,) * len(outs),
+        scratch_shapes=[
+            *scratch,
+            *[pltpu.VMEM(v.shape, v.dtype) for v in ins],
+            *[pltpu.VMEM(v.shape, v.dtype) for v in outs],
+            pltpu.SemaphoreType.DMA((len(ins),)),
+            pltpu.SemaphoreType.DMA((slots,)),
+        ],
+        compiler_params=pltpu.CompilerParams(vmem_limit_bytes=vmem * 2**20),
+        cost_estimate=pl.CostEstimate(flops=flops, bytes_accessed=2_000_000, transcendentals=0),
+    )(*ins, *after)
+    return jax.tree.unflatten(tree, results)
+
+
 def group_matrix(channels, lanes):
     size = channels // NORM_GROUPS
     group = iota((channels, lanes), 1) & (NORM_GROUPS - 1)
@@ -89,7 +152,7 @@
     return out
 
 
-def stats_kernel(batch, w, x_load, g_load, top_ref, low_ref, pay_ref, west_ref, east_ref):
+def stats_kernel(batch, w, emit, x_load, g_load, top_ref, low_ref, pay_ref, west_ref, east_ref):
     sums = []
     step = 64
     t = step // w
@@ -228,7 +291,7 @@
     return ap[kw, b, kh : kh + tall - 2].reshape((tall - 2) * w, c).astype(BF16)
 
 
-def dacts_kernel(batch, relative, share, *refs):
+def dacts_kernel(batch, relative, share, emit, *refs):
     g_load, w_load = refs[:2]
     halo = refs[2:6]
     da_ref, gsum_ref, gp_ref, ap, gt = refs[6:]
@@ -241,18 +304,6 @@
     )
     totals = [jnp.sum(v, axis=0, keepdims=True) for v in totals]
     gsum_ref[...] = stack_rows([jnp.zeros((1, c), F32)] * (2 * batch) + totals, c)
-    w_ref = w_load()
-    for b in range(batch):
-        acc = jnp.zeros((per, c), F32)
-        for kh in range(3):
-            for kw in range(3):
-                acc = acc + lax.dot_general(
-                    tap_rows(ap, b, 2 - kh, 2 - kw),
-                    w_ref[kh * 3 + kw],
-                    (((1,), (1,)), ((), ())),
-                    preferred_element_type=F32,
-                )
-        da_ref[b * per : (b + 1) * per, :] = acc
     wide = gt.shape[0]
     step = LANES
     for i in range(n // step):
@@ -266,15 +317,31 @@
             gp_ref[q * share : (q + 1) * share, :] = gt[pl.ds(pl.multiple_of(other, 16), share), :]
     else:
         gp_ref[...] = gt[:c, :]
-
-
-def wgrad_kernel(batch, count, scale, *refs):
+    emit(1)
+    emit(2)
+    w_ref = w_load()
+    for b in range(batch):
+        acc = jnp.zeros((per, c), F32)
+        for kh in range(3):
+            for kw in range(3):
+                acc = acc + lax.dot_general(
+                    tap_rows(ap, b, 2 - kh, 2 - kw),
+                    w_ref[kh * 3 + kw],
+                    (((1,), (1,)), ((), ())),
+                    preferred_element_type=F32,
+                )
+        da_ref[b * per : (b + 1) * per, :] = acc
+        emit(0, b * per, per)
+
+
+def wgrad_kernel(batch, count, scale, emit, *refs):
     x_load, gp_load, gain_load, bias_load, st_ref = refs[:5]
     halo = refs[5:9]
     aff_ref, keep_ref, send_ref = refs[9:12]
     ap, part = refs[12:]
     aff = affine_rows(st_ref, gain_load(), bias_load(), batch, count)
     aff_ref[...] = aff
+    emit(0)
     x_ref = x_load()
     n, channels = x_ref.shape
     _, rows, pieces, share, width = send_ref.shape
@@ -296,12 +363,17 @@
     for r in range(rows):
         for p in range(pieces):
             lane = slice(p * width, (p + 1) * width)
-            keep_ref[r, p] = part[r * share : (r + 1) * share, lane]
             low = (rows + r) * share
             send_ref[0, r, p] = part[low : low + share, lane].astype(BF16)
-
-
-def back_kernel(batch, *refs):
+    emit(2)
+    for r in range(rows):
+        for p in range(pieces):
+            lane = slice(p * width, (p + 1) * width)
+            keep_ref[r, p] = part[r * share : (r + 1) * share, lane]
+        emit(1, r, 1)
+
+
+def back_kernel(batch, emit, *refs):
     x_load, da_load, aff_ref, gsum_ref, dn_ref, sums_ref = refs
     n, c = dn_ref.shape
     per = n // batch
@@ -326,6 +398,7 @@
 
         zero = jnp.zeros((8, c), F32)
         rows.append(lax.fori_loop(0, per // 64, body, (zero, zero)))
+        emit(0, b * per, per)
     sums_ref[...] = gsum_ref[...] + stack_rows(
         [jnp.sum(v[0], axis=0, keepdims=True) for v in rows]
         + [jnp.sum(v[1], axis=0, keepdims=True) for v in rows],
@@ -333,7 +406,7 @@
     )
 
 
-def conv_kernel(batch, *refs):
+def conv_kernel(batch, emit, *refs):
     x_load, w_load, cb_load, aff_ref = refs[:4]
     halo = refs[4:8]
     temb_ref, out_ref, done_ref, ap = refs[8:]
@@ -354,9 +427,10 @@
         here = slice(b * per, (b + 1) * per)
         out = x_ref[here, :].astype(F32) + acc + bias + temb_ref[b : b + 1, :]
         out_ref[here, :] = out.astype(BF16)
-
-
-def input_kernel(batch, count, scale, *refs):
+        emit(0, b * per, per)
+
+
+def input_kernel(batch, count, scale, emit, *refs):
     x_load, g_load, dn_load, gain_load, aff_ref, part_ref, other_ref, emb_ref = refs[:8]
     out_ref, gain_out, bias_out, cb_out, tw_out, done_ref = refs[8:]
     done_ref[...] = jnp.zeros_like(done_ref)
@@ -381,6 +455,7 @@
         lax.dot_general(p, emb, (((0,), (0,)), ((), ())), preferred_element_type=F32)
         for p in reversed(parts)
     )
+    emit(4)
     x_ref, g_ref, dn_ref = x_load(), g_load(), dn_load()
     for b in range(batch):
         a, r, o = (aff[k * batch + b : k * batch + b + 1] for k in (0, 2, 3))
@@ -394,6 +469,7 @@
             return 0
 
         lax.fori_loop(0, per // 64, body, 0)
+        emit(0, b * per, per)
 
 
 def place():
@@ -533,7 +609,7 @@
         low = top
     else:
         top, low = shift(edge(high - 1), 1, 0), shift(edge(0), -1, 0)
-    pay, west, east = call(
+    pay, west, east = call_far(
         functools.partial(stats_kernel, batch, wide),
         (of((devices, 1, lanes), F32), column, column),
         (top, low),
@@ -555,7 +631,7 @@
     if not relative:
         share = channels // 2
     keep_rows = rows if relative else 1
-    dacts, gsum, flipped = call(
+    dacts, gsum, flipped = call_far(
         functools.partial(dacts_kernel, batch, relative, share),
         (of((n, channels), F32), of((8, channels), F32), of((channels, n), BF16)),
         halo,
@@ -564,7 +640,7 @@
         scratch=(shifted, pltpu.VMEM((padded, n), BF16)),
         flops=conv_flops,
     )
-    aff, keep, send = call(
+    aff, keep, send = call_far(
         functools.partial(wgrad_kernel, batch, count, scale),
         (
             of((8, channels), F32),
@@ -593,7 +669,7 @@
     else:
         first = ()
 
-    dn, sums = call(
+    dn, sums = call_far(
         functools.partial(back_kernel, batch),
         (of((n, channels), F32), of((8, channels), F32)),
         (aff, gsum),
@@ -605,24 +681,12 @@
     emb = embed(timestep, embed_in, embed_out)
     temb = jnp.dot(emb, time_w, preferred_element_type=F32)
 
-    block_out, done = call(
-        functools.partial(conv_kernel, batch),
-        (of((n, channels), BF16), token),
-        (aff, *halo, temb),
-        far=(x2, w9, conv_b),
-        after=(sums,),
-        vmem=58,
-        scratch=(shifted,),
-        flops=conv_flops,
-    )
-
     if relative:
         s_shape = of(sums.shape, F32)
         a_send, a_keep, b_send, b_keep, sums = call(
             functools.partial(step_two, nz),
             (many((half,), BF16), many((half,), F32)) * 2 + (s_shape,),
             (a_got, a_keep, b_got, b_keep, sums, partner(sums, 1)),
-            after=(done,),
         )
         a_got, b_got = partner(a_send, 2), partner(b_send, cols)
         own, sums, *sends = call(
@@ -633,12 +697,28 @@
         )
         gots = [partner(v, 4 * (k + 1)) for k, v in enumerate(sends)]
         gots += [partner(sums, 4 * k) for k in range(1, nz)]
+        second = (sums,)
+    else:
+        second = ()
+
+
+    block_out, done = call_far(
+        functools.partial(conv_kernel, batch),
+        (of((n, channels), BF16), token),
+        (aff, *halo, temb),
+        far=(x2, w9, conv_b),
+        after=second,
+        vmem=58,
+        scratch=(shifted,),
+        flops=conv_flops,
+    )
 
     if relative:
         own, sums = call(
             functools.partial(step_four, nz),
             (many((), BF16), s_shape),
             (own, sums, *gots),
+            after=(done,),
         )
         others = [partner(own, 2 * k) for k in range(1, pieces)]
     else:
@@ -648,7 +728,7 @@
             bit *= 2
 
     vector = of((channels,), F32)
-    input_grad, gain_grad, bias_grad, conv_b_grad, time_grad, done = call(
+    input_grad, gain_grad, bias_grad, conv_b_grad, time_grad, done = call_far(
         functools.partial(input_kernel, batch, count, scale),
         (of((n, channels), F32), *[vector] * 3, of((channels, emb.shape[1]), F32), token),
         (aff, sums, partner(sums, cols if relative else bit), emb),

time: 110 us -> 106 us (0.964)
  waiting for transfers between devices: 13.5 us -> 9.42 us
  Pallas kernels: 43.8 us -> 39.9 us
  local copies, waits for them, and re-layouts: 2.71 us -> 5.67 us
    pallas_call x12 -> x6, Pallas kernels: 43.8 us -> 2.34 us  [call(): pl.pallas_call(kernel, out_shape=out_shape, in_specs=[pl.BlockSpec(memory...]
    pallas_call x0 -> x6, Pallas kernels: none -> 37.5 us  [call_far(): pl.pallas_call(kernel, out_shape=tuple(outs), in_specs=[hbm] * len(ins) +...]
    ppermute x23, waiting for transfers between devices: 13.5 us -> 9.42 us  [partner(): return lax.ppermute(value, AXES, [(i, i ^ bit) for i in range(size)])]
    unnamed x20 -> x26, local copies, waits for them, and re-layouts: 1.97 us -> 4.94 us
  transfers between devices with their start and end apart: 26 -> 26, of which waited for: 6 -> 7; matrix products, arithmetic and copies ran while one was open for 4% -> 4% of each run, Pallas kernels for 26% -> 25%
where the time goes in v6:
time: 106 us; the launch traced here: 105 us
  starting transfers between devices  44.8 us (42%)
  Pallas kernels  39.9 us (38%)
  waiting for transfers between devices  9.42 us (9%)
  local copies, waits for them, and re-layouts  5.67 us (5%)
  matrix products  3.74 us (4%)
    pallas_call x6, Pallas kernels, call_far(): pl.pallas_call(kernel, out_shape=tuple(outs), in_specs=[hbm] * len(ins) +...  37.5 us
    ppermute x23, starting transfers between devices, partner(): return lax.ppermute(value, AXES, [(i, i ^ bit) for i in range(size)])  32.7 us
    ppermute x23, waiting for transfers between devices, partner(): return lax.ppermute(value, AXES, [(i, i ^ bit) for i in range(size)])  9.42 us
    all_to_all x1, starting transfers between devices, local(): stats = lax.all_to_all(pay, AXES, 0, 0)  8.72 us
    unnamed x26, local copies, waits for them, and re-layouts  4.94 us
    ppermute x2, starting transfers between devices, shift(): return lax.ppermute(value, AXES, pairs)  3.34 us
    dot_general x1, matrix products, embed(): jnp.dot(first_hidden, embed_out, preferred_element_type=F32)  2.81 us
    pallas_call x6, Pallas kernels, call(): pl.pallas_call(kernel, out_shape=out_shape, in_specs=[pl.BlockSpec(memory...  2.34 us
  transfers between devices with their start and end apart: 26, of which 7 were waited for; matrix products, arithmetic and copies ran while one was open for 4% of the time, Pallas kernels for 25%

profile of v6, /device:TPU:0, one launch (start us, length us, event | category | flops | bytes accessed | tf_op | source)
XLA Modules:
  0.0 104.6 jit_solution(4564706011642489582)
XLA Ops:
  0.6 0.7 constant_dynamic-slice_fusion
  1.4 3.0 %collective-permute-start = (bf16[32,320]{1,0:T(8,128)(2,1)S(1)}, bf16[32,320]{1,0:T(8,128)(2,1)}, u32[]{:S(2)}, u32[]{:S(2)}) collective-permute-start(bf16[32,320]{1,0:T(8,128)(2,1)S(1)} %maximum_bitcast_fusion), channel_id=1, source_target_pairs={{0,16},{1,17},{2,18},{3,19},{4,20},{5,21},{6,22},{7,23},{8,24},{9,... | collective-permute-start | bytes 61448 | tf_op jit(solution)/shard_map/ppermute | solution.py:558
  4.4 1.9 %collective-permute-done.refs_2_.refs_3_.refs_4_.refs_5_.refs_7_.refs_8_.refs_6_ = bf16[32,320]{1,0:T(8,128)(2,1)} collective-permute-done((bf16[32,320]{1,0:T(8,128)(2,1)S(1)}, bf16[32,320]{1,0:T(8,128)(2,1)}, u32[]{:S(2)}, u32[]{:S(2)}) %collective-permute-start) | collective-permute-done | bytes 20512 | tf_op jit(solution)/shard_map/ppermute | solution.py:558
  6.3 3.3 %shard_map.153 = (f32[32,1,128]{2,1,0:T(1,128)}, f32[4,66,1,320]{3,2,1,0:T(1,128)}, f32[4,66,1,320]{3,2,1,0:T(1,128)}) custom-call(bf16[1024,320]{1,0:T(8,128)(2,1)} %bitcast.16, bf16[1024,320]{1,0:T(8,128)(2,1)} %bitcast.21, bf16[32,320]{1,0:T(8,128)(2,1)} %collective-permute-done.refs_2_.refs_3_.refs_4_.refs_5_.refs_7_.refs_8_.refs_6_, ...), custom_call_target="tpu_custom_call" | custom-call | bytes 2000000 | tf_op jit(solution)/shard_map/pallas_call | solution.py:111
  9.6 2.1 %collective-permute-start.1 = (f32[4,66,1,320]{3,2,1,0:T(1,128)}, f32[4,66,1,320]{3,2,1,0:T(1,128)}, u32[]{:S(2)}, u32[]{:S(2)}) collective-permute-start(f32[4,66,1,320]{3,2,1,0:T(1,128)} %get-tuple-element.43), channel_id=1, source_target_pairs={{0,1},{1,2},{2,3},{3,4},{4,5},{5,6},{6,7},{7,8},{8,9},{9,10},{10,1... | collective-permute-start | bytes 1013768 | tf_op jit(solution)/shard_map/ppermute | solution.py:569
  11.7 1.3 %collective-permute-start.2 = (f32[4,66,1,320]{3,2,1,0:T(1,128)}, f32[4,66,1,320]{3,2,1,0:T(1,128)}, u32[]{:S(2)}, u32[]{:S(2)}) collective-permute-start(f32[4,66,1,320]{3,2,1,0:T(1,128)} %get-tuple-element.44), channel_id=1, source_target_pairs={{1,0},{2,1},{3,2},{4,3},{5,4},{6,5},{7,6},{8,7},{9,8},{10,9},{11,1... | collective-permute-start | bytes 1013768 | tf_op jit(solution)/shard_map/ppermute | solution.py:569
  13.0 8.7 %all-to-all-start = ((f32[32,1,128]{2,1,0:T(1,128)}), f32[32,1,128]{2,1,0:T(1,128)}, u32[]{:S(2)}, u32[]{:S(2)}) async-start(f32[32,1,128]{2,1,0:T(1,128)} %get-tuple-element.46), calls=%async_computation | async-start | bytes 32768 | tf_op jit(solution)/shard_map/all_to_all | solution.py:620
  21.7 0.0 collective-permute-done.1.refs_2_.refs_5_.refs_4_
  21.7 7.8 %shard_map.154 = (f32[1024,320]{1,0:T(8,128)}, f32[8,320]{1,0:T(8,128)}, bf16[320,1024]{1,0:T(8,128)(2,1)}) custom-call(bf16[1024,320]{1,0:T(8,128)(2,1)} %bitcast.22, bf16[9,320,320]{2,1,0:T(8,128)(2,1)} %bitcast.25, f32[4,66,1,320]{3,2,1,0:T(1,128)} %collective-permute-done.1.refs_2_.refs_5_.refs_4_, ...), custom_call_target="tpu_custom_call" | custom-call | flops 1887436800 | bytes 2000000 | tf_op jit(solution)/shard_map/pallas_call | solution.py:111
  29.5 8.3 %shard_map.155 = (f32[8,320]{1,0:T(8,128)}, f32[2,8,80,384]{3,2,1,0:T(8,128)}, bf16[1,2,8,80,384]{4,3,2,1,0:T(8,128)(2,1)}) custom-call(bf16[1024,320]{1,0:T(8,128)(2,1)} %bitcast.17, bf16[320,1024]{1,0:T(8,128)(2,1)} %get-tuple-element.45.refs_1_, f32[320]{0:T(512)} %refs_3_.3, f32[320]{0:T(512)} %refs_3_.2, f32[32,1,128]{2,1,0:T(1,128)} %all-to-all-done.refs_4_, ...), custom_call_target="tpu_custom_call" | custom-call | flops 1887436800 | bytes 2000000 | tf_op jit(solution)/shard_map/pallas_call | solution.py:111
  37.9 0.0 copy-start.12
  37.9 1.5 %collective-permute-start.3 = (bf16[2,8,80,384]{3,2,1,0:T(8,128)(2,1)}, bf16[2,8,80,384]{3,2,1,0:T(8,128)(2,1)S(1)}, u32[]{:S(2)}, u32[]{:S(2)}) collective-permute-start(bf16[2,8,80,384]{3,2,1,0:T(8,128)(2,1)} %bitcast.29), channel_id=1, source_target_pairs={{0,1},{1,0},{2,3},{3,2},{4,5},{5,4},{6,7},{7,6},{8,9},{9,8},{10,11... | collective-permute-start | bytes 2949128 | tf_op jit(solution)/shard_map/ppermute | solution.py:558
  39.4 2.4 %collective-permute-done.3.refs_1_ = bf16[2,8,80,384]{3,2,1,0:T(8,128)(2,1)S(1)} collective-permute-done((bf16[2,8,80,384]{3,2,1,0:T(8,128)(2,1)}, bf16[2,8,80,384]{3,2,1,0:T(8,128)(2,1)S(1)}, u32[]{:S(2)}, u32[]{:S(2)}) %collective-permute-start.3) | collective-permute-done | bytes 983072 | tf_op jit(solution)/shard_map/ppermute | solution.py:558
  41.8 1.5 %copy-done = f32[2,8,80,384]{3,2,1,0:T(8,128)S(1)} copy-done((f32[2,8,80,384]{3,2,1,0:T(8,128)S(1)}, f32[2,8,80,384]{3,2,1,0:T(8,128)}, u32[]{:S(2)}) %copy-start) | copy-done | bytes 1966104
  43.4 0.2 shard_map.156
  43.5 0.0 copy-start.7
  43.5 0.6 copy-done.7
  44.1 1.6 %collective-permute-start.4 = (bf16[2,2,80,384]{3,2,1,0:T(8,128)(2,1)S(1)}, bf16[2,2,80,384]{3,2,1,0:T(8,128)(2,1)S(1)}, u32[]{:S(2)}, u32[]{:S(2)}) collective-permute-start(bf16[2,2,80,384]{3,2,1,0:T(8,128)(2,1)S(1)} %get-tuple-element.50), channel_id=1, source_target_pairs={{0,16},{1,17},{2,18},{3,19},{4,20},{5,21},{6,22},{7,23},{8,24},{9,... | collective-permute-start | bytes 737288 | tf_op jit(solution)/shard_map/ppermute | solution.py:558
  45.8 2.6 %collective-permute-start.5 = (bf16[2,2,80,384]{3,2,1,0:T(8,128)(2,1)S(1)}, bf16[2,2,80,384]{3,2,1,0:T(8,128)(2,1)S(1)}, u32[]{:S(2)}, u32[]{:S(2)}) collective-permute-start(bf16[2,2,80,384]{3,2,1,0:T(8,128)(2,1)S(1)} %get-tuple-element.52), channel_id=1, source_target_pairs={{0,2},{1,3},{2,0},{3,1},{4,6},{5,7},{6,4},{7,5},{8,10},{9,11},{10,... | collective-permute-start | bytes 737288 | tf_op jit(solution)/shard_map/ppermute | solution.py:558
  48.4 4.5 %shard_map.157 = (f32[1024,320]{1,0:T(8,128)}, f32[8,320]{1,0:T(8,128)}) custom-call(bf16[1024,320]{1,0:T(8,128)(2,1)} %bitcast.18, f32[1024,320]{1,0:T(8,128)} %get-tuple-element.54.refs_1_, f32[8,320]{1,0:T(8,128)} %get-tuple-element.47.refs_2_.refs_3_.refs_4_, f32[8,320]{1,0:T(8,128)} %get-tuple-element.55.refs_3_, f32[8,128]{1,0:T(8,128)} %copy-done.7), custom_call_target="tpu_custom_call" | custom-call | flops 6553600 | bytes 2000000 | tf_op jit(solution)/shard_map/pallas_call | solution.py:111
  52.9 0.1 collective-permute-start.6
  53.0 0.1 fusion.7
  53.1 1.3 %collective-permute-done.6.refs_5_ = f32[8,320]{1,0:T(8,128)S(1)} collective-permute-done((f32[8,320]{1,0:T(8,128)}, f32[8,320]{1,0:T(8,128)S(1)}, u32[]{:S(2)}, u32[]{:S(2)}) %collective-permute-start.6) | collective-permute-done | bytes 10272 | tf_op jit(solution)/shard_map/ppermute | solution.py:558
  54.4 0.2 collective-permute-done.5.refs_2_
  54.6 0.7 copy-done.2
  55.3 0.1 shard_map.158
  55.4 1.8 %collective-permute-start.9 = (f32[8,320]{1,0:T(8,128)S(1)}, f32[8,320]{1,0:T(8,128)S(1)}, u32[]{:S(2)}, u32[]{:S(2)}) collective-permute-start(f32[8,320]{1,0:T(8,128)S(1)} %get-tuple-element.62.refs_4_), channel_id=1, source_target_pairs={{0,2},{1,3},{2,0},{3,1},{4,6},{5,7},{6,4},{7,5},{8,10},{9,11},{10,... | collective-permute-start | bytes 30728 | tf_op jit(solution)/shard_map/ppermute | solution.py:558
  57.2 0.3 collective-permute-start.7
  57.5 0.3 collective-permute-start.8
  57.8 2.8 %fusion.1.refs_7_ = bf16[2,1280]{1,0:T(2,128)(2,1)S(1)} fusion(bf16[1280,1280]{1,0:T(8,128)(2,1)} %param.17, bf16[320,1280]{1,0:T(8,128)(2,1)S(1)} %copy-done.8, bf16[2,160]{1,0:T(2,128)(2,1)S(1)} %get-tuple-element.80, bf16[2,160]{1,0:T(2,128)(2,1)S(1)} %get-tuple-element.79), kind=kOutput, calls=%fused_computation.4 | convolution fusion | flops 8220160 | bytes 4102400 | tf_op jit(solution)/shard_map/dot_general | solution.py:553
  60.6 0.0 copy-start.10
  60.6 0.0 collective-permute-done.9.refs_5_
  60.6 1.5 %collective-permute-done.7.refs_0_ = bf16[2,80,384]{2,1,0:T(8,128)(2,1)S(1)} collective-permute-done((bf16[2,80,384]{2,1,0:T(8,128)(2,1)S(1)}, bf16[2,80,384]{2,1,0:T(8,128)(2,1)S(1)}, u32[]{:S(2)}, u32[]{:S(2)}) %collective-permute-start.7) | collective-permute-done | bytes 122912 | tf_op jit(solution)/shard_map/ppermute | solution.py:558
  62.1 0.3 collective-permute-done.8.refs_2_
  62.4 0.1 shard_map.159
  62.5 0.0 copy-start.3
  62.5 4.5 %collective-permute-start.15 = (f32[8,320]{1,0:T(8,128)S(1)}, f32[8,320]{1,0:T(8,128)S(1)}, u32[]{:S(2)}, u32[]{:S(2)}) collective-permute-start(f32[8,320]{1,0:T(8,128)S(1)} %get-tuple-element.63.refs_9_.refs_1_), channel_id=1, source_target_pairs={{0,12},{1,13},{2,14},{3,15},{4,8},{5,9},{6,10},{7,11},{8,4},{9,5},... | collective-permute-start | bytes 30728 | tf_op jit(solution)/shard_map/ppermute | solution.py:558
  66.9 0.9 fusion.22.refs_8_
  67.9 0.0 collective-permute-start.14
  67.9 0.6 collective-permute-start.13
  68.5 1.4 %collective-permute-start.10 = (bf16[80,384]{1,0:T(8,128)(2,1)S(1)}, bf16[80,384]{1,0:T(8,128)(2,1)S(1)}, u32[]{:S(2)}, u32[]{:S(2)}) collective-permute-start(bf16[80,384]{1,0:T(8,128)(2,1)S(1)} %get-tuple-element.67), channel_id=1, source_target_pairs={{0,4},{1,5},{2,6},{3,7},{4,0},{5,1},{6,2},{7,3},{8,12},{9,13},{10,... | collective-permute-start | bytes 184328 | tf_op jit(solution)/shard_map/ppermute | solution.py:558
  69.9 2.9 %collective-permute-start.11 = (bf16[80,384]{1,0:T(8,128)(2,1)S(1)}, bf16[80,384]{1,0:T(8,128)(2,1)S(1)}, u32[]{:S(2)}, u32[]{:S(2)}) collective-permute-start(bf16[80,384]{1,0:T(8,128)(2,1)S(1)} %get-tuple-element.68), channel_id=1, source_target_pairs={{0,8},{1,9},{2,10},{3,11},{4,12},{5,13},{6,14},{7,15},{8,0},{9,1},... | collective-permute-start | bytes 184328 | tf_op jit(solution)/shard_map/ppermute | solution.py:558
  72.8 0.0 collective-permute-start.12
  72.9 9.0 %shard_map.160 = (bf16[1024,320]{1,0:T(8,128)(2,1)}, f32[8,128]{1,0:T(8,128)}) custom-call(bf16[1024,320]{1,0:T(8,128)(2,1)} %bitcast.19, bf16[9,320,320]{2,1,0:T(8,128)(2,1)} %bitcast.26, f32[320]{0:T(512)} %refs_2_.3, f32[8,320]{1,0:T(8,128)} %get-tuple-element.47.refs_2_.refs_3_.refs_4_, f32[4,66,1,320]{3,2,1,0:T(1,128)} %collective-permute-done.1.refs_2_.refs_5_.refs_4_, ...), custom_call_target="tpu_custom_call" | custom-call | flops 1887436800 | bytes 2000000 | tf_op jit(solution)/shard_map/pallas_call | solution.py:111
  81.9 0.0 collective-permute-done.14.refs_6_
  81.9 0.0 collective-permute-done.11.refs_3_
  81.9 0.0 copy-start.4
  81.9 0.7 copy-done.4
  82.6 0.7 copy-done.5
  83.4 3.6 %collective-permute-start.23 = (bf16[80,384]{1,0:T(8,128)(2,1)S(1)}, bf16[80,384]{1,0:T(8,128)(2,1)S(1)}, u32[]{:S(2)}, u32[]{:S(2)}) collective-permute-start(bf16[80,384]{1,0:T(8,128)(2,1)S(1)} %get-tuple-element.73.refs_0_), channel_id=1, source_target_pairs={{0,14},{1,15},{2,12},{3,13},{4,10},{5,11},{6,8},{7,9},{8,6},{9,7},... | collective-permute-start | bytes 184328 | tf_op jit(solution)/shard_map/ppermute | solution.py:558
  86.9 0.9 collective-permute-start.22
  87.8 0.3 collective-permute-start.16
  88.1 0.4 collective-permute-start.21
  88.5 3.3 %collective-permute-start.20 = (bf16[80,384]{1,0:T(8,128)(2,1)S(1)}, bf16[80,384]{1,0:T(8,128)(2,1)S(1)}, u32[]{:S(2)}, u32[]{:S(2)}) collective-permute-start(bf16[80,384]{1,0:T(8,128)(2,1)S(1)} %get-tuple-element.73.refs_0_), channel_id=1, source_target_pairs={{0,8},{1,9},{2,10},{3,11},{4,12},{5,13},{6,14},{7,15},{8,0},{9,1},... | collective-permute-start | bytes 184328 | tf_op jit(solution)/shard_map/ppermute | solution.py:558
  91.8 0.0 collective-permute-done.16.refs_6_
  91.8 1.4 %collective-permute-start.19 = (bf16[80,384]{1,0:T(8,128)(2,1)S(1)}, bf16[80,384]{1,0:T(8,128)(2,1)S(1)}, u32[]{:S(2)}, u32[]{:S(2)}) collective-permute-start(bf16[80,384]{1,0:T(8,128)(2,1)S(1)} %get-tuple-element.73.refs_0_), channel_id=1, source_target_pairs={{0,6},{1,7},{2,4},{3,5},{4,2},{5,3},{6,0},{7,1},{8,14},{9,15},{10,... | collective-permute-start | bytes 184328 | tf_op jit(solution)/shard_map/ppermute | solution.py:558
  93.2 0.8 collective-permute-start.18
  94.0 1.3 %collective-permute-start.17 = (bf16[80,384]{1,0:T(8,128)(2,1)S(1)}, bf16[80,384]{1,0:T(8,128)(2,1)S(1)}, u32[]{:S(2)}, u32[]{:S(2)}) collective-permute-start(bf16[80,384]{1,0:T(8,128)(2,1)S(1)} %get-tuple-element.73.refs_0_), channel_id=1, source_target_pairs={{0,2},{1,3},{2,0},{3,1},{4,6},{5,7},{6,4},{7,5},{8,10},{9,11},{10,... | collective-permute-start | bytes 184328 | tf_op jit(solution)/shard_map/ppermute | solution.py:558
  95.3 4.6 %shard_map.162 = (f32[1024,320]{1,0:T(8,128)}, f32[320]{0:T(512)}, f32[320]{0:T(512)}, f32[320]{0:T(512)}, f32[320,1280]{1,0:T(8,128)}, /*index=5*/f32[8,128]{1,0:T(8,128)}) custom-call(bf16[1024,320]{1,0:T(8,128)(2,1)} %bitcast.20, bf16[1024,320]{1,0:T(8,128)(2,1)} %bitcast.23, f32[1024,320]{1,0:T(8,128)} %get-tuple-element.65.refs_2_, f32[320]{0:T(512)} %refs_3_.3, ...), custom_call_target="tpu_custom_call" | custom-call | flops 2621440 | bytes 2000000 | tf_op jit(solution)/shard_map/pallas_call | solution.py:111
  100.0 0.7 copy-done.6
  100.7 0.1 shard_map.163.refs_0_
  100.8 0.1 collective-permute-start.24
  100.8 1.9 %collective-permute-done.24.refs_1_ = bf16[80,3072]{1,0:T(8,128)(2,1)S(1)} collective-permute-done((bf16[80,3072]{1,0:T(8,128)(2,1)S(1)}, bf16[80,3072]{1,0:T(8,128)(2,1)S(1)}, u32[]{:S(2)}, u32[]{:S(2)}) %collective-permute-start.24) | collective-permute-done | bytes 491552 | tf_op jit(solution)/shard_map/ppermute | solution.py:558
  102.7 1.9 %shard_map.164 = f32[9,160,320]{2,1,0:T(8,128)} custom-call(bf16[80,3072]{1,0:T(8,128)(2,1)S(1)} %shard_map.163.refs_0_, bf16[80,3072]{1,0:T(8,128)(2,1)S(1)} %collective-permute-done.24.refs_1_), custom_call_target="tpu_custom_call" | custom-call | bytes 2000000 | tf_op jit(solution)/shard_map/pallas_call | solution.py:53
  (33 shorter events, 0.1 us)
Async XLA Ops:
  1.4 4.9 %collective-permute-start = (bf16[32,320]{1,0:T(8,128)(2,1)S(1)}, bf16[32,320]{1,0:T(8,128)(2,1)}, u32[]{:S(2)}, u32[]{:S(2)}) collective-permute-start(bf16[32,320]{1,0:T(8,128)(2,1)S(1)} %maximum_bitcast_fusion), channel_id=1, source_target_pairs={{0,16},{1,17},{2,18},{3,19},{4,20},{5,21},{6,22},{7,23},{8,24},{9,... | collective-permute-start | bytes 61448 | tf_op jit(solution)/shard_map/ppermute | solution.py:558
  9.6 12.1 %collective-permute-start.1 = (f32[4,66,1,320]{3,2,1,0:T(1,128)}, f32[4,66,1,320]{3,2,1,0:T(1,128)}, u32[]{:S(2)}, u32[]{:S(2)}) collective-permute-start(f32[4,66,1,320]{3,2,1,0:T(1,128)} %get-tuple-element.43), channel_id=1, source_target_pairs={{0,1},{1,2},{2,3},{3,4},{4,5},{5,6},{6,7},{7,8},{8,9},{9,10},{10,1... | collective-permute-start | bytes 1013768 | tf_op jit(solution)/shard_map/ppermute | solution.py:569
  11.7 10.0 %collective-permute-start.2 = (f32[4,66,1,320]{3,2,1,0:T(1,128)}, f32[4,66,1,320]{3,2,1,0:T(1,128)}, u32[]{:S(2)}, u32[]{:S(2)}) collective-permute-start(f32[4,66,1,320]{3,2,1,0:T(1,128)} %get-tuple-element.44), channel_id=1, source_target_pairs={{1,0},{2,1},{3,2},{4,3},{5,4},{6,5},{7,6},{8,7},{9,8},{10,9},{11,1... | collective-permute-start | bytes 1013768 | tf_op jit(solution)/shard_map/ppermute | solution.py:569
  13.0 16.6 %all-to-all-start = ((f32[32,1,128]{2,1,0:T(1,128)}), f32[32,1,128]{2,1,0:T(1,128)}, u32[]{:S(2)}, u32[]{:S(2)}) async-start(f32[32,1,128]{2,1,0:T(1,128)} %get-tuple-element.46), calls=%async_computation | async-start | bytes 32768 | tf_op jit(solution)/shard_map/all_to_all | solution.py:620
  37.9 10.5 %copy-start.12 = (s32[2]{0:T(128)S(1)}, s32[2]{0:T(128)}, u32[]{:S(2)}) copy-start(s32[2]{0:T(128)} %param.11) | copy-start | bytes 28
  37.9 3.9 %collective-permute-start.3 = (bf16[2,8,80,384]{3,2,1,0:T(8,128)(2,1)}, bf16[2,8,80,384]{3,2,1,0:T(8,128)(2,1)S(1)}, u32[]{:S(2)}, u32[]{:S(2)}) collective-permute-start(bf16[2,8,80,384]{3,2,1,0:T(8,128)(2,1)} %bitcast.29), channel_id=1, source_target_pairs={{0,1},{1,0},{2,3},{3,2},{4,5},{5,4},{6,7},{7,6},{8,9},{9,8},{10,11... | collective-permute-start | bytes 2949128 | tf_op jit(solution)/shard_map/ppermute | solution.py:558
  41.8 1.5 %copy-start = (f32[2,8,80,384]{3,2,1,0:T(8,128)S(1)}, f32[2,8,80,384]{3,2,1,0:T(8,128)}, u32[]{:S(2)}) copy-start(f32[2,8,80,384]{3,2,1,0:T(8,128)} %get-tuple-element.48.refs_0_) | copy-start | bytes 5898244
  43.5 0.6 copy-start.7
  44.1 13.7 %copy-start.8 = (bf16[320,1280]{1,0:T(8,128)(2,1)S(1)}, bf16[320,1280]{1,0:T(8,128)(2,1)}, u32[]{:S(2)}) copy-start(bf16[320,1280]{1,0:T(8,128)(2,1)} %param.16) | copy-start | bytes 2457604
  44.1 10.3 %collective-permute-start.4 = (bf16[2,2,80,384]{3,2,1,0:T(8,128)(2,1)S(1)}, bf16[2,2,80,384]{3,2,1,0:T(8,128)(2,1)S(1)}, u32[]{:S(2)}, u32[]{:S(2)}) collective-permute-start(bf16[2,2,80,384]{3,2,1,0:T(8,128)(2,1)S(1)} %get-tuple-element.50), channel_id=1, source_target_pairs={{0,16},{1,17},{2,18},{3,19},{4,20},{5,21},{6,22},{7,23},{8,24},{9,... | collective-permute-start | bytes 737288 | tf_op jit(solution)/shard_map/ppermute | solution.py:558
  45.8 8.8 %collective-permute-start.5 = (bf16[2,2,80,384]{3,2,1,0:T(8,128)(2,1)S(1)}, bf16[2,2,80,384]{3,2,1,0:T(8,128)(2,1)S(1)}, u32[]{:S(2)}, u32[]{:S(2)}) collective-permute-start(bf16[2,2,80,384]{3,2,1,0:T(8,128)(2,1)S(1)} %get-tuple-element.52), channel_id=1, source_target_pairs={{0,2},{1,3},{2,0},{3,1},{4,6},{5,7},{6,4},{7,5},{8,10},{9,11},{10,... | collective-permute-start | bytes 737288 | tf_op jit(solution)/shard_map/ppermute | solution.py:558
  52.9 1.5 %collective-permute-start.6 = (f32[8,320]{1,0:T(8,128)}, f32[8,320]{1,0:T(8,128)S(1)}, u32[]{:S(2)}, u32[]{:S(2)}) collective-permute-start(f32[8,320]{1,0:T(8,128)} %get-tuple-element.57.refs_4_), channel_id=1, source_target_pairs={{0,1},{1,0},{2,3},{3,2},{4,5},{5,4},{6,7},{7,6},{8,9},{9,8},{10,11... | collective-permute-start | bytes 30728 | tf_op jit(solution)/shard_map/ppermute | solution.py:558
  54.6 0.7 copy-start.2
  55.4 5.2 %collective-permute-start.9 = (f32[8,320]{1,0:T(8,128)S(1)}, f32[8,320]{1,0:T(8,128)S(1)}, u32[]{:S(2)}, u32[]{:S(2)}) collective-permute-start(f32[8,320]{1,0:T(8,128)S(1)} %get-tuple-element.62.refs_4_), channel_id=1, source_target_pairs={{0,2},{1,3},{2,0},{3,1},{4,6},{5,7},{6,4},{7,5},{8,10},{9,11},{10,... | collective-permute-start | bytes 30728 | tf_op jit(solution)/shard_map/ppermute | solution.py:558
  57.2 4.9 %collective-permute-start.7 = (bf16[2,80,384]{2,1,0:T(8,128)(2,1)S(1)}, bf16[2,80,384]{2,1,0:T(8,128)(2,1)S(1)}, u32[]{:S(2)}, u32[]{:S(2)}) collective-permute-start(bf16[2,80,384]{2,1,0:T(8,128)(2,1)S(1)} %get-tuple-element.58), channel_id=1, source_target_pairs={{0,2},{1,3},{2,0},{3,1},{4,6},{5,7},{6,4},{7,5},{8,10},{9,11},{10,... | collective-permute-start | bytes 368648 | tf_op jit(solution)/shard_map/ppermute | solution.py:558
  57.5 4.9 %collective-permute-start.8 = (bf16[2,80,384]{2,1,0:T(8,128)(2,1)S(1)}, bf16[2,80,384]{2,1,0:T(8,128)(2,1)S(1)}, u32[]{:S(2)}, u32[]{:S(2)}) collective-permute-start(bf16[2,80,384]{2,1,0:T(8,128)(2,1)S(1)} %get-tuple-element.60), channel_id=1, source_target_pairs={{0,16},{1,17},{2,18},{3,19},{4,20},{5,21},{6,22},{7,23},{8,24},{9,... | collective-permute-start | bytes 368648 | tf_op jit(solution)/shard_map/ppermute | solution.py:558
  57.8 9.2 %copy-start.9 = (bf16[1280,320]{0,1:T(8,128)(2,1)S(1)}, bf16[1280,320]{0,1:T(8,128)(2,1)}, u32[]{:S(2)}) copy-start(bf16[1280,320]{0,1:T(8,128)(2,1)} %param.18) | copy-start | bytes 2457604
  60.6 21.2 %copy-start.10 = (bf16[2,1280]{1,0:T(2,128)(2,1)}, bf16[2,1280]{1,0:T(2,128)(2,1)S(1)}, u32[]{:S(2)}) copy-start(bf16[2,1280]{1,0:T(2,128)(2,1)S(1)} %fusion.1.refs_7_) | copy-start | bytes 15364
  62.5 10.4 %copy-start.3 = (f32[8,320]{1,0:T(8,128)}, f32[8,320]{1,0:T(8,128)S(1)}, u32[]{:S(2)}) copy-start(f32[8,320]{1,0:T(8,128)S(1)} %get-tuple-element.63.refs_9_.refs_1_) | copy-start | bytes 30724
  62.5 10.4 %collective-permute-start.15 = (f32[8,320]{1,0:T(8,128)S(1)}, f32[8,320]{1,0:T(8,128)S(1)}, u32[]{:S(2)}, u32[]{:S(2)}) collective-permute-start(f32[8,320]{1,0:T(8,128)S(1)} %get-tuple-element.63.refs_9_.refs_1_), channel_id=1, source_target_pairs={{0,12},{1,13},{2,14},{3,15},{4,8},{5,9},{6,10},{7,11},{8,4},{9,5},... | collective-permute-start | bytes 30728 | tf_op jit(solution)/shard_map/ppermute | solution.py:558
  67.9 14.0 %collective-permute-start.14 = (f32[8,320]{1,0:T(8,128)S(1)}, f32[8,320]{1,0:T(8,128)S(1)}, u32[]{:S(2)}, u32[]{:S(2)}) collective-permute-start(f32[8,320]{1,0:T(8,128)S(1)} %get-tuple-element.63.refs_9_.refs_1_), channel_id=1, source_target_pairs={{0,8},{1,9},{2,10},{3,11},{4,12},{5,13},{6,14},{7,15},{8,0},{9,1},... | collective-permute-start | bytes 30728 | tf_op jit(solution)/shard_map/ppermute | solution.py:558
  67.9 14.0 %collective-permute-start.13 = (f32[8,320]{1,0:T(8,128)S(1)}, f32[8,320]{1,0:T(8,128)S(1)}, u32[]{:S(2)}, u32[]{:S(2)}) collective-permute-start(f32[8,320]{1,0:T(8,128)S(1)} %get-tuple-element.63.refs_9_.refs_1_), channel_id=1, source_target_pairs={{0,4},{1,5},{2,6},{3,7},{4,0},{5,1},{6,2},{7,3},{8,12},{9,13},{10,... | collective-permute-start | bytes 30728 | tf_op jit(solution)/shard_map/ppermute | solution.py:558
  68.5 13.4 %collective-permute-start.10 = (bf16[80,384]{1,0:T(8,128)(2,1)S(1)}, bf16[80,384]{1,0:T(8,128)(2,1)S(1)}, u32[]{:S(2)}, u32[]{:S(2)}) collective-permute-start(bf16[80,384]{1,0:T(8,128)(2,1)S(1)} %get-tuple-element.67), channel_id=1, source_target_pairs={{0,4},{1,5},{2,6},{3,7},{4,0},{5,1},{6,2},{7,3},{8,12},{9,13},{10,... | collective-permute-start | bytes 184328 | tf_op jit(solution)/shard_map/ppermute | solution.py:558
  69.9 12.0 %collective-permute-start.11 = (bf16[80,384]{1,0:T(8,128)(2,1)S(1)}, bf16[80,384]{1,0:T(8,128)(2,1)S(1)}, u32[]{:S(2)}, u32[]{:S(2)}) collective-permute-start(bf16[80,384]{1,0:T(8,128)(2,1)S(1)} %get-tuple-element.68), channel_id=1, source_target_pairs={{0,8},{1,9},{2,10},{3,11},{4,12},{5,13},{6,14},{7,15},{8,0},{9,1},... | collective-permute-start | bytes 184328 | tf_op jit(solution)/shard_map/ppermute | solution.py:558
  72.8 9.1 %collective-permute-start.12 = (bf16[80,384]{1,0:T(8,128)(2,1)S(1)}, bf16[80,384]{1,0:T(8,128)(2,1)S(1)}, u32[]{:S(2)}, u32[]{:S(2)}) collective-permute-start(bf16[80,384]{1,0:T(8,128)(2,1)S(1)} %get-tuple-element.69), channel_id=1, source_target_pairs={{0,12},{1,13},{2,14},{3,15},{4,8},{5,9},{6,10},{7,11},{8,4},{9,5},... | collective-permute-start | bytes 184328 | tf_op jit(solution)/shard_map/ppermute | solution.py:558
  81.9 0.7 copy-start.4
  82.6 0.7 copy-start.5
  83.3 12.0 %copy-start.1 = (f32[8,320]{1,0:T(8,128)}, f32[8,320]{1,0:T(8,128)S(1)}, u32[]{:S(2)}) copy-start(f32[8,320]{1,0:T(8,128)S(1)} %get-tuple-element.71.refs_5_) | copy-start | bytes 30724
  83.4 9.9 %collective-permute-start.23 = (bf16[80,384]{1,0:T(8,128)(2,1)S(1)}, bf16[80,384]{1,0:T(8,128)(2,1)S(1)}, u32[]{:S(2)}, u32[]{:S(2)}) collective-permute-start(bf16[80,384]{1,0:T(8,128)(2,1)S(1)} %get-tuple-element.73.refs_0_), channel_id=1, source_target_pairs={{0,14},{1,15},{2,12},{3,13},{4,10},{5,11},{6,8},{7,9},{8,6},{9,7},... | collective-permute-start | bytes 184328 | tf_op jit(solution)/shard_map/ppermute | solution.py:558
  86.9 7.0 %collective-permute-start.22 = (bf16[80,384]{1,0:T(8,128)(2,1)S(1)}, bf16[80,384]{1,0:T(8,128)(2,1)S(1)}, u32[]{:S(2)}, u32[]{:S(2)}) collective-permute-start(bf16[80,384]{1,0:T(8,128)(2,1)S(1)} %get-tuple-element.73.refs_0_), channel_id=1, source_target_pairs={{0,12},{1,13},{2,14},{3,15},{4,8},{5,9},{6,10},{7,11},{8,4},{9,5},... | collective-permute-start | bytes 184328 | tf_op jit(solution)/shard_map/ppermute | solution.py:558
  87.8 3.9 %collective-permute-start.16 = (f32[8,320]{1,0:T(8,128)S(1)}, f32[8,320]{1,0:T(8,128)S(1)}, u32[]{:S(2)}, u32[]{:S(2)}) collective-permute-start(f32[8,320]{1,0:T(8,128)S(1)} %get-tuple-element.71.refs_5_), channel_id=1, source_target_pairs={{0,16},{1,17},{2,18},{3,19},{4,20},{5,21},{6,22},{7,23},{8,24},{9,... | collective-permute-start | bytes 30728 | tf_op jit(solution)/shard_map/ppermute | solution.py:558
  88.1 11.9 %collective-permute-start.21 = (bf16[80,384]{1,0:T(8,128)(2,1)S(1)}, bf16[80,384]{1,0:T(8,128)(2,1)S(1)}, u32[]{:S(2)}, u32[]{:S(2)}) collective-permute-start(bf16[80,384]{1,0:T(8,128)(2,1)S(1)} %get-tuple-element.73.refs_0_), channel_id=1, source_target_pairs={{0,10},{1,11},{2,8},{3,9},{4,14},{5,15},{6,12},{7,13},{8,2},{9,3},... | collective-permute-start | bytes 184328 | tf_op jit(solution)/shard_map/ppermute | solution.py:558
  88.5 11.5 %collective-permute-start.20 = (bf16[80,384]{1,0:T(8,128)(2,1)S(1)}, bf16[80,384]{1,0:T(8,128)(2,1)S(1)}, u32[]{:S(2)}, u32[]{:S(2)}) collective-permute-start(bf16[80,384]{1,0:T(8,128)(2,1)S(1)} %get-tuple-element.73.refs_0_), channel_id=1, source_target_pairs={{0,8},{1,9},{2,10},{3,11},{4,12},{5,13},{6,14},{7,15},{8,0},{9,1},... | collective-permute-start | bytes 184328 | tf_op jit(solution)/shard_map/ppermute | solution.py:558
  91.8 3.5 %copy-start.11 = (f32[8,320]{1,0:T(8,128)}, f32[8,320]{1,0:T(8,128)S(1)}, u32[]{:S(2)}) copy-start(f32[8,320]{1,0:T(8,128)S(1)} %collective-permute-done.16.refs_6_) | copy-start | bytes 30724
  91.8 8.2 %collective-permute-start.19 = (bf16[80,384]{1,0:T(8,128)(2,1)S(1)}, bf16[80,384]{1,0:T(8,128)(2,1)S(1)}, u32[]{:S(2)}, u32[]{:S(2)}) collective-permute-start(bf16[80,384]{1,0:T(8,128)(2,1)S(1)} %get-tuple-element.73.refs_0_), channel_id=1, source_target_pairs={{0,6},{1,7},{2,4},{3,5},{4,2},{5,3},{6,0},{7,1},{8,14},{9,15},{10,... | collective-permute-start | bytes 184328 | tf_op jit(solution)/shard_map/ppermute | solution.py:558
  93.2 6.8 %collective-permute-start.18 = (bf16[80,384]{1,0:T(8,128)(2,1)S(1)}, bf16[80,384]{1,0:T(8,128)(2,1)S(1)}, u32[]{:S(2)}, u32[]{:S(2)}) collective-permute-start(bf16[80,384]{1,0:T(8,128)(2,1)S(1)} %get-tuple-element.73.refs_0_), channel_id=1, source_target_pairs={{0,4},{1,5},{2,6},{3,7},{4,0},{5,1},{6,2},{7,3},{8,12},{9,13},{10,... | collective-permute-start | bytes 184328 | tf_op jit(solution)/shard_map/ppermute | solution.py:558
  94.0 6.0 %collective-permute-start.17 = (bf16[80,384]{1,0:T(8,128)(2,1)S(1)}, bf16[80,384]{1,0:T(8,128)(2,1)S(1)}, u32[]{:S(2)}, u32[]{:S(2)}) collective-permute-start(bf16[80,384]{1,0:T(8,128)(2,1)S(1)} %get-tuple-element.73.refs_0_), channel_id=1, source_target_pairs={{0,2},{1,3},{2,0},{3,1},{4,6},{5,7},{6,4},{7,5},{8,10},{9,11},{10,... | collective-permute-start | bytes 184328 | tf_op jit(solution)/shard_map/ppermute | solution.py:558
  100.0 0.7 copy-start.6
  100.8 1.9 %collective-permute-start.24 = (bf16[80,3072]{1,0:T(8,128)(2,1)S(1)}, bf16[80,3072]{1,0:T(8,128)(2,1)S(1)}, u32[]{:S(2)}, u32[]{:S(2)}) collective-permute-start(bf16[80,3072]{1,0:T(8,128)(2,1)S(1)} %shard_map.163.refs_0_), channel_id=1, source_target_pairs={{0,1},{1,0},{2,3},{3,2},{4,5},{5,4},{6,7},{7,6},{8,9},{9,8},{10,11... | collective-permute-start | bytes 1474568 | tf_op jit(solution)/shard_map/ppermute | solution.py:558

commit v7 on v6

--- a/solution.py
+++ b/solution.py
@@ -55,7 +55,7 @@
         out_shape=out_shape,
         in_specs=[pl.BlockSpec(memory_space=pltpu.HBM)] * count
         + [near] * used
-        + [near] * waits,
+        + [pl.BlockSpec(memory_space=pl.ANY)] * waits,
         out_specs=jax.tree.map(lambda _: near, out_shape),
         scratch_shapes=scratch,
         compiler_params=pltpu.CompilerParams(vmem_limit_bytes=vmem * 2**20),
@@ -286,15 +286,22 @@
         pass
 
 
-def tap_rows(ap, b, kh, kw):
-    _, _, tall, w, c = ap.shape
-    return ap[kw, b, kh : kh + tall - 2].reshape((tall - 2) * w, c).astype(BF16)
+def gather_taps(im, ap, flip):
+    _, batch, tall, w, c = ap.shape
+    per = (tall - 2) * w
+    for b in range(batch):
+        for tap in range(9):
+            kh, kw = tap // 3, tap % 3
+            if flip:
+                kh, kw = 2 - kh, 2 - kw
+            rows = ap[kw, b, kh : kh + tall - 2].reshape(per, c).astype(BF16)
+            im[b * per : (b + 1) * per, tap * c : (tap + 1) * c] = rows
 
 
 def dacts_kernel(batch, relative, share, emit, *refs):
     g_load, w_load = refs[:2]
     halo = refs[2:6]
-    da_ref, gsum_ref, gp_ref, ap, gt = refs[6:]
+    da_ref, gsum_ref, gp_ref, ap, gt, im, wt = refs[6:]
     g_ref = g_load()
     n, c = g_ref.shape
     _, _, tall, w, _ = ap.shape
@@ -319,18 +326,17 @@
         gp_ref[...] = gt[:c, :]
     emit(1)
     emit(2)
+    gather_taps(im, ap, True)
     w_ref = w_load()
+    for tap in range(9):
+        wt[:, tap * c : (tap + 1) * c] = w_ref[tap]
     for b in range(batch):
-        acc = jnp.zeros((per, c), F32)
-        for kh in range(3):
-            for kw in range(3):
-                acc = acc + lax.dot_general(
-                    tap_rows(ap, b, 2 - kh, 2 - kw),
-                    w_ref[kh * 3 + kw],
-                    (((1,), (1,)), ((), ())),
-                    preferred_element_type=F32,
-                )
-        da_ref[b * per : (b + 1) * per, :] = acc
+        da_ref[b * per : (b + 1) * per, :] = lax.dot_general(
+            im[b * per : (b + 1) * per, : 9 * c],
+            wt[...],
+            (((1,), (1,)), ((), ())),
+            preferred_element_type=F32,
+        )
         emit(0, b * per, per)
 
 
@@ -338,7 +344,7 @@
     x_load, gp_load, gain_load, bias_load, st_ref = refs[:5]
     halo = refs[5:9]
     aff_ref, keep_ref, send_ref = refs[9:12]
-    ap, part = refs[12:]
+    ap, part, im = refs[12:]
     aff = affine_rows(st_ref, gain_load(), bias_load(), batch, count)
     aff_ref[...] = aff
     emit(0)
@@ -347,19 +353,11 @@
     _, rows, pieces, share, width = send_ref.shape
     fill_acts(ap, aff, batch, x_ref, halo)
     part[:, 9 * channels :] = jnp.zeros((channels, part.shape[1] - 9 * channels), F32)
-    per = n // batch
+    gather_taps(im, ap, False)
     gp = gp_load()
-    for kh in range(3):
-        for kw in range(3):
-            tap = kh * 3 + kw
-            acc = jnp.zeros((channels, channels), F32)
-            for b in range(batch):
-                acc = acc + jnp.dot(
-                    gp[:, b * per : (b + 1) * per],
-                    tap_rows(ap, b, kh, kw),
-                    preferred_element_type=F32,
-                )
-            part[:, tap * channels : (tap + 1) * channels] = acc * scale
+    part[:, : 9 * channels] = (
+        jnp.dot(gp[...], im[...], preferred_element_type=F32) * scale
+    )
     for r in range(rows):
         for p in range(pieces):
             lane = slice(p * width, (p + 1) * width)
@@ -409,21 +407,18 @@
 def conv_kernel(batch, emit, *refs):
     x_load, w_load, cb_load, aff_ref = refs[:4]
     halo = refs[4:8]
-    temb_ref, out_ref, done_ref, ap = refs[8:]
+    temb_ref, out_ref, done_ref, ap, im = refs[8:]
     x_ref = x_load()
     done_ref[...] = jnp.zeros_like(done_ref)
     _, _, tall, w, c = ap.shape
     per = (tall - 2) * w
     fill_acts(ap, aff_ref[...], batch, x_ref, halo)
+    gather_taps(im, ap, False)
     w_ref = w_load()
     bias = cb_load()[...].reshape(1, c)
+    w = w_ref[...].reshape(9 * c, c)
     for b in range(batch):
-        acc = jnp.zeros((per, c), F32)
-        for kh in range(3):
-            for kw in range(3):
-                acc = acc + jnp.dot(
-                    tap_rows(ap, b, kh, kw), w_ref[kh * 3 + kw], preferred_element_type=F32
-                )
+        acc = jnp.dot(im[b * per : (b + 1) * per, :], w, preferred_element_type=F32)
         here = slice(b * per, (b + 1) * per)
         out = x_ref[here, :].astype(F32) + acc + bias + temb_ref[b : b + 1, :]
         out_ref[here, :] = out.astype(BF16)
@@ -620,6 +615,7 @@
     stats = lax.all_to_all(pay, AXES, 0, 0)
     halo = (left, right, top, low)
 
+    neighbours = pltpu.VMEM((n, 9 * channels), BF16)
     shifted = pltpu.VMEM((3, batch, high + 2, wide, channels), F32)
     nz = cols // 4
     share = channels // (2 * rows)
@@ -637,7 +633,12 @@
         halo,
         far=(g2, w9),
         vmem=64,
-        scratch=(shifted, pltpu.VMEM((padded, n), BF16)),
+        scratch=(
+            shifted,
+            pltpu.VMEM((padded, n), BF16),
+            neighbours,
+            pltpu.VMEM((channels, 9 * channels), BF16),
+        ),
         flops=conv_flops,
     )
     aff, keep, send = call_far(
@@ -650,7 +651,7 @@
         (stats, *halo),
         far=(x2, flipped, group_norm_gain, group_norm_bias),
         vmem=56,
-        scratch=(shifted, pltpu.VMEM((channels, pieces * width), F32)),
+        scratch=(shifted, pltpu.VMEM((channels, pieces * width), F32), neighbours),
         flops=conv_flops,
     )
 
@@ -709,7 +710,7 @@
         far=(x2, w9, conv_b),
         after=second,
         vmem=58,
-        scratch=(shifted,),
+        scratch=(shifted, neighbours),
         flops=conv_flops,
     )
 

time: 106 us -> 106 us (level)
  no operation moved by 1% of the time
where the time goes in v7:
time: 106 us; the launch traced here: 105 us
  starting transfers between devices  44.8 us (42%)
  Pallas kernels  40.6 us (38%)
  waiting for transfers between devices  9.42 us (9%)
  local copies, waits for them, and re-layouts  5.67 us (5%)
  matrix products  3.74 us (4%)
    pallas_call x6, Pallas kernels, call_far(): pl.pallas_call(kernel, out_shape=tuple(outs), in_specs=[hbm] * len(ins) +...  38.2 us
    ppermute x23, starting transfers between devices, partner(): return lax.ppermute(value, AXES, [(i, i ^ bit) for i in range(size)])  32.8 us
    ppermute x23, waiting for transfers between devices, partner(): return lax.ppermute(value, AXES, [(i, i ^ bit) for i in range(size)])  9.42 us
    all_to_all x1, starting transfers between devices, local(): stats = lax.all_to_all(pay, AXES, 0, 0)  8.72 us
    unnamed x26, local copies, waits for them, and re-layouts  4.94 us
    ppermute x2, starting transfers between devices, shift(): return lax.ppermute(value, AXES, pairs)  3.34 us
    dot_general x1, matrix products, embed(): jnp.dot(first_hidden, embed_out, preferred_element_type=F32)  2.81 us
    pallas_call x6, Pallas kernels, call(): pl.pallas_call(kernel, out_shape=out_shape, in_specs=[pl.BlockSpec(memory...  2.34 us
  transfers between devices with their start and end apart: 26, of which 7 were waited for; matrix products, arithmetic and copies ran while one was open for 4% of the time, Pallas kernels for 25%

profile of v7, /device:TPU:0, one launch (start us, length us, event | category | flops | bytes accessed | tf_op | source)
XLA Modules:
  0.0 105.3 jit_solution(3372044394010415888)
XLA Ops:
  0.6 0.7 constant_dynamic-slice_fusion
  1.4 3.0 %collective-permute-start = (bf16[32,320]{1,0:T(8,128)(2,1)S(1)}, bf16[32,320]{1,0:T(8,128)(2,1)}, u32[]{:S(2)}, u32[]{:S(2)}) collective-permute-start(bf16[32,320]{1,0:T(8,128)(2,1)S(1)} %maximum_bitcast_fusion), channel_id=1, source_target_pairs={{0,16},{1,17},{2,18},{3,19},{4,20},{5,21},{6,22},{7,23},{8,24},{9,... | collective-permute-start | bytes 61448 | tf_op jit(solution)/shard_map/ppermute | solution.py:553
  4.4 1.9 %collective-permute-done.refs_2_.refs_3_.refs_4_.refs_5_.refs_7_.refs_8_.refs_6_ = bf16[32,320]{1,0:T(8,128)(2,1)} collective-permute-done((bf16[32,320]{1,0:T(8,128)(2,1)S(1)}, bf16[32,320]{1,0:T(8,128)(2,1)}, u32[]{:S(2)}, u32[]{:S(2)}) %collective-permute-start) | collective-permute-done | bytes 20512 | tf_op jit(solution)/shard_map/ppermute | solution.py:553
  6.3 3.3 %shard_map.153 = (f32[32,1,128]{2,1,0:T(1,128)}, f32[4,66,1,320]{3,2,1,0:T(1,128)}, f32[4,66,1,320]{3,2,1,0:T(1,128)}) custom-call(bf16[1024,320]{1,0:T(8,128)(2,1)} %bitcast.16, bf16[1024,320]{1,0:T(8,128)(2,1)} %bitcast.21, bf16[32,320]{1,0:T(8,128)(2,1)} %collective-permute-done.refs_2_.refs_3_.refs_4_.refs_5_.refs_7_.refs_8_.refs_6_, ...), custom_call_target="tpu_custom_call" | custom-call | bytes 2000000 | tf_op jit(solution)/shard_map/pallas_call | solution.py:111
  9.6 2.1 %collective-permute-start.1 = (f32[4,66,1,320]{3,2,1,0:T(1,128)}, f32[4,66,1,320]{3,2,1,0:T(1,128)}, u32[]{:S(2)}, u32[]{:S(2)}) collective-permute-start(f32[4,66,1,320]{3,2,1,0:T(1,128)} %get-tuple-element.43), channel_id=1, source_target_pairs={{0,1},{1,2},{2,3},{3,4},{4,5},{5,6},{6,7},{7,8},{8,9},{9,10},{10,1... | collective-permute-start | bytes 1013768 | tf_op jit(solution)/shard_map/ppermute | solution.py:564
  11.7 1.3 %collective-permute-start.2 = (f32[4,66,1,320]{3,2,1,0:T(1,128)}, f32[4,66,1,320]{3,2,1,0:T(1,128)}, u32[]{:S(2)}, u32[]{:S(2)}) collective-permute-start(f32[4,66,1,320]{3,2,1,0:T(1,128)} %get-tuple-element.44), channel_id=1, source_target_pairs={{1,0},{2,1},{3,2},{4,3},{5,4},{6,5},{7,6},{8,7},{9,8},{10,9},{11,1... | collective-permute-start | bytes 1013768 | tf_op jit(solution)/shard_map/ppermute | solution.py:564
  13.0 8.7 %all-to-all-start = ((f32[32,1,128]{2,1,0:T(1,128)}), f32[32,1,128]{2,1,0:T(1,128)}, u32[]{:S(2)}, u32[]{:S(2)}) async-start(f32[32,1,128]{2,1,0:T(1,128)} %get-tuple-element.46), calls=%async_computation | async-start | bytes 32768 | tf_op jit(solution)/shard_map/all_to_all | solution.py:615
  21.7 0.0 collective-permute-done.2.refs_3_.refs_6_.refs_5_
  21.7 8.0 %shard_map.154 = (f32[1024,320]{1,0:T(8,128)}, f32[8,320]{1,0:T(8,128)}, bf16[320,1024]{1,0:T(8,128)(2,1)}) custom-call(bf16[1024,320]{1,0:T(8,128)(2,1)} %bitcast.22, bf16[9,320,320]{2,1,0:T(8,128)(2,1)} %bitcast.25, f32[4,66,1,320]{3,2,1,0:T(1,128)} %collective-permute-done.1.refs_2_.refs_5_.refs_4_, ...), custom_call_target="tpu_custom_call" | custom-call | flops 1887436800 | bytes 2000000 | tf_op jit(solution)/shard_map/pallas_call | solution.py:111
  29.8 8.5 %shard_map.155 = (f32[8,320]{1,0:T(8,128)}, f32[2,8,80,384]{3,2,1,0:T(8,128)}, bf16[1,2,8,80,384]{4,3,2,1,0:T(8,128)(2,1)}) custom-call(bf16[1024,320]{1,0:T(8,128)(2,1)} %bitcast.17, bf16[320,1024]{1,0:T(8,128)(2,1)} %get-tuple-element.45.refs_1_, f32[320]{0:T(512)} %refs_3_.3, f32[320]{0:T(512)} %refs_3_.2, f32[32,1,128]{2,1,0:T(1,128)} %all-to-all-done.refs_4_, ...), custom_call_target="tpu_custom_call" | custom-call | flops 1887436800 | bytes 2000000 | tf_op jit(solution)/shard_map/pallas_call | solution.py:111
  38.3 0.0 copy-start.12
  38.3 1.5 %collective-permute-start.3 = (bf16[2,8,80,384]{3,2,1,0:T(8,128)(2,1)}, bf16[2,8,80,384]{3,2,1,0:T(8,128)(2,1)S(1)}, u32[]{:S(2)}, u32[]{:S(2)}) collective-permute-start(bf16[2,8,80,384]{3,2,1,0:T(8,128)(2,1)} %bitcast.29), channel_id=1, source_target_pairs={{0,1},{1,0},{2,3},{3,2},{4,5},{5,4},{6,7},{7,6},{8,9},{9,8},{10,11... | collective-permute-start | bytes 2949128 | tf_op jit(solution)/shard_map/ppermute | solution.py:553
  39.8 2.4 %collective-permute-done.3.refs_1_ = bf16[2,8,80,384]{3,2,1,0:T(8,128)(2,1)S(1)} collective-permute-done((bf16[2,8,80,384]{3,2,1,0:T(8,128)(2,1)}, bf16[2,8,80,384]{3,2,1,0:T(8,128)(2,1)S(1)}, u32[]{:S(2)}, u32[]{:S(2)}) %collective-permute-start.3) | collective-permute-done | bytes 983072 | tf_op jit(solution)/shard_map/ppermute | solution.py:553
  42.2 1.5 %copy-done = f32[2,8,80,384]{3,2,1,0:T(8,128)S(1)} copy-done((f32[2,8,80,384]{3,2,1,0:T(8,128)S(1)}, f32[2,8,80,384]{3,2,1,0:T(8,128)}, u32[]{:S(2)}) %copy-start) | copy-done | bytes 1966104
  43.8 0.2 shard_map.156
  43.9 0.0 copy-start.7
  44.0 0.6 copy-done.7
  44.5 1.6 %collective-permute-start.4 = (bf16[2,2,80,384]{3,2,1,0:T(8,128)(2,1)S(1)}, bf16[2,2,80,384]{3,2,1,0:T(8,128)(2,1)S(1)}, u32[]{:S(2)}, u32[]{:S(2)}) collective-permute-start(bf16[2,2,80,384]{3,2,1,0:T(8,128)(2,1)S(1)} %get-tuple-element.50), channel_id=1, source_target_pairs={{0,16},{1,17},{2,18},{3,19},{4,20},{5,21},{6,22},{7,23},{8,24},{9,... | collective-permute-start | bytes 737288 | tf_op jit(solution)/shard_map/ppermute | solution.py:553
  46.2 2.6 %collective-permute-start.5 = (bf16[2,2,80,384]{3,2,1,0:T(8,128)(2,1)S(1)}, bf16[2,2,80,384]{3,2,1,0:T(8,128)(2,1)S(1)}, u32[]{:S(2)}, u32[]{:S(2)}) collective-permute-start(bf16[2,2,80,384]{3,2,1,0:T(8,128)(2,1)S(1)} %get-tuple-element.52), channel_id=1, source_target_pairs={{0,2},{1,3},{2,0},{3,1},{4,6},{5,7},{6,4},{7,5},{8,10},{9,11},{10,... | collective-permute-start | bytes 737288 | tf_op jit(solution)/shard_map/ppermute | solution.py:553
  48.8 4.5 %shard_map.157 = (f32[1024,320]{1,0:T(8,128)}, f32[8,320]{1,0:T(8,128)}) custom-call(bf16[1024,320]{1,0:T(8,128)(2,1)} %bitcast.18, f32[1024,320]{1,0:T(8,128)} %get-tuple-element.54.refs_1_, f32[8,320]{1,0:T(8,128)} %get-tuple-element.47.refs_2_.refs_3_.refs_4_, f32[8,320]{1,0:T(8,128)} %get-tuple-element.55.refs_3_, f32[8,128]{1,0:T(8,128)} %copy-done.7), custom_call_target="tpu_custom_call" | custom-call | flops 6553600 | bytes 2000000 | tf_op jit(solution)/shard_map/pallas_call | solution.py:111
  53.4 0.1 collective-permute-start.6
  53.4 0.1 fusion.7
  53.6 1.3 %collective-permute-done.6.refs_5_ = f32[8,320]{1,0:T(8,128)S(1)} collective-permute-done((f32[8,320]{1,0:T(8,128)}, f32[8,320]{1,0:T(8,128)S(1)}, u32[]{:S(2)}, u32[]{:S(2)}) %collective-permute-start.6) | collective-permute-done | bytes 10272 | tf_op jit(solution)/shard_map/ppermute | solution.py:553
  54.8 0.2 collective-permute-done.5.refs_2_
  55.0 0.7 copy-done.2
  55.7 0.1 shard_map.158
  55.8 1.8 %collective-permute-start.9 = (f32[8,320]{1,0:T(8,128)S(1)}, f32[8,320]{1,0:T(8,128)S(1)}, u32[]{:S(2)}, u32[]{:S(2)}) collective-permute-start(f32[8,320]{1,0:T(8,128)S(1)} %get-tuple-element.62.refs_4_), channel_id=1, source_target_pairs={{0,2},{1,3},{2,0},{3,1},{4,6},{5,7},{6,4},{7,5},{8,10},{9,11},{10,... | collective-permute-start | bytes 30728 | tf_op jit(solution)/shard_map/ppermute | solution.py:553
  57.6 0.3 collective-permute-start.7
  57.9 0.3 collective-permute-start.8
  58.2 2.8 %fusion.1.refs_7_ = bf16[2,1280]{1,0:T(2,128)(2,1)S(1)} fusion(bf16[1280,1280]{1,0:T(8,128)(2,1)} %param.17, bf16[320,1280]{1,0:T(8,128)(2,1)S(1)} %copy-done.8, bf16[2,160]{1,0:T(2,128)(2,1)S(1)} %get-tuple-element.80, bf16[2,160]{1,0:T(2,128)(2,1)S(1)} %get-tuple-element.79), kind=kOutput, calls=%fused_computation.4 | convolution fusion | flops 8220160 | bytes 4102400 | tf_op jit(solution)/shard_map/dot_general | solution.py:548
  61.0 0.0 copy-start.10
  61.0 0.0 collective-permute-done.9.refs_5_
  61.0 1.5 %collective-permute-done.7.refs_0_ = bf16[2,80,384]{2,1,0:T(8,128)(2,1)S(1)} collective-permute-done((bf16[2,80,384]{2,1,0:T(8,128)(2,1)S(1)}, bf16[2,80,384]{2,1,0:T(8,128)(2,1)S(1)}, u32[]{:S(2)}, u32[]{:S(2)}) %collective-permute-start.7) | collective-permute-done | bytes 122912 | tf_op jit(solution)/shard_map/ppermute | solution.py:553
  62.5 0.3 collective-permute-done.8.refs_2_
  62.8 0.1 shard_map.159
  62.9 0.0 copy-start.3
  62.9 4.5 %collective-permute-start.15 = (f32[8,320]{1,0:T(8,128)S(1)}, f32[8,320]{1,0:T(8,128)S(1)}, u32[]{:S(2)}, u32[]{:S(2)}) collective-permute-start(f32[8,320]{1,0:T(8,128)S(1)} %get-tuple-element.63.refs_9_.refs_1_), channel_id=1, source_target_pairs={{0,12},{1,13},{2,14},{3,15},{4,8},{5,9},{6,10},{7,11},{8,4},{9,5},... | collective-permute-start | bytes 30728 | tf_op jit(solution)/shard_map/ppermute | solution.py:553
  67.4 0.9 fusion.22.refs_8_
  68.3 0.0 collective-permute-start.14
  68.3 0.6 collective-permute-start.13
  68.9 1.4 %collective-permute-start.10 = (bf16[80,384]{1,0:T(8,128)(2,1)S(1)}, bf16[80,384]{1,0:T(8,128)(2,1)S(1)}, u32[]{:S(2)}, u32[]{:S(2)}) collective-permute-start(bf16[80,384]{1,0:T(8,128)(2,1)S(1)} %get-tuple-element.67), channel_id=1, source_target_pairs={{0,4},{1,5},{2,6},{3,7},{4,0},{5,1},{6,2},{7,3},{8,12},{9,13},{10,... | collective-permute-start | bytes 184328 | tf_op jit(solution)/shard_map/ppermute | solution.py:553
  70.3 2.9 %collective-permute-start.11 = (bf16[80,384]{1,0:T(8,128)(2,1)S(1)}, bf16[80,384]{1,0:T(8,128)(2,1)S(1)}, u32[]{:S(2)}, u32[]{:S(2)}) collective-permute-start(bf16[80,384]{1,0:T(8,128)(2,1)S(1)} %get-tuple-element.68), channel_id=1, source_target_pairs={{0,8},{1,9},{2,10},{3,11},{4,12},{5,13},{6,14},{7,15},{8,0},{9,1},... | collective-permute-start | bytes 184328 | tf_op jit(solution)/shard_map/ppermute | solution.py:553
  73.2 0.0 collective-permute-start.12
  73.3 9.3 %shard_map.160 = (bf16[1024,320]{1,0:T(8,128)(2,1)}, f32[8,128]{1,0:T(8,128)}) custom-call(bf16[1024,320]{1,0:T(8,128)(2,1)} %bitcast.19, bf16[9,320,320]{2,1,0:T(8,128)(2,1)} %bitcast.26, f32[320]{0:T(512)} %refs_2_.3, f32[8,320]{1,0:T(8,128)} %get-tuple-element.47.refs_2_.refs_3_.refs_4_, f32[4,66,1,320]{3,2,1,0:T(1,128)} %collective-permute-done.1.refs_2_.refs_5_.refs_4_, ...), custom_call_target="tpu_custom_call" | custom-call | flops 1887436800 | bytes 2000000 | tf_op jit(solution)/shard_map/pallas_call | solution.py:111
  82.6 0.0 collective-permute-done.13.refs_5_
  82.6 0.0 collective-permute-done.10.refs_2_
  82.6 0.0 collective-permute-done.12.refs_4_
  82.6 0.0 copy-start.4
  82.6 0.7 copy-done.4
  83.3 0.7 copy-done.5
  84.0 3.6 %collective-permute-start.23 = (bf16[80,384]{1,0:T(8,128)(2,1)S(1)}, bf16[80,384]{1,0:T(8,128)(2,1)S(1)}, u32[]{:S(2)}, u32[]{:S(2)}) collective-permute-start(bf16[80,384]{1,0:T(8,128)(2,1)S(1)} %get-tuple-element.73.refs_0_), channel_id=1, source_target_pairs={{0,14},{1,15},{2,12},{3,13},{4,10},{5,11},{6,8},{7,9},{8,6},{9,7},... | collective-permute-start | bytes 184328 | tf_op jit(solution)/shard_map/ppermute | solution.py:553
  87.6 0.9 collective-permute-start.22
  88.5 0.3 collective-permute-start.16
  88.8 0.4 collective-permute-start.21
  89.2 3.2 %collective-permute-start.20 = (bf16[80,384]{1,0:T(8,128)(2,1)S(1)}, bf16[80,384]{1,0:T(8,128)(2,1)S(1)}, u32[]{:S(2)}, u32[]{:S(2)}) collective-permute-start(bf16[80,384]{1,0:T(8,128)(2,1)S(1)} %get-tuple-element.73.refs_0_), channel_id=1, source_target_pairs={{0,8},{1,9},{2,10},{3,11},{4,12},{5,13},{6,14},{7,15},{8,0},{9,1},... | collective-permute-start | bytes 184328 | tf_op jit(solution)/shard_map/ppermute | solution.py:553
  92.5 1.4 %collective-permute-start.19 = (bf16[80,384]{1,0:T(8,128)(2,1)S(1)}, bf16[80,384]{1,0:T(8,128)(2,1)S(1)}, u32[]{:S(2)}, u32[]{:S(2)}) collective-permute-start(bf16[80,384]{1,0:T(8,128)(2,1)S(1)} %get-tuple-element.73.refs_0_), channel_id=1, source_target_pairs={{0,6},{1,7},{2,4},{3,5},{4,2},{5,3},{6,0},{7,1},{8,14},{9,15},{10,... | collective-permute-start | bytes 184328 | tf_op jit(solution)/shard_map/ppermute | solution.py:553
  93.9 0.8 collective-permute-start.18
  94.7 1.4 %collective-permute-start.17 = (bf16[80,384]{1,0:T(8,128)(2,1)S(1)}, bf16[80,384]{1,0:T(8,128)(2,1)S(1)}, u32[]{:S(2)}, u32[]{:S(2)}) collective-permute-start(bf16[80,384]{1,0:T(8,128)(2,1)S(1)} %get-tuple-element.73.refs_0_), channel_id=1, source_target_pairs={{0,2},{1,3},{2,0},{3,1},{4,6},{5,7},{6,4},{7,5},{8,10},{9,11},{10,... | collective-permute-start | bytes 184328 | tf_op jit(solution)/shard_map/ppermute | solution.py:553
  96.0 4.6 %shard_map.162 = (f32[1024,320]{1,0:T(8,128)}, f32[320]{0:T(512)}, f32[320]{0:T(512)}, f32[320]{0:T(512)}, f32[320,1280]{1,0:T(8,128)}, /*index=5*/f32[8,128]{1,0:T(8,128)}) custom-call(bf16[1024,320]{1,0:T(8,128)(2,1)} %bitcast.20, bf16[1024,320]{1,0:T(8,128)(2,1)} %bitcast.23, f32[1024,320]{1,0:T(8,128)} %get-tuple-element.65.refs_2_, f32[320]{0:T(512)} %refs_3_.3, ...), custom_call_target="tpu_custom_call" | custom-call | flops 2621440 | bytes 2000000 | tf_op jit(solution)/shard_map/pallas_call | solution.py:111
  100.7 0.7 copy-done.6
  101.4 0.1 shard_map.163.refs_0_
  101.5 0.1 collective-permute-start.24
  101.5 1.9 %collective-permute-done.24.refs_1_ = bf16[80,3072]{1,0:T(8,128)(2,1)S(1)} collective-permute-done((bf16[80,3072]{1,0:T(8,128)(2,1)S(1)}, bf16[80,3072]{1,0:T(8,128)(2,1)S(1)}, u32[]{:S(2)}, u32[]{:S(2)}) %collective-permute-start.24) | collective-permute-done | bytes 491552 | tf_op jit(solution)/shard_map/ppermute | solution.py:553
  103.4 1.9 %shard_map.164 = f32[9,160,320]{2,1,0:T(8,128)} custom-call(bf16[80,3072]{1,0:T(8,128)(2,1)S(1)} %shard_map.163.refs_0_, bf16[80,3072]{1,0:T(8,128)(2,1)S(1)} %collective-permute-done.24.refs_1_), custom_call_target="tpu_custom_call" | custom-call | bytes 2000000 | tf_op jit(solution)/shard_map/pallas_call | solution.py:53
  (33 shorter events, 0.1 us)
Async XLA Ops:
  1.4 4.9 %collective-permute-start = (bf16[32,320]{1,0:T(8,128)(2,1)S(1)}, bf16[32,320]{1,0:T(8,128)(2,1)}, u32[]{:S(2)}, u32[]{:S(2)}) collective-permute-start(bf16[32,320]{1,0:T(8,128)(2,1)S(1)} %maximum_bitcast_fusion), channel_id=1, source_target_pairs={{0,16},{1,17},{2,18},{3,19},{4,20},{5,21},{6,22},{7,23},{8,24},{9,... | collective-permute-start | bytes 61448 | tf_op jit(solution)/shard_map/ppermute | solution.py:553
  9.6 12.1 %collective-permute-start.1 = (f32[4,66,1,320]{3,2,1,0:T(1,128)}, f32[4,66,1,320]{3,2,1,0:T(1,128)}, u32[]{:S(2)}, u32[]{:S(2)}) collective-permute-start(f32[4,66,1,320]{3,2,1,0:T(1,128)} %get-tuple-element.43), channel_id=1, source_target_pairs={{0,1},{1,2},{2,3},{3,4},{4,5},{5,6},{6,7},{7,8},{8,9},{9,10},{10,1... | collective-permute-start | bytes 1013768 | tf_op jit(solution)/shard_map/ppermute | solution.py:564
  11.7 10.0 %collective-permute-start.2 = (f32[4,66,1,320]{3,2,1,0:T(1,128)}, f32[4,66,1,320]{3,2,1,0:T(1,128)}, u32[]{:S(2)}, u32[]{:S(2)}) collective-permute-start(f32[4,66,1,320]{3,2,1,0:T(1,128)} %get-tuple-element.44), channel_id=1, source_target_pairs={{1,0},{2,1},{3,2},{4,3},{5,4},{6,5},{7,6},{8,7},{9,8},{10,9},{11,1... | collective-permute-start | bytes 1013768 | tf_op jit(solution)/shard_map/ppermute | solution.py:564
  13.0 16.8 %all-to-all-start = ((f32[32,1,128]{2,1,0:T(1,128)}), f32[32,1,128]{2,1,0:T(1,128)}, u32[]{:S(2)}, u32[]{:S(2)}) async-start(f32[32,1,128]{2,1,0:T(1,128)} %get-tuple-element.46), calls=%async_computation | async-start | bytes 32768 | tf_op jit(solution)/shard_map/all_to_all | solution.py:615
  38.3 10.5 %copy-start.12 = (s32[2]{0:T(128)S(1)}, s32[2]{0:T(128)}, u32[]{:S(2)}) copy-start(s32[2]{0:T(128)} %param.11) | copy-start | bytes 28
  38.3 3.9 %collective-permute-start.3 = (bf16[2,8,80,384]{3,2,1,0:T(8,128)(2,1)}, bf16[2,8,80,384]{3,2,1,0:T(8,128)(2,1)S(1)}, u32[]{:S(2)}, u32[]{:S(2)}) collective-permute-start(bf16[2,8,80,384]{3,2,1,0:T(8,128)(2,1)} %bitcast.29), channel_id=1, source_target_pairs={{0,1},{1,0},{2,3},{3,2},{4,5},{5,4},{6,7},{7,6},{8,9},{9,8},{10,11... | collective-permute-start | bytes 2949128 | tf_op jit(solution)/shard_map/ppermute | solution.py:553
  42.2 1.5 %copy-start = (f32[2,8,80,384]{3,2,1,0:T(8,128)S(1)}, f32[2,8,80,384]{3,2,1,0:T(8,128)}, u32[]{:S(2)}) copy-start(f32[2,8,80,384]{3,2,1,0:T(8,128)} %get-tuple-element.48.refs_0_) | copy-start | bytes 5898244
  43.9 0.6 copy-start.7
  44.5 13.7 %copy-start.8 = (bf16[320,1280]{1,0:T(8,128)(2,1)S(1)}, bf16[320,1280]{1,0:T(8,128)(2,1)}, u32[]{:S(2)}) copy-start(bf16[320,1280]{1,0:T(8,128)(2,1)} %param.16) | copy-start | bytes 2457604
  44.5 10.3 %collective-permute-start.4 = (bf16[2,2,80,384]{3,2,1,0:T(8,128)(2,1)S(1)}, bf16[2,2,80,384]{3,2,1,0:T(8,128)(2,1)S(1)}, u32[]{:S(2)}, u32[]{:S(2)}) collective-permute-start(bf16[2,2,80,384]{3,2,1,0:T(8,128)(2,1)S(1)} %get-tuple-element.50), channel_id=1, source_target_pairs={{0,16},{1,17},{2,18},{3,19},{4,20},{5,21},{6,22},{7,23},{8,24},{9,... | collective-permute-start | bytes 737288 | tf_op jit(solution)/shard_map/ppermute | solution.py:553
  46.2 8.8 %collective-permute-start.5 = (bf16[2,2,80,384]{3,2,1,0:T(8,128)(2,1)S(1)}, bf16[2,2,80,384]{3,2,1,0:T(8,128)(2,1)S(1)}, u32[]{:S(2)}, u32[]{:S(2)}) collective-permute-start(bf16[2,2,80,384]{3,2,1,0:T(8,128)(2,1)S(1)} %get-tuple-element.52), channel_id=1, source_target_pairs={{0,2},{1,3},{2,0},{3,1},{4,6},{5,7},{6,4},{7,5},{8,10},{9,11},{10,... | collective-permute-start | bytes 737288 | tf_op jit(solution)/shard_map/ppermute | solution.py:553
  53.4 1.5 %collective-permute-start.6 = (f32[8,320]{1,0:T(8,128)}, f32[8,320]{1,0:T(8,128)S(1)}, u32[]{:S(2)}, u32[]{:S(2)}) collective-permute-start(f32[8,320]{1,0:T(8,128)} %get-tuple-element.57.refs_4_), channel_id=1, source_target_pairs={{0,1},{1,0},{2,3},{3,2},{4,5},{5,4},{6,7},{7,6},{8,9},{9,8},{10,11... | collective-permute-start | bytes 30728 | tf_op jit(solution)/shard_map/ppermute | solution.py:553
  55.0 0.7 copy-start.2
  55.8 5.2 %collective-permute-start.9 = (f32[8,320]{1,0:T(8,128)S(1)}, f32[8,320]{1,0:T(8,128)S(1)}, u32[]{:S(2)}, u32[]{:S(2)}) collective-permute-start(f32[8,320]{1,0:T(8,128)S(1)} %get-tuple-element.62.refs_4_), channel_id=1, source_target_pairs={{0,2},{1,3},{2,0},{3,1},{4,6},{5,7},{6,4},{7,5},{8,10},{9,11},{10,... | collective-permute-start | bytes 30728 | tf_op jit(solution)/shard_map/ppermute | solution.py:553
  57.6 4.9 %collective-permute-start.7 = (bf16[2,80,384]{2,1,0:T(8,128)(2,1)S(1)}, bf16[2,80,384]{2,1,0:T(8,128)(2,1)S(1)}, u32[]{:S(2)}, u32[]{:S(2)}) collective-permute-start(bf16[2,80,384]{2,1,0:T(8,128)(2,1)S(1)} %get-tuple-element.58), channel_id=1, source_target_pairs={{0,2},{1,3},{2,0},{3,1},{4,6},{5,7},{6,4},{7,5},{8,10},{9,11},{10,... | collective-permute-start | bytes 368648 | tf_op jit(solution)/shard_map/ppermute | solution.py:553
  57.9 4.9 %collective-permute-start.8 = (bf16[2,80,384]{2,1,0:T(8,128)(2,1)S(1)}, bf16[2,80,384]{2,1,0:T(8,128)(2,1)S(1)}, u32[]{:S(2)}, u32[]{:S(2)}) collective-permute-start(bf16[2,80,384]{2,1,0:T(8,128)(2,1)S(1)} %get-tuple-element.60), channel_id=1, source_target_pairs={{0,16},{1,17},{2,18},{3,19},{4,20},{5,21},{6,22},{7,23},{8,24},{9,... | collective-permute-start | bytes 368648 | tf_op jit(solution)/shard_map/ppermute | solution.py:553
  58.2 9.2 %copy-start.9 = (bf16[1280,320]{0,1:T(8,128)(2,1)S(1)}, bf16[1280,320]{0,1:T(8,128)(2,1)}, u32[]{:S(2)}) copy-start(bf16[1280,320]{0,1:T(8,128)(2,1)} %param.18) | copy-start | bytes 2457604
  61.0 21.5 %copy-start.10 = (bf16[2,1280]{1,0:T(2,128)(2,1)}, bf16[2,1280]{1,0:T(2,128)(2,1)S(1)}, u32[]{:S(2)}) copy-start(bf16[2,1280]{1,0:T(2,128)(2,1)S(1)} %fusion.1.refs_7_) | copy-start | bytes 15364
  62.9 10.4 %copy-start.3 = (f32[8,320]{1,0:T(8,128)}, f32[8,320]{1,0:T(8,128)S(1)}, u32[]{:S(2)}) copy-start(f32[8,320]{1,0:T(8,128)S(1)} %get-tuple-element.63.refs_9_.refs_1_) | copy-start | bytes 30724
  62.9 10.4 %collective-permute-start.15 = (f32[8,320]{1,0:T(8,128)S(1)}, f32[8,320]{1,0:T(8,128)S(1)}, u32[]{:S(2)}, u32[]{:S(2)}) collective-permute-start(f32[8,320]{1,0:T(8,128)S(1)} %get-tuple-element.63.refs_9_.refs_1_), channel_id=1, source_target_pairs={{0,12},{1,13},{2,14},{3,15},{4,8},{5,9},{6,10},{7,11},{8,4},{9,5},... | collective-permute-start | bytes 30728 | tf_op jit(solution)/shard_map/ppermute | solution.py:553
  68.3 14.3 %collective-permute-start.14 = (f32[8,320]{1,0:T(8,128)S(1)}, f32[8,320]{1,0:T(8,128)S(1)}, u32[]{:S(2)}, u32[]{:S(2)}) collective-permute-start(f32[8,320]{1,0:T(8,128)S(1)} %get-tuple-element.63.refs_9_.refs_1_), channel_id=1, source_target_pairs={{0,8},{1,9},{2,10},{3,11},{4,12},{5,13},{6,14},{7,15},{8,0},{9,1},... | collective-permute-start | bytes 30728 | tf_op jit(solution)/shard_map/ppermute | solution.py:553
  68.3 14.3 %collective-permute-start.13 = (f32[8,320]{1,0:T(8,128)S(1)}, f32[8,320]{1,0:T(8,128)S(1)}, u32[]{:S(2)}, u32[]{:S(2)}) collective-permute-start(f32[8,320]{1,0:T(8,128)S(1)} %get-tuple-element.63.refs_9_.refs_1_), channel_id=1, source_target_pairs={{0,4},{1,5},{2,6},{3,7},{4,0},{5,1},{6,2},{7,3},{8,12},{9,13},{10,... | collective-permute-start | bytes 30728 | tf_op jit(solution)/shard_map/ppermute | solution.py:553
  68.9 13.7 %collective-permute-start.10 = (bf16[80,384]{1,0:T(8,128)(2,1)S(1)}, bf16[80,384]{1,0:T(8,128)(2,1)S(1)}, u32[]{:S(2)}, u32[]{:S(2)}) collective-permute-start(bf16[80,384]{1,0:T(8,128)(2,1)S(1)} %get-tuple-element.67), channel_id=1, source_target_pairs={{0,4},{1,5},{2,6},{3,7},{4,0},{5,1},{6,2},{7,3},{8,12},{9,13},{10,... | collective-permute-start | bytes 184328 | tf_op jit(solution)/shard_map/ppermute | solution.py:553
  70.3 12.3 %collective-permute-start.11 = (bf16[80,384]{1,0:T(8,128)(2,1)S(1)}, bf16[80,384]{1,0:T(8,128)(2,1)S(1)}, u32[]{:S(2)}, u32[]{:S(2)}) collective-permute-start(bf16[80,384]{1,0:T(8,128)(2,1)S(1)} %get-tuple-element.68), channel_id=1, source_target_pairs={{0,8},{1,9},{2,10},{3,11},{4,12},{5,13},{6,14},{7,15},{8,0},{9,1},... | collective-permute-start | bytes 184328 | tf_op jit(solution)/shard_map/ppermute | solution.py:553
  73.2 9.3 %collective-permute-start.12 = (bf16[80,384]{1,0:T(8,128)(2,1)S(1)}, bf16[80,384]{1,0:T(8,128)(2,1)S(1)}, u32[]{:S(2)}, u32[]{:S(2)}) collective-permute-start(bf16[80,384]{1,0:T(8,128)(2,1)S(1)} %get-tuple-element.69), channel_id=1, source_target_pairs={{0,12},{1,13},{2,14},{3,15},{4,8},{5,9},{6,10},{7,11},{8,4},{9,5},... | collective-permute-start | bytes 184328 | tf_op jit(solution)/shard_map/ppermute | solution.py:553
  82.6 0.7 copy-start.4
  83.3 0.7 copy-start.5
  84.0 12.0 %copy-start.1 = (f32[8,320]{1,0:T(8,128)}, f32[8,320]{1,0:T(8,128)S(1)}, u32[]{:S(2)}) copy-start(f32[8,320]{1,0:T(8,128)S(1)} %get-tuple-element.71.refs_5_) | copy-start | bytes 30724
  84.0 9.9 %collective-permute-start.23 = (bf16[80,384]{1,0:T(8,128)(2,1)S(1)}, bf16[80,384]{1,0:T(8,128)(2,1)S(1)}, u32[]{:S(2)}, u32[]{:S(2)}) collective-permute-start(bf16[80,384]{1,0:T(8,128)(2,1)S(1)} %get-tuple-element.73.refs_0_), channel_id=1, source_target_pairs={{0,14},{1,15},{2,12},{3,13},{4,10},{5,11},{6,8},{7,9},{8,6},{9,7},... | collective-permute-start | bytes 184328 | tf_op jit(solution)/shard_map/ppermute | solution.py:553
  87.6 7.0 %collective-permute-start.22 = (bf16[80,384]{1,0:T(8,128)(2,1)S(1)}, bf16[80,384]{1,0:T(8,128)(2,1)S(1)}, u32[]{:S(2)}, u32[]{:S(2)}) collective-permute-start(bf16[80,384]{1,0:T(8,128)(2,1)S(1)} %get-tuple-element.73.refs_0_), channel_id=1, source_target_pairs={{0,12},{1,13},{2,14},{3,15},{4,8},{5,9},{6,10},{7,11},{8,4},{9,5},... | collective-permute-start | bytes 184328 | tf_op jit(solution)/shard_map/ppermute | solution.py:553
  88.5 3.9 %collective-permute-start.16 = (f32[8,320]{1,0:T(8,128)S(1)}, f32[8,320]{1,0:T(8,128)S(1)}, u32[]{:S(2)}, u32[]{:S(2)}) collective-permute-start(f32[8,320]{1,0:T(8,128)S(1)} %get-tuple-element.71.refs_5_), channel_id=1, source_target_pairs={{0,16},{1,17},{2,18},{3,19},{4,20},{5,21},{6,22},{7,23},{8,24},{9,... | collective-permute-start | bytes 30728 | tf_op jit(solution)/shard_map/ppermute | solution.py:553
  88.8 11.9 %collective-permute-start.21 = (bf16[80,384]{1,0:T(8,128)(2,1)S(1)}, bf16[80,384]{1,0:T(8,128)(2,1)S(1)}, u32[]{:S(2)}, u32[]{:S(2)}) collective-permute-start(bf16[80,384]{1,0:T(8,128)(2,1)S(1)} %get-tuple-element.73.refs_0_), channel_id=1, source_target_pairs={{0,10},{1,11},{2,8},{3,9},{4,14},{5,15},{6,12},{7,13},{8,2},{9,3},... | collective-permute-start | bytes 184328 | tf_op jit(solution)/shard_map/ppermute | solution.py:553
  89.2 11.5 %collective-permute-start.20 = (bf16[80,384]{1,0:T(8,128)(2,1)S(1)}, bf16[80,384]{1,0:T(8,128)(2,1)S(1)}, u32[]{:S(2)}, u32[]{:S(2)}) collective-permute-start(bf16[80,384]{1,0:T(8,128)(2,1)S(1)} %get-tuple-element.73.refs_0_), channel_id=1, source_target_pairs={{0,8},{1,9},{2,10},{3,11},{4,12},{5,13},{6,14},{7,15},{8,0},{9,1},... | collective-permute-start | bytes 184328 | tf_op jit(solution)/shard_map/ppermute | solution.py:553
  92.5 3.6 %copy-start.11 = (f32[8,320]{1,0:T(8,128)}, f32[8,320]{1,0:T(8,128)S(1)}, u32[]{:S(2)}) copy-start(f32[8,320]{1,0:T(8,128)S(1)} %collective-permute-done.16.refs_6_) | copy-start | bytes 30724
  92.5 8.2 %collective-permute-start.19 = (bf16[80,384]{1,0:T(8,128)(2,1)S(1)}, bf16[80,384]{1,0:T(8,128)(2,1)S(1)}, u32[]{:S(2)}, u32[]{:S(2)}) collective-permute-start(bf16[80,384]{1,0:T(8,128)(2,1)S(1)} %get-tuple-element.73.refs_0_), channel_id=1, source_target_pairs={{0,6},{1,7},{2,4},{3,5},{4,2},{5,3},{6,0},{7,1},{8,14},{9,15},{10,... | collective-permute-start | bytes 184328 | tf_op jit(solution)/shard_map/ppermute | solution.py:553
  93.9 6.8 %collective-permute-start.18 = (bf16[80,384]{1,0:T(8,128)(2,1)S(1)}, bf16[80,384]{1,0:T(8,128)(2,1)S(1)}, u32[]{:S(2)}, u32[]{:S(2)}) collective-permute-start(bf16[80,384]{1,0:T(8,128)(2,1)S(1)} %get-tuple-element.73.refs_0_), channel_id=1, source_target_pairs={{0,4},{1,5},{2,6},{3,7},{4,0},{5,1},{6,2},{7,3},{8,12},{9,13},{10,... | collective-permute-start | bytes 184328 | tf_op jit(solution)/shard_map/ppermute | solution.py:553
  94.7 6.1 %collective-permute-start.17 = (bf16[80,384]{1,0:T(8,128)(2,1)S(1)}, bf16[80,384]{1,0:T(8,128)(2,1)S(1)}, u32[]{:S(2)}, u32[]{:S(2)}) collective-permute-start(bf16[80,384]{1,0:T(8,128)(2,1)S(1)} %get-tuple-element.73.refs_0_), channel_id=1, source_target_pairs={{0,2},{1,3},{2,0},{3,1},{4,6},{5,7},{6,4},{7,5},{8,10},{9,11},{10,... | collective-permute-start | bytes 184328 | tf_op jit(solution)/shard_map/ppermute | solution.py:553
  100.7 0.7 copy-start.6
  101.5 1.9 %collective-permute-start.24 = (bf16[80,3072]{1,0:T(8,128)(2,1)S(1)}, bf16[80,3072]{1,0:T(8,128)(2,1)S(1)}, u32[]{:S(2)}, u32[]{:S(2)}) collective-permute-start(bf16[80,3072]{1,0:T(8,128)(2,1)S(1)} %shard_map.163.refs_0_), channel_id=1, source_target_pairs={{0,1},{1,0},{2,3},{3,2},{4,5},{5,4},{6,7},{7,6},{8,9},{9,8},{10,11... | collective-permute-start | bytes 1474568 | tf_op jit(solution)/shard_map/ppermute | solution.py:553

commit v8 on v7

--- a/solution.py
+++ b/solution.py
@@ -221,12 +221,12 @@
     return stack_rows(a + s + r + t, channels)
 
 
-def put_shifted(ap, b, h, v, left, right):
+def put_shifted(ap, b, h, v, sides):
     t, w, c = v.shape
     j = iota((t, w, c), 1)
-    ap[0, b, pl.ds(h, t)] = jnp.where(j == 0, left, pltpu.roll(v, 1, 1))
+    ap[0, b, pl.ds(h, t)] = jnp.where(j == 0, sides, pltpu.roll(v, 1, 1))
     ap[1, b, pl.ds(h, t)] = v
-    ap[2, b, pl.ds(h, t)] = jnp.where(j == w - 1, right, pltpu.roll(v, w - 1, 1))
+    ap[2, b, pl.ds(h, t)] = jnp.where(j == w - 1, sides, pltpu.roll(v, w - 1, 1))
 
 
 def edge_masks():
@@ -244,6 +244,11 @@
     top, low = top[...].astype(F32), low[...].astype(F32)
     t = 8
     first = part * batch
+
+    def sides(b, l, r, scale):
+        j = iota((l.shape[0], w, c), 1)
+        return fn(b, jnp.where(j == 0, l, r)) * (jnp.where(j == 0, west, east) * scale)
+
     for b in range(batch):
 
         def body(i, carry, b=b):
@@ -255,8 +260,7 @@
                 b,
                 h + 1,
                 fn(b, v),
-                fn(b, left[first + b, pl.ds(h + 1, t)]) * west,
-                fn(b, right[first + b, pl.ds(h + 1, t)]) * east,
+                sides(b, left[first + b, pl.ds(h + 1, t)], right[first + b, pl.ds(h + 1, t)], 1.0),
             )
             return carry if visit is None else visit(carry, v)
 
@@ -270,8 +274,7 @@
                 b,
                 h,
                 fn(b, line[at * w : (at + 1) * w].reshape(1, w, c)) * edge,
-                fn(b, left[at, h : h + 1]) * (west * edge),
-                fn(b, right[at, h : h + 1]) * (east * edge),
+                sides(b, left[at, h : h + 1], right[at, h : h + 1], edge),
             )
 
 
@@ -286,16 +289,14 @@
         pass
 
 
-def gather_taps(im, ap, flip):
-    _, batch, tall, w, c = ap.shape
-    per = (tall - 2) * w
-    for b in range(batch):
-        for tap in range(9):
-            kh, kw = tap // 3, tap % 3
-            if flip:
-                kh, kw = 2 - kh, 2 - kw
-            rows = ap[kw, b, kh : kh + tall - 2].reshape(per, c).astype(BF16)
-            im[b * per : (b + 1) * per, tap * c : (tap + 1) * c] = rows
+def gather_taps(im, b, ap, flip):
+    _, _, tall, w, c = ap.shape
+    for tap in range(9):
+        kh, kw = tap // 3, tap % 3
+        if flip:
+            kh, kw = 2 - kh, 2 - kw
+        rows = ap[kw, b, kh : kh + tall - 2].reshape((tall - 2) * w, c).astype(BF16)
+        im[:, tap * c : (tap + 1) * c] = rows
 
 
 def dacts_kernel(batch, relative, share, emit, *refs):
@@ -326,13 +327,13 @@
         gp_ref[...] = gt[:c, :]
     emit(1)
     emit(2)
-    gather_taps(im, ap, True)
     w_ref = w_load()
     for tap in range(9):
         wt[:, tap * c : (tap + 1) * c] = w_ref[tap]
     for b in range(batch):
+        gather_taps(im, b, ap, True)
         da_ref[b * per : (b + 1) * per, :] = lax.dot_general(
-            im[b * per : (b + 1) * per, : 9 * c],
+            im[...],
             wt[...],
             (((1,), (1,)), ((), ())),
             preferred_element_type=F32,
@@ -344,7 +345,8 @@
     x_load, gp_load, gain_load, bias_load, st_ref = refs[:5]
     halo = refs[5:9]
     aff_ref, keep_ref, send_ref = refs[9:12]
-    ap, part, im = refs[12:]
+    ims = refs[12 : 12 + batch]
+    ap, part = refs[12 + batch :]
     aff = affine_rows(st_ref, gain_load(), bias_load(), batch, count)
     aff_ref[...] = aff
     emit(0)
@@ -353,11 +355,16 @@
     _, rows, pieces, share, width = send_ref.shape
     fill_acts(ap, aff, batch, x_ref, halo)
     part[:, 9 * channels :] = jnp.zeros((channels, part.shape[1] - 9 * channels), F32)
-    gather_taps(im, ap, False)
+    per = n // batch
+    total = jnp.zeros((channels, 9 * channels), F32)
     gp = gp_load()
-    part[:, : 9 * channels] = (
-        jnp.dot(gp[...], im[...], preferred_element_type=F32) * scale
-    )
+    for b in range(batch):
+        gather_taps(ims[b], b, ap, False)
+        emit(3 + b)
+        total = total + jnp.dot(
+            gp[:, b * per : (b + 1) * per], ims[b][...], preferred_element_type=F32
+        )
+    part[:, : 9 * channels] = total * scale
     for r in range(rows):
         for p in range(pieces):
             lane = slice(p * width, (p + 1) * width)
@@ -405,20 +412,16 @@
 
 
 def conv_kernel(batch, emit, *refs):
-    x_load, w_load, cb_load, aff_ref = refs[:4]
-    halo = refs[4:8]
-    temb_ref, out_ref, done_ref, ap, im = refs[8:]
-    x_ref = x_load()
+    w_load, x_load, cb_load = refs[:3]
+    im_loads = refs[3 : 3 + batch]
+    temb_ref, out_ref, done_ref = refs[3 + batch :]
     done_ref[...] = jnp.zeros_like(done_ref)
-    _, _, tall, w, c = ap.shape
-    per = (tall - 2) * w
-    fill_acts(ap, aff_ref[...], batch, x_ref, halo)
-    gather_taps(im, ap, False)
-    w_ref = w_load()
+    n, c = out_ref.shape
+    per = n // batch
+    x_ref, w = x_load(), w_load()[...].reshape(9 * c, c)
     bias = cb_load()[...].reshape(1, c)
-    w = w_ref[...].reshape(9 * c, c)
     for b in range(batch):
-        acc = jnp.dot(im[b * per : (b + 1) * per, :], w, preferred_element_type=F32)
+        acc = jnp.dot(im_loads[b]()[...], w, preferred_element_type=F32)
         here = slice(b * per, (b + 1) * per)
         out = x_ref[here, :].astype(F32) + acc + bias + temb_ref[b : b + 1, :]
         out_ref[here, :] = out.astype(BF16)
@@ -499,23 +502,32 @@
 
 
 def step_three(nz, a_got, a_keep, b_got, b_keep, s, s_got, own_ref, s_next, *refs):
-    s_next[...] = s[...] + s_got[...]
+    sums = s[...] + s_got[...]
+    high = sums.astype(BF16).astype(F32)
+    low = (sums - high).astype(BF16).astype(F32)
+    s_next[...] = high + low
     sends, held = refs[: nz - 1], refs[nz - 1]
     _, _, zb = place()
     half = nz // 2
+    share, width = own_ref.shape
+    rider = jnp.concatenate([high, low], axis=0)
+    rider = jnp.concatenate([rider, jnp.zeros((16, width - rider.shape[1]), F32)], axis=1)
     for z in range(half):
         held[z] = a_keep[z] + a_got[z].astype(F32)
         held[half + z] = b_keep[z] + b_got[z].astype(F32)
     own_ref[...] = held[zb]
     for k in range(1, nz):
-        sends[k - 1][...] = held[zb ^ k].astype(BF16)
+        sends[k - 1][:share, :] = held[zb ^ k].astype(BF16)
+        sends[k - 1][share:, :] = rider.astype(BF16)
 
 
 def step_four(nz, own_ref, s, *refs):
     total, sums = own_ref[...], s[...]
+    share, c = total.shape[0], sums.shape[1]
     for k in range(nz - 1):
-        total = total + refs[k][...].astype(F32)
-        sums = sums + refs[nz - 1 + k][...]
+        total = total + refs[k][:share, :].astype(F32)
+        rider = refs[k][share:, :].astype(F32)[:, :c]
+        sums = sums + (rider[:8] + rider[8:])
     refs[-2][...] = total.astype(BF16)
     refs[-1][...] = sums
 
@@ -615,13 +627,15 @@
     stats = lax.all_to_all(pay, AXES, 0, 0)
     halo = (left, right, top, low)
 
-    neighbours = pltpu.VMEM((n, 9 * channels), BF16)
+    per = n // batch
+    neighbours = pltpu.VMEM((per, 9 * channels), BF16)
     shifted = pltpu.VMEM((3, batch, high + 2, wide, channels), F32)
     nz = cols // 4
     share = channels // (2 * rows)
     relative = rows == 2 and nz >= 2 and share % 16 == 0
     pieces = cols // 2 if relative else 1
     width = -(-9 * channels // (LANES * pieces)) * LANES
+    width = max(width, -(-(channels + 1) // LANES) * LANES)
     padded = -(-channels // LANES) * LANES
     conv_flops = 2 * 9 * n * channels * channels
     if not relative:
@@ -641,17 +655,18 @@
         ),
         flops=conv_flops,
     )
-    aff, keep, send = call_far(
+    aff, keep, send, *taps = call_far(
         functools.partial(wgrad_kernel, batch, count, scale),
         (
             of((8, channels), F32),
             of((keep_rows, pieces, share, width), F32),
             of((1, keep_rows, pieces, share, width), BF16),
+            *[of((per, 9 * channels), BF16)] * batch,
         ),
         (stats, *halo),
         far=(x2, flipped, group_norm_gain, group_norm_bias),
         vmem=56,
-        scratch=(shifted, pltpu.VMEM((channels, pieces * width), F32), neighbours),
+        scratch=(shifted, pltpu.VMEM((channels, pieces * width), F32)),
         flops=conv_flops,
     )
 
@@ -692,12 +707,11 @@
         a_got, b_got = partner(a_send, 2), partner(b_send, cols)
         own, sums, *sends = call(
             functools.partial(step_three, nz),
-            (many((), F32), s_shape, *[many((), BF16)] * (nz - 1)),
+            (many((), F32), s_shape, *[of((share + 16, width), BF16)] * (nz - 1)),
             (a_got, a_keep, b_got, b_keep, sums, partner(sums, 2)),
             scratch=(pltpu.VMEM((nz, share, width), F32),),
         )
         gots = [partner(v, 4 * (k + 1)) for k, v in enumerate(sends)]
-        gots += [partner(sums, 4 * k) for k in range(1, nz)]
         second = (sums,)
     else:
         second = ()
@@ -706,11 +720,9 @@
     block_out, done = call_far(
         functools.partial(conv_kernel, batch),
         (of((n, channels), BF16), token),
-        (aff, *halo, temb),
-        far=(x2, w9, conv_b),
+        (temb,),
+        far=(w9, x2, conv_b, *taps),
         after=second,
-        vmem=58,
-        scratch=(shifted, neighbours),
         flops=conv_flops,
     )
 

time: 106 us -> 103 us (0.972)
  starting transfers between devices: 44.8 us -> 42 us
  waiting for transfers between devices: 9.42 us -> 11.5 us
  Pallas kernels: 40.6 us -> 38.6 us
    ppermute x23 -> x20, starting transfers between devices: 32.8 us -> 30 us  [partner(): return lax.ppermute(value, AXES, [(i, i ^ bit) for i in range(size)])]
    ppermute x23 -> x20, waiting for transfers between devices: 9.42 us -> 11.4 us  [partner(): return lax.ppermute(value, AXES, [(i, i ^ bit) for i in range(size)])]
    pallas_call x6, Pallas kernels: 38.2 us -> 36.2 us  [call_far(): pl.pallas_call(kernel, out_shape=tuple(outs), in_specs=[hbm] * len(ins) +...]
    dot_general x1, matrix products: 0.92 us -> 2.06 us  [local(): temb = jnp.dot(emb, time_w, preferred_element_type=F32)]
    unnamed x26 -> x24, local copies, waits for them, and re-layouts: 4.94 us -> 4.1 us
  transfers between devices with their start and end apart: 26 -> 23, of which waited for: 7 -> 8; matrix products, arithmetic and copies ran while one was open for 4% -> 5% of each run, Pallas kernels for 25% -> 19%
where the time goes in v8:
time: 103 us
  starting transfers between devices  42 us (41%)
  Pallas kernels  38.6 us (37%)
  waiting for transfers between devices  11.5 us (11%)
  local copies, waits for them, and re-layouts  4.84 us (5%)
  matrix products  4.8 us (5%)
    pallas_call x6, Pallas kernels, call_far(): pl.pallas_call(kernel, out_shape=tuple(outs), in_specs=[hbm] * len(ins) +...  36.2 us
    ppermute x20, starting transfers between devices, partner(): return lax.ppermute(value, AXES, [(i, i ^ bit) for i in range(size)])  30 us
    ppermute x20, waiting for transfers between devices, partner(): return lax.ppermute(value, AXES, [(i, i ^ bit) for i in range(size)])  11.4 us
    all_to_all x1, starting transfers between devices, local(): stats = lax.all_to_all(pay, AXES, 0, 0)  8.73 us
    unnamed x24, local copies, waits for them, and re-layouts  4.1 us
    ppermute x2, starting transfers between devices, shift(): return lax.ppermute(value, AXES, pairs)  3.33 us
    dot_general x1, matrix products, embed(): jnp.dot(first_hidden, embed_out, preferred_element_type=F32)  2.74 us
    pallas_call x6, Pallas kernels, call(): pl.pallas_call(kernel, out_shape=out_shape, in_specs=[pl.BlockSpec(memory...  2.35 us
  transfers between devices with their start and end apart: 23, of which 8 were waited for; matrix products, arithmetic and copies ran while one was open for 5% of the time, Pallas kernels for 19%

profile of v8, /device:TPU:0, one launch (start us, length us, event | category | flops | bytes accessed | tf_op | source)
XLA Modules:
  0.0 102.8 jit_solution(6293671974368648284)
XLA Ops:
  0.6 0.7 constant_dynamic-slice_fusion
  1.4 3.0 %collective-permute-start = (bf16[32,320]{1,0:T(8,128)(2,1)S(1)}, bf16[32,320]{1,0:T(8,128)(2,1)}, u32[]{:S(2)}, u32[]{:S(2)}) collective-permute-start(bf16[32,320]{1,0:T(8,128)(2,1)S(1)} %maximum_bitcast_fusion), channel_id=1, source_target_pairs={{0,16},{1,17},{2,18},{3,19},{4,20},{5,21},{6,22},{7,23},{8,24},{9,... | collective-permute-start | bytes 61448 | tf_op jit(solution)/shard_map/ppermute | solution.py:565
  4.4 1.9 %collective-permute-done.refs_2_.refs_3_.refs_4_.refs_5_.refs_7_.refs_8_ = bf16[32,320]{1,0:T(8,128)(2,1)} collective-permute-done((bf16[32,320]{1,0:T(8,128)(2,1)S(1)}, bf16[32,320]{1,0:T(8,128)(2,1)}, u32[]{:S(2)}, u32[]{:S(2)}) %collective-permute-start) | collective-permute-done | bytes 20512 | tf_op jit(solution)/shard_map/ppermute | solution.py:565
  6.3 3.3 %shard_map.153 = (f32[32,1,128]{2,1,0:T(1,128)}, f32[4,66,1,320]{3,2,1,0:T(1,128)}, f32[4,66,1,320]{3,2,1,0:T(1,128)}) custom-call(bf16[1024,320]{1,0:T(8,128)(2,1)} %bitcast.16, bf16[1024,320]{1,0:T(8,128)(2,1)} %bitcast.21, bf16[32,320]{1,0:T(8,128)(2,1)} %collective-permute-done.refs_2_.refs_3_.refs_4_.refs_5_.refs_7_.refs_8_, ...), custom_call_target="tpu_custom_call" | custom-call | bytes 2000000 | tf_op jit(solution)/shard_map/pallas_call | solution.py:111
  9.6 2.1 %collective-permute-start.1 = (f32[4,66,1,320]{3,2,1,0:T(1,128)}, f32[4,66,1,320]{3,2,1,0:T(1,128)}, u32[]{:S(2)}, u32[]{:S(2)}) collective-permute-start(f32[4,66,1,320]{3,2,1,0:T(1,128)} %get-tuple-element.45), channel_id=1, source_target_pairs={{0,1},{1,2},{2,3},{3,4},{4,5},{5,6},{6,7},{7,8},{8,9},{9,10},{10,1... | collective-permute-start | bytes 1013768 | tf_op jit(solution)/shard_map/ppermute | solution.py:576
  11.7 1.3 %collective-permute-start.2 = (f32[4,66,1,320]{3,2,1,0:T(1,128)}, f32[4,66,1,320]{3,2,1,0:T(1,128)}, u32[]{:S(2)}, u32[]{:S(2)}) collective-permute-start(f32[4,66,1,320]{3,2,1,0:T(1,128)} %get-tuple-element.46), channel_id=1, source_target_pairs={{1,0},{2,1},{3,2},{4,3},{5,4},{6,5},{7,6},{8,7},{9,8},{10,9},{11,1... | collective-permute-start | bytes 1013768 | tf_op jit(solution)/shard_map/ppermute | solution.py:576
  13.0 8.7 %all-to-all-start = ((f32[32,1,128]{2,1,0:T(1,128)}), f32[32,1,128]{2,1,0:T(1,128)}, u32[]{:S(2)}, u32[]{:S(2)}) async-start(f32[32,1,128]{2,1,0:T(1,128)} %get-tuple-element.48), calls=%async_computation | async-start | bytes 32768 | tf_op jit(solution)/shard_map/all_to_all | solution.py:627
  21.7 0.0 collective-permute-done.1.refs_2_.refs_5_
  21.7 0.0 collective-permute-done.2.refs_3_.refs_6_
  21.7 6.8 %shard_map.154 = (f32[1024,320]{1,0:T(8,128)}, f32[8,320]{1,0:T(8,128)}, bf16[320,1024]{1,0:T(8,128)(2,1)}) custom-call(bf16[1024,320]{1,0:T(8,128)(2,1)} %bitcast.22, bf16[9,320,320]{2,1,0:T(8,128)(2,1)} %bitcast.25, f32[4,66,1,320]{3,2,1,0:T(1,128)} %collective-permute-done.1.refs_2_.refs_5_, f32[4,66,1,320]{3,2,1,0:T(1,128)} %collective-permute-done.2.refs_3_.refs_6_, ...), custom_call_target="tpu_custom_call" | custom-call | flops 1887436800 | bytes 2000000 | tf_op jit(solution)/shard_map/pallas_call | solution.py:111
  28.5 0.1 all-to-all-done.refs_4_
  28.6 9.0 %shard_map.155 = (f32[8,320]{1,0:T(8,128)}, f32[2,8,80,384]{3,2,1,0:T(8,128)}, bf16[1,2,8,80,384]{4,3,2,1,0:T(8,128)(2,1)}, bf16[512,2880]{1,0:T(8,128)(2,1)}, bf16[512,2880]{1,0:T(8,128)(2,1)}) custom-call(bf16[1024,320]{1,0:T(8,128)(2,1)} %bitcast.17, bf16[320,1024]{1,0:T(8,128)(2,1)} %get-tuple-element.47.refs_1_, f32[320]{0:T(512)} %refs_3_.3, ...), custom_call_target="tpu_custom_call" | custom-call | flops 1887436800 | bytes 2000000 | tf_op jit(solution)/shard_map/pallas_call | solution.py:111
  37.6 1.5 %collective-permute-start.3 = (bf16[2,8,80,384]{3,2,1,0:T(8,128)(2,1)}, bf16[2,8,80,384]{3,2,1,0:T(8,128)(2,1)S(1)}, u32[]{:S(2)}, u32[]{:S(2)}) collective-permute-start(bf16[2,8,80,384]{3,2,1,0:T(8,128)(2,1)} %bitcast.29), channel_id=1, source_target_pairs={{0,1},{1,0},{2,3},{3,2},{4,5},{5,4},{6,7},{7,6},{8,9},{9,8},{10,11... | collective-permute-start | bytes 2949128 | tf_op jit(solution)/shard_map/ppermute | solution.py:565
  39.1 0.1 fusion.7
  39.3 2.3 %collective-permute-done.3.refs_1_ = bf16[2,8,80,384]{3,2,1,0:T(8,128)(2,1)S(1)} collective-permute-done((bf16[2,8,80,384]{3,2,1,0:T(8,128)(2,1)}, bf16[2,8,80,384]{3,2,1,0:T(8,128)(2,1)S(1)}, u32[]{:S(2)}, u32[]{:S(2)}) %collective-permute-start.3) | collective-permute-done | bytes 983072 | tf_op jit(solution)/shard_map/ppermute | solution.py:565
  41.5 1.5 %copy-done = f32[2,8,80,384]{3,2,1,0:T(8,128)S(1)} copy-done((f32[2,8,80,384]{3,2,1,0:T(8,128)S(1)}, f32[2,8,80,384]{3,2,1,0:T(8,128)}, u32[]{:S(2)}) %copy-start) | copy-done | bytes 1966104
  43.1 0.2 shard_map.156
  43.2 0.0 copy-start.7
  43.2 0.6 copy-done.7
  43.8 4.5 %shard_map.157 = (f32[1024,320]{1,0:T(8,128)}, f32[8,320]{1,0:T(8,128)}) custom-call(bf16[1024,320]{1,0:T(8,128)(2,1)} %bitcast.18, f32[1024,320]{1,0:T(8,128)} %get-tuple-element.57.refs_1_, f32[8,320]{1,0:T(8,128)} %get-tuple-element.58.refs_2_.refs_4_, f32[8,320]{1,0:T(8,128)} %get-tuple-element.59.refs_3_, f32[8,128]{1,0:T(8,128)} %copy-done.7), custom_call_target="tpu_custom_call" | custom-call | flops 6553600 | bytes 2000000 | tf_op jit(solution)/shard_map/pallas_call | solution.py:111
  48.3 0.0 copy-start.4
  48.3 0.4 collective-permute-start.6
  48.8 1.7 %collective-permute-start.4 = (bf16[2,2,80,384]{3,2,1,0:T(8,128)(2,1)S(1)}, bf16[2,2,80,384]{3,2,1,0:T(8,128)(2,1)S(1)}, u32[]{:S(2)}, u32[]{:S(2)}) collective-permute-start(bf16[2,2,80,384]{3,2,1,0:T(8,128)(2,1)S(1)} %get-tuple-element.53), channel_id=1, source_target_pairs={{0,16},{1,17},{2,18},{3,19},{4,20},{5,21},{6,22},{7,23},{8,24},{9,... | collective-permute-start | bytes 737288 | tf_op jit(solution)/shard_map/ppermute | solution.py:565
  50.5 2.4 %collective-permute-start.5 = (bf16[2,2,80,384]{3,2,1,0:T(8,128)(2,1)S(1)}, bf16[2,2,80,384]{3,2,1,0:T(8,128)(2,1)S(1)}, u32[]{:S(2)}, u32[]{:S(2)}) collective-permute-start(bf16[2,2,80,384]{3,2,1,0:T(8,128)(2,1)S(1)} %get-tuple-element.55), channel_id=1, source_target_pairs={{0,2},{1,3},{2,0},{3,1},{4,6},{5,7},{6,4},{7,5},{8,10},{9,11},{10,... | collective-permute-start | bytes 737288 | tf_op jit(solution)/shard_map/ppermute | solution.py:565
  52.9 2.7 %fusion.1.refs_7_ = bf16[2,1280]{1,0:T(2,128)(2,1)S(1)} fusion(bf16[1280,1280]{1,0:T(8,128)(2,1)} %param.17, bf16[320,1280]{1,0:T(8,128)(2,1)S(1)} %copy-done.8, bf16[2,160]{1,0:T(2,128)(2,1)S(1)} %get-tuple-element.84, bf16[2,160]{1,0:T(2,128)(2,1)S(1)} %get-tuple-element.83), kind=kOutput, calls=%fused_computation.4 | convolution fusion | flops 8220160 | bytes 4102400 | tf_op jit(solution)/shard_map/dot_general | solution.py:560
  55.7 0.0 collective-permute-done.6.refs_5_
  55.7 1.1 %collective-permute-done.4.refs_0_ = bf16[2,2,80,384]{3,2,1,0:T(8,128)(2,1)S(1)} collective-permute-done((bf16[2,2,80,384]{3,2,1,0:T(8,128)(2,1)S(1)}, bf16[2,2,80,384]{3,2,1,0:T(8,128)(2,1)S(1)}, u32[]{:S(2)}, u32[]{:S(2)}) %collective-permute-start.4) | collective-permute-done | bytes 245792 | tf_op jit(solution)/shard_map/ppermute | solution.py:565
  56.8 2.1 %collective-permute-done.5.refs_2_ = bf16[2,2,80,384]{3,2,1,0:T(8,128)(2,1)S(1)} collective-permute-done((bf16[2,2,80,384]{3,2,1,0:T(8,128)(2,1)S(1)}, bf16[2,2,80,384]{3,2,1,0:T(8,128)(2,1)S(1)}, u32[]{:S(2)}, u32[]{:S(2)}) %collective-permute-start.5) | collective-permute-done | bytes 245792 | tf_op jit(solution)/shard_map/ppermute | solution.py:565
  58.9 0.1 shard_map.158
  59.0 1.8 %collective-permute-start.7 = (bf16[2,80,384]{2,1,0:T(8,128)(2,1)S(1)}, bf16[2,80,384]{2,1,0:T(8,128)(2,1)S(1)}, u32[]{:S(2)}, u32[]{:S(2)}) collective-permute-start(bf16[2,80,384]{2,1,0:T(8,128)(2,1)S(1)} %get-tuple-element.62), channel_id=1, source_target_pairs={{0,2},{1,3},{2,0},{3,1},{4,6},{5,7},{6,4},{7,5},{8,10},{9,11},{10,... | collective-permute-start | bytes 368648 | tf_op jit(solution)/shard_map/ppermute | solution.py:565
  60.8 0.4 collective-permute-start.8
  61.2 0.3 collective-permute-start.9
  61.5 2.1 %fusion.22.refs_5_ = f32[2,320]{1,0:T(2,128)} fusion(bf16[2,1280]{1,0:T(2,128)(2,1)S(1)} %fusion.1.refs_7_, bf16[1280,320]{0,1:T(8,128)(2,1)} %param.18), kind=kOutput, calls=%fused_computation.20 | convolution fusion | flops 1638400 | bytes 826880 | tf_op jit(solution)/shard_map/dot_general | solution.py:698
  63.5 1.4 %collective-permute-done.9.refs_5_ = f32[8,320]{1,0:T(8,128)S(1)} collective-permute-done((f32[8,320]{1,0:T(8,128)S(1)}, f32[8,320]{1,0:T(8,128)S(1)}, u32[]{:S(2)}, u32[]{:S(2)}) %collective-permute-start.9) | collective-permute-done | bytes 10272 | tf_op jit(solution)/shard_map/ppermute | solution.py:565
  64.9 0.0 collective-permute-done.7.refs_0_
  64.9 0.8 collective-permute-done.8.refs_2_
  65.7 0.1 shard_map.159
  65.8 0.0 copy-start.1
  65.8 0.6 copy-done.1
  66.4 1.7 %collective-permute-start.10 = (bf16[96,384]{1,0:T(8,128)(2,1)S(1)}, bf16[96,384]{1,0:T(8,128)(2,1)S(1)}, u32[]{:S(2)}, u32[]{:S(2)}) collective-permute-start(bf16[96,384]{1,0:T(8,128)(2,1)S(1)} %get-tuple-element.71), channel_id=1, source_target_pairs={{0,4},{1,5},{2,6},{3,7},{4,0},{5,1},{6,2},{7,3},{8,12},{9,13},{10,... | collective-permute-start | bytes 221192 | tf_op jit(solution)/shard_map/ppermute | solution.py:565
  68.1 2.0 %collective-permute-start.11 = (bf16[96,384]{1,0:T(8,128)(2,1)S(1)}, bf16[96,384]{1,0:T(8,128)(2,1)S(1)}, u32[]{:S(2)}, u32[]{:S(2)}) collective-permute-start(bf16[96,384]{1,0:T(8,128)(2,1)S(1)} %get-tuple-element.72), channel_id=1, source_target_pairs={{0,8},{1,9},{2,10},{3,11},{4,12},{5,13},{6,14},{7,15},{8,0},{9,1},... | collective-permute-start | bytes 221192 | tf_op jit(solution)/shard_map/ppermute | solution.py:565
  70.1 0.7 collective-permute-start.12
  70.8 8.0 %shard_map.160 = (bf16[1024,320]{1,0:T(8,128)(2,1)}, f32[8,128]{1,0:T(8,128)}) custom-call(bf16[9,320,320]{2,1,0:T(8,128)(2,1)} %bitcast.26, bf16[1024,320]{1,0:T(8,128)(2,1)} %bitcast.19, f32[320]{0:T(512)} %refs_2_.3, bf16[512,2880]{1,0:T(8,128)(2,1)} %get-tuple-element.49.refs_3_, bf16[512,2880]{1,0:T(8,128)(2,1)} %get-tuple-element.50.refs_4_, ...), custom_call_target="tpu_custom_call" | custom-call | flops 1887436800 | bytes 2000000 | tf_op jit(solution)/shard_map/pallas_call | solution.py:111
  78.8 0.0 collective-permute-done.10.refs_2_
  78.8 0.0 collective-permute-done.11.refs_3_
  78.8 0.0 copy-start.6
  78.8 0.7 copy-done.6
  79.6 1.1 %collective-permute-start.14 = (bf16[80,384]{1,0:T(8,128)(2,1)S(1)}, bf16[80,384]{1,0:T(8,128)(2,1)S(1)}, u32[]{:S(2)}, u32[]{:S(2)}) collective-permute-start(bf16[80,384]{1,0:T(8,128)(2,1)S(1)} %get-tuple-element.77.refs_0_), channel_id=1, source_target_pairs={{0,2},{1,3},{2,0},{3,1},{4,6},{5,7},{6,4},{7,5},{8,10},{9,11},{10,... | collective-permute-start | bytes 184328 | tf_op jit(solution)/shard_map/ppermute | solution.py:565
  80.7 0.9 collective-permute-start.15
  81.6 0.8 collective-permute-start.13
  82.5 1.5 %collective-permute-start.16 = (bf16[80,384]{1,0:T(8,128)(2,1)S(1)}, bf16[80,384]{1,0:T(8,128)(2,1)S(1)}, u32[]{:S(2)}, u32[]{:S(2)}) collective-permute-start(bf16[80,384]{1,0:T(8,128)(2,1)S(1)} %get-tuple-element.77.refs_0_), channel_id=1, source_target_pairs={{0,6},{1,7},{2,4},{3,5},{4,2},{5,3},{6,0},{7,1},{8,14},{9,15},{10,... | collective-permute-start | bytes 184328 | tf_op jit(solution)/shard_map/ppermute | solution.py:565
  84.0 2.0 %collective-permute-start.17 = (bf16[80,384]{1,0:T(8,128)(2,1)S(1)}, bf16[80,384]{1,0:T(8,128)(2,1)S(1)}, u32[]{:S(2)}, u32[]{:S(2)}) collective-permute-start(bf16[80,384]{1,0:T(8,128)(2,1)S(1)} %get-tuple-element.77.refs_0_), channel_id=1, source_target_pairs={{0,8},{1,9},{2,10},{3,11},{4,12},{5,13},{6,14},{7,15},{8,0},{9,1},... | collective-permute-start | bytes 184328 | tf_op jit(solution)/shard_map/ppermute | solution.py:565
  86.0 2.6 %collective-permute-start.18 = (bf16[80,384]{1,0:T(8,128)(2,1)S(1)}, bf16[80,384]{1,0:T(8,128)(2,1)S(1)}, u32[]{:S(2)}, u32[]{:S(2)}) collective-permute-start(bf16[80,384]{1,0:T(8,128)(2,1)S(1)} %get-tuple-element.77.refs_0_), channel_id=1, source_target_pairs={{0,10},{1,11},{2,8},{3,9},{4,14},{5,15},{6,12},{7,13},{8,2},{9,3},... | collective-permute-start | bytes 184328 | tf_op jit(solution)/shard_map/ppermute | solution.py:565
  88.5 0.0 collective-permute-done.14.refs_1_
  88.5 2.7 %collective-permute-start.19 = (bf16[80,384]{1,0:T(8,128)(2,1)S(1)}, bf16[80,384]{1,0:T(8,128)(2,1)S(1)}, u32[]{:S(2)}, u32[]{:S(2)}) collective-permute-start(bf16[80,384]{1,0:T(8,128)(2,1)S(1)} %get-tuple-element.77.refs_0_), channel_id=1, source_target_pairs={{0,12},{1,13},{2,14},{3,15},{4,8},{5,9},{6,10},{7,11},{8,4},{9,5},... | collective-permute-start | bytes 184328 | tf_op jit(solution)/shard_map/ppermute | solution.py:565
  91.3 2.3 %collective-permute-start.20 = (bf16[80,384]{1,0:T(8,128)(2,1)S(1)}, bf16[80,384]{1,0:T(8,128)(2,1)S(1)}, u32[]{:S(2)}, u32[]{:S(2)}) collective-permute-start(bf16[80,384]{1,0:T(8,128)(2,1)S(1)} %get-tuple-element.77.refs_0_), channel_id=1, source_target_pairs={{0,14},{1,15},{2,12},{3,13},{4,10},{5,11},{6,8},{7,9},{8,6},{9,7},... | collective-permute-start | bytes 184328 | tf_op jit(solution)/shard_map/ppermute | solution.py:565
  93.5 4.6 %shard_map.162 = (f32[1024,320]{1,0:T(8,128)}, f32[320]{0:T(512)}, f32[320]{0:T(512)}, f32[320]{0:T(512)}, f32[320,1280]{1,0:T(8,128)}, /*index=5*/f32[8,128]{1,0:T(8,128)}) custom-call(bf16[1024,320]{1,0:T(8,128)(2,1)} %bitcast.20, bf16[1024,320]{1,0:T(8,128)(2,1)} %bitcast.23, f32[1024,320]{1,0:T(8,128)} %get-tuple-element.69.refs_2_, f32[320]{0:T(512)} %refs_3_.3, ...), custom_call_target="tpu_custom_call" | custom-call | flops 2621440 | bytes 2000000 | tf_op jit(solution)/shard_map/pallas_call | solution.py:111
  98.2 0.0 collective-permute-done.16.refs_3_
  98.2 0.0 collective-permute-done.19.refs_6_
  98.3 0.7 copy-done.5
  98.9 0.1 shard_map.163.refs_0_
  99.0 0.1 collective-permute-start.21
  99.1 1.9 %collective-permute-done.21.refs_1_ = bf16[80,3072]{1,0:T(8,128)(2,1)S(1)} collective-permute-done((bf16[80,3072]{1,0:T(8,128)(2,1)S(1)}, bf16[80,3072]{1,0:T(8,128)(2,1)S(1)}, u32[]{:S(2)}, u32[]{:S(2)}) %collective-permute-start.21) | collective-permute-done | bytes 491552 | tf_op jit(solution)/shard_map/ppermute | solution.py:565
  100.9 1.9 %shard_map.164 = f32[9,160,320]{2,1,0:T(8,128)} custom-call(bf16[80,3072]{1,0:T(8,128)(2,1)S(1)} %shard_map.163.refs_0_, bf16[80,3072]{1,0:T(8,128)(2,1)S(1)} %collective-permute-done.21.refs_1_), custom_call_target="tpu_custom_call" | custom-call | bytes 2000000 | tf_op jit(solution)/shard_map/pallas_call | solution.py:53
  (25 shorter events, 0.1 us)
Async XLA Ops:
  1.4 4.9 %collective-permute-start = (bf16[32,320]{1,0:T(8,128)(2,1)S(1)}, bf16[32,320]{1,0:T(8,128)(2,1)}, u32[]{:S(2)}, u32[]{:S(2)}) collective-permute-start(bf16[32,320]{1,0:T(8,128)(2,1)S(1)} %maximum_bitcast_fusion), channel_id=1, source_target_pairs={{0,16},{1,17},{2,18},{3,19},{4,20},{5,21},{6,22},{7,23},{8,24},{9,... | collective-permute-start | bytes 61448 | tf_op jit(solution)/shard_map/ppermute | solution.py:565
  9.6 12.1 %collective-permute-start.1 = (f32[4,66,1,320]{3,2,1,0:T(1,128)}, f32[4,66,1,320]{3,2,1,0:T(1,128)}, u32[]{:S(2)}, u32[]{:S(2)}) collective-permute-start(f32[4,66,1,320]{3,2,1,0:T(1,128)} %get-tuple-element.45), channel_id=1, source_target_pairs={{0,1},{1,2},{2,3},{3,4},{4,5},{5,6},{6,7},{7,8},{8,9},{9,10},{10,1... | collective-permute-start | bytes 1013768 | tf_op jit(solution)/shard_map/ppermute | solution.py:576
  11.7 10.0 %collective-permute-start.2 = (f32[4,66,1,320]{3,2,1,0:T(1,128)}, f32[4,66,1,320]{3,2,1,0:T(1,128)}, u32[]{:S(2)}, u32[]{:S(2)}) collective-permute-start(f32[4,66,1,320]{3,2,1,0:T(1,128)} %get-tuple-element.46), channel_id=1, source_target_pairs={{1,0},{2,1},{3,2},{4,3},{5,4},{6,5},{7,6},{8,7},{9,8},{10,9},{11,1... | collective-permute-start | bytes 1013768 | tf_op jit(solution)/shard_map/ppermute | solution.py:576
  13.0 15.6 %all-to-all-start = ((f32[32,1,128]{2,1,0:T(1,128)}), f32[32,1,128]{2,1,0:T(1,128)}, u32[]{:S(2)}, u32[]{:S(2)}) async-start(f32[32,1,128]{2,1,0:T(1,128)} %get-tuple-element.48), calls=%async_computation | async-start | bytes 32768 | tf_op jit(solution)/shard_map/all_to_all | solution.py:627
  28.6 10.5 %copy-start.11 = (s32[2]{0:T(128)S(1)}, s32[2]{0:T(128)}, u32[]{:S(2)}) copy-start(s32[2]{0:T(128)} %param.11) | copy-start | bytes 28
  37.6 3.9 %collective-permute-start.3 = (bf16[2,8,80,384]{3,2,1,0:T(8,128)(2,1)}, bf16[2,8,80,384]{3,2,1,0:T(8,128)(2,1)S(1)}, u32[]{:S(2)}, u32[]{:S(2)}) collective-permute-start(bf16[2,8,80,384]{3,2,1,0:T(8,128)(2,1)} %bitcast.29), channel_id=1, source_target_pairs={{0,1},{1,0},{2,3},{3,2},{4,5},{5,4},{6,7},{7,6},{8,9},{9,8},{10,11... | collective-permute-start | bytes 2949128 | tf_op jit(solution)/shard_map/ppermute | solution.py:565
  41.5 1.5 %copy-start = (f32[2,8,80,384]{3,2,1,0:T(8,128)S(1)}, f32[2,8,80,384]{3,2,1,0:T(8,128)}, u32[]{:S(2)}) copy-start(f32[2,8,80,384]{3,2,1,0:T(8,128)} %get-tuple-element.51.refs_0_) | copy-start | bytes 5898244
  43.1 9.9 %copy-start.8 = (bf16[320,1280]{1,0:T(8,128)(2,1)S(1)}, bf16[320,1280]{1,0:T(8,128)(2,1)}, u32[]{:S(2)}) copy-start(bf16[320,1280]{1,0:T(8,128)(2,1)} %param.16) | copy-start | bytes 2457604
  43.2 0.6 copy-start.7
  48.3 10.6 %copy-start.4 = (f32[8,320]{1,0:T(8,128)S(1)}, f32[8,320]{1,0:T(8,128)}, u32[]{:S(2)}) copy-start(f32[8,320]{1,0:T(8,128)} %get-tuple-element.61.refs_4_) | copy-start | bytes 30724
  48.3 7.3 %collective-permute-start.6 = (f32[8,320]{1,0:T(8,128)}, f32[8,320]{1,0:T(8,128)S(1)}, u32[]{:S(2)}, u32[]{:S(2)}) collective-permute-start(f32[8,320]{1,0:T(8,128)} %get-tuple-element.61.refs_4_), channel_id=1, source_target_pairs={{0,1},{1,0},{2,3},{3,2},{4,5},{5,4},{6,7},{7,6},{8,9},{9,8},{10,11... | collective-permute-start | bytes 30728 | tf_op jit(solution)/shard_map/ppermute | solution.py:565
  48.8 8.0 %collective-permute-start.4 = (bf16[2,2,80,384]{3,2,1,0:T(8,128)(2,1)S(1)}, bf16[2,2,80,384]{3,2,1,0:T(8,128)(2,1)S(1)}, u32[]{:S(2)}, u32[]{:S(2)}) collective-permute-start(bf16[2,2,80,384]{3,2,1,0:T(8,128)(2,1)S(1)} %get-tuple-element.53), channel_id=1, source_target_pairs={{0,16},{1,17},{2,18},{3,19},{4,20},{5,21},{6,22},{7,23},{8,24},{9,... | collective-permute-start | bytes 737288 | tf_op jit(solution)/shard_map/ppermute | solution.py:565
  50.5 8.4 %collective-permute-start.5 = (bf16[2,2,80,384]{3,2,1,0:T(8,128)(2,1)S(1)}, bf16[2,2,80,384]{3,2,1,0:T(8,128)(2,1)S(1)}, u32[]{:S(2)}, u32[]{:S(2)}) collective-permute-start(bf16[2,2,80,384]{3,2,1,0:T(8,128)(2,1)S(1)} %get-tuple-element.55), channel_id=1, source_target_pairs={{0,2},{1,3},{2,0},{3,1},{4,6},{5,7},{6,4},{7,5},{8,10},{9,11},{10,... | collective-permute-start | bytes 737288 | tf_op jit(solution)/shard_map/ppermute | solution.py:565
  55.7 23.1 %copy-start.9 = (bf16[2,1280]{1,0:T(2,128)(2,1)}, bf16[2,1280]{1,0:T(2,128)(2,1)S(1)}, u32[]{:S(2)}) copy-start(bf16[2,1280]{1,0:T(2,128)(2,1)S(1)} %fusion.1.refs_7_) | copy-start | bytes 15364
  59.0 5.9 %collective-permute-start.7 = (bf16[2,80,384]{2,1,0:T(8,128)(2,1)S(1)}, bf16[2,80,384]{2,1,0:T(8,128)(2,1)S(1)}, u32[]{:S(2)}, u32[]{:S(2)}) collective-permute-start(bf16[2,80,384]{2,1,0:T(8,128)(2,1)S(1)} %get-tuple-element.62), channel_id=1, source_target_pairs={{0,2},{1,3},{2,0},{3,1},{4,6},{5,7},{6,4},{7,5},{8,10},{9,11},{10,... | collective-permute-start | bytes 368648 | tf_op jit(solution)/shard_map/ppermute | solution.py:565
  60.8 4.9 %collective-permute-start.8 = (bf16[2,80,384]{2,1,0:T(8,128)(2,1)S(1)}, bf16[2,80,384]{2,1,0:T(8,128)(2,1)S(1)}, u32[]{:S(2)}, u32[]{:S(2)}) collective-permute-start(bf16[2,80,384]{2,1,0:T(8,128)(2,1)S(1)} %get-tuple-element.64), channel_id=1, source_target_pairs={{0,16},{1,17},{2,18},{3,19},{4,20},{5,21},{6,22},{7,23},{8,24},{9,... | collective-permute-start | bytes 368648 | tf_op jit(solution)/shard_map/ppermute | solution.py:565
  61.2 3.7 %collective-permute-start.9 = (f32[8,320]{1,0:T(8,128)S(1)}, f32[8,320]{1,0:T(8,128)S(1)}, u32[]{:S(2)}, u32[]{:S(2)}) collective-permute-start(f32[8,320]{1,0:T(8,128)S(1)} %get-tuple-element.66.refs_4_), channel_id=1, source_target_pairs={{0,2},{1,3},{2,0},{3,1},{4,6},{5,7},{6,4},{7,5},{8,10},{9,11},{10,... | collective-permute-start | bytes 30728 | tf_op jit(solution)/shard_map/ppermute | solution.py:565
  65.8 0.6 copy-start.1
  66.4 12.4 %collective-permute-start.10 = (bf16[96,384]{1,0:T(8,128)(2,1)S(1)}, bf16[96,384]{1,0:T(8,128)(2,1)S(1)}, u32[]{:S(2)}, u32[]{:S(2)}) collective-permute-start(bf16[96,384]{1,0:T(8,128)(2,1)S(1)} %get-tuple-element.71), channel_id=1, source_target_pairs={{0,4},{1,5},{2,6},{3,7},{4,0},{5,1},{6,2},{7,3},{8,12},{9,13},{10,... | collective-permute-start | bytes 221192 | tf_op jit(solution)/shard_map/ppermute | solution.py:565
  68.1 10.7 %collective-permute-start.11 = (bf16[96,384]{1,0:T(8,128)(2,1)S(1)}, bf16[96,384]{1,0:T(8,128)(2,1)S(1)}, u32[]{:S(2)}, u32[]{:S(2)}) collective-permute-start(bf16[96,384]{1,0:T(8,128)(2,1)S(1)} %get-tuple-element.72), channel_id=1, source_target_pairs={{0,8},{1,9},{2,10},{3,11},{4,12},{5,13},{6,14},{7,15},{8,0},{9,1},... | collective-permute-start | bytes 221192 | tf_op jit(solution)/shard_map/ppermute | solution.py:565
  70.1 8.7 %collective-permute-start.12 = (bf16[96,384]{1,0:T(8,128)(2,1)S(1)}, bf16[96,384]{1,0:T(8,128)(2,1)S(1)}, u32[]{:S(2)}, u32[]{:S(2)}) collective-permute-start(bf16[96,384]{1,0:T(8,128)(2,1)S(1)} %get-tuple-element.73), channel_id=1, source_target_pairs={{0,12},{1,13},{2,14},{3,15},{4,8},{5,9},{6,10},{7,11},{8,4},{9,5},... | collective-permute-start | bytes 221192 | tf_op jit(solution)/shard_map/ppermute | solution.py:565
  70.8 8.1 %copy-start.2 = (f32[8,320]{1,0:T(8,128)S(1)}, f32[8,320]{1,0:T(8,128)}, u32[]{:S(2)}) copy-start(f32[8,320]{1,0:T(8,128)} %copy-done.1) | copy-start | bytes 30724
  78.8 0.7 copy-start.6
  79.6 14.0 %copy-start.3 = (f32[8,320]{1,0:T(8,128)}, f32[8,320]{1,0:T(8,128)S(1)}, u32[]{:S(2)}) copy-start(f32[8,320]{1,0:T(8,128)S(1)} %get-tuple-element.75.refs_5_) | copy-start | bytes 30724
  79.6 9.0 %collective-permute-start.14 = (bf16[80,384]{1,0:T(8,128)(2,1)S(1)}, bf16[80,384]{1,0:T(8,128)(2,1)S(1)}, u32[]{:S(2)}, u32[]{:S(2)}) collective-permute-start(bf16[80,384]{1,0:T(8,128)(2,1)S(1)} %get-tuple-element.77.refs_0_), channel_id=1, source_target_pairs={{0,2},{1,3},{2,0},{3,1},{4,6},{5,7},{6,4},{7,5},{8,10},{9,11},{10,... | collective-permute-start | bytes 184328 | tf_op jit(solution)/shard_map/ppermute | solution.py:565
  80.7 10.5 %collective-permute-start.15 = (bf16[80,384]{1,0:T(8,128)(2,1)S(1)}, bf16[80,384]{1,0:T(8,128)(2,1)S(1)}, u32[]{:S(2)}, u32[]{:S(2)}) collective-permute-start(bf16[80,384]{1,0:T(8,128)(2,1)S(1)} %get-tuple-element.77.refs_0_), channel_id=1, source_target_pairs={{0,4},{1,5},{2,6},{3,7},{4,0},{5,1},{6,2},{7,3},{8,12},{9,13},{10,... | collective-permute-start | bytes 184328 | tf_op jit(solution)/shard_map/ppermute | solution.py:565
  81.6 4.4 %collective-permute-start.13 = (f32[8,320]{1,0:T(8,128)S(1)}, f32[8,320]{1,0:T(8,128)S(1)}, u32[]{:S(2)}, u32[]{:S(2)}) collective-permute-start(f32[8,320]{1,0:T(8,128)S(1)} %get-tuple-element.75.refs_5_), channel_id=1, source_target_pairs={{0,16},{1,17},{2,18},{3,19},{4,20},{5,21},{6,22},{7,23},{8,24},{9,... | collective-permute-start | bytes 30728 | tf_op jit(solution)/shard_map/ppermute | solution.py:565
  82.5 15.7 %collective-permute-start.16 = (bf16[80,384]{1,0:T(8,128)(2,1)S(1)}, bf16[80,384]{1,0:T(8,128)(2,1)S(1)}, u32[]{:S(2)}, u32[]{:S(2)}) collective-permute-start(bf16[80,384]{1,0:T(8,128)(2,1)S(1)} %get-tuple-element.77.refs_0_), channel_id=1, source_target_pairs={{0,6},{1,7},{2,4},{3,5},{4,2},{5,3},{6,0},{7,1},{8,14},{9,15},{10,... | collective-permute-start | bytes 184328 | tf_op jit(solution)/shard_map/ppermute | solution.py:565
  84.0 14.2 %collective-permute-start.17 = (bf16[80,384]{1,0:T(8,128)(2,1)S(1)}, bf16[80,384]{1,0:T(8,128)(2,1)S(1)}, u32[]{:S(2)}, u32[]{:S(2)}) collective-permute-start(bf16[80,384]{1,0:T(8,128)(2,1)S(1)} %get-tuple-element.77.refs_0_), channel_id=1, source_target_pairs={{0,8},{1,9},{2,10},{3,11},{4,12},{5,13},{6,14},{7,15},{8,0},{9,1},... | collective-permute-start | bytes 184328 | tf_op jit(solution)/shard_map/ppermute | solution.py:565
  86.0 7.6 %copy-start.10 = (f32[8,320]{1,0:T(8,128)}, f32[8,320]{1,0:T(8,128)S(1)}, u32[]{:S(2)}) copy-start(f32[8,320]{1,0:T(8,128)S(1)} %collective-permute-done.13.refs_6_) | copy-start | bytes 30724
  86.0 12.2 %collective-permute-start.18 = (bf16[80,384]{1,0:T(8,128)(2,1)S(1)}, bf16[80,384]{1,0:T(8,128)(2,1)S(1)}, u32[]{:S(2)}, u32[]{:S(2)}) collective-permute-start(bf16[80,384]{1,0:T(8,128)(2,1)S(1)} %get-tuple-element.77.refs_0_), channel_id=1, source_target_pairs={{0,10},{1,11},{2,8},{3,9},{4,14},{5,15},{6,12},{7,13},{8,2},{9,3},... | collective-permute-start | bytes 184328 | tf_op jit(solution)/shard_map/ppermute | solution.py:565
  88.5 9.7 %collective-permute-start.19 = (bf16[80,384]{1,0:T(8,128)(2,1)S(1)}, bf16[80,384]{1,0:T(8,128)(2,1)S(1)}, u32[]{:S(2)}, u32[]{:S(2)}) collective-permute-start(bf16[80,384]{1,0:T(8,128)(2,1)S(1)} %get-tuple-element.77.refs_0_), channel_id=1, source_target_pairs={{0,12},{1,13},{2,14},{3,15},{4,8},{5,9},{6,10},{7,11},{8,4},{9,5},... | collective-permute-start | bytes 184328 | tf_op jit(solution)/shard_map/ppermute | solution.py:565
  91.3 7.0 %collective-permute-start.20 = (bf16[80,384]{1,0:T(8,128)(2,1)S(1)}, bf16[80,384]{1,0:T(8,128)(2,1)S(1)}, u32[]{:S(2)}, u32[]{:S(2)}) collective-permute-start(bf16[80,384]{1,0:T(8,128)(2,1)S(1)} %get-tuple-element.77.refs_0_), channel_id=1, source_target_pairs={{0,14},{1,15},{2,12},{3,13},{4,10},{5,11},{6,8},{7,9},{8,6},{9,7},... | collective-permute-start | bytes 184328 | tf_op jit(solution)/shard_map/ppermute | solution.py:565
  98.3 0.7 copy-start.5
  99.0 1.9 %collective-permute-start.21 = (bf16[80,3072]{1,0:T(8,128)(2,1)S(1)}, bf16[80,3072]{1,0:T(8,128)(2,1)S(1)}, u32[]{:S(2)}, u32[]{:S(2)}) collective-permute-start(bf16[80,3072]{1,0:T(8,128)(2,1)S(1)} %shard_map.163.refs_0_), channel_id=1, source_target_pairs={{0,1},{1,0},{2,3},{3,2},{4,5},{5,4},{6,7},{7,6},{8,9},{9,8},{10,11... | collective-permute-start | bytes 1474568 | tf_op jit(solution)/shard_map/ppermute | solution.py:565

commit v9 on v8

--- a/solution.py
+++ b/solution.py
@@ -412,16 +412,19 @@
 
 
 def conv_kernel(batch, emit, *refs):
-    w_load, x_load, cb_load = refs[:3]
-    im_loads = refs[3 : 3 + batch]
+    w_load = refs[0]
+    im_loads = refs[1 : 1 + batch]
+    x_load, cb_load = refs[1 + batch : 3 + batch]
     temb_ref, out_ref, done_ref = refs[3 + batch :]
     done_ref[...] = jnp.zeros_like(done_ref)
     n, c = out_ref.shape
     per = n // batch
-    x_ref, w = x_load(), w_load()[...].reshape(9 * c, c)
-    bias = cb_load()[...].reshape(1, c)
+    w = w_load()[...].reshape(9 * c, c)
     for b in range(batch):
         acc = jnp.dot(im_loads[b]()[...], w, preferred_element_type=F32)
+        if b == 0:
+            x_ref = x_load()
+            bias = cb_load()[...].reshape(1, c)
         here = slice(b * per, (b + 1) * per)
         out = x_ref[here, :].astype(F32) + acc + bias + temb_ref[b : b + 1, :]
         out_ref[here, :] = out.astype(BF16)
@@ -430,8 +433,7 @@
 
 def input_kernel(batch, count, scale, emit, *refs):
     x_load, g_load, dn_load, gain_load, aff_ref, part_ref, other_ref, emb_ref = refs[:8]
-    out_ref, gain_out, bias_out, cb_out, tw_out, done_ref = refs[8:]
-    done_ref[...] = jnp.zeros_like(done_ref)
+    out_ref, gain_out, bias_out, cb_out, tw_out = refs[8:]
     gain_ref = gain_load()
     n, c = out_ref.shape
     per = n // batch
@@ -475,10 +477,9 @@
     return col & 1, (col >> 1) & 1, col >> 2
 
 
-def step_one(nz, keep_ref, got_ref, a_send, a_keep, b_send, b_keep, done_ref):
+def step_one(nz, keep_ref, got_ref, a_send, a_keep, b_send, b_keep):
     _, xb, _ = place()
     half = nz // 2
-    done_ref[...] = jnp.zeros_like(done_ref)
     total = lambda r, p: keep_ref[r, p] + got_ref[r, p].astype(F32)
     for x in range(2):
         for z in range(half):
@@ -670,30 +671,28 @@
         flops=conv_flops,
     )
 
-    token = of((8, LANES), F32)
-    if relative:
-        half = nz // 2
-        many = lambda k, dtype: of((*k, share, width), dtype)
-        got = partner(send[0], 1)
-        a_send, a_keep, b_send, b_keep, done = call(
-            functools.partial(step_one, nz),
-            (many((2, half), BF16), many((2, half), F32)) * 2 + (token,),
-            (keep, got),
-        )
-        a_got, b_got = partner(a_send, cols), partner(b_send, 2)
-        first = (done,)
-    else:
-        first = ()
-
     dn, sums = call_far(
         functools.partial(back_kernel, batch),
         (of((n, channels), F32), of((8, channels), F32)),
         (aff, gsum),
         far=(x2, dacts),
         vmem=58,
-        after=first,
-        flops=20 * n * channels,
-    )
+        flops=conv_flops,
+    )
+
+    token = of((8, LANES), F32)
+    if relative:
+        half = nz // 2
+        many = lambda k, dtype: of((*k, share, width), dtype)
+        got = partner(send[0], 1)
+        a_send, a_keep, b_send, b_keep = call(
+            functools.partial(step_one, nz),
+            (many((2, half), BF16), many((2, half), F32)) * 2,
+            (keep, got),
+            after=(sums,),
+        )
+        a_got, b_got = partner(a_send, cols), partner(b_send, 2)
+
     emb = embed(timestep, embed_in, embed_out)
     temb = jnp.dot(emb, time_w, preferred_element_type=F32)
 
@@ -721,7 +720,7 @@
         functools.partial(conv_kernel, batch),
         (of((n, channels), BF16), token),
         (temb,),
-        far=(w9, x2, conv_b, *taps),
+        far=(w9, *taps, x2, conv_b),
         after=second,
         flops=conv_flops,
     )
@@ -740,23 +739,30 @@
             sums = sums + partner(sums, bit)
             bit *= 2
 
-    vector = of((channels,), F32)
-    input_grad, gain_grad, bias_grad, conv_b_grad, time_grad, done = call_far(
-        functools.partial(input_kernel, batch, count, scale),
-        (of((n, channels), F32), *[vector] * 3, of((channels, emb.shape[1]), F32), token),
-        (aff, sums, partner(sums, cols if relative else bit), emb),
-        far=(x2, g2, dn, group_norm_gain),
-        vmem=60,
-        flops=8 * n * channels,
-    )
-
+    other_sums = partner(sums, cols if relative else bit)
     if relative:
         mine = call(
             functools.partial(step_five, nz),
             of((share, pieces * width), BF16),
             (own, *others),
-            after=(done,),
+            after=(other_sums,),
         )
+        last = (mine,)
+    else:
+        last = ()
+
+    vector = of((channels,), F32)
+    input_grad, gain_grad, bias_grad, conv_b_grad, time_grad = call_far(
+        functools.partial(input_kernel, batch, count, scale),
+        (of((n, channels), F32), *[vector] * 3, of((channels, emb.shape[1]), F32)),
+        (aff, sums, other_sums, emb),
+        far=(x2, g2, dn, group_norm_gain),
+        vmem=60,
+        after=last,
+        flops=conv_flops,
+    )
+
+    if relative:
         grad = call(
             step_six,
             of((9, 2 * share, channels), F32),

time: 103 us -> 104 us (level)
    unnamed x24 -> x26, local copies, waits for them, and re-layouts: 4.1 us -> 3.72 us
  transfers between devices with their start and end apart: 23 -> 23, of which waited for: 8 -> 8; matrix products, arithmetic and copies ran while one was open for 5% -> 5% of each run, Pallas kernels for 19% -> 24%
where the time goes in v9:
time: 104 us; the launch traced here: 103 us
  starting transfers between devices  41.6 us (40%)
  Pallas kernels  39.1 us (38%)
  waiting for transfers between devices  12.5 us (12%)
  matrix products  4.79 us (5%)
  local copies, waits for them, and re-layouts  4.45 us (4%)
    pallas_call x6, Pallas kernels, call_far(): pl.pallas_call(kernel, out_shape=tuple(outs), in_specs=[hbm] * len(ins) +...  36.8 us
    ppermute x20, starting transfers between devices, partner(): return lax.ppermute(value, AXES, [(i, i ^ bit) for i in range(size)])  29.5 us
    ppermute x20, waiting for transfers between devices, partner(): return lax.ppermute(value, AXES, [(i, i ^ bit) for i in range(size)])  12.3 us
    all_to_all x1, starting transfers between devices, local(): stats = lax.all_to_all(pay, AXES, 0, 0)  8.71 us
    unnamed x26, local copies, waits for them, and re-layouts  3.72 us
    ppermute x2, starting transfers between devices, shift(): return lax.ppermute(value, AXES, pairs)  3.34 us
    dot_general x1, matrix products, embed(): jnp.dot(first_hidden, embed_out, preferred_element_type=F32)  2.74 us
    pallas_call x6, Pallas kernels, call(): pl.pallas_call(kernel, out_shape=out_shape, in_specs=[pl.BlockSpec(memory...  2.35 us
  transfers between devices with their start and end apart: 23, of which 8 were waited for; matrix products, arithmetic and copies ran while one was open for 5% of the time, Pallas kernels for 24%

profile of v9, /device:TPU:0, one launch (start us, length us, event | category | flops | bytes accessed | tf_op | source)
XLA Modules:
  0.0 103.5 jit_solution(8765642430025693012)
XLA Ops:
  0.6 0.7 constant_dynamic-slice_fusion
  1.4 3.0 %collective-permute-start = (bf16[32,320]{1,0:T(8,128)(2,1)S(1)}, bf16[32,320]{1,0:T(8,128)(2,1)}, u32[]{:S(2)}, u32[]{:S(2)}) collective-permute-start(bf16[32,320]{1,0:T(8,128)(2,1)S(1)} %maximum_bitcast_fusion), channel_id=1, source_target_pairs={{0,16},{1,17},{2,18},{3,19},{4,20},{5,21},{6,22},{7,23},{8,24},{9,... | collective-permute-start | bytes 61448 | tf_op jit(solution)/shard_map/ppermute | solution.py:566
  4.4 1.9 %collective-permute-done.refs_2_.refs_3_.refs_4_.refs_5_.refs_7_.refs_8_ = bf16[32,320]{1,0:T(8,128)(2,1)} collective-permute-done((bf16[32,320]{1,0:T(8,128)(2,1)S(1)}, bf16[32,320]{1,0:T(8,128)(2,1)}, u32[]{:S(2)}, u32[]{:S(2)}) %collective-permute-start) | collective-permute-done | bytes 20512 | tf_op jit(solution)/shard_map/ppermute | solution.py:566
  6.3 3.3 %shard_map.153 = (f32[32,1,128]{2,1,0:T(1,128)}, f32[4,66,1,320]{3,2,1,0:T(1,128)}, f32[4,66,1,320]{3,2,1,0:T(1,128)}) custom-call(bf16[1024,320]{1,0:T(8,128)(2,1)} %bitcast.16, bf16[1024,320]{1,0:T(8,128)(2,1)} %bitcast.24, bf16[32,320]{1,0:T(8,128)(2,1)} %collective-permute-done.refs_2_.refs_3_.refs_4_.refs_5_.refs_7_.refs_8_, ...), custom_call_target="tpu_custom_call" | custom-call | bytes 2000000 | tf_op jit(solution)/shard_map/pallas_call | solution.py:111
  9.6 2.1 %collective-permute-start.1 = (f32[4,66,1,320]{3,2,1,0:T(1,128)}, f32[4,66,1,320]{3,2,1,0:T(1,128)}, u32[]{:S(2)}, u32[]{:S(2)}) collective-permute-start(f32[4,66,1,320]{3,2,1,0:T(1,128)} %get-tuple-element.43), channel_id=1, source_target_pairs={{0,1},{1,2},{2,3},{3,4},{4,5},{5,6},{6,7},{7,8},{8,9},{9,10},{10,1... | collective-permute-start | bytes 1013768 | tf_op jit(solution)/shard_map/ppermute | solution.py:577
  11.7 1.3 %collective-permute-start.2 = (f32[4,66,1,320]{3,2,1,0:T(1,128)}, f32[4,66,1,320]{3,2,1,0:T(1,128)}, u32[]{:S(2)}, u32[]{:S(2)}) collective-permute-start(f32[4,66,1,320]{3,2,1,0:T(1,128)} %get-tuple-element.44), channel_id=1, source_target_pairs={{1,0},{2,1},{3,2},{4,3},{5,4},{6,5},{7,6},{8,7},{9,8},{10,9},{11,1... | collective-permute-start | bytes 1013768 | tf_op jit(solution)/shard_map/ppermute | solution.py:577
  13.0 8.7 %all-to-all-start = ((f32[32,1,128]{2,1,0:T(1,128)}), f32[32,1,128]{2,1,0:T(1,128)}, u32[]{:S(2)}, u32[]{:S(2)}) async-start(f32[32,1,128]{2,1,0:T(1,128)} %get-tuple-element.46), calls=%async_computation | async-start | bytes 32768 | tf_op jit(solution)/shard_map/all_to_all | solution.py:628
  21.7 0.0 collective-permute-done.1.refs_2_.refs_5_
  21.7 0.0 collective-permute-done.2.refs_3_.refs_6_
  21.7 6.9 %shard_map.154 = (f32[1024,320]{1,0:T(8,128)}, f32[8,320]{1,0:T(8,128)}, bf16[320,1024]{1,0:T(8,128)(2,1)}) custom-call(bf16[1024,320]{1,0:T(8,128)(2,1)} %bitcast.25, bf16[9,320,320]{2,1,0:T(8,128)(2,1)} %bitcast.22, f32[4,66,1,320]{3,2,1,0:T(1,128)} %collective-permute-done.1.refs_2_.refs_5_, f32[4,66,1,320]{3,2,1,0:T(1,128)} %collective-permute-done.2.refs_3_.refs_6_, ...), custom_call_target="tpu_custom_call" | custom-call | flops 1887436800 | bytes 2000000 | tf_op jit(solution)/shard_map/pallas_call | solution.py:111
  28.6 0.2 all-to-all-done.refs_4_
  28.8 9.1 %shard_map.155 = (f32[8,320]{1,0:T(8,128)}, f32[2,8,80,384]{3,2,1,0:T(8,128)}, bf16[1,2,8,80,384]{4,3,2,1,0:T(8,128)(2,1)}, bf16[512,2880]{1,0:T(8,128)(2,1)}, bf16[512,2880]{1,0:T(8,128)(2,1)}) custom-call(bf16[1024,320]{1,0:T(8,128)(2,1)} %bitcast.17, bf16[320,1024]{1,0:T(8,128)(2,1)} %get-tuple-element.45.refs_1_, f32[320]{0:T(512)} %refs_3_.3, ...), custom_call_target="tpu_custom_call" | custom-call | flops 1887436800 | bytes 2000000 | tf_op jit(solution)/shard_map/pallas_call | solution.py:111
  37.8 1.4 %collective-permute-start.3 = (bf16[2,8,80,384]{3,2,1,0:T(8,128)(2,1)}, bf16[2,8,80,384]{3,2,1,0:T(8,128)(2,1)S(1)}, u32[]{:S(2)}, u32[]{:S(2)}) collective-permute-start(bf16[2,8,80,384]{3,2,1,0:T(8,128)(2,1)} %bitcast.27), channel_id=1, source_target_pairs={{0,1},{1,0},{2,3},{3,2},{4,5},{5,4},{6,7},{7,6},{8,9},{9,8},{10,11... | collective-permute-start | bytes 2949128 | tf_op jit(solution)/shard_map/ppermute | solution.py:566
  39.3 0.1 fusion.7
  39.4 0.0 copy-start.2
  39.4 0.0 copy-start.10
  39.4 4.0 %shard_map.156 = (f32[1024,320]{1,0:T(8,128)}, f32[8,320]{1,0:T(8,128)}) custom-call(bf16[1024,320]{1,0:T(8,128)(2,1)} %bitcast.18, f32[1024,320]{1,0:T(8,128)} %get-tuple-element.51.refs_1_, f32[8,320]{1,0:T(8,128)} %get-tuple-element.52.refs_2_.refs_4_, f32[8,320]{1,0:T(8,128)} %get-tuple-element.53.refs_3_), custom_call_target="tpu_custom_call" | custom-call | flops 1887436800 | bytes 2000000 | tf_op jit(solution)/shard_map/pallas_call | solution.py:111
  43.4 0.1 collective-permute-start.6
  43.5 0.0 collective-permute-done.3.refs_1_
  43.5 0.7 copy-done.3
  44.2 0.2 shard_map.157
  44.4 0.0 copy-start.4
  44.4 1.7 %collective-permute-start.4 = (bf16[2,2,80,384]{3,2,1,0:T(8,128)(2,1)S(1)}, bf16[2,2,80,384]{3,2,1,0:T(8,128)(2,1)S(1)}, u32[]{:S(2)}, u32[]{:S(2)}) collective-permute-start(bf16[2,2,80,384]{3,2,1,0:T(8,128)(2,1)S(1)} %get-tuple-element.55), channel_id=1, source_target_pairs={{0,16},{1,17},{2,18},{3,19},{4,20},{5,21},{6,22},{7,23},{8,24},{9,... | collective-permute-start | bytes 737288 | tf_op jit(solution)/shard_map/ppermute | solution.py:566
  46.1 2.5 %collective-permute-start.5 = (bf16[2,2,80,384]{3,2,1,0:T(8,128)(2,1)S(1)}, bf16[2,2,80,384]{3,2,1,0:T(8,128)(2,1)S(1)}, u32[]{:S(2)}, u32[]{:S(2)}) collective-permute-start(bf16[2,2,80,384]{3,2,1,0:T(8,128)(2,1)S(1)} %get-tuple-element.57), channel_id=1, source_target_pairs={{0,2},{1,3},{2,0},{3,1},{4,6},{5,7},{6,4},{7,5},{8,10},{9,11},{10,... | collective-permute-start | bytes 737288 | tf_op jit(solution)/shard_map/ppermute | solution.py:566
  48.6 2.7 %fusion.1.refs_7_ = bf16[2,1280]{1,0:T(2,128)(2,1)S(1)} fusion(bf16[1280,1280]{1,0:T(8,128)(2,1)} %param.17, bf16[320,1280]{1,0:T(8,128)(2,1)S(1)} %copy-done.10, bf16[2,160]{1,0:T(2,128)(2,1)S(1)} %get-tuple-element.80, bf16[2,160]{1,0:T(2,128)(2,1)S(1)} %get-tuple-element.79), kind=kOutput, calls=%fused_computation.4 | convolution fusion | flops 8220160 | bytes 4102400 | tf_op jit(solution)/shard_map/dot_general | solution.py:561
  51.4 1.4 %collective-permute-done.4.refs_0_ = bf16[2,2,80,384]{3,2,1,0:T(8,128)(2,1)S(1)} collective-permute-done((bf16[2,2,80,384]{3,2,1,0:T(8,128)(2,1)S(1)}, bf16[2,2,80,384]{3,2,1,0:T(8,128)(2,1)S(1)}, u32[]{:S(2)}, u32[]{:S(2)}) %collective-permute-start.4) | collective-permute-done | bytes 245792 | tf_op jit(solution)/shard_map/ppermute | solution.py:566
  52.8 2.1 %collective-permute-done.5.refs_2_ = bf16[2,2,80,384]{3,2,1,0:T(8,128)(2,1)S(1)} collective-permute-done((bf16[2,2,80,384]{3,2,1,0:T(8,128)(2,1)S(1)}, bf16[2,2,80,384]{3,2,1,0:T(8,128)(2,1)S(1)}, u32[]{:S(2)}, u32[]{:S(2)}) %collective-permute-start.5) | collective-permute-done | bytes 245792 | tf_op jit(solution)/shard_map/ppermute | solution.py:566
  55.0 0.1 shard_map.158
  55.0 1.8 %collective-permute-start.7 = (bf16[2,80,384]{2,1,0:T(8,128)(2,1)S(1)}, bf16[2,80,384]{2,1,0:T(8,128)(2,1)S(1)}, u32[]{:S(2)}, u32[]{:S(2)}) collective-permute-start(bf16[2,80,384]{2,1,0:T(8,128)(2,1)S(1)} %get-tuple-element.59), channel_id=1, source_target_pairs={{0,2},{1,3},{2,0},{3,1},{4,6},{5,7},{6,4},{7,5},{8,10},{9,11},{10,... | collective-permute-start | bytes 368648 | tf_op jit(solution)/shard_map/ppermute | solution.py:566
  56.9 0.4 collective-permute-start.8
  57.2 0.3 collective-permute-start.9
  57.5 2.1 %fusion.22.refs_5_ = f32[2,320]{1,0:T(2,128)} fusion(bf16[2,1280]{1,0:T(2,128)(2,1)S(1)} %fusion.1.refs_7_, bf16[1280,320]{0,1:T(8,128)(2,1)} %param.18), kind=kOutput, calls=%fused_computation.20 | convolution fusion | flops 1638400 | bytes 826880 | tf_op jit(solution)/shard_map/dot_general | solution.py:697
  59.6 1.4 %collective-permute-done.9.refs_5_ = f32[8,320]{1,0:T(8,128)S(1)} collective-permute-done((f32[8,320]{1,0:T(8,128)S(1)}, f32[8,320]{1,0:T(8,128)S(1)}, u32[]{:S(2)}, u32[]{:S(2)}) %collective-permute-start.9) | collective-permute-done | bytes 10272 | tf_op jit(solution)/shard_map/ppermute | solution.py:566
  60.9 0.0 collective-permute-done.7.refs_0_
  60.9 0.8 collective-permute-done.8.refs_2_
  61.7 0.1 shard_map.159
  61.8 0.0 copy-start.5
  61.8 0.6 copy-done.5
  62.4 1.7 %collective-permute-start.10 = (bf16[96,384]{1,0:T(8,128)(2,1)S(1)}, bf16[96,384]{1,0:T(8,128)(2,1)S(1)}, u32[]{:S(2)}, u32[]{:S(2)}) collective-permute-start(bf16[96,384]{1,0:T(8,128)(2,1)S(1)} %get-tuple-element.68), channel_id=1, source_target_pairs={{0,4},{1,5},{2,6},{3,7},{4,0},{5,1},{6,2},{7,3},{8,12},{9,13},{10,... | collective-permute-start | bytes 221192 | tf_op jit(solution)/shard_map/ppermute | solution.py:566
  64.1 1.9 %collective-permute-start.11 = (bf16[96,384]{1,0:T(8,128)(2,1)S(1)}, bf16[96,384]{1,0:T(8,128)(2,1)S(1)}, u32[]{:S(2)}, u32[]{:S(2)}) collective-permute-start(bf16[96,384]{1,0:T(8,128)(2,1)S(1)} %get-tuple-element.69), channel_id=1, source_target_pairs={{0,8},{1,9},{2,10},{3,11},{4,12},{5,13},{6,14},{7,15},{8,0},{9,1},... | collective-permute-start | bytes 221192 | tf_op jit(solution)/shard_map/ppermute | solution.py:566
  66.0 0.8 collective-permute-start.12
  66.8 7.9 %shard_map.160 = (bf16[1024,320]{1,0:T(8,128)(2,1)}, f32[8,128]{1,0:T(8,128)}) custom-call(bf16[9,320,320]{2,1,0:T(8,128)(2,1)} %bitcast.23, bf16[512,2880]{1,0:T(8,128)(2,1)} %get-tuple-element.47.refs_1_, bf16[512,2880]{1,0:T(8,128)(2,1)} %get-tuple-element.48.refs_2_, bf16[1024,320]{1,0:T(8,128)(2,1)} %bitcast.19, f32[320]{0:T(512)} %refs_4_.1, ...), custom_call_target="tpu_custom_call" | custom-call | flops 1887436800 | bytes 2000000 | tf_op jit(solution)/shard_map/pallas_call | solution.py:111
  74.7 0.0 collective-permute-done.10.refs_2_
  74.8 0.0 copy-start.8
  74.8 0.7 copy-done.8
  75.5 1.0 %collective-permute-start.14 = (bf16[80,384]{1,0:T(8,128)(2,1)S(1)}, bf16[80,384]{1,0:T(8,128)(2,1)S(1)}, u32[]{:S(2)}, u32[]{:S(2)}) collective-permute-start(bf16[80,384]{1,0:T(8,128)(2,1)S(1)} %get-tuple-element.73.refs_0_), channel_id=1, source_target_pairs={{0,2},{1,3},{2,0},{3,1},{4,6},{5,7},{6,4},{7,5},{8,10},{9,11},{10,... | collective-permute-start | bytes 184328 | tf_op jit(solution)/shard_map/ppermute | solution.py:566
  76.6 1.0 collective-permute-start.15
  77.5 0.8 collective-permute-start.13
  78.4 1.5 %collective-permute-start.16 = (bf16[80,384]{1,0:T(8,128)(2,1)S(1)}, bf16[80,384]{1,0:T(8,128)(2,1)S(1)}, u32[]{:S(2)}, u32[]{:S(2)}) collective-permute-start(bf16[80,384]{1,0:T(8,128)(2,1)S(1)} %get-tuple-element.73.refs_0_), channel_id=1, source_target_pairs={{0,6},{1,7},{2,4},{3,5},{4,2},{5,3},{6,0},{7,1},{8,14},{9,15},{10,... | collective-permute-start | bytes 184328 | tf_op jit(solution)/shard_map/ppermute | solution.py:566
  79.9 1.9 %collective-permute-start.17 = (bf16[80,384]{1,0:T(8,128)(2,1)S(1)}, bf16[80,384]{1,0:T(8,128)(2,1)S(1)}, u32[]{:S(2)}, u32[]{:S(2)}) collective-permute-start(bf16[80,384]{1,0:T(8,128)(2,1)S(1)} %get-tuple-element.73.refs_0_), channel_id=1, source_target_pairs={{0,8},{1,9},{2,10},{3,11},{4,12},{5,13},{6,14},{7,15},{8,0},{9,1},... | collective-permute-start | bytes 184328 | tf_op jit(solution)/shard_map/ppermute | solution.py:566
  81.8 2.6 %collective-permute-start.18 = (bf16[80,384]{1,0:T(8,128)(2,1)S(1)}, bf16[80,384]{1,0:T(8,128)(2,1)S(1)}, u32[]{:S(2)}, u32[]{:S(2)}) collective-permute-start(bf16[80,384]{1,0:T(8,128)(2,1)S(1)} %get-tuple-element.73.refs_0_), channel_id=1, source_target_pairs={{0,10},{1,11},{2,8},{3,9},{4,14},{5,15},{6,12},{7,13},{8,2},{9,3},... | collective-permute-start | bytes 184328 | tf_op jit(solution)/shard_map/ppermute | solution.py:566
  84.4 2.7 %collective-permute-start.19 = (bf16[80,384]{1,0:T(8,128)(2,1)S(1)}, bf16[80,384]{1,0:T(8,128)(2,1)S(1)}, u32[]{:S(2)}, u32[]{:S(2)}) collective-permute-start(bf16[80,384]{1,0:T(8,128)(2,1)S(1)} %get-tuple-element.73.refs_0_), channel_id=1, source_target_pairs={{0,12},{1,13},{2,14},{3,15},{4,8},{5,9},{6,10},{7,11},{8,4},{9,5},... | collective-permute-start | bytes 184328 | tf_op jit(solution)/shard_map/ppermute | solution.py:566
  87.1 2.3 %collective-permute-start.20 = (bf16[80,384]{1,0:T(8,128)(2,1)S(1)}, bf16[80,384]{1,0:T(8,128)(2,1)S(1)}, u32[]{:S(2)}, u32[]{:S(2)}) collective-permute-start(bf16[80,384]{1,0:T(8,128)(2,1)S(1)} %get-tuple-element.73.refs_0_), channel_id=1, source_target_pairs={{0,14},{1,15},{2,12},{3,13},{4,10},{5,11},{6,8},{7,9},{8,6},{9,7},... | collective-permute-start | bytes 184328 | tf_op jit(solution)/shard_map/ppermute | solution.py:566
  89.4 0.0 collective-permute-done.18.refs_5_
  89.4 1.0 collective-permute-done.19.refs_6_
  90.4 3.6 %collective-permute-done.20.refs_7_ = bf16[80,384]{1,0:T(8,128)(2,1)S(1)} collective-permute-done((bf16[80,384]{1,0:T(8,128)(2,1)S(1)}, bf16[80,384]{1,0:T(8,128)(2,1)S(1)}, u32[]{:S(2)}, u32[]{:S(2)}) %collective-permute-start.20) | collective-permute-done | bytes 61472 | tf_op jit(solution)/shard_map/ppermute | solution.py:566
  94.0 0.1 shard_map.162.refs_8_.refs_0_
  94.1 0.0 copy-start
  94.1 0.1 collective-permute-start.21
  94.2 0.7 copy-done
  94.8 5.7 %shard_map.163 = (f32[1024,320]{1,0:T(8,128)}, f32[320]{0:T(512)}, f32[320]{0:T(512)}, f32[320]{0:T(512)}, f32[320,1280]{1,0:T(8,128)}) custom-call(bf16[1024,320]{1,0:T(8,128)(2,1)} %bitcast.20, bf16[1024,320]{1,0:T(8,128)(2,1)} %bitcast.26, f32[1024,320]{1,0:T(8,128)} %get-tuple-element.66.refs_2_, f32[320]{0:T(512)} %refs_3_.3, ...), custom_call_target="tpu_custom_call" | custom-call | flops 1887436800 | bytes 2000000 | tf_op jit(solution)/shard_map/pallas_call | solution.py:111
  100.5 0.0 copy-start.1
  100.5 1.0 copy-done.1
  101.6 1.9 %shard_map.164 = f32[9,160,320]{2,1,0:T(8,128)} custom-call(bf16[80,3072]{1,0:T(8,128)(2,1)S(1)} %copy-done.1, bf16[80,3072]{1,0:T(8,128)(2,1)S(1)} %collective-permute-done.21.refs_1_), custom_call_target="tpu_custom_call" | custom-call | bytes 2000000 | tf_op jit(solution)/shard_map/pallas_call | solution.py:53
  (27 shorter events, 0.1 us)
Async XLA Ops:
  1.4 4.9 %collective-permute-start = (bf16[32,320]{1,0:T(8,128)(2,1)S(1)}, bf16[32,320]{1,0:T(8,128)(2,1)}, u32[]{:S(2)}, u32[]{:S(2)}) collective-permute-start(bf16[32,320]{1,0:T(8,128)(2,1)S(1)} %maximum_bitcast_fusion), channel_id=1, source_target_pairs={{0,16},{1,17},{2,18},{3,19},{4,20},{5,21},{6,22},{7,23},{8,24},{9,... | collective-permute-start | bytes 61448 | tf_op jit(solution)/shard_map/ppermute | solution.py:566
  9.6 12.1 %collective-permute-start.1 = (f32[4,66,1,320]{3,2,1,0:T(1,128)}, f32[4,66,1,320]{3,2,1,0:T(1,128)}, u32[]{:S(2)}, u32[]{:S(2)}) collective-permute-start(f32[4,66,1,320]{3,2,1,0:T(1,128)} %get-tuple-element.43), channel_id=1, source_target_pairs={{0,1},{1,2},{2,3},{3,4},{4,5},{5,6},{6,7},{7,8},{8,9},{9,10},{10,1... | collective-permute-start | bytes 1013768 | tf_op jit(solution)/shard_map/ppermute | solution.py:577
  11.7 10.0 %collective-permute-start.2 = (f32[4,66,1,320]{3,2,1,0:T(1,128)}, f32[4,66,1,320]{3,2,1,0:T(1,128)}, u32[]{:S(2)}, u32[]{:S(2)}) collective-permute-start(f32[4,66,1,320]{3,2,1,0:T(1,128)} %get-tuple-element.44), channel_id=1, source_target_pairs={{1,0},{2,1},{3,2},{4,3},{5,4},{6,5},{7,6},{8,7},{9,8},{10,9},{11,1... | collective-permute-start | bytes 1013768 | tf_op jit(solution)/shard_map/ppermute | solution.py:577
  13.0 15.8 %all-to-all-start = ((f32[32,1,128]{2,1,0:T(1,128)}), f32[32,1,128]{2,1,0:T(1,128)}, u32[]{:S(2)}, u32[]{:S(2)}) async-start(f32[32,1,128]{2,1,0:T(1,128)} %get-tuple-element.46), calls=%async_computation | async-start | bytes 32768 | tf_op jit(solution)/shard_map/all_to_all | solution.py:628
  28.7 10.5 %copy-start.12 = (s32[2]{0:T(128)S(1)}, s32[2]{0:T(128)}, u32[]{:S(2)}) copy-start(s32[2]{0:T(128)} %param.11) | copy-start | bytes 28
  37.8 5.7 %collective-permute-start.3 = (bf16[2,8,80,384]{3,2,1,0:T(8,128)(2,1)}, bf16[2,8,80,384]{3,2,1,0:T(8,128)(2,1)S(1)}, u32[]{:S(2)}, u32[]{:S(2)}) collective-permute-start(bf16[2,8,80,384]{3,2,1,0:T(8,128)(2,1)} %bitcast.27), channel_id=1, source_target_pairs={{0,1},{1,0},{2,3},{3,2},{4,5},{5,4},{6,7},{7,6},{8,9},{9,8},{10,11... | collective-permute-start | bytes 2949128 | tf_op jit(solution)/shard_map/ppermute | solution.py:566
  39.4 4.1 %copy-start.2 = (f32[2,8,80,384]{3,2,1,0:T(8,128)S(1)}, f32[2,8,80,384]{3,2,1,0:T(8,128)}, u32[]{:S(2)}) copy-start(f32[2,8,80,384]{3,2,1,0:T(8,128)} %get-tuple-element.49.refs_0_) | copy-start | bytes 5898244
  39.4 9.2 %copy-start.10 = (bf16[320,1280]{1,0:T(8,128)(2,1)S(1)}, bf16[320,1280]{1,0:T(8,128)(2,1)}, u32[]{:S(2)}) copy-start(bf16[320,1280]{1,0:T(8,128)(2,1)} %param.16) | copy-start | bytes 2457604
  43.4 8.0 %collective-permute-start.6 = (f32[8,320]{1,0:T(8,128)}, f32[8,320]{1,0:T(8,128)S(1)}, u32[]{:S(2)}, u32[]{:S(2)}) collective-permute-start(f32[8,320]{1,0:T(8,128)} %get-tuple-element.54.refs_2_.refs_4_), channel_id=1, source_target_pairs={{0,1},{1,0},{2,3},{3,2},{4,5},{5,4},{6,7},{7,6},{8,9},{9,8},{10,11... | collective-permute-start | bytes 30728 | tf_op jit(solution)/shard_map/ppermute | solution.py:566
  43.5 0.7 copy-start.3
  44.4 10.5 %copy-start.4 = (f32[8,320]{1,0:T(8,128)S(1)}, f32[8,320]{1,0:T(8,128)}, u32[]{:S(2)}) copy-start(f32[8,320]{1,0:T(8,128)} %get-tuple-element.54.refs_2_.refs_4_) | copy-start | bytes 30724
  44.4 8.4 %collective-permute-start.4 = (bf16[2,2,80,384]{3,2,1,0:T(8,128)(2,1)S(1)}, bf16[2,2,80,384]{3,2,1,0:T(8,128)(2,1)S(1)}, u32[]{:S(2)}, u32[]{:S(2)}) collective-permute-start(bf16[2,2,80,384]{3,2,1,0:T(8,128)(2,1)S(1)} %get-tuple-element.55), channel_id=1, source_target_pairs={{0,16},{1,17},{2,18},{3,19},{4,20},{5,21},{6,22},{7,23},{8,24},{9,... | collective-permute-start | bytes 737288 | tf_op jit(solution)/shard_map/ppermute | solution.py:566
  46.1 8.8 %collective-permute-start.5 = (bf16[2,2,80,384]{3,2,1,0:T(8,128)(2,1)S(1)}, bf16[2,2,80,384]{3,2,1,0:T(8,128)(2,1)S(1)}, u32[]{:S(2)}, u32[]{:S(2)}) collective-permute-start(bf16[2,2,80,384]{3,2,1,0:T(8,128)(2,1)S(1)} %get-tuple-element.57), channel_id=1, source_target_pairs={{0,2},{1,3},{2,0},{3,1},{4,6},{5,7},{6,4},{7,5},{8,10},{9,11},{10,... | collective-permute-start | bytes 737288 | tf_op jit(solution)/shard_map/ppermute | solution.py:566
  51.4 23.3 %copy-start.11 = (bf16[2,1280]{1,0:T(2,128)(2,1)}, bf16[2,1280]{1,0:T(2,128)(2,1)S(1)}, u32[]{:S(2)}) copy-start(bf16[2,1280]{1,0:T(2,128)(2,1)S(1)} %fusion.1.refs_7_) | copy-start | bytes 15364
  55.0 5.9 %collective-permute-start.7 = (bf16[2,80,384]{2,1,0:T(8,128)(2,1)S(1)}, bf16[2,80,384]{2,1,0:T(8,128)(2,1)S(1)}, u32[]{:S(2)}, u32[]{:S(2)}) collective-permute-start(bf16[2,80,384]{2,1,0:T(8,128)(2,1)S(1)} %get-tuple-element.59), channel_id=1, source_target_pairs={{0,2},{1,3},{2,0},{3,1},{4,6},{5,7},{6,4},{7,5},{8,10},{9,11},{10,... | collective-permute-start | bytes 368648 | tf_op jit(solution)/shard_map/ppermute | solution.py:566
  56.9 4.9 %collective-permute-start.8 = (bf16[2,80,384]{2,1,0:T(8,128)(2,1)S(1)}, bf16[2,80,384]{2,1,0:T(8,128)(2,1)S(1)}, u32[]{:S(2)}, u32[]{:S(2)}) collective-permute-start(bf16[2,80,384]{2,1,0:T(8,128)(2,1)S(1)} %get-tuple-element.61), channel_id=1, source_target_pairs={{0,16},{1,17},{2,18},{3,19},{4,20},{5,21},{6,22},{7,23},{8,24},{9,... | collective-permute-start | bytes 368648 | tf_op jit(solution)/shard_map/ppermute | solution.py:566
  57.2 3.7 %collective-permute-start.9 = (f32[8,320]{1,0:T(8,128)S(1)}, f32[8,320]{1,0:T(8,128)S(1)}, u32[]{:S(2)}, u32[]{:S(2)}) collective-permute-start(f32[8,320]{1,0:T(8,128)S(1)} %get-tuple-element.63.refs_4_), channel_id=1, source_target_pairs={{0,2},{1,3},{2,0},{3,1},{4,6},{5,7},{6,4},{7,5},{8,10},{9,11},{10,... | collective-permute-start | bytes 30728 | tf_op jit(solution)/shard_map/ppermute | solution.py:566
  61.8 0.6 copy-start.5
  62.4 12.3 %collective-permute-start.10 = (bf16[96,384]{1,0:T(8,128)(2,1)S(1)}, bf16[96,384]{1,0:T(8,128)(2,1)S(1)}, u32[]{:S(2)}, u32[]{:S(2)}) collective-permute-start(bf16[96,384]{1,0:T(8,128)(2,1)S(1)} %get-tuple-element.68), channel_id=1, source_target_pairs={{0,4},{1,5},{2,6},{3,7},{4,0},{5,1},{6,2},{7,3},{8,12},{9,13},{10,... | collective-permute-start | bytes 221192 | tf_op jit(solution)/shard_map/ppermute | solution.py:566
  64.1 10.6 %collective-permute-start.11 = (bf16[96,384]{1,0:T(8,128)(2,1)S(1)}, bf16[96,384]{1,0:T(8,128)(2,1)S(1)}, u32[]{:S(2)}, u32[]{:S(2)}) collective-permute-start(bf16[96,384]{1,0:T(8,128)(2,1)S(1)} %get-tuple-element.69), channel_id=1, source_target_pairs={{0,8},{1,9},{2,10},{3,11},{4,12},{5,13},{6,14},{7,15},{8,0},{9,1},... | collective-permute-start | bytes 221192 | tf_op jit(solution)/shard_map/ppermute | solution.py:566
  66.0 8.7 %collective-permute-start.12 = (bf16[96,384]{1,0:T(8,128)(2,1)S(1)}, bf16[96,384]{1,0:T(8,128)(2,1)S(1)}, u32[]{:S(2)}, u32[]{:S(2)}) collective-permute-start(bf16[96,384]{1,0:T(8,128)(2,1)S(1)} %get-tuple-element.70), channel_id=1, source_target_pairs={{0,12},{1,13},{2,14},{3,15},{4,8},{5,9},{6,10},{7,11},{8,4},{9,5},... | collective-permute-start | bytes 221192 | tf_op jit(solution)/shard_map/ppermute | solution.py:566
  66.8 7.9 %copy-start.6 = (f32[8,320]{1,0:T(8,128)S(1)}, f32[8,320]{1,0:T(8,128)}, u32[]{:S(2)}) copy-start(f32[8,320]{1,0:T(8,128)} %copy-done.5) | copy-start | bytes 30724
  74.8 0.7 copy-start.8
  75.5 18.7 %copy-start.9 = (f32[8,320]{1,0:T(8,128)}, f32[8,320]{1,0:T(8,128)S(1)}, u32[]{:S(2)}) copy-start(f32[8,320]{1,0:T(8,128)S(1)} %get-tuple-element.72.refs_5_) | copy-start | bytes 30724
  75.5 8.9 %collective-permute-start.14 = (bf16[80,384]{1,0:T(8,128)(2,1)S(1)}, bf16[80,384]{1,0:T(8,128)(2,1)S(1)}, u32[]{:S(2)}, u32[]{:S(2)}) collective-permute-start(bf16[80,384]{1,0:T(8,128)(2,1)S(1)} %get-tuple-element.73.refs_0_), channel_id=1, source_target_pairs={{0,2},{1,3},{2,0},{3,1},{4,6},{5,7},{6,4},{7,5},{8,10},{9,11},{10,... | collective-permute-start | bytes 184328 | tf_op jit(solution)/shard_map/ppermute | solution.py:566
  76.6 10.5 %collective-permute-start.15 = (bf16[80,384]{1,0:T(8,128)(2,1)S(1)}, bf16[80,384]{1,0:T(8,128)(2,1)S(1)}, u32[]{:S(2)}, u32[]{:S(2)}) collective-permute-start(bf16[80,384]{1,0:T(8,128)(2,1)S(1)} %get-tuple-element.73.refs_0_), channel_id=1, source_target_pairs={{0,4},{1,5},{2,6},{3,7},{4,0},{5,1},{6,2},{7,3},{8,12},{9,13},{10,... | collective-permute-start | bytes 184328 | tf_op jit(solution)/shard_map/ppermute | solution.py:566
  77.5 4.3 %collective-permute-start.13 = (f32[8,320]{1,0:T(8,128)S(1)}, f32[8,320]{1,0:T(8,128)S(1)}, u32[]{:S(2)}, u32[]{:S(2)}) collective-permute-start(f32[8,320]{1,0:T(8,128)S(1)} %get-tuple-element.72.refs_5_), channel_id=1, source_target_pairs={{0,16},{1,17},{2,18},{3,19},{4,20},{5,21},{6,22},{7,23},{8,24},{9,... | collective-permute-start | bytes 30728 | tf_op jit(solution)/shard_map/ppermute | solution.py:566
  78.4 11.0 %collective-permute-start.16 = (bf16[80,384]{1,0:T(8,128)(2,1)S(1)}, bf16[80,384]{1,0:T(8,128)(2,1)S(1)}, u32[]{:S(2)}, u32[]{:S(2)}) collective-permute-start(bf16[80,384]{1,0:T(8,128)(2,1)S(1)} %get-tuple-element.73.refs_0_), channel_id=1, source_target_pairs={{0,6},{1,7},{2,4},{3,5},{4,2},{5,3},{6,0},{7,1},{8,14},{9,15},{10,... | collective-permute-start | bytes 184328 | tf_op jit(solution)/shard_map/ppermute | solution.py:566
  79.9 9.5 %collective-permute-start.17 = (bf16[80,384]{1,0:T(8,128)(2,1)S(1)}, bf16[80,384]{1,0:T(8,128)(2,1)S(1)}, u32[]{:S(2)}, u32[]{:S(2)}) collective-permute-start(bf16[80,384]{1,0:T(8,128)(2,1)S(1)} %get-tuple-element.73.refs_0_), channel_id=1, source_target_pairs={{0,8},{1,9},{2,10},{3,11},{4,12},{5,13},{6,14},{7,15},{8,0},{9,1},... | collective-permute-start | bytes 184328 | tf_op jit(solution)/shard_map/ppermute | solution.py:566
  81.8 12.4 %copy-start.7 = (f32[8,320]{1,0:T(8,128)}, f32[8,320]{1,0:T(8,128)S(1)}, u32[]{:S(2)}) copy-start(f32[8,320]{1,0:T(8,128)S(1)} %collective-permute-done.13.refs_8_.refs_6_) | copy-start | bytes 30724
  81.8 7.6 %collective-permute-start.18 = (bf16[80,384]{1,0:T(8,128)(2,1)S(1)}, bf16[80,384]{1,0:T(8,128)(2,1)S(1)}, u32[]{:S(2)}, u32[]{:S(2)}) collective-permute-start(bf16[80,384]{1,0:T(8,128)(2,1)S(1)} %get-tuple-element.73.refs_0_), channel_id=1, source_target_pairs={{0,10},{1,11},{2,8},{3,9},{4,14},{5,15},{6,12},{7,13},{8,2},{9,3},... | collective-permute-start | bytes 184328 | tf_op jit(solution)/shard_map/ppermute | solution.py:566
  84.4 6.0 %collective-permute-start.19 = (bf16[80,384]{1,0:T(8,128)(2,1)S(1)}, bf16[80,384]{1,0:T(8,128)(2,1)S(1)}, u32[]{:S(2)}, u32[]{:S(2)}) collective-permute-start(bf16[80,384]{1,0:T(8,128)(2,1)S(1)} %get-tuple-element.73.refs_0_), channel_id=1, source_target_pairs={{0,12},{1,13},{2,14},{3,15},{4,8},{5,9},{6,10},{7,11},{8,4},{9,5},... | collective-permute-start | bytes 184328 | tf_op jit(solution)/shard_map/ppermute | solution.py:566
  87.1 6.9 %collective-permute-start.20 = (bf16[80,384]{1,0:T(8,128)(2,1)S(1)}, bf16[80,384]{1,0:T(8,128)(2,1)S(1)}, u32[]{:S(2)}, u32[]{:S(2)}) collective-permute-start(bf16[80,384]{1,0:T(8,128)(2,1)S(1)} %get-tuple-element.73.refs_0_), channel_id=1, source_target_pairs={{0,14},{1,15},{2,12},{3,13},{4,10},{5,11},{6,8},{7,9},{8,6},{9,7},... | collective-permute-start | bytes 184328 | tf_op jit(solution)/shard_map/ppermute | solution.py:566
  94.1 0.8 copy-start
  94.1 6.4 %collective-permute-start.21 = (bf16[80,3072]{1,0:T(8,128)(2,1)S(1)}, bf16[80,3072]{1,0:T(8,128)(2,1)S(1)}, u32[]{:S(2)}, u32[]{:S(2)}) collective-permute-start(bf16[80,3072]{1,0:T(8,128)(2,1)S(1)} %shard_map.162.refs_8_.refs_0_), channel_id=1, source_target_pairs={{0,1},{1,0},{2,3},{3,2},{4,5},{5,4},{6,7},{7,6},{8,9},{9,8},{10,11... | collective-permute-start | bytes 1474568 | tf_op jit(solution)/shard_map/ppermute | solution.py:566
  100.5 1.0 copy-start.1

commit v10 on v9

--- a/solution.py
+++ b/solution.py
@@ -433,7 +433,8 @@
 
 def input_kernel(batch, count, scale, emit, *refs):
     x_load, g_load, dn_load, gain_load, aff_ref, part_ref, other_ref, emb_ref = refs[:8]
-    out_ref, gain_out, bias_out, cb_out, tw_out = refs[8:]
+    out_ref, gain_out, bias_out, cb_out, tw_out, done_ref = refs[8:]
+    done_ref[...] = jnp.zeros_like(done_ref)
     gain_ref = gain_load()
     n, c = out_ref.shape
     per = n // batch
@@ -739,30 +740,23 @@
             sums = sums + partner(sums, bit)
             bit *= 2
 
-    other_sums = partner(sums, cols if relative else bit)
+    vector = of((channels,), F32)
+    input_grad, gain_grad, bias_grad, conv_b_grad, time_grad, done = call_far(
+        functools.partial(input_kernel, batch, count, scale),
+        (of((n, channels), F32), *[vector] * 3, of((channels, emb.shape[1]), F32), token),
+        (aff, sums, partner(sums, cols if relative else bit), emb),
+        far=(x2, g2, dn, group_norm_gain),
+        vmem=60,
+        flops=8 * n * channels,
+    )
+
     if relative:
         mine = call(
             functools.partial(step_five, nz),
             of((share, pieces * width), BF16),
             (own, *others),
-            after=(other_sums,),
+            after=(done,),
         )
-        last = (mine,)
-    else:
-        last = ()
-
-    vector = of((channels,), F32)
-    input_grad, gain_grad, bias_grad, conv_b_grad, time_grad = call_far(
-        functools.partial(input_kernel, batch, count, scale),
-        (of((n, channels), F32), *[vector] * 3, of((channels, emb.shape[1]), F32)),
-        (aff, sums, other_sums, emb),
-        far=(x2, g2, dn, group_norm_gain),
-        vmem=60,
-        after=last,
-        flops=conv_flops,
-    )
-
-    if relative:
         grad = call(
             step_six,
             of((9, 2 * share, channels), F32),

time: 104 us -> 99.2 us (0.954)
  waiting for transfers between devices: 12.5 us -> 9.6 us
  Pallas kernels: 39.1 us -> 37.9 us
    ppermute x20, waiting for transfers between devices: 12.3 us -> 9.53 us  [partner(): return lax.ppermute(value, AXES, [(i, i ^ bit) for i in range(size)])]
    pallas_call x6, Pallas kernels: 36.8 us -> 35.6 us  [call_far(): pl.pallas_call(kernel, out_shape=tuple(outs), in_specs=[hbm] * len(ins) +...]
    unnamed x26 -> x24, local copies, waits for them, and re-layouts: 3.72 us -> 2.69 us
  transfers between devices with their start and end apart: 23 -> 23, of which waited for: 8 -> 7; matrix products, arithmetic and copies ran while one was open for 5% -> 5% of each run, Pallas kernels for 24% -> 24%
where the time goes in v10:
time: 99.2 us; the launch traced here: 98.6 us
  starting transfers between devices  41.8 us (42%)
  Pallas kernels  37.9 us (38%)
  waiting for transfers between devices  9.6 us (10%)
  matrix products  4.79 us (5%)
  local copies, waits for them, and re-layouts  3.42 us (3%)
    pallas_call x6, Pallas kernels, call_far(): pl.pallas_call(kernel, out_shape=tuple(outs), in_specs=[hbm] * len(ins) +...  35.6 us
    ppermute x20, starting transfers between devices, partner(): return lax.ppermute(value, AXES, [(i, i ^ bit) for i in range(size)])  29.7 us
    ppermute x20, waiting for transfers between devices, partner(): return lax.ppermute(value, AXES, [(i, i ^ bit) for i in range(size)])  9.53 us
    all_to_all x1, starting transfers between devices, local(): stats = lax.all_to_all(pay, AXES, 0, 0)  8.73 us
    ppermute x2, starting transfers between devices, shift(): return lax.ppermute(value, AXES, pairs)  3.33 us
    dot_general x1, matrix products, embed(): jnp.dot(first_hidden, embed_out, preferred_element_type=F32)  2.74 us
    unnamed x24, local copies, waits for them, and re-layouts  2.69 us
    pallas_call x6, Pallas kernels, call(): pl.pallas_call(kernel, out_shape=out_shape, in_specs=[pl.BlockSpec(memory...  2.35 us
  transfers between devices with their start and end apart: 23, of which 7 were waited for; matrix products, arithmetic and copies ran while one was open for 5% of the time, Pallas kernels for 24%

profile of v10, /device:TPU:0, one launch (start us, length us, event | category | flops | bytes accessed | tf_op | source)
XLA Modules:
  0.0 98.6 jit_solution(1036383582309248970)
XLA Ops:
  0.6 0.7 constant_dynamic-slice_fusion
  1.4 3.0 %collective-permute-start = (bf16[32,320]{1,0:T(8,128)(2,1)S(1)}, bf16[32,320]{1,0:T(8,128)(2,1)}, u32[]{:S(2)}, u32[]{:S(2)}) collective-permute-start(bf16[32,320]{1,0:T(8,128)(2,1)S(1)} %maximum_bitcast_fusion), channel_id=1, source_target_pairs={{0,16},{1,17},{2,18},{3,19},{4,20},{5,21},{6,22},{7,23},{8,24},{9,... | collective-permute-start | bytes 61448 | tf_op jit(solution)/shard_map/ppermute | solution.py:567
  4.4 1.9 %collective-permute-done.refs_2_.refs_3_.refs_4_.refs_5_.refs_7_.refs_8_ = bf16[32,320]{1,0:T(8,128)(2,1)} collective-permute-done((bf16[32,320]{1,0:T(8,128)(2,1)S(1)}, bf16[32,320]{1,0:T(8,128)(2,1)}, u32[]{:S(2)}, u32[]{:S(2)}) %collective-permute-start) | collective-permute-done | bytes 20512 | tf_op jit(solution)/shard_map/ppermute | solution.py:567
  6.3 3.3 %shard_map.153 = (f32[32,1,128]{2,1,0:T(1,128)}, f32[4,66,1,320]{3,2,1,0:T(1,128)}, f32[4,66,1,320]{3,2,1,0:T(1,128)}) custom-call(bf16[1024,320]{1,0:T(8,128)(2,1)} %bitcast.16, bf16[1024,320]{1,0:T(8,128)(2,1)} %bitcast.21, bf16[32,320]{1,0:T(8,128)(2,1)} %collective-permute-done.refs_2_.refs_3_.refs_4_.refs_5_.refs_7_.refs_8_, ...), custom_call_target="tpu_custom_call" | custom-call | bytes 2000000 | tf_op jit(solution)/shard_map/pallas_call | solution.py:111
  9.6 2.1 %collective-permute-start.1 = (f32[4,66,1,320]{3,2,1,0:T(1,128)}, f32[4,66,1,320]{3,2,1,0:T(1,128)}, u32[]{:S(2)}, u32[]{:S(2)}) collective-permute-start(f32[4,66,1,320]{3,2,1,0:T(1,128)} %get-tuple-element.44), channel_id=1, source_target_pairs={{0,1},{1,2},{2,3},{3,4},{4,5},{5,6},{6,7},{7,8},{8,9},{9,10},{10,1... | collective-permute-start | bytes 1013768 | tf_op jit(solution)/shard_map/ppermute | solution.py:578
  11.7 1.3 %collective-permute-start.2 = (f32[4,66,1,320]{3,2,1,0:T(1,128)}, f32[4,66,1,320]{3,2,1,0:T(1,128)}, u32[]{:S(2)}, u32[]{:S(2)}) collective-permute-start(f32[4,66,1,320]{3,2,1,0:T(1,128)} %get-tuple-element.45), channel_id=1, source_target_pairs={{1,0},{2,1},{3,2},{4,3},{5,4},{6,5},{7,6},{8,7},{9,8},{10,9},{11,1... | collective-permute-start | bytes 1013768 | tf_op jit(solution)/shard_map/ppermute | solution.py:578
  13.0 8.7 %all-to-all-start = ((f32[32,1,128]{2,1,0:T(1,128)}), f32[32,1,128]{2,1,0:T(1,128)}, u32[]{:S(2)}, u32[]{:S(2)}) async-start(f32[32,1,128]{2,1,0:T(1,128)} %get-tuple-element.47), calls=%async_computation | async-start | bytes 32768 | tf_op jit(solution)/shard_map/all_to_all | solution.py:629
  21.7 6.8 %shard_map.154 = (f32[1024,320]{1,0:T(8,128)}, f32[8,320]{1,0:T(8,128)}, bf16[320,1024]{1,0:T(8,128)(2,1)}) custom-call(bf16[1024,320]{1,0:T(8,128)(2,1)} %bitcast.22, bf16[9,320,320]{2,1,0:T(8,128)(2,1)} %bitcast.25, f32[4,66,1,320]{3,2,1,0:T(1,128)} %collective-permute-done.1.refs_2_.refs_5_, f32[4,66,1,320]{3,2,1,0:T(1,128)} %collective-permute-done.2.refs_3_.refs_6_, ...), custom_call_target="tpu_custom_call" | custom-call | flops 1887436800 | bytes 2000000 | tf_op jit(solution)/shard_map/pallas_call | solution.py:111
  28.5 0.1 all-to-all-done.refs_4_
  28.6 9.0 %shard_map.155 = (f32[8,320]{1,0:T(8,128)}, f32[2,8,80,384]{3,2,1,0:T(8,128)}, bf16[1,2,8,80,384]{4,3,2,1,0:T(8,128)(2,1)}, bf16[512,2880]{1,0:T(8,128)(2,1)}, bf16[512,2880]{1,0:T(8,128)(2,1)}) custom-call(bf16[1024,320]{1,0:T(8,128)(2,1)} %bitcast.17, bf16[320,1024]{1,0:T(8,128)(2,1)} %get-tuple-element.46.refs_1_, f32[320]{0:T(512)} %refs_3_.3, ...), custom_call_target="tpu_custom_call" | custom-call | flops 1887436800 | bytes 2000000 | tf_op jit(solution)/shard_map/pallas_call | solution.py:111
  37.6 1.5 %collective-permute-start.3 = (bf16[2,8,80,384]{3,2,1,0:T(8,128)(2,1)}, bf16[2,8,80,384]{3,2,1,0:T(8,128)(2,1)S(1)}, u32[]{:S(2)}, u32[]{:S(2)}) collective-permute-start(bf16[2,8,80,384]{3,2,1,0:T(8,128)(2,1)} %bitcast.29), channel_id=1, source_target_pairs={{0,1},{1,0},{2,3},{3,2},{4,5},{5,4},{6,7},{7,6},{8,9},{9,8},{10,11... | collective-permute-start | bytes 2949128 | tf_op jit(solution)/shard_map/ppermute | solution.py:567
  39.1 0.1 fusion.7
  39.3 0.0 copy-start
  39.3 0.0 copy-start.8
  39.3 4.0 %shard_map.156 = (f32[1024,320]{1,0:T(8,128)}, f32[8,320]{1,0:T(8,128)}) custom-call(bf16[1024,320]{1,0:T(8,128)(2,1)} %bitcast.18, f32[1024,320]{1,0:T(8,128)} %get-tuple-element.52.refs_1_, f32[8,320]{1,0:T(8,128)} %get-tuple-element.53.refs_2_.refs_4_, f32[8,320]{1,0:T(8,128)} %get-tuple-element.54.refs_3_), custom_call_target="tpu_custom_call" | custom-call | flops 1887436800 | bytes 2000000 | tf_op jit(solution)/shard_map/pallas_call | solution.py:111
  43.3 0.1 collective-permute-start.6
  43.4 0.0 collective-permute-done.3.refs_1_
  43.4 0.7 copy-done.1
  44.1 0.2 shard_map.157
  44.2 0.0 copy-start.2
  44.2 1.8 %collective-permute-start.4 = (bf16[2,2,80,384]{3,2,1,0:T(8,128)(2,1)S(1)}, bf16[2,2,80,384]{3,2,1,0:T(8,128)(2,1)S(1)}, u32[]{:S(2)}, u32[]{:S(2)}) collective-permute-start(bf16[2,2,80,384]{3,2,1,0:T(8,128)(2,1)S(1)} %get-tuple-element.56), channel_id=1, source_target_pairs={{0,16},{1,17},{2,18},{3,19},{4,20},{5,21},{6,22},{7,23},{8,24},{9,... | collective-permute-start | bytes 737288 | tf_op jit(solution)/shard_map/ppermute | solution.py:567
  46.0 2.4 %collective-permute-start.5 = (bf16[2,2,80,384]{3,2,1,0:T(8,128)(2,1)S(1)}, bf16[2,2,80,384]{3,2,1,0:T(8,128)(2,1)S(1)}, u32[]{:S(2)}, u32[]{:S(2)}) collective-permute-start(bf16[2,2,80,384]{3,2,1,0:T(8,128)(2,1)S(1)} %get-tuple-element.58), channel_id=1, source_target_pairs={{0,2},{1,3},{2,0},{3,1},{4,6},{5,7},{6,4},{7,5},{8,10},{9,11},{10,... | collective-permute-start | bytes 737288 | tf_op jit(solution)/shard_map/ppermute | solution.py:567
  48.5 2.7 %fusion.1.refs_7_ = bf16[2,1280]{1,0:T(2,128)(2,1)S(1)} fusion(bf16[1280,1280]{1,0:T(8,128)(2,1)} %param.17, bf16[320,1280]{1,0:T(8,128)(2,1)S(1)} %copy-done.8, bf16[2,160]{1,0:T(2,128)(2,1)S(1)} %get-tuple-element.82, bf16[2,160]{1,0:T(2,128)(2,1)S(1)} %get-tuple-element.81), kind=kOutput, calls=%fused_computation.4 | convolution fusion | flops 8220160 | bytes 4102400 | tf_op jit(solution)/shard_map/dot_general | solution.py:562
  51.2 0.0 collective-permute-done.6.refs_5_
  51.2 1.4 %collective-permute-done.4.refs_0_ = bf16[2,2,80,384]{3,2,1,0:T(8,128)(2,1)S(1)} collective-permute-done((bf16[2,2,80,384]{3,2,1,0:T(8,128)(2,1)S(1)}, bf16[2,2,80,384]{3,2,1,0:T(8,128)(2,1)S(1)}, u32[]{:S(2)}, u32[]{:S(2)}) %collective-permute-start.4) | collective-permute-done | bytes 245792 | tf_op jit(solution)/shard_map/ppermute | solution.py:567
  52.7 2.1 %collective-permute-done.5.refs_2_ = bf16[2,2,80,384]{3,2,1,0:T(8,128)(2,1)S(1)} collective-permute-done((bf16[2,2,80,384]{3,2,1,0:T(8,128)(2,1)S(1)}, bf16[2,2,80,384]{3,2,1,0:T(8,128)(2,1)S(1)}, u32[]{:S(2)}, u32[]{:S(2)}) %collective-permute-start.5) | collective-permute-done | bytes 245792 | tf_op jit(solution)/shard_map/ppermute | solution.py:567
  54.8 0.1 shard_map.158
  54.9 1.8 %collective-permute-start.7 = (bf16[2,80,384]{2,1,0:T(8,128)(2,1)S(1)}, bf16[2,80,384]{2,1,0:T(8,128)(2,1)S(1)}, u32[]{:S(2)}, u32[]{:S(2)}) collective-permute-start(bf16[2,80,384]{2,1,0:T(8,128)(2,1)S(1)} %get-tuple-element.60), channel_id=1, source_target_pairs={{0,2},{1,3},{2,0},{3,1},{4,6},{5,7},{6,4},{7,5},{8,10},{9,11},{10,... | collective-permute-start | bytes 368648 | tf_op jit(solution)/shard_map/ppermute | solution.py:567
  56.7 0.4 collective-permute-start.8
  57.1 0.3 collective-permute-start.9
  57.3 2.1 %fusion.22.refs_5_ = f32[2,320]{1,0:T(2,128)} fusion(bf16[2,1280]{1,0:T(2,128)(2,1)S(1)} %fusion.1.refs_7_, bf16[1280,320]{0,1:T(8,128)(2,1)} %param.18), kind=kOutput, calls=%fused_computation.20 | convolution fusion | flops 1638400 | bytes 826880 | tf_op jit(solution)/shard_map/dot_general | solution.py:698
  59.4 1.4 %collective-permute-done.9.refs_5_ = f32[8,320]{1,0:T(8,128)S(1)} collective-permute-done((f32[8,320]{1,0:T(8,128)S(1)}, f32[8,320]{1,0:T(8,128)S(1)}, u32[]{:S(2)}, u32[]{:S(2)}) %collective-permute-start.9) | collective-permute-done | bytes 10272 | tf_op jit(solution)/shard_map/ppermute | solution.py:567
  60.7 0.0 collective-permute-done.7.refs_0_
  60.8 0.8 collective-permute-done.8.refs_2_
  61.6 0.1 shard_map.159
  61.7 0.0 copy-start.3
  61.7 0.6 copy-done.3
  62.3 1.7 %collective-permute-start.10 = (bf16[96,384]{1,0:T(8,128)(2,1)S(1)}, bf16[96,384]{1,0:T(8,128)(2,1)S(1)}, u32[]{:S(2)}, u32[]{:S(2)}) collective-permute-start(bf16[96,384]{1,0:T(8,128)(2,1)S(1)} %get-tuple-element.69), channel_id=1, source_target_pairs={{0,4},{1,5},{2,6},{3,7},{4,0},{5,1},{6,2},{7,3},{8,12},{9,13},{10,... | collective-permute-start | bytes 221192 | tf_op jit(solution)/shard_map/ppermute | solution.py:567
  63.9 2.0 %collective-permute-start.11 = (bf16[96,384]{1,0:T(8,128)(2,1)S(1)}, bf16[96,384]{1,0:T(8,128)(2,1)S(1)}, u32[]{:S(2)}, u32[]{:S(2)}) collective-permute-start(bf16[96,384]{1,0:T(8,128)(2,1)S(1)} %get-tuple-element.70), channel_id=1, source_target_pairs={{0,8},{1,9},{2,10},{3,11},{4,12},{5,13},{6,14},{7,15},{8,0},{9,1},... | collective-permute-start | bytes 221192 | tf_op jit(solution)/shard_map/ppermute | solution.py:567
  66.0 0.7 collective-permute-start.12
  66.6 7.9 %shard_map.160 = (bf16[1024,320]{1,0:T(8,128)(2,1)}, f32[8,128]{1,0:T(8,128)}) custom-call(bf16[9,320,320]{2,1,0:T(8,128)(2,1)} %bitcast.26, bf16[512,2880]{1,0:T(8,128)(2,1)} %get-tuple-element.48.refs_1_, bf16[512,2880]{1,0:T(8,128)(2,1)} %get-tuple-element.49.refs_2_, bf16[1024,320]{1,0:T(8,128)(2,1)} %bitcast.19, f32[320]{0:T(512)} %refs_4_.1, ...), custom_call_target="tpu_custom_call" | custom-call | flops 1887436800 | bytes 2000000 | tf_op jit(solution)/shard_map/pallas_call | solution.py:111
  74.5 0.0 collective-permute-done.10.refs_2_
  74.6 0.0 collective-permute-done.11.refs_3_
  74.6 0.0 copy-start.7
  74.6 0.7 copy-done.7
  75.3 0.0 copy-start.5
  75.3 1.2 %collective-permute-start.14 = (bf16[80,384]{1,0:T(8,128)(2,1)S(1)}, bf16[80,384]{1,0:T(8,128)(2,1)S(1)}, u32[]{:S(2)}, u32[]{:S(2)}) collective-permute-start(bf16[80,384]{1,0:T(8,128)(2,1)S(1)} %get-tuple-element.75.refs_0_), channel_id=1, source_target_pairs={{0,2},{1,3},{2,0},{3,1},{4,6},{5,7},{6,4},{7,5},{8,10},{9,11},{10,... | collective-permute-start | bytes 184328 | tf_op jit(solution)/shard_map/ppermute | solution.py:567
  76.5 0.9 collective-permute-start.15
  77.4 0.9 collective-permute-start.13
  78.2 1.5 %collective-permute-start.16 = (bf16[80,384]{1,0:T(8,128)(2,1)S(1)}, bf16[80,384]{1,0:T(8,128)(2,1)S(1)}, u32[]{:S(2)}, u32[]{:S(2)}) collective-permute-start(bf16[80,384]{1,0:T(8,128)(2,1)S(1)} %get-tuple-element.75.refs_0_), channel_id=1, source_target_pairs={{0,6},{1,7},{2,4},{3,5},{4,2},{5,3},{6,0},{7,1},{8,14},{9,15},{10,... | collective-permute-start | bytes 184328 | tf_op jit(solution)/shard_map/ppermute | solution.py:567
  79.7 2.0 %collective-permute-start.17 = (bf16[80,384]{1,0:T(8,128)(2,1)S(1)}, bf16[80,384]{1,0:T(8,128)(2,1)S(1)}, u32[]{:S(2)}, u32[]{:S(2)}) collective-permute-start(bf16[80,384]{1,0:T(8,128)(2,1)S(1)} %get-tuple-element.75.refs_0_), channel_id=1, source_target_pairs={{0,8},{1,9},{2,10},{3,11},{4,12},{5,13},{6,14},{7,15},{8,0},{9,1},... | collective-permute-start | bytes 184328 | tf_op jit(solution)/shard_map/ppermute | solution.py:567
  81.7 0.0 collective-permute-done.13.refs_6_
  81.7 2.6 %collective-permute-start.18 = (bf16[80,384]{1,0:T(8,128)(2,1)S(1)}, bf16[80,384]{1,0:T(8,128)(2,1)S(1)}, u32[]{:S(2)}, u32[]{:S(2)}) collective-permute-start(bf16[80,384]{1,0:T(8,128)(2,1)S(1)} %get-tuple-element.75.refs_0_), channel_id=1, source_target_pairs={{0,10},{1,11},{2,8},{3,9},{4,14},{5,15},{6,12},{7,13},{8,2},{9,3},... | collective-permute-start | bytes 184328 | tf_op jit(solution)/shard_map/ppermute | solution.py:567
  84.3 0.0 collective-permute-done.14.refs_1_
  84.3 2.7 %collective-permute-start.19 = (bf16[80,384]{1,0:T(8,128)(2,1)S(1)}, bf16[80,384]{1,0:T(8,128)(2,1)S(1)}, u32[]{:S(2)}, u32[]{:S(2)}) collective-permute-start(bf16[80,384]{1,0:T(8,128)(2,1)S(1)} %get-tuple-element.75.refs_0_), channel_id=1, source_target_pairs={{0,12},{1,13},{2,14},{3,15},{4,8},{5,9},{6,10},{7,11},{8,4},{9,5},... | collective-permute-start | bytes 184328 | tf_op jit(solution)/shard_map/ppermute | solution.py:567
  87.0 0.0 collective-permute-done.15.refs_2_
  87.0 2.3 %collective-permute-start.20 = (bf16[80,384]{1,0:T(8,128)(2,1)S(1)}, bf16[80,384]{1,0:T(8,128)(2,1)S(1)}, u32[]{:S(2)}, u32[]{:S(2)}) collective-permute-start(bf16[80,384]{1,0:T(8,128)(2,1)S(1)} %get-tuple-element.75.refs_0_), channel_id=1, source_target_pairs={{0,14},{1,15},{2,12},{3,13},{4,10},{5,11},{6,8},{7,9},{8,6},{9,7},... | collective-permute-start | bytes 184328 | tf_op jit(solution)/shard_map/ppermute | solution.py:567
  89.3 4.6 %shard_map.162 = (f32[1024,320]{1,0:T(8,128)}, f32[320]{0:T(512)}, f32[320]{0:T(512)}, f32[320]{0:T(512)}, f32[320,1280]{1,0:T(8,128)}, /*index=5*/f32[8,128]{1,0:T(8,128)}) custom-call(bf16[1024,320]{1,0:T(8,128)(2,1)} %bitcast.20, bf16[1024,320]{1,0:T(8,128)(2,1)} %bitcast.23, f32[1024,320]{1,0:T(8,128)} %get-tuple-element.67.refs_2_, f32[320]{0:T(512)} %refs_3_.3, ...), custom_call_target="tpu_custom_call" | custom-call | flops 2621440 | bytes 2000000 | tf_op jit(solution)/shard_map/pallas_call | solution.py:111
  94.0 0.0 collective-permute-done.16.refs_3_
  94.0 0.7 copy-done.6
  94.7 0.1 shard_map.163.refs_0_
  94.7 0.1 collective-permute-start.21
  94.8 1.9 %collective-permute-done.21.refs_1_ = bf16[80,3072]{1,0:T(8,128)(2,1)S(1)} collective-permute-done((bf16[80,3072]{1,0:T(8,128)(2,1)S(1)}, bf16[80,3072]{1,0:T(8,128)(2,1)S(1)}, u32[]{:S(2)}, u32[]{:S(2)}) %collective-permute-start.21) | collective-permute-done | bytes 491552 | tf_op jit(solution)/shard_map/ppermute | solution.py:567
  96.7 1.9 %shard_map.164 = f32[9,160,320]{2,1,0:T(8,128)} custom-call(bf16[80,3072]{1,0:T(8,128)(2,1)S(1)} %shard_map.163.refs_0_, bf16[80,3072]{1,0:T(8,128)(2,1)S(1)} %collective-permute-done.21.refs_1_), custom_call_target="tpu_custom_call" | custom-call | bytes 2000000 | tf_op jit(solution)/shard_map/pallas_call | solution.py:53
  (25 shorter events, 0.1 us)
Async XLA Ops:
  1.4 4.9 %collective-permute-start = (bf16[32,320]{1,0:T(8,128)(2,1)S(1)}, bf16[32,320]{1,0:T(8,128)(2,1)}, u32[]{:S(2)}, u32[]{:S(2)}) collective-permute-start(bf16[32,320]{1,0:T(8,128)(2,1)S(1)} %maximum_bitcast_fusion), channel_id=1, source_target_pairs={{0,16},{1,17},{2,18},{3,19},{4,20},{5,21},{6,22},{7,23},{8,24},{9,... | collective-permute-start | bytes 61448 | tf_op jit(solution)/shard_map/ppermute | solution.py:567
  9.6 12.1 %collective-permute-start.1 = (f32[4,66,1,320]{3,2,1,0:T(1,128)}, f32[4,66,1,320]{3,2,1,0:T(1,128)}, u32[]{:S(2)}, u32[]{:S(2)}) collective-permute-start(f32[4,66,1,320]{3,2,1,0:T(1,128)} %get-tuple-element.44), channel_id=1, source_target_pairs={{0,1},{1,2},{2,3},{3,4},{4,5},{5,6},{6,7},{7,8},{8,9},{9,10},{10,1... | collective-permute-start | bytes 1013768 | tf_op jit(solution)/shard_map/ppermute | solution.py:578
  11.7 10.0 %collective-permute-start.2 = (f32[4,66,1,320]{3,2,1,0:T(1,128)}, f32[4,66,1,320]{3,2,1,0:T(1,128)}, u32[]{:S(2)}, u32[]{:S(2)}) collective-permute-start(f32[4,66,1,320]{3,2,1,0:T(1,128)} %get-tuple-element.45), channel_id=1, source_target_pairs={{1,0},{2,1},{3,2},{4,3},{5,4},{6,5},{7,6},{8,7},{9,8},{10,9},{11,1... | collective-permute-start | bytes 1013768 | tf_op jit(solution)/shard_map/ppermute | solution.py:578
  13.0 15.6 %all-to-all-start = ((f32[32,1,128]{2,1,0:T(1,128)}), f32[32,1,128]{2,1,0:T(1,128)}, u32[]{:S(2)}, u32[]{:S(2)}) async-start(f32[32,1,128]{2,1,0:T(1,128)} %get-tuple-element.47), calls=%async_computation | async-start | bytes 32768 | tf_op jit(solution)/shard_map/all_to_all | solution.py:629
  28.6 10.5 %copy-start.11 = (s32[2]{0:T(128)S(1)}, s32[2]{0:T(128)}, u32[]{:S(2)}) copy-start(s32[2]{0:T(128)} %param.11) | copy-start | bytes 28
  37.6 5.8 %collective-permute-start.3 = (bf16[2,8,80,384]{3,2,1,0:T(8,128)(2,1)}, bf16[2,8,80,384]{3,2,1,0:T(8,128)(2,1)S(1)}, u32[]{:S(2)}, u32[]{:S(2)}) collective-permute-start(bf16[2,8,80,384]{3,2,1,0:T(8,128)(2,1)} %bitcast.29), channel_id=1, source_target_pairs={{0,1},{1,0},{2,3},{3,2},{4,5},{5,4},{6,7},{7,6},{8,9},{9,8},{10,11... | collective-permute-start | bytes 2949128 | tf_op jit(solution)/shard_map/ppermute | solution.py:567
  39.3 4.1 %copy-start = (f32[2,8,80,384]{3,2,1,0:T(8,128)S(1)}, f32[2,8,80,384]{3,2,1,0:T(8,128)}, u32[]{:S(2)}) copy-start(f32[2,8,80,384]{3,2,1,0:T(8,128)} %get-tuple-element.50.refs_0_) | copy-start | bytes 5898244
  39.3 9.2 %copy-start.8 = (bf16[320,1280]{1,0:T(8,128)(2,1)S(1)}, bf16[320,1280]{1,0:T(8,128)(2,1)}, u32[]{:S(2)}) copy-start(bf16[320,1280]{1,0:T(8,128)(2,1)} %param.16) | copy-start | bytes 2457604
  43.3 8.0 %collective-permute-start.6 = (f32[8,320]{1,0:T(8,128)}, f32[8,320]{1,0:T(8,128)S(1)}, u32[]{:S(2)}, u32[]{:S(2)}) collective-permute-start(f32[8,320]{1,0:T(8,128)} %get-tuple-element.55.refs_2_.refs_4_), channel_id=1, source_target_pairs={{0,1},{1,0},{2,3},{3,2},{4,5},{5,4},{6,7},{7,6},{8,9},{9,8},{10,11... | collective-permute-start | bytes 30728 | tf_op jit(solution)/shard_map/ppermute | solution.py:567
  43.4 0.7 copy-start.1
  44.2 10.5 %copy-start.2 = (f32[8,320]{1,0:T(8,128)S(1)}, f32[8,320]{1,0:T(8,128)}, u32[]{:S(2)}) copy-start(f32[8,320]{1,0:T(8,128)} %get-tuple-element.55.refs_2_.refs_4_) | copy-start | bytes 30724
  44.2 8.4 %collective-permute-start.4 = (bf16[2,2,80,384]{3,2,1,0:T(8,128)(2,1)S(1)}, bf16[2,2,80,384]{3,2,1,0:T(8,128)(2,1)S(1)}, u32[]{:S(2)}, u32[]{:S(2)}) collective-permute-start(bf16[2,2,80,384]{3,2,1,0:T(8,128)(2,1)S(1)} %get-tuple-element.56), channel_id=1, source_target_pairs={{0,16},{1,17},{2,18},{3,19},{4,20},{5,21},{6,22},{7,23},{8,24},{9,... | collective-permute-start | bytes 737288 | tf_op jit(solution)/shard_map/ppermute | solution.py:567
  46.0 8.7 %collective-permute-start.5 = (bf16[2,2,80,384]{3,2,1,0:T(8,128)(2,1)S(1)}, bf16[2,2,80,384]{3,2,1,0:T(8,128)(2,1)S(1)}, u32[]{:S(2)}, u32[]{:S(2)}) collective-permute-start(bf16[2,2,80,384]{3,2,1,0:T(8,128)(2,1)S(1)} %get-tuple-element.58), channel_id=1, source_target_pairs={{0,2},{1,3},{2,0},{3,1},{4,6},{5,7},{6,4},{7,5},{8,10},{9,11},{10,... | collective-permute-start | bytes 737288 | tf_op jit(solution)/shard_map/ppermute | solution.py:567
  51.2 23.3 %copy-start.9 = (bf16[2,1280]{1,0:T(2,128)(2,1)}, bf16[2,1280]{1,0:T(2,128)(2,1)S(1)}, u32[]{:S(2)}) copy-start(bf16[2,1280]{1,0:T(2,128)(2,1)S(1)} %fusion.1.refs_7_) | copy-start | bytes 15364
  54.9 5.9 %collective-permute-start.7 = (bf16[2,80,384]{2,1,0:T(8,128)(2,1)S(1)}, bf16[2,80,384]{2,1,0:T(8,128)(2,1)S(1)}, u32[]{:S(2)}, u32[]{:S(2)}) collective-permute-start(bf16[2,80,384]{2,1,0:T(8,128)(2,1)S(1)} %get-tuple-element.60), channel_id=1, source_target_pairs={{0,2},{1,3},{2,0},{3,1},{4,6},{5,7},{6,4},{7,5},{8,10},{9,11},{10,... | collective-permute-start | bytes 368648 | tf_op jit(solution)/shard_map/ppermute | solution.py:567
  56.7 4.9 %collective-permute-start.8 = (bf16[2,80,384]{2,1,0:T(8,128)(2,1)S(1)}, bf16[2,80,384]{2,1,0:T(8,128)(2,1)S(1)}, u32[]{:S(2)}, u32[]{:S(2)}) collective-permute-start(bf16[2,80,384]{2,1,0:T(8,128)(2,1)S(1)} %get-tuple-element.62), channel_id=1, source_target_pairs={{0,16},{1,17},{2,18},{3,19},{4,20},{5,21},{6,22},{7,23},{8,24},{9,... | collective-permute-start | bytes 368648 | tf_op jit(solution)/shard_map/ppermute | solution.py:567
  57.1 3.7 %collective-permute-start.9 = (f32[8,320]{1,0:T(8,128)S(1)}, f32[8,320]{1,0:T(8,128)S(1)}, u32[]{:S(2)}, u32[]{:S(2)}) collective-permute-start(f32[8,320]{1,0:T(8,128)S(1)} %get-tuple-element.64.refs_4_), channel_id=1, source_target_pairs={{0,2},{1,3},{2,0},{3,1},{4,6},{5,7},{6,4},{7,5},{8,10},{9,11},{10,... | collective-permute-start | bytes 30728 | tf_op jit(solution)/shard_map/ppermute | solution.py:567
  61.7 0.6 copy-start.3
  62.3 12.3 %collective-permute-start.10 = (bf16[96,384]{1,0:T(8,128)(2,1)S(1)}, bf16[96,384]{1,0:T(8,128)(2,1)S(1)}, u32[]{:S(2)}, u32[]{:S(2)}) collective-permute-start(bf16[96,384]{1,0:T(8,128)(2,1)S(1)} %get-tuple-element.69), channel_id=1, source_target_pairs={{0,4},{1,5},{2,6},{3,7},{4,0},{5,1},{6,2},{7,3},{8,12},{9,13},{10,... | collective-permute-start | bytes 221192 | tf_op jit(solution)/shard_map/ppermute | solution.py:567
  63.9 10.6 %collective-permute-start.11 = (bf16[96,384]{1,0:T(8,128)(2,1)S(1)}, bf16[96,384]{1,0:T(8,128)(2,1)S(1)}, u32[]{:S(2)}, u32[]{:S(2)}) collective-permute-start(bf16[96,384]{1,0:T(8,128)(2,1)S(1)} %get-tuple-element.70), channel_id=1, source_target_pairs={{0,8},{1,9},{2,10},{3,11},{4,12},{5,13},{6,14},{7,15},{8,0},{9,1},... | collective-permute-start | bytes 221192 | tf_op jit(solution)/shard_map/ppermute | solution.py:567
  66.0 8.6 %collective-permute-start.12 = (bf16[96,384]{1,0:T(8,128)(2,1)S(1)}, bf16[96,384]{1,0:T(8,128)(2,1)S(1)}, u32[]{:S(2)}, u32[]{:S(2)}) collective-permute-start(bf16[96,384]{1,0:T(8,128)(2,1)S(1)} %get-tuple-element.71), channel_id=1, source_target_pairs={{0,12},{1,13},{2,14},{3,15},{4,8},{5,9},{6,10},{7,11},{8,4},{9,5},... | collective-permute-start | bytes 221192 | tf_op jit(solution)/shard_map/ppermute | solution.py:567
  66.6 7.9 %copy-start.4 = (f32[8,320]{1,0:T(8,128)S(1)}, f32[8,320]{1,0:T(8,128)}, u32[]{:S(2)}) copy-start(f32[8,320]{1,0:T(8,128)} %copy-done.3) | copy-start | bytes 30724
  74.6 0.7 copy-start.7
  75.3 14.0 %copy-start.5 = (f32[8,320]{1,0:T(8,128)}, f32[8,320]{1,0:T(8,128)S(1)}, u32[]{:S(2)}) copy-start(f32[8,320]{1,0:T(8,128)S(1)} %get-tuple-element.73.refs_5_) | copy-start | bytes 30724
  75.3 9.0 %collective-permute-start.14 = (bf16[80,384]{1,0:T(8,128)(2,1)S(1)}, bf16[80,384]{1,0:T(8,128)(2,1)S(1)}, u32[]{:S(2)}, u32[]{:S(2)}) collective-permute-start(bf16[80,384]{1,0:T(8,128)(2,1)S(1)} %get-tuple-element.75.refs_0_), channel_id=1, source_target_pairs={{0,2},{1,3},{2,0},{3,1},{4,6},{5,7},{6,4},{7,5},{8,10},{9,11},{10,... | collective-permute-start | bytes 184328 | tf_op jit(solution)/shard_map/ppermute | solution.py:567
  76.5 10.5 %collective-permute-start.15 = (bf16[80,384]{1,0:T(8,128)(2,1)S(1)}, bf16[80,384]{1,0:T(8,128)(2,1)S(1)}, u32[]{:S(2)}, u32[]{:S(2)}) collective-permute-start(bf16[80,384]{1,0:T(8,128)(2,1)S(1)} %get-tuple-element.75.refs_0_), channel_id=1, source_target_pairs={{0,4},{1,5},{2,6},{3,7},{4,0},{5,1},{6,2},{7,3},{8,12},{9,13},{10,... | collective-permute-start | bytes 184328 | tf_op jit(solution)/shard_map/ppermute | solution.py:567
  77.4 4.4 %collective-permute-start.13 = (f32[8,320]{1,0:T(8,128)S(1)}, f32[8,320]{1,0:T(8,128)S(1)}, u32[]{:S(2)}, u32[]{:S(2)}) collective-permute-start(f32[8,320]{1,0:T(8,128)S(1)} %get-tuple-element.73.refs_5_), channel_id=1, source_target_pairs={{0,16},{1,17},{2,18},{3,19},{4,20},{5,21},{6,22},{7,23},{8,24},{9,... | collective-permute-start | bytes 30728 | tf_op jit(solution)/shard_map/ppermute | solution.py:567
  78.2 15.7 %collective-permute-start.16 = (bf16[80,384]{1,0:T(8,128)(2,1)S(1)}, bf16[80,384]{1,0:T(8,128)(2,1)S(1)}, u32[]{:S(2)}, u32[]{:S(2)}) collective-permute-start(bf16[80,384]{1,0:T(8,128)(2,1)S(1)} %get-tuple-element.75.refs_0_), channel_id=1, source_target_pairs={{0,6},{1,7},{2,4},{3,5},{4,2},{5,3},{6,0},{7,1},{8,14},{9,15},{10,... | collective-permute-start | bytes 184328 | tf_op jit(solution)/shard_map/ppermute | solution.py:567
  79.7 14.2 %collective-permute-start.17 = (bf16[80,384]{1,0:T(8,128)(2,1)S(1)}, bf16[80,384]{1,0:T(8,128)(2,1)S(1)}, u32[]{:S(2)}, u32[]{:S(2)}) collective-permute-start(bf16[80,384]{1,0:T(8,128)(2,1)S(1)} %get-tuple-element.75.refs_0_), channel_id=1, source_target_pairs={{0,8},{1,9},{2,10},{3,11},{4,12},{5,13},{6,14},{7,15},{8,0},{9,1},... | collective-permute-start | bytes 184328 | tf_op jit(solution)/shard_map/ppermute | solution.py:567
  81.7 7.6 %copy-start.10 = (f32[8,320]{1,0:T(8,128)}, f32[8,320]{1,0:T(8,128)S(1)}, u32[]{:S(2)}) copy-start(f32[8,320]{1,0:T(8,128)S(1)} %collective-permute-done.13.refs_6_) | copy-start | bytes 30724
  81.7 12.2 %collective-permute-start.18 = (bf16[80,384]{1,0:T(8,128)(2,1)S(1)}, bf16[80,384]{1,0:T(8,128)(2,1)S(1)}, u32[]{:S(2)}, u32[]{:S(2)}) collective-permute-start(bf16[80,384]{1,0:T(8,128)(2,1)S(1)} %get-tuple-element.75.refs_0_), channel_id=1, source_target_pairs={{0,10},{1,11},{2,8},{3,9},{4,14},{5,15},{6,12},{7,13},{8,2},{9,3},... | collective-permute-start | bytes 184328 | tf_op jit(solution)/shard_map/ppermute | solution.py:567
  84.3 9.7 %collective-permute-start.19 = (bf16[80,384]{1,0:T(8,128)(2,1)S(1)}, bf16[80,384]{1,0:T(8,128)(2,1)S(1)}, u32[]{:S(2)}, u32[]{:S(2)}) collective-permute-start(bf16[80,384]{1,0:T(8,128)(2,1)S(1)} %get-tuple-element.75.refs_0_), channel_id=1, source_target_pairs={{0,12},{1,13},{2,14},{3,15},{4,8},{5,9},{6,10},{7,11},{8,4},{9,5},... | collective-permute-start | bytes 184328 | tf_op jit(solution)/shard_map/ppermute | solution.py:567
  87.0 7.0 %collective-permute-start.20 = (bf16[80,384]{1,0:T(8,128)(2,1)S(1)}, bf16[80,384]{1,0:T(8,128)(2,1)S(1)}, u32[]{:S(2)}, u32[]{:S(2)}) collective-permute-start(bf16[80,384]{1,0:T(8,128)(2,1)S(1)} %get-tuple-element.75.refs_0_), channel_id=1, source_target_pairs={{0,14},{1,15},{2,12},{3,13},{4,10},{5,11},{6,8},{7,9},{8,6},{9,7},... | collective-permute-start | bytes 184328 | tf_op jit(solution)/shard_map/ppermute | solution.py:567
  94.0 0.7 copy-start.6
  94.7 1.9 %collective-permute-start.21 = (bf16[80,3072]{1,0:T(8,128)(2,1)S(1)}, bf16[80,3072]{1,0:T(8,128)(2,1)S(1)}, u32[]{:S(2)}, u32[]{:S(2)}) collective-permute-start(bf16[80,3072]{1,0:T(8,128)(2,1)S(1)} %shard_map.163.refs_0_), channel_id=1, source_target_pairs={{0,1},{1,0},{2,3},{3,2},{4,5},{5,4},{6,7},{7,6},{8,9},{9,8},{10,11... | collective-permute-start | bytes 1474568 | tf_op jit(solution)/shard_map/ppermute | solution.py:567
